TPU v7x, 128 devices: a whole 4x4x4 slice. The times are simulated.
128 devices in a mesh: tile: 64 (over y, x, z_lo, core), mem: 2 (over z_hi).
Axes of the slice: x: 4, y: 4, z: 4 (z_hi: 2, z_lo: 2; z = z_hi * 2 + z_lo), core: 2. Of those that a mesh axis runs over, the one named last changes fastest.
Arguments:
- fields: float32 [52, 4, 512, 640], P('mem', None, 'tile'), may hold values from 0 to 150, as said below
- scaling: float32 [52, 4, 512, 640], P('mem', None, 'tile'), may hold values from 0.5 to 2, as said below
- counts: int32 [52], P('mem'), may hold values from 1 to 8
- land_mask: int32 [512, 640], P('tile'), may hold values 0 or 1
Outputs:
- barycenter: float32 [4, 512, 640], P(None, 'tile')
- updated: float32 [52, 4, 512, 640], P('mem', None, 'tile')
Inputs may be any that keep to these rules, and one draw needn't show every extreme that they name: `fields`: positive cloud-water amounts. Positive scaling fields.
All inputs are finite; a program needn't handle non-finite values. No bound on the sum of `land_mask` on one device may be relied on, other than what follows from the above.
Results may differ from a plain program's by a relative error of at most 0.0028.
Values sent between devices are 32-bit elements; how exact they have to be, the bound alone decides.
No kernel may reach another device: no remote copies, remote signals or barrier semaphores. Data moves between devices by JAX's collectives and lax.ppermute only.
A program may use at most 128 MiB of HBM per device.

v0:
```python
import math

import jax
import jax.numpy as jnp
from jax import lax
from jax.sharding import PartitionSpec as P

BACKGROUND = 0.01


def with_halo(cells, sides, width):
    for axis, dim in sides:
        count = lax.axis_size(axis)
        head = lax.slice_in_dim(cells, 0, width, axis=dim)
        tail = lax.slice_in_dim(cells, cells.shape[dim] - width, cells.shape[dim], axis=dim)
        cells = jnp.concatenate(
            [
                lax.ppermute(tail, axis, [(i, (i + 1) % count) for i in range(count)]),
                cells,
                lax.ppermute(head, axis, [((i + 1) % count, i) for i in range(count)]),
            ],
            axis=dim,
        )
    return cells


def coefficients(lat_cells):
    row_index = jnp.arange(lat_cells)
    spacing = math.pi / lat_cells
    latitude = -0.5 * math.pi + (row_index.astype(jnp.float32) + 0.5) * spacing
    cell_area = jnp.cos(latitude)
    zonal_coef = 0.2 * jnp.minimum(2.2, 1.0 / (cell_area * cell_area))
    north_coef = jnp.where(
        row_index == lat_cells - 1, 0.0, 0.05 * jnp.cos(latitude + 0.5 * spacing) / cell_area
    )
    south_coef = jnp.where(
        row_index == 0, 0.0, 0.05 * jnp.cos(latitude - 0.5 * spacing) / cell_area
    )
    return (cell_area, zonal_coef, north_coef, south_coef)


def diffuse_padded(padded, coefs):
    cell_area, zonal_coef, north_coef, south_coef = coefs
    middle = padded[:, :, 1:-1, :]
    eastern = padded[:, :, 2:, :]
    western = padded[:, :, :-2, :]
    zeros_row = jnp.zeros_like(middle[..., :1])
    northern = jnp.concatenate([middle[..., 1:], zeros_row], axis=-1)
    southern = jnp.concatenate([zeros_row, middle[..., :-1]], axis=-1)
    return (
        middle
        + zonal_coef * (eastern + western - 2.0 * middle)
        + north_coef * (northern - middle)
        + south_coef * (southern - middle)
    )


def kernel(values, coefs):
    for repeat in range(4):
        padded = with_halo(values, (("tile", 2),), 1)
        values = diffuse_padded(padded, coefs)
    return values


def body(fields, scaling, counts, land_mask):
    lon_cells = fields.shape[2]
    lat_cells = fields.shape[3]
    cell_count = lon_cells * lax.axis_size("tile") * lat_cells
    coefs = coefficients(lat_cells)
    cell_area = coefs[0]
    weights = counts.astype(jnp.float32)
    filled = jnp.where(land_mask[None, None] == 1, fields, 0.0) + BACKGROUND
    local_mass = jnp.sum(filled * cell_area, axis=(2, 3))
    masses = lax.psum(local_mass, "tile") / cell_count
    divisor = masses[:, :, None, None]
    density = filled / divisor
    smoothed = kernel(cell_area * scaling, coefs)
    returned = scaling * kernel(cell_area * density / smoothed, coefs)
    log_terms = jnp.log(returned)
    weighted = jnp.einsum("m,mlxy->lxy", weights, log_terms)
    log_sum, count_sum = lax.psum((weighted, jnp.sum(weights)), "mem")
    merged = jnp.exp(log_sum / count_sum)
    level_mass = lax.psum(jnp.sum(merged * cell_area, axis=(1, 2)), "tile") / cell_count
    barycenter = merged / level_mass[:, None, None]
    updated = scaling * barycenter / returned
    return (barycenter, updated)


def solution(mesh):
    return jax.shard_map(
        body,
        mesh=mesh,
        in_specs=(
            P("mem", None, "tile", None),
            P("mem", None, "tile", None),
            P("mem"),
            P("tile", None),
        ),
        out_specs=(P(None, "tile", None), P("mem", None, "tile", None)),
        check_vma=False,
    )
```

profile of v0, /device:TPU:1, one launch (start us, length us, event | category | flops | bytes accessed | tf_op | source)
XLA Modules:
  0.0 444.1 jit_solution(819403827837322056)
XLA Ops:
  7.2 0.0 all-reduce.18.cloned.1.call-start
  7.3 0.7 broadcast_compare_fusion
  8.0 4.9 %multiply_reduce_fusion = (f32[26,4]{0,1:T(4,128)S(1)}, f32[26,4,8,640]{3,0,2,1:T(8,128)S(1)}) fusion(f32[26,4,8,640]{3,2,1,0:T(8,128)} %param.4, f32[640]{0:T(1024)S(1)} %add_cosine_fusion, pred[8,640]{1,0:T(8,128)(4,1)S(1)} %broadcast_compare_fusion, f32[26,4,8,640]{3,2,1,0:T(8,128)} %param.5), kind=kLoop, calls=%fused_computation.73 | loop fusion | flops 2662296 | bytes 6397856 | tf_op jit(solution)/shard_map/reduce_sum | solution.py:73
  12.9 0.9 fusion.70
  13.8 1.4 collective-permute-start
  15.2 1.6 collective-permute-start.1
  16.8 0.1 divide_select_fusion
  16.9 3.2 fusion.69
  20.2 142.3 %psum.28 = f32[26,4]{0,1:T(4,128)S(1)} all-reduce(f32[26,4]{0,1:T(4,128)S(1)} %get-tuple-element.36), channel_id=1, replica_groups=mesh['tile'=64,'mem'=2] {'tile'}, use_global_device_ids=true, to_apply=%region_1.2 | all-reduce | flops 104 | bytes 832 | tf_op jit(solution)/shard_map/psum | solution.py:74
  162.5 0.0 collective-permute-done
  162.5 0.0 collective-permute-done.1
  162.5 3.3 fusion.49
  165.8 6.7 %collective-permute-start.2 = (f32[26,4,1,640]{3,0,2,1:T(8,128)S(1)}, f32[26,4,1,640]{3,0,2,1:T(8,128)S(1)}, u32[]{:S(2)}, u32[]{:S(2)}) collective-permute-start(f32[26,4,1,640]{3,0,2,1:T(8,128)S(1)} %get-tuple-element.30), channel_id=1, source_target_pairs={{2,0},{4,2},{6,4},{8,6},{10,8},{12,10},{14,12},{16,14},{18,16},{20... | collective-permute-start | bytes 798728 | tf_op jit(solution)/shard_map/ppermute | solution.py:20
  172.5 0.0 collective-permute-start.3
  172.5 0.9 fusion.67
  173.4 0.3 collective-permute-done.2
  173.7 2.8 collective-permute-done.3
  176.5 1.6 fusion.43
  178.2 6.8 %collective-permute-start.4 = (f32[26,4,1,640]{3,0,2,1:T(8,128)S(1)}, f32[26,4,1,640]{3,0,2,1:T(8,128)S(1)}, u32[]{:S(2)}, u32[]{:S(2)}) collective-permute-start(f32[26,4,1,640]{3,0,2,1:T(8,128)S(1)} %get-tuple-element.26), channel_id=1, source_target_pairs={{2,0},{4,2},{6,4},{8,6},{10,8},{12,10},{14,12},{16,14},{18,16},{20... | collective-permute-start | bytes 798728 | tf_op jit(solution)/shard_map/ppermute | solution.py:20
  185.0 0.0 collective-permute-start.5
  185.0 0.9 fusion.65
  186.0 3.0 collective-permute-done.4
  189.0 0.1 collective-permute-done.5
  189.1 1.6 fusion.37
  190.7 6.9 %collective-permute-start.6 = (f32[26,4,1,640]{3,0,2,1:T(8,128)S(1)}, f32[26,4,1,640]{3,0,2,1:T(8,128)S(1)}, u32[]{:S(2)}, u32[]{:S(2)}) collective-permute-start(f32[26,4,1,640]{3,0,2,1:T(8,128)S(1)} %get-tuple-element.22), channel_id=1, source_target_pairs={{2,0},{4,2},{6,4},{8,6},{10,8},{12,10},{14,12},{16,14},{18,16},{20... | collective-permute-start | bytes 798728 | tf_op jit(solution)/shard_map/ppermute | solution.py:20
  197.7 0.0 collective-permute-start.7
  197.7 0.9 fusion.63
  198.6 0.3 collective-permute-done.6
  198.9 2.8 collective-permute-done.7
  201.7 2.9 fusion.31
  204.6 7.0 %collective-permute-start.8 = (f32[26,4,1,640]{3,0,2,1:T(8,128)S(1)}, f32[26,4,1,640]{3,0,2,1:T(8,128)S(1)}, u32[]{:S(2)}, u32[]{:S(2)}) collective-permute-start(f32[26,4,1,640]{3,0,2,1:T(8,128)S(1)} %get-tuple-element.18), channel_id=1, source_target_pairs={{2,0},{4,2},{6,4},{8,6},{10,8},{12,10},{14,12},{16,14},{18,16},{20... | collective-permute-start | bytes 798728 | tf_op jit(solution)/shard_map/ppermute | solution.py:20
  211.7 0.0 collective-permute-start.9
  211.7 0.9 fusion.61
  212.6 0.3 collective-permute-done.8
  212.9 2.8 collective-permute-done.9
  215.7 1.6 fusion.24
  217.4 6.9 %collective-permute-start.10 = (f32[26,4,1,640]{3,0,2,1:T(8,128)S(1)}, f32[26,4,1,640]{3,0,2,1:T(8,128)S(1)}, u32[]{:S(2)}, u32[]{:S(2)}) collective-permute-start(f32[26,4,1,640]{3,0,2,1:T(8,128)S(1)} %get-tuple-element.14), channel_id=1, source_target_pairs={{2,0},{4,2},{6,4},{8,6},{10,8},{12,10},{14,12},{16,14},{18,16},{20... | collective-permute-start | bytes 798728 | tf_op jit(solution)/shard_map/ppermute | solution.py:20
  224.3 0.9 fusion.59
  225.2 0.3 collective-permute-done.10
  225.5 2.8 collective-permute-done.11
  228.3 1.6 fusion.18
  230.0 6.9 %collective-permute-start.12 = (f32[26,4,1,640]{3,0,2,1:T(8,128)S(1)}, f32[26,4,1,640]{3,0,2,1:T(8,128)S(1)}, u32[]{:S(2)}, u32[]{:S(2)}) collective-permute-start(f32[26,4,1,640]{3,0,2,1:T(8,128)S(1)} %get-tuple-element.10), channel_id=1, source_target_pairs={{2,0},{4,2},{6,4},{8,6},{10,8},{12,10},{14,12},{16,14},{18,16},{20... | collective-permute-start | bytes 798728 | tf_op jit(solution)/shard_map/ppermute | solution.py:20
  236.9 0.9 fusion.57
  237.9 0.3 collective-permute-done.12
  238.2 2.8 collective-permute-done.13
  240.9 1.6 fusion.12
  242.6 6.9 %collective-permute-start.14 = (f32[26,4,1,640]{3,0,2,1:T(8,128)S(1)}, f32[26,4,1,640]{3,0,2,1:T(8,128)S(1)}, u32[]{:S(2)}, u32[]{:S(2)}) collective-permute-start(f32[26,4,1,640]{3,0,2,1:T(8,128)S(1)} %get-tuple-element.6), channel_id=1, source_target_pairs={{2,0},{4,2},{6,4},{8,6},{10,8},{12,10},{14,12},{16,14},{18,16},{20... | collective-permute-start | bytes 798728 | tf_op jit(solution)/shard_map/ppermute | solution.py:20
  249.5 0.0 collective-permute-start.15
  249.5 0.9 fusion.55
  250.5 0.3 collective-permute-done.14
  250.8 2.8 collective-permute-done.15
  253.6 2.7 copy_multiply_fusion.2
  256.3 0.5 fusion.51
  256.7 0.6 copy.26
  257.4 0.0 all-reduce.18.cloned.1.call-update
  257.4 0.6 convert_reduce_fusion
  258.0 6.2 %psum.30 = f32[]{:T(128)} all-reduce(f32[]{:T(128)} %convert_reduce_fusion), channel_id=1, replica_groups=mesh['tile'=64,'mem'=2] {'mem'}, use_global_device_ids=true, to_apply=%region_4.5 | all-reduce | flops 1 | bytes 8 | tf_op jit(solution)/shard_map/psum | solution.py:81
  264.2 25.2 %all-reduce.18.cloned.1.call-done = f32[4,8,640]{2,1,0:T(8,128)} async-done(((f32[4,8,640]{2,1,0:T(8,128)}), f32[4,8,640]{2,1,0:T(8,128)}) %all-reduce.18.cloned.1.call-update) | async-done | bytes 81936 | tf_op jit(solution)/shard_map/psum | solution.py:81
  289.4 1.7 multiply_reduce_fusion.1
  291.1 138.9 %psum.31 = f32[4]{0:T(128)S(1)} all-reduce(f32[4]{0:T(128)S(1)} %multiply_reduce_fusion.1), channel_id=1, replica_groups=mesh['tile'=64,'mem'=2] {'tile'}, use_global_device_ids=true, to_apply=%region_6.7 | all-reduce | flops 4 | bytes 32 | tf_op jit(solution)/shard_map/psum | solution.py:83
  430.0 1.6 broadcast_divide_fusion
  431.6 0.0 copy-start.2
  431.6 3.1 fusion
  434.7 2.6 copy.10
  (20 shorter events, 0.4 us)
Async XLA Ops:
  7.2 282.2 %all-reduce.18.cloned.1.call-start = ((), (), s32[]{:S(2)}) async-start(), calls=%async_computation | async-start | bytes 163840 | tf_op jit(solution)/shard_map/psum | solution.py:81
  13.8 148.7 %collective-permute-start = (f32[26,4,1,640]{3,0,2,1:T(8,128)}, f32[26,4,1,640]{3,0,2,1:T(8,128)S(1)}, u32[]{:S(2)}, u32[]{:S(2)}) collective-permute-start(f32[26,4,1,640]{3,0,2,1:T(8,128)} %get-tuple-element.34), channel_id=1, source_target_pairs={{2,0},{4,2},{6,4},{8,6},{10,8},{12,10},{14,12},{16,14},{18,16},{20... | collective-permute-start | bytes 798728 | tf_op jit(solution)/shard_map/ppermute | solution.py:20
  15.2 147.3 %collective-permute-start.1 = (f32[26,4,1,640]{3,0,2,1:T(8,128)}, f32[26,4,1,640]{3,0,2,1:T(8,128)S(1)}, u32[]{:S(2)}, u32[]{:S(2)}) collective-permute-start(f32[26,4,1,640]{3,0,2,1:T(8,128)} %get-tuple-element.35), channel_id=1, source_target_pairs={{0,2},{2,4},{4,6},{6,8},{8,10},{10,12},{12,14},{14,16},{16,18},{18... | collective-permute-start | bytes 798728 | tf_op jit(solution)/shard_map/ppermute | solution.py:18
  165.8 7.9 %collective-permute-start.2 = (f32[26,4,1,640]{3,0,2,1:T(8,128)S(1)}, f32[26,4,1,640]{3,0,2,1:T(8,128)S(1)}, u32[]{:S(2)}, u32[]{:S(2)}) collective-permute-start(f32[26,4,1,640]{3,0,2,1:T(8,128)S(1)} %get-tuple-element.30), channel_id=1, source_target_pairs={{2,0},{4,2},{6,4},{8,6},{10,8},{12,10},{14,12},{16,14},{18,16},{20... | collective-permute-start | bytes 798728 | tf_op jit(solution)/shard_map/ppermute | solution.py:20
  172.5 4.0 collective-permute-start.3
  178.2 10.8 %collective-permute-start.4 = (f32[26,4,1,640]{3,0,2,1:T(8,128)S(1)}, f32[26,4,1,640]{3,0,2,1:T(8,128)S(1)}, u32[]{:S(2)}, u32[]{:S(2)}) collective-permute-start(f32[26,4,1,640]{3,0,2,1:T(8,128)S(1)} %get-tuple-element.26), channel_id=1, source_target_pairs={{2,0},{4,2},{6,4},{8,6},{10,8},{12,10},{14,12},{16,14},{18,16},{20... | collective-permute-start | bytes 798728 | tf_op jit(solution)/shard_map/ppermute | solution.py:20
  185.0 4.0 collective-permute-start.5
  190.7 8.2 %collective-permute-start.6 = (f32[26,4,1,640]{3,0,2,1:T(8,128)S(1)}, f32[26,4,1,640]{3,0,2,1:T(8,128)S(1)}, u32[]{:S(2)}, u32[]{:S(2)}) collective-permute-start(f32[26,4,1,640]{3,0,2,1:T(8,128)S(1)} %get-tuple-element.22), channel_id=1, source_target_pairs={{2,0},{4,2},{6,4},{8,6},{10,8},{12,10},{14,12},{16,14},{18,16},{20... | collective-permute-start | bytes 798728 | tf_op jit(solution)/shard_map/ppermute | solution.py:20
  197.7 4.0 copy-start.1
  197.7 4.0 collective-permute-start.7
  204.6 8.3 %collective-permute-start.8 = (f32[26,4,1,640]{3,0,2,1:T(8,128)S(1)}, f32[26,4,1,640]{3,0,2,1:T(8,128)S(1)}, u32[]{:S(2)}, u32[]{:S(2)}) collective-permute-start(f32[26,4,1,640]{3,0,2,1:T(8,128)S(1)} %get-tuple-element.18), channel_id=1, source_target_pairs={{2,0},{4,2},{6,4},{8,6},{10,8},{12,10},{14,12},{16,14},{18,16},{20... | collective-permute-start | bytes 798728 | tf_op jit(solution)/shard_map/ppermute | solution.py:20
  211.7 4.0 collective-permute-start.9
  217.4 8.2 %collective-permute-start.10 = (f32[26,4,1,640]{3,0,2,1:T(8,128)S(1)}, f32[26,4,1,640]{3,0,2,1:T(8,128)S(1)}, u32[]{:S(2)}, u32[]{:S(2)}) collective-permute-start(f32[26,4,1,640]{3,0,2,1:T(8,128)S(1)} %get-tuple-element.14), channel_id=1, source_target_pairs={{2,0},{4,2},{6,4},{8,6},{10,8},{12,10},{14,12},{16,14},{18,16},{20... | collective-permute-start | bytes 798728 | tf_op jit(solution)/shard_map/ppermute | solution.py:20
  224.3 4.0 collective-permute-start.11
  230.0 8.2 %collective-permute-start.12 = (f32[26,4,1,640]{3,0,2,1:T(8,128)S(1)}, f32[26,4,1,640]{3,0,2,1:T(8,128)S(1)}, u32[]{:S(2)}, u32[]{:S(2)}) collective-permute-start(f32[26,4,1,640]{3,0,2,1:T(8,128)S(1)} %get-tuple-element.10), channel_id=1, source_target_pairs={{2,0},{4,2},{6,4},{8,6},{10,8},{12,10},{14,12},{16,14},{18,16},{20... | collective-permute-start | bytes 798728 | tf_op jit(solution)/shard_map/ppermute | solution.py:20
  236.9 4.0 collective-permute-start.13
  242.6 8.2 %collective-permute-start.14 = (f32[26,4,1,640]{3,0,2,1:T(8,128)S(1)}, f32[26,4,1,640]{3,0,2,1:T(8,128)S(1)}, u32[]{:S(2)}, u32[]{:S(2)}) collective-permute-start(f32[26,4,1,640]{3,0,2,1:T(8,128)S(1)} %get-tuple-element.6), channel_id=1, source_target_pairs={{2,0},{4,2},{6,4},{8,6},{10,8},{12,10},{14,12},{16,14},{18,16},{20... | collective-permute-start | bytes 798728 | tf_op jit(solution)/shard_map/ppermute | solution.py:20
  249.5 4.0 copy-start
  249.5 4.0 collective-permute-start.15
  253.6 2.7 copy-start.3
  431.6 3.1 copy-start.2
Sparse Core Ops, SparseCore 0:
  257.5 31.8 all-reduce.17
where the time goes:
time: 448 us; the launch traced here: 444 us
  blocking collectives  287 us (64%)
  starting transfers between devices  51.3 us (11%)
  waiting for transfers between devices  46.7 us (10%)
  other arithmetic  29.7 us (7%)
  local copies, waits for them, and re-layouts  14.3 us (3%)
  between operations  14.3 us (3%)
    psum x1, blocking collectives, body(): masses = lax.psum(local_mass, 'tile') / cell_count  142 us
    psum x1, blocking collectives, body(): lax.psum(jnp.sum(merged * cell_area, axis=(1, 2)), 'tile') / cell_count  139 us
    ppermute x8, starting transfers between devices, with_halo(): lax.ppermute(head, axis, [((i + 1) % count, i) for i in range(count)])  49.6 us
    psum x1, waiting for transfers between devices, body(): log_sum, count_sum = lax.psum((weighted, jnp.sum(weights)), 'mem')  25.2 us
    ppermute x8, waiting for transfers between devices, with_halo(): lax.ppermute(tail, axis, [(i, (i + 1) % count) for i in range(count)])  16.7 us
    add x6, other arithmetic, diffuse_padded(): middle + zonal_coef * (eastern + western - 2.0 * middle)  11.4 us
    slice x8, local copies, waits for them, and re-layouts, diffuse_padded(): northern = jnp.concatenate([middle[..., 1:], zeros_row], axis=-1)  9.87 us
  transfers between devices with their start and end apart: 17, of which 15 were waited for; matrix products, arithmetic and copies ran while one was open for 2% of the time, Pallas kernels for 0%

commit v1 on v0

v1 whole, which is shorter than its diff:
```python
import math

import jax
import jax.numpy as jnp
import numpy as np
from jax import lax
from jax.experimental import pallas as pl
from jax.experimental.pallas import tpu as pltpu
from jax.sharding import PartitionSpec as P

BACKGROUND = 0.01
REACH = 4
SUB = 8
VMEM = pl.BlockSpec(memory_space=pltpu.VMEM)
HBM = pl.BlockSpec(memory_space=pl.ANY)
AREA, ZONAL, NORTH, SOUTH, CENTER = range(5)


def coefficients(lat_cells):
    spacing = math.pi / lat_cells
    index = np.arange(lat_cells)
    latitude = -0.5 * math.pi + (index + 0.5) * spacing
    cell_area = np.cos(latitude)
    zonal = 0.2 * np.minimum(2.2, 1.0 / cell_area**2)
    north = np.where(index == lat_cells - 1, 0.0, 0.05 * np.cos(latitude + 0.5 * spacing) / cell_area)
    south = np.where(index == 0, 0.0, 0.05 * np.cos(latitude - 0.5 * spacing) / cell_area)
    center = 1.0 - 2.0 * zonal - north - south
    rows = np.stack([cell_area, zonal, north, south, center]).astype(np.float32)
    return np.ascontiguousarray(np.broadcast_to(rows[:, None, :], (5, SUB, lat_cells)))


def params(mib=20):
    return pltpu.CompilerParams(vmem_limit_bytes=mib * 2**20)


def rows_of(group):
    return pl.ds(pl.multiple_of(group * SUB, SUB), SUB)


def block_of(group):
    return pl.ds(pl.multiple_of(group * SUB * SUB, SUB * SUB), SUB * SUB)


def by_longitude(block, lat):
    return jnp.swapaxes(block.reshape(SUB, SUB, lat), 0, 1)


def diffuse(columns, coef_ref):
    lat = columns[0].shape[-1]
    for _ in range(REACH):
        columns = [
            coef_ref[CENTER] * here
            + coef_ref[ZONAL] * (west + east)
            + coef_ref[NORTH] * pltpu.roll(here, lat - 1, 1)
            + coef_ref[SOUTH] * pltpu.roll(here, 1, 1)
            for west, here, east in zip(columns[:-2], columns[1:-1], columns[2:])
        ]
    return columns


def gather_columns(refs, group):
    rows = rows_of(group)
    return [ref[c, rows, :] for ref in refs for c in range(REACH)]


def spread_kernel(scaling_ref, coef_ref, left_ref, right_ref):
    groups = left_ref.shape[1] // SUB
    lat = left_ref.shape[2]

    def step(group, carry):
        columns = by_longitude(scaling_ref[block_of(group), :], lat)
        for c in range(REACH):
            left_ref[c, rows_of(group), :] = columns[c] * coef_ref[AREA]
            right_ref[c, rows_of(group), :] = columns[c + REACH] * coef_ref[AREA]
        return carry

    lax.fori_loop(0, groups, step, 0)


def lane_fold(value):
    lat = value.shape[-1]
    total = value[:, :128]
    for t in range(1, lat // 128):
        total = total + value[:, t * 128 : (t + 1) * 128]
    return total


def smooth_kernel(west_ref, left_ref, right_ref, east_ref, fields_ref, mask_ref, coef_ref, outl_ref, outr_ref, mass_ref):
    groups = left_ref.shape[1] // SUB
    lat = left_ref.shape[2]

    def step(group, carry):
        smoothed = diffuse(gather_columns((west_ref, left_ref, right_ref, east_ref), group), coef_ref)
        fields = by_longitude(fields_ref[block_of(group), :], lat)
        mass = jnp.zeros((SUB, lat), jnp.float32)
        for c in range(2 * REACH):
            valid = jnp.broadcast_to(mask_ref[c : c + 1, :], (SUB, lat)) == 1
            filled = (jnp.where(valid, fields[c], 0.0) + BACKGROUND) * coef_ref[AREA]
            mass = mass + filled
            out_ref = outl_ref if c < REACH else outr_ref
            out_ref[c % REACH, rows_of(group), :] = filled / smoothed[c]
        mass_ref[rows_of(group), :] = lane_fold(mass)
        return carry

    lax.fori_loop(0, groups, step, 0)


def low_half(shape):
    return lax.broadcasted_iota(jnp.int32, shape, 0) < SUB // 2


def return_kernel(west_ref, left_ref, right_ref, east_ref, scaling_ref, weight_ref, coef_ref, result_ref, logs_ref, total_ref):
    groups = left_ref.shape[1] // SUB
    lat = left_ref.shape[2]
    total_ref[...] = jnp.zeros_like(total_ref)

    def step(group, carry):
        result = diffuse(gather_columns((west_ref, left_ref, right_ref, east_ref), group), coef_ref)
        scaling = by_longitude(scaling_ref[block_of(group), :], lat)
        weight = jnp.broadcast_to(weight_ref[rows_of(group), :1], (SUB, lat))
        for c in range(2 * REACH):
            result_ref[c, rows_of(group), :] = result[c]
            total_ref[c] = total_ref[c] + weight * jnp.log(scaling[c] * result[c])
        return carry

    lax.fori_loop(0, groups, step, 0)
    low = low_half((SUB, lat))
    for c in range(REACH):
        first, second = total_ref[c], total_ref[c + REACH]
        first = first + pltpu.roll(first, SUB // 2, 0)
        second = second + pltpu.roll(second, SUB // 2, 0)
        logs_ref[c] = jnp.where(low, first, second)


def merge_kernel(own_ref, other_ref, count_ref, mass_ref, coef_ref, merged_ref, payload_ref):
    members = mass_ref.shape[0]
    lat = own_ref.shape[2]
    scale = 1.0 / count_ref[...]
    scale = jnp.broadcast_to(scale[:, :1], (SUB, lat))
    level = jnp.zeros((SUB, lat), jnp.float32)
    for c in range(REACH):
        merged = jnp.exp((own_ref[c] + other_ref[c]) * scale)
        merged_ref[c] = merged
        level = level + merged * coef_ref[AREA]
    level = lane_fold(level)
    level = level + pltpu.roll(level, SUB // 2, 0)
    spare = jnp.zeros((128 - members - SUB, 128), jnp.float32)
    table = jnp.concatenate([mass_ref[...], level, spare], axis=0)
    row = jnp.sum(table.T, axis=0, keepdims=True)
    payload_ref[...] = jnp.broadcast_to(row[None], payload_ref.shape)


def finish_kernel(cells, got_ref, merged_ref, result_ref, bary_ref, updated_ref, staged_ref, sem):
    members, lat = result_ref.shape[1:]
    groups = members // SUB
    total = jnp.sum(got_ref[...], axis=0)
    table = jnp.broadcast_to(total, (128, 128)).T
    level = table[members : members + SUB, :]
    low = low_half((SUB, lat))
    wide = lambda v: jnp.concatenate([v] * (lat // 128), axis=1)
    merged = [None] * (2 * REACH)
    for c in range(REACH):
        both = merged_ref[c]
        swapped = pltpu.roll(both, SUB // 2, 0)
        merged[c] = jnp.where(low, both, swapped)
        merged[c + REACH] = jnp.where(low, swapped, both)
    inverse = wide(cells / level)
    bary = [m * inverse for m in merged]
    bary_ref[...] = jnp.swapaxes(jnp.stack(bary), 0, 1)[: SUB // 2]
    for group in range(groups):
        rows = slice(group * SUB, (group + 1) * SUB)
        factor = wide(table[rows, :] / cells)
        out = jnp.stack([bary[c] * factor / result_ref[c, rows, :] for c in range(2 * REACH)])
        span = pl.ds(group * SUB * SUB, SUB * SUB)
        staged_ref[span, :] = jnp.swapaxes(out, 0, 1).reshape(SUB * SUB, lat)
        pltpu.make_async_copy(staged_ref.at[span, :], updated_ref.at[span, :], sem.at[group]).start()
    for group in range(groups):
        span = pl.ds(group * SUB * SUB, SUB * SUB)
        pltpu.make_async_copy(staged_ref.at[span, :], updated_ref.at[span, :], sem.at[group]).wait()


def shape(*dims):
    return jax.ShapeDtypeStruct(dims, jnp.float32)


def body(fields, scaling, counts, land_mask):
    members, levels, lon, lat = fields.shape
    tiles = lax.axis_size("tile")
    rows = members * levels
    cells = lon * tiles * lat
    half = shape(REACH, rows, lat)
    coef = jnp.asarray(coefficients(lat))
    eastward = [(i, (i + 1) % tiles) for i in range(tiles)]
    westward = [((i + 1) % tiles, i) for i in range(tiles)]
    scaling = scaling.reshape(rows * lon, lat)
    fields = fields.reshape(rows * lon, lat)
    weights = counts.astype(jnp.float32)
    weight_rows = jnp.broadcast_to(jnp.repeat(weights, levels)[:, None], (rows, 128))
    count = jnp.broadcast_to(jnp.sum(weights), (SUB, 128))
    count = count + lax.ppermute(count, "mem", [(0, 1), (1, 0)])

    left, right = pl.pallas_call(
        spread_kernel, out_shape=(half, half), in_specs=[VMEM] * 2, out_specs=(VMEM,) * 2, compiler_params=params()
    )(scaling, coef)
    west = lax.ppermute(right, "tile", eastward)
    east = lax.ppermute(left, "tile", westward)
    left, right, mass = pl.pallas_call(
        smooth_kernel,
        out_shape=(half, half, shape(rows, 128)),
        in_specs=[VMEM] * 7,
        out_specs=(VMEM,) * 3,
        compiler_params=params(),
    )(west, left, right, east, fields, land_mask, coef)
    west = lax.ppermute(right, "tile", eastward)
    east = lax.ppermute(left, "tile", westward)
    result, logs = pl.pallas_call(
        return_kernel,
        out_shape=(shape(2 * REACH, rows, lat), shape(REACH, SUB, lat)),
        in_specs=[VMEM] * 7,
        out_specs=(VMEM,) * 2,
        scratch_shapes=[pltpu.VMEM((2 * REACH, SUB, lat), jnp.float32)],
        compiler_params=params(),
    )(west, left, right, east, scaling, weight_rows, coef)
    other = lax.ppermute(logs, "mem", [(0, 1), (1, 0)])
    merged, payload = pl.pallas_call(
        merge_kernel,
        out_shape=(shape(REACH, SUB, lat), shape(tiles, 1, 128)),
        in_specs=[VMEM] * 5,
        out_specs=(VMEM,) * 2,
        compiler_params=params(),
    )(logs, other, count, mass, coef)
    got = lax.all_to_all(payload, "tile", split_axis=0, concat_axis=0)
    barycenter, updated = pl.pallas_call(
        lambda *refs: finish_kernel(float(cells), *refs),
        out_shape=(shape(levels, lon, lat), shape(rows * lon, lat)),
        in_specs=[VMEM] * 3,
        out_specs=(VMEM, HBM),
        scratch_shapes=[pltpu.VMEM((rows * lon, lat), jnp.float32), pltpu.SemaphoreType.DMA((rows // SUB,))],
        compiler_params=params(),
    )(got, merged, result)
    return barycenter, updated.reshape(members, levels, lon, lat)


def solution(mesh):
    return jax.shard_map(
        body,
        mesh=mesh,
        in_specs=(
            P("mem", None, "tile", None),
            P("mem", None, "tile", None),
            P("mem"),
            P("tile", None),
        ),
        out_specs=(P(None, "tile", None), P("mem", None, "tile", None)),
        check_vma=False,
    )
```

time: 448 us -> 101 us (0.23)
  blocking collectives: 287 us -> 18.1 us
  starting transfers between devices: 51.3 us -> 10.8 us
  other arithmetic: 29.7 us -> 1.25 us
  Pallas kernels: 0 us -> 20.6 us
  between operations: 14.3 us -> 0.7 us
  local copies, waits for them, and re-layouts: 14.3 us -> 4.12 us
    psum x3 -> x0, blocking collectives: 287 us -> none  [the longest x1 142 us: body(): masses = lax.psum(local_mass, 'tile') / cell_count]
    ppermute x16 -> x6, starting transfers between devices: 51.2 us -> 10.8 us  [the longest x1 3.79 us: body(): other = lax.ppermute(logs, 'mem', [(0, 1), (1, 0)])]
    psum x1 -> x0, waiting for transfers between devices: 25.2 us -> none  [body(): log_sum, count_sum = lax.psum((weighted, jnp.sum(weights)), 'mem')]
    ppermute x16 -> x6, waiting for transfers between devices: 21.5 us -> 45.4 us  [the longest x2 41.7 us: body(): west = lax.ppermute(right, 'tile', eastward)]
    pallas_call x0 -> x5, Pallas kernels: none -> 20.6 us  [the longest x1 9.24 us: body(): pl.pallas_call(return_kernel, out_shape=(shape(2 * REACH, rows, lat), sha...]
    all_to_all x0 -> x1, blocking collectives: none -> 18.1 us  [body(): got = lax.all_to_all(payload, 'tile', split_axis=0, concat_axis=0)]
    slice x16 -> x0, local copies, waits for them, and re-layouts: 11.1 us -> none  [the longest x8 9.87 us: diffuse_padded(): northern = jnp.concatenate([middle[..., 1:], zeros_row], axis=-1)]
    add x6 -> x1, other arithmetic: 11.4 us -> 0.65 us  [body(): count = count + lax.ppermute(count, 'mem', [(0, 1), (1, 0)])]
  transfers between devices with their start and end apart: 17 -> 6, of which waited for: 15 -> 4; matrix products, arithmetic and copies ran while one was open for 2% -> 2% of each run, Pallas kernels for 0% -> 9%
where the time goes in v1:
time: 101 us
  waiting for transfers between devices  45.4 us (45%)
  Pallas kernels  20.6 us (20%)
  blocking collectives  18.1 us (18%)
  starting transfers between devices  10.8 us (11%)
  local copies, waits for them, and re-layouts  4.12 us (4%)
  other arithmetic  1.25 us (1%)
    ppermute x2, waiting for transfers between devices, body(): west = lax.ppermute(right, 'tile', eastward)  41.7 us
    all_to_all x1, blocking collectives, body(): got = lax.all_to_all(payload, 'tile', split_axis=0, concat_axis=0)  18.1 us
    pallas_call x1, Pallas kernels, body(): pl.pallas_call(return_kernel, out_shape=(shape(2 * REACH, rows, lat), sha...  9.24 us
    pallas_call x1, Pallas kernels, body(): pl.pallas_call(smooth_kernel, out_shape=(half, half, shape(rows, 128)), i...  8.39 us
    ppermute x1, starting transfers between devices, body(): other = lax.ppermute(logs, 'mem', [(0, 1), (1, 0)])  3.79 us
    ppermute x1, starting transfers between devices, body(): count = count + lax.ppermute(count, 'mem', [(0, 1), (1, 0)])  3.38 us
    unnamed x14, local copies, waits for them, and re-layouts  3.23 us
    ppermute x2, starting transfers between devices, body(): west = lax.ppermute(right, 'tile', eastward)  3.1 us
  transfers between devices with their start and end apart: 6, of which 4 were waited for; matrix products, arithmetic and copies ran while one was open for 2% of the time, Pallas kernels for 9%

profile of v1, /device:TPU:1, one launch (start us, length us, event | category | flops | bytes accessed | tf_op | source)
XLA Modules:
  0.0 100.8 jit_solution(8885254047173867088)
XLA Ops:
  0.6 0.0 copy-start
  0.6 1.6 %copy-done = f32[26,4,8,640]{3,2,1,0:T(8,128)S(1)} copy-done((f32[26,4,8,640]{3,2,1,0:T(8,128)S(1)}, f32[26,4,8,640]{3,2,1,0:T(8,128)}, u32[]{:S(2)}) %copy-start) | copy-done | bytes 2129944
  2.2 0.0 copy-start.3
  2.2 0.9 copy-done.3
  3.1 0.0 copy-start.2
  3.1 0.0 copy-start.4
  3.1 0.4 shard_map.68
  3.6 3.1 %collective-permute-start = (f32[4,104,640]{2,1,0:T(8,128)S(1)}, f32[4,104,640]{2,1,0:T(8,128)S(1)}, u32[]{:S(2)}, u32[]{:S(2)}) collective-permute-start(f32[4,104,640]{2,1,0:T(8,128)S(1)} %get-tuple-element.13.right_ref), channel_id=1, source_target_pairs={{0,2},{2,4},{4,6},{6,8},{8,10},{10,12},{12,14},{14,16},{16,18},{18... | collective-permute-start | bytes 3194888 | tf_op jit(solution)/shard_map/ppermute | solution.py:205
  6.7 0.0 collective-permute-start.1
  6.7 23.3 %collective-permute-done.west_ref = f32[4,104,640]{2,1,0:T(8,128)S(1)} collective-permute-done((f32[4,104,640]{2,1,0:T(8,128)S(1)}, f32[4,104,640]{2,1,0:T(8,128)S(1)}, u32[]{:S(2)}, u32[]{:S(2)}) %collective-permute-start) | collective-permute-done | bytes 1064992 | tf_op jit(solution)/shard_map/ppermute | solution.py:205
  30.0 2.5 %collective-permute-done.1.east_ref = f32[4,104,640]{2,1,0:T(8,128)S(1)} collective-permute-done((f32[4,104,640]{2,1,0:T(8,128)S(1)}, f32[4,104,640]{2,1,0:T(8,128)S(1)}, u32[]{:S(2)}, u32[]{:S(2)}) %collective-permute-start.1) | collective-permute-done | bytes 1064992 | tf_op jit(solution)/shard_map/ppermute | solution.py:206
  32.5 0.0 copy-done.2
  32.5 0.0 copy-done.4
  32.5 0.0 copy-start.5
  32.5 0.7 copy-done.5
  33.2 0.0 copy-start.6
  33.2 0.0 copy-start.1
  33.2 8.4 %shard_map.69 = (f32[4,104,640]{2,1,0:T(8,128)S(1)}, f32[4,104,640]{2,1,0:T(8,128)}, f32[104,128]{1,0:T(8,128)S(1)}) custom-call(f32[4,104,640]{2,1,0:T(8,128)S(1)} %collective-permute-done.west_ref, f32[4,104,640]{2,1,0:T(8,128)S(1)} %get-tuple-element.14.left_ref, f32[4,104,640]{2,1,0:T(8,128)S(1)} %get-tuple-element.13.right_ref, ...), custom_call_target="tpu_custom_call" | custom-call | tf_op jit(solution)/shard_map/pallas_call | solution.py:207
  41.6 0.0 collective-permute-start.2
  41.6 0.5 collective-permute-start.3
  42.1 0.0 copy-done.6
  42.1 0.6 convert_reduce_fusion
  42.7 0.6 broadcast_in_dim.16
  43.4 3.4 %collective-permute-start.5 = (f32[8,128]{1,0:T(8,128)S(1)}, f32[8,128]{1,0:T(8,128)S(1)}, u32[]{:S(2)}, u32[]{:S(2)}) collective-permute-start(f32[8,128]{1,0:T(8,128)S(1)} %broadcast_in_dim.16), channel_id=1, source_target_pairs={{0,1},{1,0},{2,3},{3,2},{4,5},{5,4},{6,7},{7,6},{8,9},{9,8},{10,11... | collective-permute-start | bytes 12296 | tf_op jit(solution)/shard_map/ppermute | solution.py:200
  46.8 0.1 broadcast_in_dim.13
  46.8 0.1 broadcast_in_dim.14
  46.9 18.4 %collective-permute-done.2.west_ref = f32[4,104,640]{2,1,0:T(8,128)} collective-permute-done((f32[4,104,640]{2,1,0:T(8,128)}, f32[4,104,640]{2,1,0:T(8,128)}, u32[]{:S(2)}, u32[]{:S(2)}) %collective-permute-start.2) | collective-permute-done | bytes 1064992 | tf_op jit(solution)/shard_map/ppermute | solution.py:214
  65.3 0.0 collective-permute-done.3.east_ref
  65.3 0.1 broadcast_in_dim.15.weight_ref
  65.4 0.0 copy-done.1
  65.4 9.2 %shard_map.70 = (f32[8,104,640]{2,1,0:T(8,128)S(1)}, f32[4,8,640]{2,1,0:T(8,128)S(1)}) custom-call(f32[4,104,640]{2,1,0:T(8,128)} %collective-permute-done.2.west_ref, f32[4,104,640]{2,1,0:T(8,128)S(1)} %get-tuple-element.16.left_ref, f32[4,104,640]{2,1,0:T(8,128)} %get-tuple-element.15.right_ref, f32[4,104,640]{2,1,0:T(8,128)} %collective-permute-done.3.east_ref, ...), custom_call_target="tpu_custom_call" | custom-call | tf_op jit(solution)/shard_map/pallas_call | solution.py:216
  74.6 3.8 %collective-permute-start.4 = (f32[4,8,640]{2,1,0:T(8,128)S(1)}, f32[4,8,640]{2,1,0:T(8,128)S(1)}, u32[]{:S(2)}, u32[]{:S(2)}) collective-permute-start(f32[4,8,640]{2,1,0:T(8,128)S(1)} %get-tuple-element.17.own_ref), channel_id=1, source_target_pairs={{0,1},{1,0},{2,3},{3,2},{4,5},{5,4},{6,7},{7,6},{8,9},{9,8},{10,11... | collective-permute-start | bytes 245768 | tf_op jit(solution)/shard_map/ppermute | solution.py:224
  78.4 0.0 collective-permute-done.5
  78.4 0.6 broadcast_add_fusion.count_ref
  79.1 1.2 %collective-permute-done.4.other_ref = f32[4,8,640]{2,1,0:T(8,128)S(1)} collective-permute-done((f32[4,8,640]{2,1,0:T(8,128)S(1)}, f32[4,8,640]{2,1,0:T(8,128)S(1)}, u32[]{:S(2)}, u32[]{:S(2)}) %collective-permute-start.4) | collective-permute-done | bytes 81952 | tf_op jit(solution)/shard_map/ppermute | solution.py:224
  80.3 0.2 shard_map.71
  80.5 18.1 %all_to_all.5.refs_0_ = f32[64,1,128]{2,1,0:T(1,128)S(1)} all-to-all(f32[64,1,128]{2,1,0:T(1,128)S(1)} %get-tuple-element.19), channel_id=1, replica_groups=mesh['tile'=64,'mem'=2] {'tile'}, dimensions={0} | all-to-all | bytes 65536 | tf_op jit(solution)/shard_map/all_to_all | solution.py:232
  98.5 2.3 %shard_map.72 = (f32[4,8,640]{2,1,0:T(8,128)}, f32[832,640]{1,0:T(8,128)}) custom-call(f32[64,1,128]{2,1,0:T(1,128)S(1)} %all_to_all.5.refs_0_, f32[4,8,640]{2,1,0:T(8,128)S(1)} %get-tuple-element.20.refs_1_, f32[8,104,640]{2,1,0:T(8,128)S(1)} %get-tuple-element.21.refs_2_), custom_call_target="tpu_custom_call" | custom-call | tf_op jit(solution)/shard_map/pallas_call | solution.py:233
  (1 shorter events, 0.0 us)
Async XLA Ops:
  0.6 1.6 %copy-start = (f32[26,4,8,640]{3,2,1,0:T(8,128)S(1)}, f32[26,4,8,640]{3,2,1,0:T(8,128)}, u32[]{:S(2)}) copy-start(f32[26,4,8,640]{3,2,1,0:T(8,128)} %param.6) | copy-start | bytes 6389764
  2.2 0.9 copy-start.3
  3.1 29.3 %copy-start.2 = (f32[26,4,8,640]{3,2,1,0:T(8,128)S(1)}, f32[26,4,8,640]{3,2,1,0:T(8,128)}, u32[]{:S(2)}) copy-start(f32[26,4,8,640]{3,2,1,0:T(8,128)} %param.5) | copy-start | bytes 6389764
  3.1 29.3 %copy-start.4 = (f32[5,8,640]{2,1,0:T(8,128)S(1)}, f32[5,8,640]{2,1,0:T(8,128)}, u32[]{:S(2)}) copy-start(f32[5,8,640]{2,1,0:T(8,128)} %constant.4.clone.coef_ref) | copy-start | bytes 307204
  3.6 26.4 %collective-permute-start = (f32[4,104,640]{2,1,0:T(8,128)S(1)}, f32[4,104,640]{2,1,0:T(8,128)S(1)}, u32[]{:S(2)}, u32[]{:S(2)}) collective-permute-start(f32[4,104,640]{2,1,0:T(8,128)S(1)} %get-tuple-element.13.right_ref), channel_id=1, source_target_pairs={{0,2},{2,4},{4,6},{6,8},{8,10},{10,12},{12,14},{14,16},{16,18},{18... | collective-permute-start | bytes 3194888 | tf_op jit(solution)/shard_map/ppermute | solution.py:205
  6.7 25.8 %collective-permute-start.1 = (f32[4,104,640]{2,1,0:T(8,128)S(1)}, f32[4,104,640]{2,1,0:T(8,128)S(1)}, u32[]{:S(2)}, u32[]{:S(2)}) collective-permute-start(f32[4,104,640]{2,1,0:T(8,128)S(1)} %get-tuple-element.14.left_ref), channel_id=1, source_target_pairs={{2,0},{4,2},{6,4},{8,6},{10,8},{12,10},{14,12},{16,14},{18,16},{20... | collective-permute-start | bytes 3194888 | tf_op jit(solution)/shard_map/ppermute | solution.py:206
  32.5 0.7 copy-start.5
  33.2 8.9 %copy-start.6 = (s32[26]{0:T(128)S(1)}, s32[26]{0:T(128)}, u32[]{:S(2)}) copy-start(s32[26]{0:T(128)} %param.7) | copy-start | bytes 316
  33.2 32.2 %copy-start.1 = (f32[26,4,8,640]{3,2,1,0:T(8,128)S(1)}, f32[26,4,8,640]{3,2,1,0:T(8,128)}, u32[]{:S(2)}) copy-start(f32[26,4,8,640]{3,2,1,0:T(8,128)} %param.6) | copy-start | bytes 6389764
  41.6 23.7 %collective-permute-start.2 = (f32[4,104,640]{2,1,0:T(8,128)}, f32[4,104,640]{2,1,0:T(8,128)}, u32[]{:S(2)}, u32[]{:S(2)}) collective-permute-start(f32[4,104,640]{2,1,0:T(8,128)} %get-tuple-element.15.right_ref), channel_id=1, source_target_pairs={{0,2},{2,4},{4,6},{6,8},{8,10},{10,12},{12,14},{14,16},{16,18},{18... | collective-permute-start | bytes 3194888 | tf_op jit(solution)/shard_map/ppermute | solution.py:214
  41.6 23.7 %collective-permute-start.3 = (f32[4,104,640]{2,1,0:T(8,128)S(1)}, f32[4,104,640]{2,1,0:T(8,128)}, u32[]{:S(2)}, u32[]{:S(2)}) collective-permute-start(f32[4,104,640]{2,1,0:T(8,128)S(1)} %get-tuple-element.16.left_ref), channel_id=1, source_target_pairs={{2,0},{4,2},{6,4},{8,6},{10,8},{12,10},{14,12},{16,14},{18,16},{20... | collective-permute-start | bytes 3194888 | tf_op jit(solution)/shard_map/ppermute | solution.py:215
  43.4 35.1 %collective-permute-start.5 = (f32[8,128]{1,0:T(8,128)S(1)}, f32[8,128]{1,0:T(8,128)S(1)}, u32[]{:S(2)}, u32[]{:S(2)}) collective-permute-start(f32[8,128]{1,0:T(8,128)S(1)} %broadcast_in_dim.16), channel_id=1, source_target_pairs={{0,1},{1,0},{2,3},{3,2},{4,5},{5,4},{6,7},{7,6},{8,9},{9,8},{10,11... | collective-permute-start | bytes 12296 | tf_op jit(solution)/shard_map/ppermute | solution.py:200
  74.6 5.6 %collective-permute-start.4 = (f32[4,8,640]{2,1,0:T(8,128)S(1)}, f32[4,8,640]{2,1,0:T(8,128)S(1)}, u32[]{:S(2)}, u32[]{:S(2)}) collective-permute-start(f32[4,8,640]{2,1,0:T(8,128)S(1)} %get-tuple-element.17.own_ref), channel_id=1, source_target_pairs={{0,1},{1,0},{2,3},{3,2},{4,5},{5,4},{6,7},{7,6},{8,9},{9,8},{10,11... | collective-permute-start | bytes 245768 | tf_op jit(solution)/shard_map/ppermute | solution.py:224

commit v2 on v1

v2 whole, which is shorter than its diff:
```python
import math

import jax
import jax.numpy as jnp
import numpy as np
from jax import lax
from jax.experimental import pallas as pl
from jax.experimental.pallas import tpu as pltpu
from jax.sharding import PartitionSpec as P

BACKGROUND = 0.01
REACH = 4
SUB = 8
VMEM = pl.BlockSpec(memory_space=pltpu.VMEM)
HBM = pl.BlockSpec(memory_space=pl.ANY)
AREA, ZONAL, NORTH, SOUTH, CENTER = range(5)


def coefficients(lat_cells):
    spacing = math.pi / lat_cells
    index = np.arange(lat_cells)
    latitude = -0.5 * math.pi + (index + 0.5) * spacing
    cell_area = np.cos(latitude)
    zonal = 0.2 * np.minimum(2.2, 1.0 / cell_area**2)
    north = np.where(index == lat_cells - 1, 0.0, 0.05 * np.cos(latitude + 0.5 * spacing) / cell_area)
    south = np.where(index == 0, 0.0, 0.05 * np.cos(latitude - 0.5 * spacing) / cell_area)
    center = 1.0 - 2.0 * zonal - north - south
    rows = np.stack([cell_area, zonal, north, south, center]).astype(np.float32)
    return np.ascontiguousarray(np.broadcast_to(rows[:, None, :], (5, SUB, lat_cells)))


def params(mib=20):
    return pltpu.CompilerParams(vmem_limit_bytes=mib * 2**20)


def rows_of(group):
    return pl.ds(pl.multiple_of(group * SUB, SUB), SUB)


def block_of(group):
    return pl.ds(pl.multiple_of(group * SUB * SUB, SUB * SUB), SUB * SUB)


def by_longitude(block, lat):
    return jnp.swapaxes(block.reshape(SUB, SUB, lat), 0, 1)


def stack_of(ref, group, order=range(REACH)):
    return [ref[c, rows_of(group), :] for c in order]


def odd_core():
    return lax.rem(lax.axis_index("tile"), 2) == 1


def from_outside(columns, odd):
    last = len(columns) - 1
    return [jnp.where(odd, columns[last - c], columns[c]) for c in range(len(columns))]


def spread_kernel(scaling_ref, coef_ref, outer_ref, inner_ref):
    groups, lat = outer_ref.shape[1] // SUB, outer_ref.shape[2]
    odd = odd_core()

    def step(group, carry):
        columns = from_outside(by_longitude(scaling_ref[block_of(group), :], lat), odd)
        for c in range(REACH):
            outer_ref[c, rows_of(group), :] = columns[c] * coef_ref[AREA]
            inner_ref[c, rows_of(group), :] = columns[c + REACH] * coef_ref[AREA]
        return carry

    lax.fori_loop(0, groups, step, 0)


def lane_fold(value):
    lat = value.shape[-1]
    total = value[:, :128]
    for t in range(1, lat // 128):
        total = total + value[:, t * 128 : (t + 1) * 128]
    return total


def diffuse(columns, coef_ref):
    lat = columns[0].shape[-1]
    return [
        coef_ref[CENTER] * here
        + coef_ref[ZONAL] * (west + east)
        + coef_ref[NORTH] * pltpu.roll(here, lat - 1, 1)
        + coef_ref[SOUTH] * pltpu.roll(here, 1, 1)
        for west, here, east in zip(columns[:-2], columns[1:-1], columns[2:])
    ]


def inner_half(group, halo_ref, outer_ref, inner_ref, coef_ref, edge_ref):
    columns = stack_of(outer_ref, group) + stack_of(inner_ref, group) + stack_of(halo_ref, group, (3, 2, 1, 0))
    for s in range(REACH):
        columns = diffuse(columns, coef_ref)
        if s < REACH - 1:
            edge_ref[2 * s, rows_of(group), :] = columns[0]
            edge_ref[2 * s + 1, rows_of(group), :] = columns[1]
    return columns


def outer_half(group, halo_ref, outer_ref, edge_ref, coef_ref):
    columns = stack_of(halo_ref, group, (3, 2, 1, 0)) + stack_of(outer_ref, group, (0, 1))
    for s in range(REACH):
        columns = diffuse(columns, coef_ref)
        if s < REACH - 1:
            columns = columns + stack_of(edge_ref, group, (2 * s, 2 * s + 1))
    return columns


def smooth_inner_kernel(
    halo_ref, outer_ref, inner_ref, fields_ref, mask_ref, coef_ref, out_ref, edge_ref, filled_ref, mass_ref
):
    groups, lat = outer_ref.shape[1] // SUB, outer_ref.shape[2]
    odd = odd_core()

    def step(group, carry):
        smoothed = inner_half(group, halo_ref, outer_ref, inner_ref, coef_ref, edge_ref)
        fields = by_longitude(fields_ref[block_of(group), :], lat)
        filled = []
        for c in range(2 * REACH):
            valid = jnp.broadcast_to(mask_ref[c : c + 1, :], (SUB, lat)) == 1
            filled.append((jnp.where(valid, fields[c], 0.0) + BACKGROUND) * coef_ref[AREA])
        mass_ref[rows_of(group), :] = lane_fold(sum(filled))
        filled = from_outside(filled, odd)
        for c in range(REACH):
            filled_ref[c, rows_of(group), :] = filled[c]
            out_ref[c, rows_of(group), :] = filled[c + REACH] / smoothed[c]
        return carry

    lax.fori_loop(0, groups, step, 0)


def smooth_outer_kernel(halo_ref, outer_ref, edge_ref, filled_ref, coef_ref, out_ref):
    groups = outer_ref.shape[1] // SUB

    def step(group, carry):
        smoothed = outer_half(group, halo_ref, outer_ref, edge_ref, coef_ref)
        for c in range(REACH):
            out_ref[c, rows_of(group), :] = filled_ref[c, rows_of(group), :] / smoothed[c]
        return carry

    lax.fori_loop(0, groups, step, 0)


def low_half(shape):
    return lax.broadcasted_iota(jnp.int32, shape, 0) < SUB // 2


def add_logs(group, result, scaled_ref, weight_ref, inverse_ref, total_ref):
    lat = scaled_ref.shape[2]
    weight = jnp.broadcast_to(weight_ref[rows_of(group), :1], (SUB, lat))
    for c in range(REACH):
        inverse_ref[c, rows_of(group), :] = 1.0 / result[c]
        total_ref[c] = total_ref[c] + weight * jnp.log(scaled_ref[c, rows_of(group), :] * result[c])


def return_inner_kernel(
    halo_ref, outer_ref, inner_ref, scaled_ref, weight_ref, coef_ref, inverse_ref, edge_ref, total_ref
):
    groups = outer_ref.shape[1] // SUB
    total_ref[...] = jnp.zeros_like(total_ref)

    def step(group, carry):
        result = inner_half(group, halo_ref, outer_ref, inner_ref, coef_ref, edge_ref)
        add_logs(group, result, scaled_ref, weight_ref, inverse_ref, total_ref)
        return carry

    lax.fori_loop(0, groups, step, 0)


def return_outer_kernel(
    halo_ref, outer_ref, edge_ref, scaled_ref, weight_ref, inner_ref, coef_ref, inverse_ref, logs_ref, total_ref
):
    groups, lat = outer_ref.shape[1] // SUB, outer_ref.shape[2]
    total_ref[...] = jnp.zeros_like(total_ref)

    def step(group, carry):
        result = outer_half(group, halo_ref, outer_ref, edge_ref, coef_ref)
        add_logs(group, result, scaled_ref, weight_ref, inverse_ref, total_ref)
        return carry

    lax.fori_loop(0, groups, step, 0)
    low = low_half((SUB, lat))
    for c in range(REACH):
        outer, inner = total_ref[c], inner_ref[c]
        outer = outer + pltpu.roll(outer, SUB // 2, 0)
        inner = inner + pltpu.roll(inner, SUB // 2, 0)
        logs_ref[c] = jnp.where(low, outer, inner)


def merge_kernel(own_ref, other_ref, count_ref, mass_ref, coef_ref, merged_ref, payload_ref):
    members, lat = mass_ref.shape[0], own_ref.shape[2]
    scale = 1.0 / count_ref[...]
    scale = jnp.broadcast_to(scale[:, :1], (SUB, lat))
    level = jnp.zeros((SUB, lat), jnp.float32)
    for c in range(REACH):
        weighted = jnp.exp((own_ref[c] + other_ref[c]) * scale)
        merged_ref[c] = weighted / coef_ref[AREA]
        level = level + weighted
    level = lane_fold(level)
    level = level + pltpu.roll(level, SUB // 2, 0)
    spare = jnp.zeros((128 - members - SUB, 128), jnp.float32)
    table = jnp.concatenate([mass_ref[...], level, spare], axis=0)
    row = jnp.sum(table.T, axis=0, keepdims=True)
    payload_ref[...] = jnp.broadcast_to(row[None], payload_ref.shape)


def finish_kernel(cells, got_ref, merged_ref, outer_ref, inner_ref, bary_ref, updated_ref, staged_ref, sem):
    members, lat = outer_ref.shape[1:]
    groups = members // SUB
    odd = odd_core()
    total = jnp.sum(got_ref[...], axis=0)
    table = jnp.broadcast_to(total, (128, 128)).T
    level = table[members : members + SUB, :]
    low = low_half((SUB, lat))
    wide = lambda v: jnp.concatenate([v] * (lat // 128), axis=1)
    inverse = wide(cells / level)
    outer, inner = [], []
    for c in range(REACH):
        both = merged_ref[c] * inverse
        swapped = pltpu.roll(both, SUB // 2, 0)
        outer.append(jnp.where(low, both, swapped))
        inner.append(jnp.where(low, swapped, both))
    bary = from_outside(outer + inner, odd)
    bary_ref[...] = jnp.swapaxes(jnp.stack(bary), 0, 1)[: SUB // 2]
    for group in range(groups):
        rows = slice(group * SUB, (group + 1) * SUB)
        factor = wide(table[rows, :] / cells)
        quotients = [ref[c, rows, :] for ref in (outer_ref, inner_ref) for c in range(REACH)]
        out = [b * factor * quotient for b, quotient in zip(bary, from_outside(quotients, odd))]
        span = pl.ds(group * SUB * SUB, SUB * SUB)
        staged_ref[span, :] = jnp.swapaxes(jnp.stack(out), 0, 1).reshape(SUB * SUB, lat)
        pltpu.make_async_copy(staged_ref.at[span, :], updated_ref.at[span, :], sem.at[group]).start()
    for group in range(groups):
        span = pl.ds(group * SUB * SUB, SUB * SUB)
        pltpu.make_async_copy(staged_ref.at[span, :], updated_ref.at[span, :], sem.at[group]).wait()


def shape(*dims):
    return jax.ShapeDtypeStruct(dims, jnp.float32)


def call(kernel, outs, *args, scratch=(), out_specs=None):
    return pl.pallas_call(
        kernel,
        out_shape=outs,
        in_specs=[VMEM] * len(args),
        out_specs=out_specs or (VMEM,) * len(outs),
        scratch_shapes=scratch,
        compiler_params=params(),
    )(*args)


def body(fields, scaling, counts, land_mask):
    members, levels, lon, lat = fields.shape
    tiles = lax.axis_size("tile")
    rows = members * levels
    cells = lon * tiles * lat
    half = shape(REACH, rows, lat)
    edge = shape(2 * REACH - 2, rows, lat)
    packed = shape(REACH, SUB, lat)
    coef = jnp.asarray(coefficients(lat))
    with_mate = [(i, i ^ 1) for i in range(tiles)]
    with_neighbour = [(i, (i + (1 if i % 2 else -1)) % tiles) for i in range(tiles)]
    scaling = scaling.reshape(rows * lon, lat)
    fields = fields.reshape(rows * lon, lat)
    weights = counts.astype(jnp.float32)
    weight_rows = jnp.broadcast_to(jnp.repeat(weights, levels)[:, None], (rows, 128))
    count = jnp.broadcast_to(jnp.sum(weights), (SUB, 128))
    count = count + lax.ppermute(count, "mem", [(0, 1), (1, 0)])

    outer, inner = call(spread_kernel, (half, half), scaling, coef)
    inner_halo = lax.ppermute(inner, "tile", with_mate)
    outer_halo = lax.ppermute(outer, "tile", with_neighbour)
    v_inner, edges, filled, mass = call(
        smooth_inner_kernel, (half, edge, half, shape(rows, 128)), inner_halo, outer, inner, fields, land_mask, coef
    )
    v_inner_halo = lax.ppermute(v_inner, "tile", with_mate)
    (v_outer,) = call(smooth_outer_kernel, (half,), outer_halo, outer, edges, filled, coef)
    v_outer_halo = lax.ppermute(v_outer, "tile", with_neighbour)
    inverse_inner, edges, inner_logs = call(
        return_inner_kernel, (half, edge, packed), v_inner_halo, v_outer, v_inner, inner, weight_rows, coef
    )
    inverse_outer, logs = call(
        return_outer_kernel,
        (half, packed),
        v_outer_halo,
        v_outer,
        edges,
        outer,
        weight_rows,
        inner_logs,
        coef,
        scratch=[pltpu.VMEM((REACH, SUB, lat), jnp.float32)],
    )
    other = lax.ppermute(logs, "mem", [(0, 1), (1, 0)])
    merged, payload = call(merge_kernel, (packed, shape(tiles, 1, 128)), logs, other, count, mass, coef)
    got = lax.all_to_all(payload, "tile", split_axis=0, concat_axis=0)
    barycenter, updated = call(
        lambda *refs: finish_kernel(float(cells), *refs),
        (shape(levels, lon, lat), shape(rows * lon, lat)),
        got,
        merged,
        inverse_outer,
        inverse_inner,
        scratch=[pltpu.VMEM((rows * lon, lat), jnp.float32), pltpu.SemaphoreType.DMA((rows // SUB,))],
        out_specs=(VMEM, HBM),
    )
    return barycenter, updated.reshape(members, levels, lon, lat)


def solution(mesh):
    return jax.shard_map(
        body,
        mesh=mesh,
        in_specs=(
            P("mem", None, "tile", None),
            P("mem", None, "tile", None),
            P("mem"),
            P("tile", None),
        ),
        out_specs=(P(None, "tile", None), P("mem", None, "tile", None)),
        check_vma=False,
    )
```

time: 101 us -> 95.2 us (0.943)
  waiting for transfers between devices: 45.4 us -> 26.2 us
  Pallas kernels: 20.6 us -> 28.8 us
  starting transfers between devices: 10.8 us -> 17.1 us
    ppermute x4, waiting for transfers between devices: 44.2 us -> 25 us  [the longest x1 23 us: body(): outer_halo = lax.ppermute(outer, 'tile', with_neighbour)]
    pallas_call x5 -> x7, Pallas kernels: 20.6 us -> 28.8 us  [call(): pl.pallas_call(kernel, out_shape=outs, in_specs=[VMEM] * len(args), out_s...]
    ppermute x4, starting transfers between devices: 3.61 us -> 10.2 us  [the longest x1 4.48 us: body(): v_inner_halo = lax.ppermute(v_inner, 'tile', with_mate)]
    unnamed x14 -> x12, local copies, waits for them, and re-layouts: 3.23 us -> 2.5 us
  transfers between devices with their start and end apart: 6 -> 6, of which waited for: 4 -> 4; matrix products, arithmetic and copies ran while one was open for 2% -> 2% of each run, Pallas kernels for 9% -> 27%
where the time goes in v2:
time: 95.2 us; the launch traced here: 94.9 us
  Pallas kernels  28.8 us (30%)
  waiting for transfers between devices  26.2 us (28%)
  blocking collectives  17.4 us (18%)
  starting transfers between devices  17.1 us (18%)
  local copies, waits for them, and re-layouts  3.39 us (4%)
  other arithmetic  1.25 us (1%)
    pallas_call x7, Pallas kernels, call(): pl.pallas_call(kernel, out_shape=outs, in_specs=[VMEM] * len(args), out_s...  28.8 us
    ppermute x1, waiting for transfers between devices, body(): outer_halo = lax.ppermute(outer, 'tile', with_neighbour)  23 us
    all_to_all x1, blocking collectives, body(): got = lax.all_to_all(payload, 'tile', split_axis=0, concat_axis=0)  17.4 us
    ppermute x1, starting transfers between devices, body(): v_inner_halo = lax.ppermute(v_inner, 'tile', with_mate)  4.48 us
    ppermute x1, starting transfers between devices, body(): other = lax.ppermute(logs, 'mem', [(0, 1), (1, 0)])  3.43 us
    ppermute x1, starting transfers between devices, body(): count = count + lax.ppermute(count, 'mem', [(0, 1), (1, 0)])  3.43 us
    ppermute x1, starting transfers between devices, body(): v_outer_halo = lax.ppermute(v_outer, 'tile', with_neighbour)  2.56 us
    unnamed x12, local copies, waits for them, and re-layouts  2.5 us
  transfers between devices with their start and end apart: 6, of which 4 were waited for; matrix products, arithmetic and copies ran while one was open for 2% of the time, Pallas kernels for 27%

profile of v2, /device:TPU:1, one launch (start us, length us, event | category | flops | bytes accessed | tf_op | source)
XLA Modules:
  0.0 94.9 jit_solution(11510173331670577270)
XLA Ops:
  0.6 0.0 copy-start
  0.6 0.9 copy-done
  1.5 0.0 copy-start.2
  1.5 1.6 %copy-done.2 = f32[26,4,8,640]{3,2,1,0:T(8,128)S(1)} copy-done((f32[26,4,8,640]{3,2,1,0:T(8,128)S(1)}, f32[26,4,8,640]{3,2,1,0:T(8,128)}, u32[]{:S(2)}) %copy-start.2) | copy-done | bytes 2129944
  3.1 0.0 copy-start.3
  3.1 0.0 copy-start.4
  3.1 0.5 shard_map.68
  3.6 1.5 %collective-permute-start.1 = (f32[4,104,640]{2,1,0:T(8,128)S(1)}, f32[4,104,640]{2,1,0:T(8,128)S(1)}, u32[]{:S(2)}, u32[]{:S(2)}) collective-permute-start(f32[4,104,640]{2,1,0:T(8,128)S(1)} %get-tuple-element.18.inner_ref.scaled_ref), channel_id=1, source_target_pairs={{0,2},{2,0},{4,6},{6,4},{8,10},{10,8},{12,14},{14,12},{16,18},{18,... | collective-permute-start | bytes 3194888 | tf_op jit(solution)/shard_map/ppermute | solution.py:276
  5.1 1.7 %collective-permute-start = (f32[4,104,640]{2,1,0:T(8,128)S(1)}, f32[4,104,640]{2,1,0:T(8,128)S(1)}, u32[]{:S(2)}, u32[]{:S(2)}) collective-permute-start(f32[4,104,640]{2,1,0:T(8,128)S(1)} %get-tuple-element.17.outer_ref.scaled_ref), channel_id=1, source_target_pairs={{0,126},{2,4},{4,2},{6,8},{8,6},{10,12},{12,10},{14,16},{16,14},{1... | collective-permute-start | bytes 3194888 | tf_op jit(solution)/shard_map/ppermute | solution.py:277
  6.8 0.6 collective-permute-done.1.halo_ref
  7.5 0.0 copy-done.3
  7.5 0.0 copy-done.4
  7.5 0.0 copy-start.1
  7.5 6.7 %shard_map.69 = (f32[4,104,640]{2,1,0:T(8,128)}, f32[6,104,640]{2,1,0:T(8,128)S(1)}, f32[4,104,640]{2,1,0:T(8,128)S(1)}, f32[104,128]{1,0:T(8,128)S(1)}) custom-call(f32[4,104,640]{2,1,0:T(8,128)S(1)} %collective-permute-done.1.halo_ref, f32[4,104,640]{2,1,0:T(8,128)S(1)} %get-tuple-element.17.outer_ref.scaled_ref, ...), custom_call_target="tpu_custom_call" | custom-call | tf_op jit(solution)/shard_map/pallas_call | solution.py:247
  14.1 4.5 %collective-permute-start.3 = (f32[4,104,640]{2,1,0:T(8,128)}, f32[4,104,640]{2,1,0:T(8,128)}, u32[]{:S(2)}, u32[]{:S(2)}) collective-permute-start(f32[4,104,640]{2,1,0:T(8,128)} %get-tuple-element.21.inner_ref), channel_id=1, source_target_pairs={{0,2},{2,0},{4,6},{6,4},{8,10},{10,8},{12,14},{14,12},{16,18},{18,... | collective-permute-start | bytes 3194888 | tf_op jit(solution)/shard_map/ppermute | solution.py:281
  18.6 23.0 %collective-permute-done.halo_ref = f32[4,104,640]{2,1,0:T(8,128)S(1)} collective-permute-done((f32[4,104,640]{2,1,0:T(8,128)S(1)}, f32[4,104,640]{2,1,0:T(8,128)S(1)}, u32[]{:S(2)}, u32[]{:S(2)}) %collective-permute-start) | collective-permute-done | bytes 1064992 | tf_op jit(solution)/shard_map/ppermute | solution.py:277
  41.6 0.0 copy-done.1
  41.6 0.0 copy-start.5
  41.6 5.3 %shard_map.70.outer_ref = f32[4,104,640]{2,1,0:T(8,128)S(1)} custom-call(f32[4,104,640]{2,1,0:T(8,128)S(1)} %collective-permute-done.halo_ref, f32[4,104,640]{2,1,0:T(8,128)S(1)} %get-tuple-element.17.outer_ref.scaled_ref, f32[6,104,640]{2,1,0:T(8,128)S(1)} %get-tuple-element.19.edge_ref, f32[4,104,640]{2,1,0:T(8,128)S(1)} %get-tuple-element.20.filled_ref, ...), custom_call_target="tpu_custom_call" | custom-call | tf_op jit(solution)/shard_map/pallas_call | solution.py:247
  46.9 2.6 %collective-permute-start.2 = (f32[4,104,640]{2,1,0:T(8,128)S(1)}, f32[4,104,640]{2,1,0:T(8,128)}, u32[]{:S(2)}, u32[]{:S(2)}) collective-permute-start(f32[4,104,640]{2,1,0:T(8,128)S(1)} %shard_map.70.outer_ref), channel_id=1, source_target_pairs={{0,126},{2,4},{4,2},{6,8},{8,6},{10,12},{12,10},{14,16},{16,14},{1... | collective-permute-start | bytes 3194888 | tf_op jit(solution)/shard_map/ppermute | solution.py:283
  49.5 0.0 copy-done.5
  49.5 0.6 convert_reduce_fusion
  50.1 0.6 broadcast_in_dim.16
  50.7 3.4 %collective-permute-start.5 = (f32[8,128]{1,0:T(8,128)S(1)}, f32[8,128]{1,0:T(8,128)S(1)}, u32[]{:S(2)}, u32[]{:S(2)}) collective-permute-start(f32[8,128]{1,0:T(8,128)S(1)} %broadcast_in_dim.16), channel_id=1, source_target_pairs={{0,1},{1,0},{2,3},{3,2},{4,5},{5,4},{6,7},{7,6},{8,9},{9,8},{10,11... | collective-permute-start | bytes 12296 | tf_op jit(solution)/shard_map/ppermute | solution.py:273
  54.1 0.1 broadcast_in_dim.13
  54.2 0.1 broadcast_in_dim.14
  54.3 0.0 collective-permute-done.3.halo_ref
  54.3 0.1 broadcast_in_dim.15.weight_ref
  54.4 7.3 %shard_map.71 = (f32[4,104,640]{2,1,0:T(8,128)S(1)}, f32[6,104,640]{2,1,0:T(8,128)S(1)}, f32[4,8,640]{2,1,0:T(8,128)S(1)}) custom-call(f32[4,104,640]{2,1,0:T(8,128)} %collective-permute-done.3.halo_ref, f32[4,104,640]{2,1,0:T(8,128)S(1)} %shard_map.70.outer_ref, f32[4,104,640]{2,1,0:T(8,128)} %get-tuple-element.21.inner_ref, ...), custom_call_target="tpu_custom_call" | custom-call | tf_op jit(solution)/shard_map/pallas_call | solution.py:247
  61.7 1.4 %collective-permute-done.2.halo_ref = f32[4,104,640]{2,1,0:T(8,128)} collective-permute-done((f32[4,104,640]{2,1,0:T(8,128)S(1)}, f32[4,104,640]{2,1,0:T(8,128)}, u32[]{:S(2)}, u32[]{:S(2)}) %collective-permute-start.2) | collective-permute-done | bytes 1064992 | tf_op jit(solution)/shard_map/ppermute | solution.py:283
  63.1 6.6 %shard_map.72 = (f32[4,104,640]{2,1,0:T(8,128)S(1)}, f32[4,8,640]{2,1,0:T(8,128)S(1)}) custom-call(f32[4,104,640]{2,1,0:T(8,128)} %collective-permute-done.2.halo_ref, f32[4,104,640]{2,1,0:T(8,128)S(1)} %shard_map.70.outer_ref, f32[6,104,640]{2,1,0:T(8,128)S(1)} %get-tuple-element.22.edge_ref, f32[4,104,640]{2,1,0:T(8,128)S(1)} %get-tuple-element.17.outer_ref.scaled_ref, ...), custom_call_target="tpu_custom_call" | custom-call | tf_op jit(solution)/shard_map/pallas_call | solution.py:247
  69.7 3.4 %collective-permute-start.4 = (f32[4,8,640]{2,1,0:T(8,128)S(1)}, f32[4,8,640]{2,1,0:T(8,128)S(1)}, u32[]{:S(2)}, u32[]{:S(2)}) collective-permute-start(f32[4,8,640]{2,1,0:T(8,128)S(1)} %get-tuple-element.24.own_ref), channel_id=1, source_target_pairs={{0,1},{1,0},{2,3},{3,2},{4,5},{5,4},{6,7},{7,6},{8,9},{9,8},{10,11... | collective-permute-start | bytes 245768 | tf_op jit(solution)/shard_map/ppermute | solution.py:299
  73.1 0.0 collective-permute-done.5
  73.1 0.6 broadcast_add_fusion.count_ref
  73.8 1.2 %collective-permute-done.4.other_ref = f32[4,8,640]{2,1,0:T(8,128)S(1)} collective-permute-done((f32[4,8,640]{2,1,0:T(8,128)S(1)}, f32[4,8,640]{2,1,0:T(8,128)S(1)}, u32[]{:S(2)}, u32[]{:S(2)}) %collective-permute-start.4) | collective-permute-done | bytes 81952 | tf_op jit(solution)/shard_map/ppermute | solution.py:299
  74.9 0.2 shard_map.73
  75.1 17.4 %all_to_all.5.refs_0_ = f32[64,1,128]{2,1,0:T(1,128)S(1)} all-to-all(f32[64,1,128]{2,1,0:T(1,128)S(1)} %get-tuple-element.26), channel_id=1, replica_groups=mesh['tile'=64,'mem'=2] {'tile'}, dimensions={0} | all-to-all | bytes 65536 | tf_op jit(solution)/shard_map/all_to_all | solution.py:301
  92.6 2.3 %shard_map.74 = (f32[4,8,640]{2,1,0:T(8,128)}, f32[832,640]{1,0:T(8,128)}) custom-call(f32[64,1,128]{2,1,0:T(1,128)S(1)} %all_to_all.5.refs_0_, f32[4,8,640]{2,1,0:T(8,128)S(1)} %get-tuple-element.27.refs_1_, f32[4,104,640]{2,1,0:T(8,128)S(1)} %get-tuple-element.28.refs_2_, f32[4,104,640]{2,1,0:T(8,128)S(1)} %get-tuple-element.29.refs_3_), custom_call_target="tpu_custom_call" | custom-call | tf_op jit(solution)/shard_map/pallas_call | solution.py:247
  (1 shorter events, 0.0 us)
Async XLA Ops:
  0.6 0.9 copy-start
  1.5 1.6 %copy-start.2 = (f32[26,4,8,640]{3,2,1,0:T(8,128)S(1)}, f32[26,4,8,640]{3,2,1,0:T(8,128)}, u32[]{:S(2)}) copy-start(f32[26,4,8,640]{3,2,1,0:T(8,128)} %param.6) | copy-start | bytes 6389764
  3.1 4.3 %copy-start.3 = (f32[26,4,8,640]{3,2,1,0:T(8,128)S(1)}, f32[26,4,8,640]{3,2,1,0:T(8,128)}, u32[]{:S(2)}) copy-start(f32[26,4,8,640]{3,2,1,0:T(8,128)} %param.5) | copy-start | bytes 6389764
  3.1 4.3 %copy-start.4 = (s32[8,640]{1,0:T(8,128)S(1)}, s32[8,640]{1,0:T(8,128)}, u32[]{:S(2)}) copy-start(s32[8,640]{1,0:T(8,128)} %mask_ref.1) | copy-start | bytes 61444
  3.6 3.8 %collective-permute-start.1 = (f32[4,104,640]{2,1,0:T(8,128)S(1)}, f32[4,104,640]{2,1,0:T(8,128)S(1)}, u32[]{:S(2)}, u32[]{:S(2)}) collective-permute-start(f32[4,104,640]{2,1,0:T(8,128)S(1)} %get-tuple-element.18.inner_ref.scaled_ref), channel_id=1, source_target_pairs={{0,2},{2,0},{4,6},{6,4},{8,10},{10,8},{12,14},{14,12},{16,18},{18,... | collective-permute-start | bytes 3194888 | tf_op jit(solution)/shard_map/ppermute | solution.py:276
  5.1 36.4 %collective-permute-start = (f32[4,104,640]{2,1,0:T(8,128)S(1)}, f32[4,104,640]{2,1,0:T(8,128)S(1)}, u32[]{:S(2)}, u32[]{:S(2)}) collective-permute-start(f32[4,104,640]{2,1,0:T(8,128)S(1)} %get-tuple-element.17.outer_ref.scaled_ref), channel_id=1, source_target_pairs={{0,126},{2,4},{4,2},{6,8},{8,6},{10,12},{12,10},{14,16},{16,14},{1... | collective-permute-start | bytes 3194888 | tf_op jit(solution)/shard_map/ppermute | solution.py:277
  7.5 34.1 %copy-start.1 = (f32[5,8,640]{2,1,0:T(8,128)S(1)}, f32[5,8,640]{2,1,0:T(8,128)}, u32[]{:S(2)}) copy-start(f32[5,8,640]{2,1,0:T(8,128)} %constant.4.clone.coef_ref) | copy-start | bytes 307204
  14.1 40.2 %collective-permute-start.3 = (f32[4,104,640]{2,1,0:T(8,128)}, f32[4,104,640]{2,1,0:T(8,128)}, u32[]{:S(2)}, u32[]{:S(2)}) collective-permute-start(f32[4,104,640]{2,1,0:T(8,128)} %get-tuple-element.21.inner_ref), channel_id=1, source_target_pairs={{0,2},{2,0},{4,6},{6,4},{8,10},{10,8},{12,14},{14,12},{16,18},{18,... | collective-permute-start | bytes 3194888 | tf_op jit(solution)/shard_map/ppermute | solution.py:281
  41.6 7.9 %copy-start.5 = (s32[26]{0:T(128)S(1)}, s32[26]{0:T(128)}, u32[]{:S(2)}) copy-start(s32[26]{0:T(128)} %param.7) | copy-start | bytes 316
  46.9 16.2 %collective-permute-start.2 = (f32[4,104,640]{2,1,0:T(8,128)S(1)}, f32[4,104,640]{2,1,0:T(8,128)}, u32[]{:S(2)}, u32[]{:S(2)}) collective-permute-start(f32[4,104,640]{2,1,0:T(8,128)S(1)} %shard_map.70.outer_ref), channel_id=1, source_target_pairs={{0,126},{2,4},{4,2},{6,8},{8,6},{10,12},{12,10},{14,16},{16,14},{1... | collective-permute-start | bytes 3194888 | tf_op jit(solution)/shard_map/ppermute | solution.py:283
  50.7 22.4 %collective-permute-start.5 = (f32[8,128]{1,0:T(8,128)S(1)}, f32[8,128]{1,0:T(8,128)S(1)}, u32[]{:S(2)}, u32[]{:S(2)}) collective-permute-start(f32[8,128]{1,0:T(8,128)S(1)} %broadcast_in_dim.16), channel_id=1, source_target_pairs={{0,1},{1,0},{2,3},{3,2},{4,5},{5,4},{6,7},{7,6},{8,9},{9,8},{10,11... | collective-permute-start | bytes 12296 | tf_op jit(solution)/shard_map/ppermute | solution.py:273
  69.7 5.3 %collective-permute-start.4 = (f32[4,8,640]{2,1,0:T(8,128)S(1)}, f32[4,8,640]{2,1,0:T(8,128)S(1)}, u32[]{:S(2)}, u32[]{:S(2)}) collective-permute-start(f32[4,8,640]{2,1,0:T(8,128)S(1)} %get-tuple-element.24.own_ref), channel_id=1, source_target_pairs={{0,1},{1,0},{2,3},{3,2},{4,5},{5,4},{6,7},{7,6},{8,9},{9,8},{10,11... | collective-permute-start | bytes 245768 | tf_op jit(solution)/shard_map/ppermute | solution.py:299

commit v3 on v2

--- a/solution.py
+++ b/solution.py
@@ -34,11 +34,15 @@
 
 
 def rows_of(group):
-    return pl.ds(pl.multiple_of(group * SUB, SUB), SUB)
+    return pl.ds(group * SUB, SUB)
 
 
 def block_of(group):
-    return pl.ds(pl.multiple_of(group * SUB * SUB, SUB * SUB), SUB * SUB)
+    return pl.ds(group * SUB * SUB, SUB * SUB)
+
+
+def batches(groups, size=4):
+    return [range(first, min(first + size, groups)) for first in range(0, groups, size)]
 
 
 def by_longitude(block, lat):
@@ -61,15 +65,11 @@
 def spread_kernel(scaling_ref, coef_ref, outer_ref, inner_ref):
     groups, lat = outer_ref.shape[1] // SUB, outer_ref.shape[2]
     odd = odd_core()
-
-    def step(group, carry):
+    for group in range(groups):
         columns = from_outside(by_longitude(scaling_ref[block_of(group), :], lat), odd)
         for c in range(REACH):
             outer_ref[c, rows_of(group), :] = columns[c] * coef_ref[AREA]
             inner_ref[c, rows_of(group), :] = columns[c + REACH] * coef_ref[AREA]
-        return carry
-
-    lax.fori_loop(0, groups, step, 0)
 
 
 def lane_fold(value):
@@ -91,23 +91,24 @@
     ]
 
 
-def inner_half(group, halo_ref, outer_ref, inner_ref, coef_ref, edge_ref):
-    columns = stack_of(outer_ref, group) + stack_of(inner_ref, group) + stack_of(halo_ref, group, (3, 2, 1, 0))
+def inner_half(batch, halo_ref, outer_ref, inner_ref, coef_ref, edge_ref):
+    columns = [stack_of(outer_ref, g) + stack_of(inner_ref, g) + stack_of(halo_ref, g, (3, 2, 1, 0)) for g in batch]
     for s in range(REACH):
-        columns = diffuse(columns, coef_ref)
+        columns = [diffuse(own, coef_ref) for own in columns]
         if s < REACH - 1:
-            edge_ref[2 * s, rows_of(group), :] = columns[0]
-            edge_ref[2 * s + 1, rows_of(group), :] = columns[1]
-    return columns
-
-
-def outer_half(group, halo_ref, outer_ref, edge_ref, coef_ref):
-    columns = stack_of(halo_ref, group, (3, 2, 1, 0)) + stack_of(outer_ref, group, (0, 1))
+            for own, group in zip(columns, batch):
+                edge_ref[2 * s, rows_of(group), :] = own[0]
+                edge_ref[2 * s + 1, rows_of(group), :] = own[1]
+    return zip(batch, columns)
+
+
+def outer_half(batch, halo_ref, outer_ref, edge_ref, coef_ref):
+    columns = [stack_of(halo_ref, g, (3, 2, 1, 0)) + stack_of(outer_ref, g, (0, 1)) for g in batch]
     for s in range(REACH):
-        columns = diffuse(columns, coef_ref)
+        columns = [diffuse(own, coef_ref) for own in columns]
         if s < REACH - 1:
-            columns = columns + stack_of(edge_ref, group, (2 * s, 2 * s + 1))
-    return columns
+            columns = [own + stack_of(edge_ref, g, (2 * s, 2 * s + 1)) for own, g in zip(columns, batch)]
+    return zip(batch, columns)
 
 
 def smooth_inner_kernel(
@@ -115,34 +116,26 @@
 ):
     groups, lat = outer_ref.shape[1] // SUB, outer_ref.shape[2]
     odd = odd_core()
-
-    def step(group, carry):
-        smoothed = inner_half(group, halo_ref, outer_ref, inner_ref, coef_ref, edge_ref)
-        fields = by_longitude(fields_ref[block_of(group), :], lat)
-        filled = []
-        for c in range(2 * REACH):
-            valid = jnp.broadcast_to(mask_ref[c : c + 1, :], (SUB, lat)) == 1
-            filled.append((jnp.where(valid, fields[c], 0.0) + BACKGROUND) * coef_ref[AREA])
-        mass_ref[rows_of(group), :] = lane_fold(sum(filled))
-        filled = from_outside(filled, odd)
-        for c in range(REACH):
-            filled_ref[c, rows_of(group), :] = filled[c]
-            out_ref[c, rows_of(group), :] = filled[c + REACH] / smoothed[c]
-        return carry
-
-    lax.fori_loop(0, groups, step, 0)
+    for batch in batches(groups):
+        for group, smoothed in inner_half(batch, halo_ref, outer_ref, inner_ref, coef_ref, edge_ref):
+            fields = by_longitude(fields_ref[block_of(group), :], lat)
+            filled = []
+            for c in range(2 * REACH):
+                valid = jnp.broadcast_to(mask_ref[c : c + 1, :], (SUB, lat)) == 1
+                filled.append((jnp.where(valid, fields[c], 0.0) + BACKGROUND) * coef_ref[AREA])
+            mass_ref[rows_of(group), :] = lane_fold(sum(filled))
+            filled = from_outside(filled, odd)
+            for c in range(REACH):
+                filled_ref[c, rows_of(group), :] = filled[c]
+                out_ref[c, rows_of(group), :] = filled[c + REACH] / smoothed[c]
 
 
 def smooth_outer_kernel(halo_ref, outer_ref, edge_ref, filled_ref, coef_ref, out_ref):
     groups = outer_ref.shape[1] // SUB
-
-    def step(group, carry):
-        smoothed = outer_half(group, halo_ref, outer_ref, edge_ref, coef_ref)
-        for c in range(REACH):
-            out_ref[c, rows_of(group), :] = filled_ref[c, rows_of(group), :] / smoothed[c]
-        return carry
-
-    lax.fori_loop(0, groups, step, 0)
+    for batch in batches(groups):
+        for group, smoothed in outer_half(batch, halo_ref, outer_ref, edge_ref, coef_ref):
+            for c in range(REACH):
+                out_ref[c, rows_of(group), :] = filled_ref[c, rows_of(group), :] / smoothed[c]
 
 
 def low_half(shape):
@@ -162,13 +155,9 @@
 ):
     groups = outer_ref.shape[1] // SUB
     total_ref[...] = jnp.zeros_like(total_ref)
-
-    def step(group, carry):
-        result = inner_half(group, halo_ref, outer_ref, inner_ref, coef_ref, edge_ref)
-        add_logs(group, result, scaled_ref, weight_ref, inverse_ref, total_ref)
-        return carry
-
-    lax.fori_loop(0, groups, step, 0)
+    for batch in batches(groups):
+        for group, result in inner_half(batch, halo_ref, outer_ref, inner_ref, coef_ref, edge_ref):
+            add_logs(group, result, scaled_ref, weight_ref, inverse_ref, total_ref)
 
 
 def return_outer_kernel(
@@ -176,13 +165,9 @@
 ):
     groups, lat = outer_ref.shape[1] // SUB, outer_ref.shape[2]
     total_ref[...] = jnp.zeros_like(total_ref)
-
-    def step(group, carry):
-        result = outer_half(group, halo_ref, outer_ref, edge_ref, coef_ref)
-        add_logs(group, result, scaled_ref, weight_ref, inverse_ref, total_ref)
-        return carry
-
-    lax.fori_loop(0, groups, step, 0)
+    for batch in batches(groups):
+        for group, result in outer_half(batch, halo_ref, outer_ref, edge_ref, coef_ref):
+            add_logs(group, result, scaled_ref, weight_ref, inverse_ref, total_ref)
     low = low_half((SUB, lat))
     for c in range(REACH):
         outer, inner = total_ref[c], inner_ref[c]

time: 95.2 us -> 89.7 us (0.942)
  Pallas kernels: 28.8 us -> 20.7 us
  waiting for transfers between devices: 26.2 us -> 28.9 us
    pallas_call x7, Pallas kernels: 28.8 us -> 20.7 us  [call(): pl.pallas_call(kernel, out_shape=outs, in_specs=[VMEM] * len(args), out_s...]
    ppermute x1, waiting for transfers between devices: 1.4 us -> 2.71 us  [body(): v_outer_halo = lax.ppermute(v_outer, 'tile', with_neighbour)]
    ppermute x1, waiting for transfers between devices: 23 us -> 24 us  [body(): outer_halo = lax.ppermute(outer, 'tile', with_neighbour)]
  transfers between devices with their start and end apart: 6 -> 6, of which waited for: 4 -> 4; matrix products, arithmetic and copies ran while one was open for 2% -> 2% of each run, Pallas kernels for 27% -> 20%
where the time goes in v3:
time: 89.7 us; the launch traced here: 89.4 us
  waiting for transfers between devices  28.9 us (32%)
  Pallas kernels  20.7 us (23%)
  blocking collectives  17.8 us (20%)
  starting transfers between devices  16.4 us (18%)
  local copies, waits for them, and re-layouts  3.39 us (4%)
  other arithmetic  1.25 us (1%)
    ppermute x1, waiting for transfers between devices, body(): outer_halo = lax.ppermute(outer, 'tile', with_neighbour)  24 us
    pallas_call x7, Pallas kernels, call(): pl.pallas_call(kernel, out_shape=outs, in_specs=[VMEM] * len(args), out_s...  20.7 us
    all_to_all x1, blocking collectives, body(): got = lax.all_to_all(payload, 'tile', split_axis=0, concat_axis=0)  17.8 us
    ppermute x1, starting transfers between devices, body(): v_inner_halo = lax.ppermute(v_inner, 'tile', with_mate)  4.47 us
    ppermute x1, starting transfers between devices, body(): count = count + lax.ppermute(count, 'mem', [(0, 1), (1, 0)])  3.56 us
    ppermute x1, waiting for transfers between devices, body(): v_outer_halo = lax.ppermute(v_outer, 'tile', with_neighbour)  2.71 us
    ppermute x1, starting transfers between devices, body(): other = lax.ppermute(logs, 'mem', [(0, 1), (1, 0)])  2.63 us
    ppermute x1, starting transfers between devices, body(): v_outer_halo = lax.ppermute(v_outer, 'tile', with_neighbour)  2.56 us
  transfers between devices with their start and end apart: 6, of which 4 were waited for; matrix products, arithmetic and copies ran while one was open for 2% of the time, Pallas kernels for 20%

profile of v3, /device:TPU:1, one launch (start us, length us, event | category | flops | bytes accessed | tf_op | source)
XLA Modules:
  0.0 89.4 jit_solution(5014364012486146230)
XLA Ops:
  0.6 0.0 copy-start
  0.6 0.9 copy-done
  1.5 0.0 copy-start.2
  1.5 1.6 %copy-done.2 = f32[26,4,8,640]{3,2,1,0:T(8,128)S(1)} copy-done((f32[26,4,8,640]{3,2,1,0:T(8,128)S(1)}, f32[26,4,8,640]{3,2,1,0:T(8,128)}, u32[]{:S(2)}) %copy-start.2) | copy-done | bytes 2129944
  3.1 0.0 copy-start.3
  3.1 0.0 copy-start.4
  3.1 0.4 shard_map.68
  3.6 1.5 %collective-permute-start.1 = (f32[4,104,640]{2,1,0:T(8,128)S(1)}, f32[4,104,640]{2,1,0:T(8,128)S(1)}, u32[]{:S(2)}, u32[]{:S(2)}) collective-permute-start(f32[4,104,640]{2,1,0:T(8,128)S(1)} %get-tuple-element.18.inner_ref.scaled_ref), channel_id=1, source_target_pairs={{0,2},{2,0},{4,6},{6,4},{8,10},{10,8},{12,14},{14,12},{16,18},{18,... | collective-permute-start | bytes 3194888 | tf_op jit(solution)/shard_map/ppermute | solution.py:261
  5.1 1.7 %collective-permute-start = (f32[4,104,640]{2,1,0:T(8,128)S(1)}, f32[4,104,640]{2,1,0:T(8,128)S(1)}, u32[]{:S(2)}, u32[]{:S(2)}) collective-permute-start(f32[4,104,640]{2,1,0:T(8,128)S(1)} %get-tuple-element.17.outer_ref.scaled_ref), channel_id=1, source_target_pairs={{0,126},{2,4},{4,2},{6,8},{8,6},{10,12},{12,10},{14,16},{16,14},{1... | collective-permute-start | bytes 3194888 | tf_op jit(solution)/shard_map/ppermute | solution.py:262
  6.8 0.6 collective-permute-done.1.halo_ref
  7.4 0.0 copy-done.3
  7.4 0.0 copy-done.4
  7.4 0.0 copy-start.1
  7.4 5.7 %shard_map.69 = (f32[4,104,640]{2,1,0:T(8,128)}, f32[6,104,640]{2,1,0:T(8,128)S(1)}, f32[4,104,640]{2,1,0:T(8,128)S(1)}, f32[104,128]{1,0:T(8,128)S(1)}) custom-call(f32[4,104,640]{2,1,0:T(8,128)S(1)} %collective-permute-done.1.halo_ref, f32[4,104,640]{2,1,0:T(8,128)S(1)} %get-tuple-element.17.outer_ref.scaled_ref, ...), custom_call_target="tpu_custom_call" | custom-call | tf_op jit(solution)/shard_map/pallas_call | solution.py:232
  13.1 4.5 %collective-permute-start.3 = (f32[4,104,640]{2,1,0:T(8,128)}, f32[4,104,640]{2,1,0:T(8,128)}, u32[]{:S(2)}, u32[]{:S(2)}) collective-permute-start(f32[4,104,640]{2,1,0:T(8,128)} %get-tuple-element.21.inner_ref), channel_id=1, source_target_pairs={{0,2},{2,0},{4,6},{6,4},{8,10},{10,8},{12,14},{14,12},{16,18},{18,... | collective-permute-start | bytes 3194888 | tf_op jit(solution)/shard_map/ppermute | solution.py:266
  17.6 24.0 %collective-permute-done.halo_ref = f32[4,104,640]{2,1,0:T(8,128)S(1)} collective-permute-done((f32[4,104,640]{2,1,0:T(8,128)S(1)}, f32[4,104,640]{2,1,0:T(8,128)S(1)}, u32[]{:S(2)}, u32[]{:S(2)}) %collective-permute-start) | collective-permute-done | bytes 1064992 | tf_op jit(solution)/shard_map/ppermute | solution.py:262
  41.6 0.0 copy-done.1
  41.6 0.0 copy-start.5
  41.6 2.6 %shard_map.70.outer_ref = f32[4,104,640]{2,1,0:T(8,128)S(1)} custom-call(f32[4,104,640]{2,1,0:T(8,128)S(1)} %collective-permute-done.halo_ref, f32[4,104,640]{2,1,0:T(8,128)S(1)} %get-tuple-element.17.outer_ref.scaled_ref, f32[6,104,640]{2,1,0:T(8,128)S(1)} %get-tuple-element.19.edge_ref, f32[4,104,640]{2,1,0:T(8,128)S(1)} %get-tuple-element.20.filled_ref, ...), custom_call_target="tpu_custom_call" | custom-call | tf_op jit(solution)/shard_map/pallas_call | solution.py:232
  44.1 2.6 %collective-permute-start.2 = (f32[4,104,640]{2,1,0:T(8,128)S(1)}, f32[4,104,640]{2,1,0:T(8,128)}, u32[]{:S(2)}, u32[]{:S(2)}) collective-permute-start(f32[4,104,640]{2,1,0:T(8,128)S(1)} %shard_map.70.outer_ref), channel_id=1, source_target_pairs={{0,126},{2,4},{4,2},{6,8},{8,6},{10,12},{12,10},{14,16},{16,14},{1... | collective-permute-start | bytes 3194888 | tf_op jit(solution)/shard_map/ppermute | solution.py:268
  46.7 0.0 copy-done.5
  46.7 0.6 convert_reduce_fusion
  47.3 0.6 broadcast_in_dim.16
  48.0 3.6 %collective-permute-start.5 = (f32[8,128]{1,0:T(8,128)S(1)}, f32[8,128]{1,0:T(8,128)S(1)}, u32[]{:S(2)}, u32[]{:S(2)}) collective-permute-start(f32[8,128]{1,0:T(8,128)S(1)} %broadcast_in_dim.16), channel_id=1, source_target_pairs={{0,1},{1,0},{2,3},{3,2},{4,5},{5,4},{6,7},{7,6},{8,9},{9,8},{10,11... | collective-permute-start | bytes 12296 | tf_op jit(solution)/shard_map/ppermute | solution.py:258
  51.5 0.1 broadcast_in_dim.13
  51.6 0.1 broadcast_in_dim.14
  51.7 0.0 collective-permute-done.3.halo_ref
  51.7 0.1 broadcast_in_dim.15.weight_ref
  51.8 5.7 %shard_map.71 = (f32[4,104,640]{2,1,0:T(8,128)S(1)}, f32[6,104,640]{2,1,0:T(8,128)S(1)}, f32[4,8,640]{2,1,0:T(8,128)S(1)}) custom-call(f32[4,104,640]{2,1,0:T(8,128)} %collective-permute-done.3.halo_ref, f32[4,104,640]{2,1,0:T(8,128)S(1)} %shard_map.70.outer_ref, f32[4,104,640]{2,1,0:T(8,128)} %get-tuple-element.21.inner_ref, ...), custom_call_target="tpu_custom_call" | custom-call | tf_op jit(solution)/shard_map/pallas_call | solution.py:232
  57.5 2.7 %collective-permute-done.2.halo_ref = f32[4,104,640]{2,1,0:T(8,128)} collective-permute-done((f32[4,104,640]{2,1,0:T(8,128)S(1)}, f32[4,104,640]{2,1,0:T(8,128)}, u32[]{:S(2)}, u32[]{:S(2)}) %collective-permute-start.2) | collective-permute-done | bytes 1064992 | tf_op jit(solution)/shard_map/ppermute | solution.py:268
  60.2 3.8 %shard_map.72 = (f32[4,104,640]{2,1,0:T(8,128)S(1)}, f32[4,8,640]{2,1,0:T(8,128)S(1)}) custom-call(f32[4,104,640]{2,1,0:T(8,128)} %collective-permute-done.2.halo_ref, f32[4,104,640]{2,1,0:T(8,128)S(1)} %shard_map.70.outer_ref, f32[6,104,640]{2,1,0:T(8,128)S(1)} %get-tuple-element.22.edge_ref, f32[4,104,640]{2,1,0:T(8,128)S(1)} %get-tuple-element.17.outer_ref.scaled_ref, ...), custom_call_target="tpu_custom_call" | custom-call | tf_op jit(solution)/shard_map/pallas_call | solution.py:232
  64.0 2.6 %collective-permute-start.4 = (f32[4,8,640]{2,1,0:T(8,128)S(1)}, f32[4,8,640]{2,1,0:T(8,128)S(1)}, u32[]{:S(2)}, u32[]{:S(2)}) collective-permute-start(f32[4,8,640]{2,1,0:T(8,128)S(1)} %get-tuple-element.24.own_ref), channel_id=1, source_target_pairs={{0,1},{1,0},{2,3},{3,2},{4,5},{5,4},{6,7},{7,6},{8,9},{9,8},{10,11... | collective-permute-start | bytes 245768 | tf_op jit(solution)/shard_map/ppermute | solution.py:284
  66.6 0.0 collective-permute-done.5
  66.6 0.6 broadcast_add_fusion.count_ref
  67.3 1.6 %collective-permute-done.4.other_ref = f32[4,8,640]{2,1,0:T(8,128)S(1)} collective-permute-done((f32[4,8,640]{2,1,0:T(8,128)S(1)}, f32[4,8,640]{2,1,0:T(8,128)S(1)}, u32[]{:S(2)}, u32[]{:S(2)}) %collective-permute-start.4) | collective-permute-done | bytes 81952 | tf_op jit(solution)/shard_map/ppermute | solution.py:284
  68.9 0.2 shard_map.73
  69.1 17.8 %all_to_all.5.refs_0_ = f32[64,1,128]{2,1,0:T(1,128)S(1)} all-to-all(f32[64,1,128]{2,1,0:T(1,128)S(1)} %get-tuple-element.26), channel_id=1, replica_groups=mesh['tile'=64,'mem'=2] {'tile'}, dimensions={0} | all-to-all | bytes 65536 | tf_op jit(solution)/shard_map/all_to_all | solution.py:286
  86.9 2.3 %shard_map.74 = (f32[4,8,640]{2,1,0:T(8,128)}, f32[832,640]{1,0:T(8,128)}) custom-call(f32[64,1,128]{2,1,0:T(1,128)S(1)} %all_to_all.5.refs_0_, f32[4,8,640]{2,1,0:T(8,128)S(1)} %get-tuple-element.27.refs_1_, f32[4,104,640]{2,1,0:T(8,128)S(1)} %get-tuple-element.28.refs_2_, f32[4,104,640]{2,1,0:T(8,128)S(1)} %get-tuple-element.29.refs_3_), custom_call_target="tpu_custom_call" | custom-call | tf_op jit(solution)/shard_map/pallas_call | solution.py:232
  (1 shorter events, 0.0 us)
Async XLA Ops:
  0.6 0.9 %copy-start = (f32[5,8,640]{2,1,0:T(8,128)S(1)}, f32[5,8,640]{2,1,0:T(8,128)}, u32[]{:S(2)}) copy-start(f32[5,8,640]{2,1,0:T(8,128)} %constant.4.clone.coef_ref) | copy-start | bytes 307204
  1.5 1.6 %copy-start.2 = (f32[26,4,8,640]{3,2,1,0:T(8,128)S(1)}, f32[26,4,8,640]{3,2,1,0:T(8,128)}, u32[]{:S(2)}) copy-start(f32[26,4,8,640]{3,2,1,0:T(8,128)} %param.6) | copy-start | bytes 6389764
  3.1 4.3 %copy-start.3 = (f32[26,4,8,640]{3,2,1,0:T(8,128)S(1)}, f32[26,4,8,640]{3,2,1,0:T(8,128)}, u32[]{:S(2)}) copy-start(f32[26,4,8,640]{3,2,1,0:T(8,128)} %param.5) | copy-start | bytes 6389764
  3.1 4.3 %copy-start.4 = (s32[8,640]{1,0:T(8,128)S(1)}, s32[8,640]{1,0:T(8,128)}, u32[]{:S(2)}) copy-start(s32[8,640]{1,0:T(8,128)} %mask_ref.1) | copy-start | bytes 61444
  3.6 3.8 %collective-permute-start.1 = (f32[4,104,640]{2,1,0:T(8,128)S(1)}, f32[4,104,640]{2,1,0:T(8,128)S(1)}, u32[]{:S(2)}, u32[]{:S(2)}) collective-permute-start(f32[4,104,640]{2,1,0:T(8,128)S(1)} %get-tuple-element.18.inner_ref.scaled_ref), channel_id=1, source_target_pairs={{0,2},{2,0},{4,6},{6,4},{8,10},{10,8},{12,14},{14,12},{16,18},{18,... | collective-permute-start | bytes 3194888 | tf_op jit(solution)/shard_map/ppermute | solution.py:261
  5.1 36.5 %collective-permute-start = (f32[4,104,640]{2,1,0:T(8,128)S(1)}, f32[4,104,640]{2,1,0:T(8,128)S(1)}, u32[]{:S(2)}, u32[]{:S(2)}) collective-permute-start(f32[4,104,640]{2,1,0:T(8,128)S(1)} %get-tuple-element.17.outer_ref.scaled_ref), channel_id=1, source_target_pairs={{0,126},{2,4},{4,2},{6,8},{8,6},{10,12},{12,10},{14,16},{16,14},{1... | collective-permute-start | bytes 3194888 | tf_op jit(solution)/shard_map/ppermute | solution.py:262
  7.4 34.2 %copy-start.1 = (f32[5,8,640]{2,1,0:T(8,128)S(1)}, f32[5,8,640]{2,1,0:T(8,128)}, u32[]{:S(2)}) copy-start(f32[5,8,640]{2,1,0:T(8,128)} %constant.4.clone.coef_ref) | copy-start | bytes 307204
  13.1 38.6 %collective-permute-start.3 = (f32[4,104,640]{2,1,0:T(8,128)}, f32[4,104,640]{2,1,0:T(8,128)}, u32[]{:S(2)}, u32[]{:S(2)}) collective-permute-start(f32[4,104,640]{2,1,0:T(8,128)} %get-tuple-element.21.inner_ref), channel_id=1, source_target_pairs={{0,2},{2,0},{4,6},{6,4},{8,10},{10,8},{12,14},{14,12},{16,18},{18,... | collective-permute-start | bytes 3194888 | tf_op jit(solution)/shard_map/ppermute | solution.py:266
  41.6 5.1 %copy-start.5 = (s32[26]{0:T(128)S(1)}, s32[26]{0:T(128)}, u32[]{:S(2)}) copy-start(s32[26]{0:T(128)} %param.7) | copy-start | bytes 316
  44.1 16.1 %collective-permute-start.2 = (f32[4,104,640]{2,1,0:T(8,128)S(1)}, f32[4,104,640]{2,1,0:T(8,128)}, u32[]{:S(2)}, u32[]{:S(2)}) collective-permute-start(f32[4,104,640]{2,1,0:T(8,128)S(1)} %shard_map.70.outer_ref), channel_id=1, source_target_pairs={{0,126},{2,4},{4,2},{6,8},{8,6},{10,12},{12,10},{14,16},{16,14},{1... | collective-permute-start | bytes 3194888 | tf_op jit(solution)/shard_map/ppermute | solution.py:268
  48.0 18.7 %collective-permute-start.5 = (f32[8,128]{1,0:T(8,128)S(1)}, f32[8,128]{1,0:T(8,128)S(1)}, u32[]{:S(2)}, u32[]{:S(2)}) collective-permute-start(f32[8,128]{1,0:T(8,128)S(1)} %broadcast_in_dim.16), channel_id=1, source_target_pairs={{0,1},{1,0},{2,3},{3,2},{4,5},{5,4},{6,7},{7,6},{8,9},{9,8},{10,11... | collective-permute-start | bytes 12296 | tf_op jit(solution)/shard_map/ppermute | solution.py:258
  64.0 4.9 %collective-permute-start.4 = (f32[4,8,640]{2,1,0:T(8,128)S(1)}, f32[4,8,640]{2,1,0:T(8,128)S(1)}, u32[]{:S(2)}, u32[]{:S(2)}) collective-permute-start(f32[4,8,640]{2,1,0:T(8,128)S(1)} %get-tuple-element.24.own_ref), channel_id=1, source_target_pairs={{0,1},{1,0},{2,3},{3,2},{4,5},{5,4},{6,7},{7,6},{8,9},{9,8},{10,11... | collective-permute-start | bytes 245768 | tf_op jit(solution)/shard_map/ppermute | solution.py:284

commit v4 on v3

--- a/solution.py
+++ b/solution.py
@@ -1,4 +1,5 @@
 import math
+from functools import partial
 
 import jax
 import jax.numpy as jnp
@@ -41,8 +42,33 @@
     return pl.ds(group * SUB * SUB, SUB * SUB)
 
 
-def batches(groups, size=4):
-    return [range(first, min(first + size, groups)) for first in range(0, groups, size)]
+def batches(last, first=0, size=4):
+    return [range(start, min(start + size, last)) for start in range(first, last, size)]
+
+
+def chunk_groups(groups):
+    half = (groups + 1) // 2
+    return [half, groups - half]
+
+
+class Chunked:
+    def __init__(self, refs):
+        self.refs = refs
+
+    def stack(self, group, order=range(REACH)):
+        for ref in self.refs:
+            held = ref.shape[1] // SUB
+            if group < held:
+                return stack_of(ref, group, order)
+            group -= held
+
+    def put(self, group, values):
+        for ref in self.refs:
+            held = ref.shape[1] // SUB
+            if 0 <= group < held:
+                for c, value in enumerate(values):
+                    ref[c, rows_of(group), :] = value
+            group -= held
 
 
 def by_longitude(block, lat):
@@ -62,14 +88,16 @@
     return [jnp.where(odd, columns[last - c], columns[c]) for c in range(len(columns))]
 
 
-def spread_kernel(scaling_ref, coef_ref, outer_ref, inner_ref):
-    groups, lat = outer_ref.shape[1] // SUB, outer_ref.shape[2]
+def spread_kernel(scaling_ref, coef_ref, inner_ref, *outer_refs):
+    groups, lat = inner_ref.shape[1] // SUB, inner_ref.shape[2]
     odd = odd_core()
+    outer = Chunked(outer_refs)
     for group in range(groups):
         columns = from_outside(by_longitude(scaling_ref[block_of(group), :], lat), odd)
+        columns = [column * coef_ref[AREA] for column in columns]
+        outer.put(group, columns[:REACH])
         for c in range(REACH):
-            outer_ref[c, rows_of(group), :] = columns[c] * coef_ref[AREA]
-            inner_ref[c, rows_of(group), :] = columns[c + REACH] * coef_ref[AREA]
+            inner_ref[c, rows_of(group), :] = columns[c + REACH]
 
 
 def lane_fold(value):
@@ -91,8 +119,9 @@
     ]
 
 
-def inner_half(batch, halo_ref, outer_ref, inner_ref, coef_ref, edge_ref):
-    columns = [stack_of(outer_ref, g) + stack_of(inner_ref, g) + stack_of(halo_ref, g, (3, 2, 1, 0)) for g in batch]
+def inner_half(batch, halo_ref, inner_ref, outer_refs, coef_ref, edge_ref):
+    outer = Chunked(outer_refs)
+    columns = [outer.stack(g) + stack_of(inner_ref, g) + stack_of(halo_ref, g, (3, 2, 1, 0)) for g in batch]
     for s in range(REACH):
         columns = [diffuse(own, coef_ref) for own in columns]
         if s < REACH - 1:
@@ -102,8 +131,8 @@
     return zip(batch, columns)
 
 
-def outer_half(batch, halo_ref, outer_ref, edge_ref, coef_ref):
-    columns = [stack_of(halo_ref, g, (3, 2, 1, 0)) + stack_of(outer_ref, g, (0, 1)) for g in batch]
+def outer_half(batch, first, halo_ref, outer_ref, edge_ref, coef_ref):
+    columns = [stack_of(halo_ref, g - first, (3, 2, 1, 0)) + stack_of(outer_ref, g - first, (0, 1)) for g in batch]
     for s in range(REACH):
         columns = [diffuse(own, coef_ref) for own in columns]
         if s < REACH - 1:
@@ -112,12 +141,13 @@
 
 
 def smooth_inner_kernel(
-    halo_ref, outer_ref, inner_ref, fields_ref, mask_ref, coef_ref, out_ref, edge_ref, filled_ref, mass_ref
+    halo_ref, inner_ref, fields_ref, mask_ref, coef_ref, *refs
 ):
-    groups, lat = outer_ref.shape[1] // SUB, outer_ref.shape[2]
+    *outer_refs, out_ref, edge_ref, filled_ref, mass_ref = refs
+    groups, lat = inner_ref.shape[1] // SUB, inner_ref.shape[2]
     odd = odd_core()
     for batch in batches(groups):
-        for group, smoothed in inner_half(batch, halo_ref, outer_ref, inner_ref, coef_ref, edge_ref):
+        for group, smoothed in inner_half(batch, halo_ref, inner_ref, outer_refs, coef_ref, edge_ref):
             fields = by_longitude(fields_ref[block_of(group), :], lat)
             filled = []
             for c in range(2 * REACH):
@@ -130,47 +160,65 @@
                 out_ref[c, rows_of(group), :] = filled[c + REACH] / smoothed[c]
 
 
-def smooth_outer_kernel(halo_ref, outer_ref, edge_ref, filled_ref, coef_ref, out_ref):
-    groups = outer_ref.shape[1] // SUB
-    for batch in batches(groups):
-        for group, smoothed in outer_half(batch, halo_ref, outer_ref, edge_ref, coef_ref):
+def smooth_outer_kernel(first, halo_ref, outer_ref, edge_ref, filled_ref, coef_ref, out_ref):
+    last = first + outer_ref.shape[1] // SUB
+    for batch in batches(last, first):
+        for group, smoothed in outer_half(batch, first, halo_ref, outer_ref, edge_ref, coef_ref):
             for c in range(REACH):
-                out_ref[c, rows_of(group), :] = filled_ref[c, rows_of(group), :] / smoothed[c]
+                out_ref[c, rows_of(group - first), :] = filled_ref[c, rows_of(group), :] / smoothed[c]
 
 
 def low_half(shape):
     return lax.broadcasted_iota(jnp.int32, shape, 0) < SUB // 2
 
 
-def add_logs(group, result, scaled_ref, weight_ref, inverse_ref, total_ref):
+def add_logs(group, held, result, scaled_ref, weight_ref, inverse_ref, total_ref):
     lat = scaled_ref.shape[2]
     weight = jnp.broadcast_to(weight_ref[rows_of(group), :1], (SUB, lat))
     for c in range(REACH):
-        inverse_ref[c, rows_of(group), :] = 1.0 / result[c]
-        total_ref[c] = total_ref[c] + weight * jnp.log(scaled_ref[c, rows_of(group), :] * result[c])
-
-
-def return_inner_kernel(
-    halo_ref, outer_ref, inner_ref, scaled_ref, weight_ref, coef_ref, inverse_ref, edge_ref, total_ref
-):
-    groups = outer_ref.shape[1] // SUB
+        inverse_ref[c, rows_of(held), :] = 1.0 / result[c]
+        total_ref[c] = total_ref[c] + weight * jnp.log(scaled_ref[c, rows_of(held), :] * result[c])
+
+
+def return_inner_kernel(halo_ref, inner_ref, scaled_ref, weight_ref, coef_ref, *refs):
+    *outer_refs, inverse_ref, edge_ref, total_ref = refs
+    groups = inner_ref.shape[1] // SUB
     total_ref[...] = jnp.zeros_like(total_ref)
     for batch in batches(groups):
-        for group, result in inner_half(batch, halo_ref, outer_ref, inner_ref, coef_ref, edge_ref):
-            add_logs(group, result, scaled_ref, weight_ref, inverse_ref, total_ref)
+        for group, result in inner_half(batch, halo_ref, inner_ref, outer_refs, coef_ref, edge_ref):
+            add_logs(group, group, result, scaled_ref, weight_ref, inverse_ref, total_ref)
 
 
 def return_outer_kernel(
-    halo_ref, outer_ref, edge_ref, scaled_ref, weight_ref, inner_ref, coef_ref, inverse_ref, logs_ref, total_ref
+    first, halo_ref, outer_ref, edge_ref, scaled_ref, weight_ref, coef_ref, inverse_ref, total_ref
 ):
-    groups, lat = outer_ref.shape[1] // SUB, outer_ref.shape[2]
+    last = first + outer_ref.shape[1] // SUB
     total_ref[...] = jnp.zeros_like(total_ref)
-    for batch in batches(groups):
-        for group, result in outer_half(batch, halo_ref, outer_ref, edge_ref, coef_ref):
-            add_logs(group, result, scaled_ref, weight_ref, inverse_ref, total_ref)
-    low = low_half((SUB, lat))
+    for batch in batches(last, first):
+        for group, result in outer_half(batch, first, halo_ref, outer_ref, edge_ref, coef_ref):
+            add_logs(group, group - first, result, scaled_ref, weight_ref, inverse_ref, total_ref)
+
+
+def last_return_kernel(
+    first,
+    halo_ref,
+    outer_ref,
+    edge_ref,
+    scaled_ref,
+    weight_ref,
+    coef_ref,
+    inner_ref,
+    earlier_ref,
+    inverse_ref,
+    logs_ref,
+    total_ref,
+):
+    return_outer_kernel(
+        first, halo_ref, outer_ref, edge_ref, scaled_ref, weight_ref, coef_ref, inverse_ref, total_ref
+    )
+    low = low_half(total_ref.shape[1:])
     for c in range(REACH):
-        outer, inner = total_ref[c], inner_ref[c]
+        outer, inner = total_ref[c] + earlier_ref[c], inner_ref[c]
         outer = outer + pltpu.roll(outer, SUB // 2, 0)
         inner = inner + pltpu.roll(inner, SUB // 2, 0)
         logs_ref[c] = jnp.where(low, outer, inner)
@@ -193,8 +241,9 @@
     payload_ref[...] = jnp.broadcast_to(row[None], payload_ref.shape)
 
 
-def finish_kernel(cells, got_ref, merged_ref, outer_ref, inner_ref, bary_ref, updated_ref, staged_ref, sem):
-    members, lat = outer_ref.shape[1:]
+def finish_kernel(cells, got_ref, merged_ref, inner_ref, *refs):
+    *outer_refs, bary_ref, updated_ref, staged_ref, sem = refs
+    members, lat = inner_ref.shape[1:]
     groups = members // SUB
     odd = odd_core()
     total = jnp.sum(got_ref[...], axis=0)
@@ -214,7 +263,7 @@
     for group in range(groups):
         rows = slice(group * SUB, (group + 1) * SUB)
         factor = wide(table[rows, :] / cells)
-        quotients = [ref[c, rows, :] for ref in (outer_ref, inner_ref) for c in range(REACH)]
+        quotients = Chunked(outer_refs).stack(group) + stack_of(inner_ref, group)
         out = [b * factor * quotient for b, quotient in zip(bary, from_outside(quotients, odd))]
         span = pl.ds(group * SUB * SUB, SUB * SUB)
         staged_ref[span, :] = jnp.swapaxes(jnp.stack(out), 0, 1).reshape(SUB * SUB, lat)
@@ -247,6 +296,9 @@
     half = shape(REACH, rows, lat)
     edge = shape(2 * REACH - 2, rows, lat)
     packed = shape(REACH, SUB, lat)
+    chunks = chunk_groups(rows // SUB)
+    firsts = [sum(chunks[:n]) for n in range(len(chunks))]
+    parts = [shape(REACH, n * SUB, lat) for n in chunks]
     coef = jnp.asarray(coefficients(lat))
     with_mate = [(i, i ^ 1) for i in range(tiles)]
     with_neighbour = [(i, (i + (1 if i % 2 else -1)) % tiles) for i in range(tiles)]
@@ -257,40 +309,56 @@
     count = jnp.broadcast_to(jnp.sum(weights), (SUB, 128))
     count = count + lax.ppermute(count, "mem", [(0, 1), (1, 0)])
 
-    outer, inner = call(spread_kernel, (half, half), scaling, coef)
+    inner, *outer = call(spread_kernel, (half, *parts), scaling, coef)
+    outer_halo = [lax.ppermute(part, "tile", with_neighbour) for part in outer]
     inner_halo = lax.ppermute(inner, "tile", with_mate)
-    outer_halo = lax.ppermute(outer, "tile", with_neighbour)
+    inner_halo, count = lax.optimization_barrier((inner_halo, count))
     v_inner, edges, filled, mass = call(
-        smooth_inner_kernel, (half, edge, half, shape(rows, 128)), inner_halo, outer, inner, fields, land_mask, coef
+        smooth_inner_kernel, (half, edge, half, shape(rows, 128)), inner_halo, inner, fields, land_mask, coef, *outer
     )
     v_inner_halo = lax.ppermute(v_inner, "tile", with_mate)
-    (v_outer,) = call(smooth_outer_kernel, (half,), outer_halo, outer, edges, filled, coef)
-    v_outer_halo = lax.ppermute(v_outer, "tile", with_neighbour)
+    v_outer, v_outer_halo = [], []
+    for first, part, halo, own in zip(firsts, parts, outer_halo, outer):
+        (value,) = call(partial(smooth_outer_kernel, first), (part,), halo, own, edges, filled, coef)
+        v_outer.append(value)
+        v_outer_halo.append(lax.ppermute(value, "tile", with_neighbour))
     inverse_inner, edges, inner_logs = call(
-        return_inner_kernel, (half, edge, packed), v_inner_halo, v_outer, v_inner, inner, weight_rows, coef
-    )
-    inverse_outer, logs = call(
-        return_outer_kernel,
-        (half, packed),
-        v_outer_halo,
-        v_outer,
+        return_inner_kernel, (half, edge, packed), v_inner_halo, v_inner, inner, weight_rows, coef, *v_outer
+    )
+    inverse_first, first_logs = call(
+        partial(return_outer_kernel, firsts[0]),
+        (parts[0], packed),
+        v_outer_halo[0],
+        v_outer[0],
         edges,
-        outer,
+        outer[0],
         weight_rows,
+        coef,
+    )
+    inverse_last, logs = call(
+        partial(last_return_kernel, firsts[1]),
+        (parts[1], packed),
+        v_outer_halo[1],
+        v_outer[1],
+        edges,
+        outer[1],
+        weight_rows,
+        coef,
         inner_logs,
-        coef,
+        first_logs,
         scratch=[pltpu.VMEM((REACH, SUB, lat), jnp.float32)],
     )
     other = lax.ppermute(logs, "mem", [(0, 1), (1, 0)])
     merged, payload = call(merge_kernel, (packed, shape(tiles, 1, 128)), logs, other, count, mass, coef)
     got = lax.all_to_all(payload, "tile", split_axis=0, concat_axis=0)
     barycenter, updated = call(
-        lambda *refs: finish_kernel(float(cells), *refs),
+        partial(finish_kernel, float(cells)),
         (shape(levels, lon, lat), shape(rows * lon, lat)),
         got,
         merged,
-        inverse_outer,
         inverse_inner,
+        inverse_first,
+        inverse_last,
         scratch=[pltpu.VMEM((rows * lon, lat), jnp.float32), pltpu.SemaphoreType.DMA((rows // SUB,))],
         out_specs=(VMEM, HBM),
     )

time: 89.7 us -> 87.6 us (0.977)
  waiting for transfers between devices: 28.9 us -> 26.5 us
  blocking collectives: 17.8 us -> 16.2 us
  Pallas kernels: 20.7 us -> 21.8 us
    ppermute x2 -> x4, waiting for transfers between devices: 26.7 us -> 21.8 us  [the longest x2 19.6 us: body(): outer_halo = [lax.ppermute(part, 'tile', with_neighbour) for part in outer]]
    ppermute x1, waiting for transfers between devices: 1.58 us -> 4.78 us  [body(): other = lax.ppermute(logs, 'mem', [(0, 1), (1, 0)])]
    ppermute x1, starting transfers between devices: 2.63 us -> 0.1 us  [body(): other = lax.ppermute(logs, 'mem', [(0, 1), (1, 0)])]
    ppermute x2 -> x4, starting transfers between devices: 4.26 us -> 6.37 us  [the longest x2 5.3 us: body(): v_outer_halo.append(lax.ppermute(value, 'tile', with_neighbour))]
    all_to_all x1, blocking collectives: 17.8 us -> 16.2 us  [body(): got = lax.all_to_all(payload, 'tile', split_axis=0, concat_axis=0)]
    pallas_call x7 -> x9, Pallas kernels: 20.7 us -> 21.8 us  [call(): pl.pallas_call(kernel, out_shape=outs, in_specs=[VMEM] * len(args), out_s...]
  transfers between devices with their start and end apart: 6 -> 8, of which waited for: 4 -> 4; matrix products, arithmetic and copies ran while one was open for 2% -> 3% of each run, Pallas kernels for 20% -> 19%
where the time goes in v4:
time: 87.6 us; the launch traced here: 87.3 us
  waiting for transfers between devices  26.5 us (30%)
  Pallas kernels  21.8 us (25%)
  starting transfers between devices  16.4 us (19%)
  blocking collectives  16.2 us (18%)
  local copies, waits for them, and re-layouts  3.4 us (4%)
  other arithmetic  1.91 us (2%)
  between operations  0.94 us (1%)
    pallas_call x9, Pallas kernels, call(): pl.pallas_call(kernel, out_shape=outs, in_specs=[VMEM] * len(args), out_s...  21.8 us
    ppermute x2, waiting for transfers between devices, body(): outer_halo = [lax.ppermute(part, 'tile', with_neighbour) for part in outer]  19.6 us
    all_to_all x1, blocking collectives, body(): got = lax.all_to_all(payload, 'tile', split_axis=0, concat_axis=0)  16.2 us
    ppermute x2, starting transfers between devices, body(): v_outer_halo.append(lax.ppermute(value, 'tile', with_neighbour))  5.3 us
    ppermute x1, waiting for transfers between devices, body(): other = lax.ppermute(logs, 'mem', [(0, 1), (1, 0)])  4.78 us
    ppermute x1, starting transfers between devices, body(): v_inner_halo = lax.ppermute(v_inner, 'tile', with_mate)  4.71 us
    ppermute x1, starting transfers between devices, body(): count = count + lax.ppermute(count, 'mem', [(0, 1), (1, 0)])  3.76 us
    unnamed x12, local copies, waits for them, and re-layouts  2.51 us
  transfers between devices with their start and end apart: 8, of which 4 were waited for; matrix products, arithmetic and copies ran while one was open for 3% of the time, Pallas kernels for 19%

profile of v4, /device:TPU:1, one launch (start us, length us, event | category | flops | bytes accessed | tf_op | source)
XLA Modules:
  0.0 87.3 jit_solution(3244949176772437471)
XLA Ops:
  0.6 0.0 copy-start
  0.6 0.9 %copy-done = f32[5,8,640]{2,1,0:T(8,128)S(1)} copy-done((f32[5,8,640]{2,1,0:T(8,128)S(1)}, f32[5,8,640]{2,1,0:T(8,128)}, u32[]{:S(2)}) %copy-start) | copy-done | bytes 102424
  1.5 0.0 copy-start.2
  1.5 1.6 %copy-done.2 = f32[26,4,8,640]{3,2,1,0:T(8,128)S(1)} copy-done((f32[26,4,8,640]{3,2,1,0:T(8,128)S(1)}, f32[26,4,8,640]{3,2,1,0:T(8,128)}, u32[]{:S(2)}) %copy-start.2) | copy-done | bytes 2129944
  3.1 0.0 copy-start.1
  3.1 0.0 copy-start.3
  3.1 0.0 copy-start.4
  3.1 0.5 shard_map.68
  3.6 1.5 %collective-permute-start.1 = (f32[4,104,640]{2,1,0:T(8,128)S(1)}, f32[4,104,640]{2,1,0:T(8,128)S(1)}, u32[]{:S(2)}, u32[]{:S(2)}) collective-permute-start(f32[4,104,640]{2,1,0:T(8,128)S(1)} %get-tuple-element.23.inner_ref.scaled_ref), channel_id=1, source_target_pairs={{0,2},{2,0},{4,6},{6,4},{8,10},{10,8},{12,14},{14,12},{16,18},{18,... | collective-permute-start | bytes 3194888 | tf_op jit(solution)/shard_map/ppermute | solution.py:314
  5.1 1.3 %convert_reduce_fusion = f32[]{:T(128)} fusion(s32[26]{0:T(128)} %param.7), kind=kLoop, calls=%fused_computation.1 | loop fusion | flops 51 | bytes 108 | tf_op jit(solution)/shard_map/reduce_sum | solution.py:309
  6.3 0.6 broadcast_in_dim.13
  7.0 3.8 %collective-permute-start.2 = (f32[8,128]{1,0:T(8,128)S(1)}, f32[8,128]{1,0:T(8,128)S(1)}, u32[]{:S(2)}, u32[]{:S(2)}) collective-permute-start(f32[8,128]{1,0:T(8,128)S(1)} %broadcast_in_dim.13), channel_id=1, source_target_pairs={{0,1},{1,0},{2,3},{3,2},{4,5},{5,4},{6,7},{7,6},{8,9},{9,8},{10,11... | collective-permute-start | bytes 12296 | tf_op jit(solution)/shard_map/ppermute | solution.py:310
  10.8 1.1 %collective-permute-start.5 = (f32[4,56,640]{2,1,0:T(8,128)S(1)}, f32[4,56,640]{2,1,0:T(8,128)S(1)}, u32[]{:S(2)}, u32[]{:S(2)}) collective-permute-start(f32[4,56,640]{2,1,0:T(8,128)S(1)} %get-tuple-element.25.refs_0_.outer_ref.scaled_ref), channel_id=1, source_target_pairs={{0,126},{2,4},{4,2},{6,8},{8,6},{10,12},{12,10},{14,16},{16,14},{1... | collective-permute-start | bytes 1720328 | tf_op jit(solution)/shard_map/ppermute | solution.py:313
  11.8 0.0 collective-permute-done.2
  11.8 0.6 broadcast_add_fusion.count_ref
  12.5 0.0 collective-permute-done.1.halo_ref
  12.5 0.0 copy-done.1
  12.5 0.0 copy-done.3
  12.5 0.0 copy-done.4
  12.5 5.8 %shard_map.69 = (f32[4,104,640]{2,1,0:T(8,128)}, f32[6,104,640]{2,1,0:T(8,128)S(1)}, f32[4,104,640]{2,1,0:T(8,128)S(1)}, f32[104,128]{1,0:T(8,128)S(1)}) custom-call(f32[4,104,640]{2,1,0:T(8,128)S(1)} %collective-permute-done.1.halo_ref, f32[4,104,640]{2,1,0:T(8,128)S(1)} %get-tuple-element.23.inner_ref.scaled_ref, f32[832,640]{1,0:T(8,128)S(1)} %bitcast.4, ...), custom_call_target="tpu_custom_call" | custom-call | tf_op jit(solution)/shard_map/pallas_call | solution.py:281
  18.3 4.7 %collective-permute-start.4 = (f32[4,104,640]{2,1,0:T(8,128)}, f32[4,104,640]{2,1,0:T(8,128)}, u32[]{:S(2)}, u32[]{:S(2)}) collective-permute-start(f32[4,104,640]{2,1,0:T(8,128)} %get-tuple-element.28.inner_ref), channel_id=1, source_target_pairs={{0,2},{2,0},{4,6},{6,4},{8,10},{10,8},{12,14},{14,12},{16,18},{18,... | collective-permute-start | bytes 3194888 | tf_op jit(solution)/shard_map/ppermute | solution.py:319
  23.0 0.0 collective-permute-start
  23.0 18.3 %collective-permute-done.5.halo_ref = f32[4,56,640]{2,1,0:T(8,128)S(1)} collective-permute-done((f32[4,56,640]{2,1,0:T(8,128)S(1)}, f32[4,56,640]{2,1,0:T(8,128)S(1)}, u32[]{:S(2)}, u32[]{:S(2)}) %collective-permute-start.5) | collective-permute-done | bytes 573472 | tf_op jit(solution)/shard_map/ppermute | solution.py:313
  41.3 1.3 %shard_map.71.refs_0_.outer_ref = f32[4,56,640]{2,1,0:T(8,128)S(1)} custom-call(f32[4,56,640]{2,1,0:T(8,128)S(1)} %collective-permute-done.5.halo_ref, f32[4,56,640]{2,1,0:T(8,128)S(1)} %get-tuple-element.25.refs_0_.outer_ref.scaled_ref, f32[6,104,640]{2,1,0:T(8,128)S(1)} %get-tuple-element.26.edge_ref, f32[4,104,640]{2,1,0:T(8,128)S(1)} %get-tuple-element.27.filled_ref, ...), custom_call_target="tpu_custom_call" | custom-call | tf_op jit(solution)/shard_map/pallas_call | solution.py:281
  42.6 0.0 copy-start.5
  42.7 2.6 %collective-permute-start.6 = (f32[4,56,640]{2,1,0:T(8,128)S(1)}, f32[4,56,640]{2,1,0:T(8,128)}, u32[]{:S(2)}, u32[]{:S(2)}) collective-permute-start(f32[4,56,640]{2,1,0:T(8,128)S(1)} %shard_map.71.refs_0_.outer_ref), channel_id=1, source_target_pairs={{0,126},{2,4},{4,2},{6,8},{8,6},{10,12},{12,10},{14,16},{16,14},{1... | collective-permute-start | bytes 1720328 | tf_op jit(solution)/shard_map/ppermute | solution.py:324
  45.2 1.4 %collective-permute-done.halo_ref = f32[4,48,640]{2,1,0:T(8,128)S(1)} collective-permute-done((f32[4,48,640]{2,1,0:T(8,128)S(1)}, f32[4,48,640]{2,1,0:T(8,128)S(1)}, u32[]{:S(2)}, u32[]{:S(2)}) %collective-permute-start) | collective-permute-done | bytes 491552 | tf_op jit(solution)/shard_map/ppermute | solution.py:313
  46.6 1.2 %shard_map.70.refs_1_.outer_ref = f32[4,48,640]{2,1,0:T(8,128)S(1)} custom-call(f32[4,48,640]{2,1,0:T(8,128)S(1)} %collective-permute-done.halo_ref, f32[4,48,640]{2,1,0:T(8,128)S(1)} %get-tuple-element.22.refs_1_.outer_ref.scaled_ref, f32[6,104,640]{2,1,0:T(8,128)S(1)} %get-tuple-element.26.edge_ref, f32[4,104,640]{2,1,0:T(8,128)S(1)} %get-tuple-element.27.filled_ref, ...), custom_call_target="tpu_custom_call" | custom-call | tf_op jit(solution)/shard_map/pallas_call | solution.py:281
  47.7 2.7 %collective-permute-start.3 = (f32[4,48,640]{2,1,0:T(8,128)S(1)}, f32[4,48,640]{2,1,0:T(8,128)}, u32[]{:S(2)}, u32[]{:S(2)}) collective-permute-start(f32[4,48,640]{2,1,0:T(8,128)S(1)} %shard_map.70.refs_1_.outer_ref), channel_id=1, source_target_pairs={{0,126},{2,4},{4,2},{6,8},{8,6},{10,12},{12,10},{14,16},{16,14},{1... | collective-permute-start | bytes 1474568 | tf_op jit(solution)/shard_map/ppermute | solution.py:324
  50.5 0.0 copy-done.5
  50.5 0.1 broadcast_in_dim.14
  50.6 0.1 broadcast_in_dim.15
  50.7 0.0 collective-permute-done.4.halo_ref
  50.7 0.1 broadcast_in_dim.16.weight_ref
  50.7 5.9 %shard_map.72 = (f32[4,104,640]{2,1,0:T(8,128)S(1)}, f32[6,104,640]{2,1,0:T(8,128)S(1)}, f32[4,8,640]{2,1,0:T(8,128)S(1)}) custom-call(f32[4,104,640]{2,1,0:T(8,128)} %collective-permute-done.4.halo_ref, f32[4,104,640]{2,1,0:T(8,128)} %get-tuple-element.28.inner_ref, f32[4,104,640]{2,1,0:T(8,128)S(1)} %get-tuple-element.23.inner_ref.scaled_ref, ...), custom_call_target="tpu_custom_call" | custom-call | tf_op jit(solution)/shard_map/pallas_call | solution.py:281
  56.6 0.0 collective-permute-done.6.halo_ref
  56.6 2.5 %shard_map.73 = (f32[4,56,640]{2,1,0:T(8,128)S(1)}, f32[4,8,640]{2,1,0:T(8,128)S(1)}) custom-call(f32[4,56,640]{2,1,0:T(8,128)} %collective-permute-done.6.halo_ref, f32[4,56,640]{2,1,0:T(8,128)S(1)} %shard_map.71.refs_0_.outer_ref, f32[6,104,640]{2,1,0:T(8,128)S(1)} %get-tuple-element.29.edge_ref, ...), custom_call_target="tpu_custom_call" | custom-call | tf_op jit(solution)/shard_map/pallas_call | solution.py:281
  59.1 2.1 %collective-permute-done.3.halo_ref = f32[4,48,640]{2,1,0:T(8,128)} collective-permute-done((f32[4,48,640]{2,1,0:T(8,128)S(1)}, f32[4,48,640]{2,1,0:T(8,128)}, u32[]{:S(2)}, u32[]{:S(2)}) %collective-permute-start.3) | collective-permute-done | bytes 491552 | tf_op jit(solution)/shard_map/ppermute | solution.py:324
  61.2 2.2 %shard_map.74 = (f32[4,48,640]{2,1,0:T(8,128)S(1)}, f32[4,8,640]{2,1,0:T(8,128)S(1)}) custom-call(f32[4,48,640]{2,1,0:T(8,128)} %collective-permute-done.3.halo_ref, f32[4,48,640]{2,1,0:T(8,128)S(1)} %shard_map.70.refs_1_.outer_ref, f32[6,104,640]{2,1,0:T(8,128)S(1)} %get-tuple-element.29.edge_ref, ...), custom_call_target="tpu_custom_call" | custom-call | tf_op jit(solution)/shard_map/pallas_call | solution.py:281
  63.5 0.1 collective-permute-start.7
  63.6 4.8 %collective-permute-done.7.other_ref = f32[4,8,640]{2,1,0:T(8,128)S(1)} collective-permute-done((f32[4,8,640]{2,1,0:T(8,128)S(1)}, f32[4,8,640]{2,1,0:T(8,128)S(1)}, u32[]{:S(2)}, u32[]{:S(2)}) %collective-permute-start.7) | collective-permute-done | bytes 81952 | tf_op jit(solution)/shard_map/ppermute | solution.py:351
  68.3 0.2 shard_map.75
  68.5 16.2 %all_to_all.5.got_ref = f32[64,1,128]{2,1,0:T(1,128)S(1)} all-to-all(f32[64,1,128]{2,1,0:T(1,128)S(1)} %get-tuple-element.35), channel_id=1, replica_groups=mesh['tile'=64,'mem'=2] {'tile'}, dimensions={0} | all-to-all | bytes 65536 | tf_op jit(solution)/shard_map/all_to_all | solution.py:353
  84.8 2.3 %shard_map.76 = (f32[4,8,640]{2,1,0:T(8,128)}, f32[832,640]{1,0:T(8,128)}) custom-call(f32[64,1,128]{2,1,0:T(1,128)S(1)} %all_to_all.5.got_ref, f32[4,8,640]{2,1,0:T(8,128)S(1)} %get-tuple-element.36.merged_ref, f32[4,104,640]{2,1,0:T(8,128)S(1)} %get-tuple-element.37.inner_ref, f32[4,56,640]{2,1,0:T(8,128)S(1)} %get-tuple-element.38.refs_0_, ...), custom_call_target="tpu_custom_call" | custom-call | tf_op jit(solution)/shard_map/pallas_call | solution.py:281
  (1 shorter events, 0.0 us)
Async XLA Ops:
  0.6 0.9 %copy-start = (f32[5,8,640]{2,1,0:T(8,128)S(1)}, f32[5,8,640]{2,1,0:T(8,128)}, u32[]{:S(2)}) copy-start(f32[5,8,640]{2,1,0:T(8,128)} %constant.4.clone.coef_ref) | copy-start | bytes 307204
  1.5 1.6 %copy-start.2 = (f32[26,4,8,640]{3,2,1,0:T(8,128)S(1)}, f32[26,4,8,640]{3,2,1,0:T(8,128)}, u32[]{:S(2)}) copy-start(f32[26,4,8,640]{3,2,1,0:T(8,128)} %param.6) | copy-start | bytes 6389764
  3.1 9.4 %copy-start.1 = (f32[5,8,640]{2,1,0:T(8,128)S(1)}, f32[5,8,640]{2,1,0:T(8,128)}, u32[]{:S(2)}) copy-start(f32[5,8,640]{2,1,0:T(8,128)} %constant.4.clone.coef_ref) | copy-start | bytes 307204
  3.1 9.4 %copy-start.3 = (f32[26,4,8,640]{3,2,1,0:T(8,128)S(1)}, f32[26,4,8,640]{3,2,1,0:T(8,128)}, u32[]{:S(2)}) copy-start(f32[26,4,8,640]{3,2,1,0:T(8,128)} %param.5) | copy-start | bytes 6389764
  3.1 9.4 %copy-start.4 = (s32[8,640]{1,0:T(8,128)S(1)}, s32[8,640]{1,0:T(8,128)}, u32[]{:S(2)}) copy-start(s32[8,640]{1,0:T(8,128)} %mask_ref.1) | copy-start | bytes 61444
  3.6 8.9 %collective-permute-start.1 = (f32[4,104,640]{2,1,0:T(8,128)S(1)}, f32[4,104,640]{2,1,0:T(8,128)S(1)}, u32[]{:S(2)}, u32[]{:S(2)}) collective-permute-start(f32[4,104,640]{2,1,0:T(8,128)S(1)} %get-tuple-element.23.inner_ref.scaled_ref), channel_id=1, source_target_pairs={{0,2},{2,0},{4,6},{6,4},{8,10},{10,8},{12,14},{14,12},{16,18},{18,... | collective-permute-start | bytes 3194888 | tf_op jit(solution)/shard_map/ppermute | solution.py:314
  7.0 4.8 %collective-permute-start.2 = (f32[8,128]{1,0:T(8,128)S(1)}, f32[8,128]{1,0:T(8,128)S(1)}, u32[]{:S(2)}, u32[]{:S(2)}) collective-permute-start(f32[8,128]{1,0:T(8,128)S(1)} %broadcast_in_dim.13), channel_id=1, source_target_pairs={{0,1},{1,0},{2,3},{3,2},{4,5},{5,4},{6,7},{7,6},{8,9},{9,8},{10,11... | collective-permute-start | bytes 12296 | tf_op jit(solution)/shard_map/ppermute | solution.py:310
  10.8 30.5 %collective-permute-start.5 = (f32[4,56,640]{2,1,0:T(8,128)S(1)}, f32[4,56,640]{2,1,0:T(8,128)S(1)}, u32[]{:S(2)}, u32[]{:S(2)}) collective-permute-start(f32[4,56,640]{2,1,0:T(8,128)S(1)} %get-tuple-element.25.refs_0_.outer_ref.scaled_ref), channel_id=1, source_target_pairs={{0,126},{2,4},{4,2},{6,8},{8,6},{10,12},{12,10},{14,16},{16,14},{1... | collective-permute-start | bytes 1720328 | tf_op jit(solution)/shard_map/ppermute | solution.py:313
  18.3 32.3 %collective-permute-start.4 = (f32[4,104,640]{2,1,0:T(8,128)}, f32[4,104,640]{2,1,0:T(8,128)}, u32[]{:S(2)}, u32[]{:S(2)}) collective-permute-start(f32[4,104,640]{2,1,0:T(8,128)} %get-tuple-element.28.inner_ref), channel_id=1, source_target_pairs={{0,2},{2,0},{4,6},{6,4},{8,10},{10,8},{12,14},{14,12},{16,18},{18,... | collective-permute-start | bytes 3194888 | tf_op jit(solution)/shard_map/ppermute | solution.py:319
  23.0 23.5 %collective-permute-start = (f32[4,48,640]{2,1,0:T(8,128)S(1)}, f32[4,48,640]{2,1,0:T(8,128)S(1)}, u32[]{:S(2)}, u32[]{:S(2)}) collective-permute-start(f32[4,48,640]{2,1,0:T(8,128)S(1)} %get-tuple-element.22.refs_1_.outer_ref.scaled_ref), channel_id=1, source_target_pairs={{0,126},{2,4},{4,2},{6,8},{8,6},{10,12},{12,10},{14,16},{16,14},{1... | collective-permute-start | bytes 1474568 | tf_op jit(solution)/shard_map/ppermute | solution.py:313
  42.6 7.8 %copy-start.5 = (s32[26]{0:T(128)S(1)}, s32[26]{0:T(128)}, u32[]{:S(2)}) copy-start(s32[26]{0:T(128)} %param.7) | copy-start | bytes 316
  42.7 14.0 %collective-permute-start.6 = (f32[4,56,640]{2,1,0:T(8,128)S(1)}, f32[4,56,640]{2,1,0:T(8,128)}, u32[]{:S(2)}, u32[]{:S(2)}) collective-permute-start(f32[4,56,640]{2,1,0:T(8,128)S(1)} %shard_map.71.refs_0_.outer_ref), channel_id=1, source_target_pairs={{0,126},{2,4},{4,2},{6,8},{8,6},{10,12},{12,10},{14,16},{16,14},{1... | collective-permute-start | bytes 1720328 | tf_op jit(solution)/shard_map/ppermute | solution.py:324
  47.7 13.5 %collective-permute-start.3 = (f32[4,48,640]{2,1,0:T(8,128)S(1)}, f32[4,48,640]{2,1,0:T(8,128)}, u32[]{:S(2)}, u32[]{:S(2)}) collective-permute-start(f32[4,48,640]{2,1,0:T(8,128)S(1)} %shard_map.70.refs_1_.outer_ref), channel_id=1, source_target_pairs={{0,126},{2,4},{4,2},{6,8},{8,6},{10,12},{12,10},{14,16},{16,14},{1... | collective-permute-start | bytes 1474568 | tf_op jit(solution)/shard_map/ppermute | solution.py:324
  63.5 4.9 %collective-permute-start.7 = (f32[4,8,640]{2,1,0:T(8,128)S(1)}, f32[4,8,640]{2,1,0:T(8,128)S(1)}, u32[]{:S(2)}, u32[]{:S(2)}) collective-permute-start(f32[4,8,640]{2,1,0:T(8,128)S(1)} %get-tuple-element.32.own_ref), channel_id=1, source_target_pairs={{0,1},{1,0},{2,3},{3,2},{4,5},{5,4},{6,7},{7,6},{8,9},{9,8},{10,11... | collective-permute-start | bytes 245768 | tf_op jit(solution)/shard_map/ppermute | solution.py:351

commit v5 on v4

--- a/solution.py
+++ b/solution.py
@@ -312,7 +312,7 @@
     inner, *outer = call(spread_kernel, (half, *parts), scaling, coef)
     outer_halo = [lax.ppermute(part, "tile", with_neighbour) for part in outer]
     inner_halo = lax.ppermute(inner, "tile", with_mate)
-    inner_halo, count = lax.optimization_barrier((inner_halo, count))
+    outer_halo[0], count = lax.optimization_barrier((outer_halo[0], count))
     v_inner, edges, filled, mass = call(
         smooth_inner_kernel, (half, edge, half, shape(rows, 128)), inner_halo, inner, fields, land_mask, coef, *outer
     )

time: 87.6 us -> 89.6 us (1.023)
  waiting for transfers between devices: 26.5 us -> 29.9 us
  starting transfers between devices: 16.4 us -> 14.2 us
    ppermute x1, waiting for transfers between devices: 0.01 us -> 22.7 us  [body(): count = count + lax.ppermute(count, 'mem', [(0, 1), (1, 0)])]
    ppermute x2, waiting for transfers between devices: 19.6 us -> 0.01 us  [body(): outer_halo = [lax.ppermute(part, 'tile', with_neighbour) for part in outer]]
    ppermute x2, starting transfers between devices: 5.3 us -> 2.07 us  [body(): v_outer_halo.append(lax.ppermute(value, 'tile', with_neighbour))]
    ppermute x1, starting transfers between devices: 0.1 us -> 1.05 us  [body(): other = lax.ppermute(logs, 'mem', [(0, 1), (1, 0)])]
    ppermute x1, waiting for transfers between devices: 4.78 us -> 3.83 us  [body(): other = lax.ppermute(logs, 'mem', [(0, 1), (1, 0)])]
  transfers between devices with their start and end apart: 8 -> 8, of which waited for: 4 -> 5; matrix products, arithmetic and copies ran while one was open for 3% -> 2% of each run, Pallas kernels for 19% -> 19%
where the time goes in v5:
time: 89.6 us; the launch traced here: 89.2 us
  waiting for transfers between devices  29.9 us (33%)
  Pallas kernels  21.8 us (24%)
  blocking collectives  17 us (19%)
  starting transfers between devices  14.2 us (16%)
  local copies, waits for them, and re-layouts  4.12 us (5%)
  other arithmetic  1.25 us (1%)
  between operations  0.91 us (1%)
    ppermute x1, waiting for transfers between devices, body(): count = count + lax.ppermute(count, 'mem', [(0, 1), (1, 0)])  22.7 us
    pallas_call x9, Pallas kernels, call(): pl.pallas_call(kernel, out_shape=outs, in_specs=[VMEM] * len(args), out_s...  21.8 us
    all_to_all x1, blocking collectives, body(): got = lax.all_to_all(payload, 'tile', split_axis=0, concat_axis=0)  17 us
    ppermute x1, starting transfers between devices, body(): v_inner_halo = lax.ppermute(v_inner, 'tile', with_mate)  4.46 us
    ppermute x1, waiting for transfers between devices, body(): other = lax.ppermute(logs, 'mem', [(0, 1), (1, 0)])  3.83 us
    ppermute x1, starting transfers between devices, body(): count = count + lax.ppermute(count, 'mem', [(0, 1), (1, 0)])  3.38 us
    unnamed x12, local copies, waits for them, and re-layouts  3.23 us
    ppermute x2, waiting for transfers between devices, body(): v_outer_halo.append(lax.ppermute(value, 'tile', with_neighbour))  2.72 us
  transfers between devices with their start and end apart: 8, of which 5 were waited for; matrix products, arithmetic and copies ran while one was open for 2% of the time, Pallas kernels for 19%

profile of v5, /device:TPU:1, one launch (start us, length us, event | category | flops | bytes accessed | tf_op | source)
XLA Modules:
  0.0 89.2 jit_solution(2359984116157550226)
XLA Ops:
  0.6 0.0 copy-start
  0.6 0.9 copy-done
  1.5 0.0 copy-start.2
  1.5 1.6 %copy-done.2 = f32[26,4,8,640]{3,2,1,0:T(8,128)S(1)} copy-done((f32[26,4,8,640]{3,2,1,0:T(8,128)S(1)}, f32[26,4,8,640]{3,2,1,0:T(8,128)}, u32[]{:S(2)}) %copy-start.2) | copy-done | bytes 2129944
  3.1 0.0 copy-start.1
  3.1 0.0 copy-start.3
  3.1 0.5 shard_map.68
  3.6 1.5 %collective-permute-start.1 = (f32[4,104,640]{2,1,0:T(8,128)S(1)}, f32[4,104,640]{2,1,0:T(8,128)S(1)}, u32[]{:S(2)}, u32[]{:S(2)}) collective-permute-start(f32[4,104,640]{2,1,0:T(8,128)S(1)} %get-tuple-element.23.inner_ref.scaled_ref), channel_id=1, source_target_pairs={{0,2},{2,0},{4,6},{6,4},{8,10},{10,8},{12,14},{14,12},{16,18},{18,... | collective-permute-start | bytes 3194888 | tf_op jit(solution)/shard_map/ppermute | solution.py:314
  5.1 1.7 %collective-permute-start.4 = (f32[4,56,640]{2,1,0:T(8,128)S(1)}, f32[4,56,640]{2,1,0:T(8,128)S(1)}, u32[]{:S(2)}, u32[]{:S(2)}) collective-permute-start(f32[4,56,640]{2,1,0:T(8,128)S(1)} %get-tuple-element.24.refs_0_.outer_ref.scaled_ref), channel_id=1, source_target_pairs={{0,126},{2,4},{4,2},{6,8},{8,6},{10,12},{12,10},{14,16},{16,14},{1... | collective-permute-start | bytes 1720328 | tf_op jit(solution)/shard_map/ppermute | solution.py:313
  6.8 0.6 collective-permute-done.1.halo_ref
  7.4 0.0 copy-done.1
  7.4 0.0 copy-done.3
  7.4 0.0 copy-start.4
  7.4 0.7 copy-done.4
  8.1 0.0 copy-start.5
  8.1 5.8 %shard_map.69 = (f32[4,104,640]{2,1,0:T(8,128)}, f32[6,104,640]{2,1,0:T(8,128)S(1)}, f32[4,104,640]{2,1,0:T(8,128)S(1)}, f32[104,128]{1,0:T(8,128)S(1)}) custom-call(f32[4,104,640]{2,1,0:T(8,128)S(1)} %collective-permute-done.1.halo_ref, f32[4,104,640]{2,1,0:T(8,128)S(1)} %get-tuple-element.23.inner_ref.scaled_ref, f32[832,640]{1,0:T(8,128)S(1)} %bitcast.4, ...), custom_call_target="tpu_custom_call" | custom-call | tf_op jit(solution)/shard_map/pallas_call | solution.py:281
  13.9 4.5 %collective-permute-start.3 = (f32[4,104,640]{2,1,0:T(8,128)}, f32[4,104,640]{2,1,0:T(8,128)}, u32[]{:S(2)}, u32[]{:S(2)}) collective-permute-start(f32[4,104,640]{2,1,0:T(8,128)} %get-tuple-element.27.inner_ref), channel_id=1, source_target_pairs={{0,2},{2,0},{4,6},{6,4},{8,10},{10,8},{12,14},{14,12},{16,18},{18,... | collective-permute-start | bytes 3194888 | tf_op jit(solution)/shard_map/ppermute | solution.py:319
  18.4 0.0 collective-permute-start
  18.4 0.0 copy-done.5
  18.4 0.6 convert_reduce_fusion
  19.0 0.6 broadcast_in_dim.16
  19.6 3.4 %collective-permute-start.5 = (f32[8,128]{1,0:T(8,128)S(1)}, f32[8,128]{1,0:T(8,128)S(1)}, u32[]{:S(2)}, u32[]{:S(2)}) collective-permute-start(f32[8,128]{1,0:T(8,128)S(1)} %broadcast_in_dim.16), channel_id=1, source_target_pairs={{0,1},{1,0},{2,3},{3,2},{4,5},{5,4},{6,7},{7,6},{8,9},{9,8},{10,11... | collective-permute-start | bytes 12296 | tf_op jit(solution)/shard_map/ppermute | solution.py:310
  23.0 22.7 %collective-permute-done.5 = f32[8,128]{1,0:T(8,128)S(1)} collective-permute-done((f32[8,128]{1,0:T(8,128)S(1)}, f32[8,128]{1,0:T(8,128)S(1)}, u32[]{:S(2)}, u32[]{:S(2)}) %collective-permute-start.5) | collective-permute-done | bytes 4128 | tf_op jit(solution)/shard_map/ppermute | solution.py:310
  45.8 0.6 broadcast_add_fusion.count_ref
  46.4 0.0 collective-permute-done.4.halo_ref
  46.4 1.3 %shard_map.71.refs_0_.outer_ref = f32[4,56,640]{2,1,0:T(8,128)S(1)} custom-call(f32[4,56,640]{2,1,0:T(8,128)S(1)} %collective-permute-done.4.halo_ref, f32[4,56,640]{2,1,0:T(8,128)S(1)} %get-tuple-element.24.refs_0_.outer_ref.scaled_ref, f32[6,104,640]{2,1,0:T(8,128)S(1)} %get-tuple-element.25.edge_ref, f32[4,104,640]{2,1,0:T(8,128)S(1)} %get-tuple-element.26.filled_ref, ...), custom_call_target="tpu_custom_call" | custom-call | tf_op jit(solution)/shard_map/pallas_call | solution.py:281
  47.8 0.1 collective-permute-start.6
  47.9 0.0 collective-permute-done.halo_ref
  47.9 1.2 %shard_map.70.refs_1_.outer_ref = f32[4,48,640]{2,1,0:T(8,128)S(1)} custom-call(f32[4,48,640]{2,1,0:T(8,128)S(1)} %collective-permute-done.halo_ref, f32[4,48,640]{2,1,0:T(8,128)S(1)} %get-tuple-element.22.refs_1_.outer_ref.scaled_ref, f32[6,104,640]{2,1,0:T(8,128)S(1)} %get-tuple-element.25.edge_ref, f32[4,104,640]{2,1,0:T(8,128)S(1)} %get-tuple-element.26.filled_ref, ...), custom_call_target="tpu_custom_call" | custom-call | tf_op jit(solution)/shard_map/pallas_call | solution.py:281
  49.0 2.0 %collective-permute-start.2 = (f32[4,48,640]{2,1,0:T(8,128)S(1)}, f32[4,48,640]{2,1,0:T(8,128)}, u32[]{:S(2)}, u32[]{:S(2)}) collective-permute-start(f32[4,48,640]{2,1,0:T(8,128)S(1)} %shard_map.70.refs_1_.outer_ref), channel_id=1, source_target_pairs={{0,126},{2,4},{4,2},{6,8},{8,6},{10,12},{12,10},{14,16},{16,14},{1... | collective-permute-start | bytes 1474568 | tf_op jit(solution)/shard_map/ppermute | solution.py:324
  51.0 0.1 broadcast_in_dim.13
  51.1 0.1 broadcast_in_dim.14
  51.2 0.0 collective-permute-done.3.halo_ref
  51.2 0.1 broadcast_in_dim.15.weight_ref
  51.3 5.9 %shard_map.72 = (f32[4,104,640]{2,1,0:T(8,128)S(1)}, f32[6,104,640]{2,1,0:T(8,128)S(1)}, f32[4,8,640]{2,1,0:T(8,128)S(1)}) custom-call(f32[4,104,640]{2,1,0:T(8,128)} %collective-permute-done.3.halo_ref, f32[4,104,640]{2,1,0:T(8,128)} %get-tuple-element.27.inner_ref, f32[4,104,640]{2,1,0:T(8,128)S(1)} %get-tuple-element.23.inner_ref.scaled_ref, ...), custom_call_target="tpu_custom_call" | custom-call | tf_op jit(solution)/shard_map/pallas_call | solution.py:281
  57.2 0.1 collective-permute-done.6.halo_ref
  57.3 2.5 %shard_map.73 = (f32[4,56,640]{2,1,0:T(8,128)S(1)}, f32[4,8,640]{2,1,0:T(8,128)S(1)}) custom-call(f32[4,56,640]{2,1,0:T(8,128)} %collective-permute-done.6.halo_ref, f32[4,56,640]{2,1,0:T(8,128)S(1)} %shard_map.71.refs_0_.outer_ref, f32[6,104,640]{2,1,0:T(8,128)S(1)} %get-tuple-element.29.edge_ref, ...), custom_call_target="tpu_custom_call" | custom-call | tf_op jit(solution)/shard_map/pallas_call | solution.py:281
  59.7 2.6 %collective-permute-done.2.halo_ref = f32[4,48,640]{2,1,0:T(8,128)} collective-permute-done((f32[4,48,640]{2,1,0:T(8,128)S(1)}, f32[4,48,640]{2,1,0:T(8,128)}, u32[]{:S(2)}, u32[]{:S(2)}) %collective-permute-start.2) | collective-permute-done | bytes 491552 | tf_op jit(solution)/shard_map/ppermute | solution.py:324
  62.3 2.2 %shard_map.74 = (f32[4,48,640]{2,1,0:T(8,128)S(1)}, f32[4,8,640]{2,1,0:T(8,128)S(1)}) custom-call(f32[4,48,640]{2,1,0:T(8,128)} %collective-permute-done.2.halo_ref, f32[4,48,640]{2,1,0:T(8,128)S(1)} %shard_map.70.refs_1_.outer_ref, f32[6,104,640]{2,1,0:T(8,128)S(1)} %get-tuple-element.29.edge_ref, ...), custom_call_target="tpu_custom_call" | custom-call | tf_op jit(solution)/shard_map/pallas_call | solution.py:281
  64.6 1.0 %collective-permute-start.7 = (f32[4,8,640]{2,1,0:T(8,128)S(1)}, f32[4,8,640]{2,1,0:T(8,128)S(1)}, u32[]{:S(2)}, u32[]{:S(2)}) collective-permute-start(f32[4,8,640]{2,1,0:T(8,128)S(1)} %get-tuple-element.32.own_ref), channel_id=1, source_target_pairs={{0,1},{1,0},{2,3},{3,2},{4,5},{5,4},{6,7},{7,6},{8,9},{9,8},{10,11... | collective-permute-start | bytes 245768 | tf_op jit(solution)/shard_map/ppermute | solution.py:351
  65.6 3.8 %collective-permute-done.7.other_ref = f32[4,8,640]{2,1,0:T(8,128)S(1)} collective-permute-done((f32[4,8,640]{2,1,0:T(8,128)S(1)}, f32[4,8,640]{2,1,0:T(8,128)S(1)}, u32[]{:S(2)}, u32[]{:S(2)}) %collective-permute-start.7) | collective-permute-done | bytes 81952 | tf_op jit(solution)/shard_map/ppermute | solution.py:351
  69.5 0.2 shard_map.75
  69.7 17.0 %all_to_all.5.got_ref = f32[64,1,128]{2,1,0:T(1,128)S(1)} all-to-all(f32[64,1,128]{2,1,0:T(1,128)S(1)} %get-tuple-element.35), channel_id=1, replica_groups=mesh['tile'=64,'mem'=2] {'tile'}, dimensions={0} | all-to-all | bytes 65536 | tf_op jit(solution)/shard_map/all_to_all | solution.py:353
  86.7 2.3 %shard_map.76 = (f32[4,8,640]{2,1,0:T(8,128)}, f32[832,640]{1,0:T(8,128)}) custom-call(f32[64,1,128]{2,1,0:T(1,128)S(1)} %all_to_all.5.got_ref, f32[4,8,640]{2,1,0:T(8,128)S(1)} %get-tuple-element.36.merged_ref, f32[4,104,640]{2,1,0:T(8,128)S(1)} %get-tuple-element.37.inner_ref, f32[4,56,640]{2,1,0:T(8,128)S(1)} %get-tuple-element.38.refs_0_, ...), custom_call_target="tpu_custom_call" | custom-call | tf_op jit(solution)/shard_map/pallas_call | solution.py:281
  (1 shorter events, 0.0 us)
Async XLA Ops:
  0.6 0.9 %copy-start = (f32[5,8,640]{2,1,0:T(8,128)S(1)}, f32[5,8,640]{2,1,0:T(8,128)}, u32[]{:S(2)}) copy-start(f32[5,8,640]{2,1,0:T(8,128)} %constant.4.clone.coef_ref) | copy-start | bytes 307204
  1.5 1.6 %copy-start.2 = (f32[26,4,8,640]{3,2,1,0:T(8,128)S(1)}, f32[26,4,8,640]{3,2,1,0:T(8,128)}, u32[]{:S(2)}) copy-start(f32[26,4,8,640]{3,2,1,0:T(8,128)} %param.6) | copy-start | bytes 6389764
  3.1 4.3 %copy-start.1 = (f32[5,8,640]{2,1,0:T(8,128)S(1)}, f32[5,8,640]{2,1,0:T(8,128)}, u32[]{:S(2)}) copy-start(f32[5,8,640]{2,1,0:T(8,128)} %constant.4.clone.coef_ref) | copy-start | bytes 307204
  3.1 4.3 %copy-start.3 = (f32[26,4,8,640]{3,2,1,0:T(8,128)S(1)}, f32[26,4,8,640]{3,2,1,0:T(8,128)}, u32[]{:S(2)}) copy-start(f32[26,4,8,640]{3,2,1,0:T(8,128)} %param.5) | copy-start | bytes 6389764
  3.6 3.8 %collective-permute-start.1 = (f32[4,104,640]{2,1,0:T(8,128)S(1)}, f32[4,104,640]{2,1,0:T(8,128)S(1)}, u32[]{:S(2)}, u32[]{:S(2)}) collective-permute-start(f32[4,104,640]{2,1,0:T(8,128)S(1)} %get-tuple-element.23.inner_ref.scaled_ref), channel_id=1, source_target_pairs={{0,2},{2,0},{4,6},{6,4},{8,10},{10,8},{12,14},{14,12},{16,18},{18,... | collective-permute-start | bytes 3194888 | tf_op jit(solution)/shard_map/ppermute | solution.py:314
  5.1 41.3 %collective-permute-start.4 = (f32[4,56,640]{2,1,0:T(8,128)S(1)}, f32[4,56,640]{2,1,0:T(8,128)S(1)}, u32[]{:S(2)}, u32[]{:S(2)}) collective-permute-start(f32[4,56,640]{2,1,0:T(8,128)S(1)} %get-tuple-element.24.refs_0_.outer_ref.scaled_ref), channel_id=1, source_target_pairs={{0,126},{2,4},{4,2},{6,8},{8,6},{10,12},{12,10},{14,16},{16,14},{1... | collective-permute-start | bytes 1720328 | tf_op jit(solution)/shard_map/ppermute | solution.py:313
  7.4 0.7 copy-start.4
  8.1 10.2 %copy-start.5 = (s32[26]{0:T(128)S(1)}, s32[26]{0:T(128)}, u32[]{:S(2)}) copy-start(s32[26]{0:T(128)} %param.7) | copy-start | bytes 316
  13.9 37.3 %collective-permute-start.3 = (f32[4,104,640]{2,1,0:T(8,128)}, f32[4,104,640]{2,1,0:T(8,128)}, u32[]{:S(2)}, u32[]{:S(2)}) collective-permute-start(f32[4,104,640]{2,1,0:T(8,128)} %get-tuple-element.27.inner_ref), channel_id=1, source_target_pairs={{0,2},{2,0},{4,6},{6,4},{8,10},{10,8},{12,14},{14,12},{16,18},{18,... | collective-permute-start | bytes 3194888 | tf_op jit(solution)/shard_map/ppermute | solution.py:319
  18.4 29.5 %collective-permute-start = (f32[4,48,640]{2,1,0:T(8,128)S(1)}, f32[4,48,640]{2,1,0:T(8,128)S(1)}, u32[]{:S(2)}, u32[]{:S(2)}) collective-permute-start(f32[4,48,640]{2,1,0:T(8,128)S(1)} %get-tuple-element.22.refs_1_.outer_ref.scaled_ref), channel_id=1, source_target_pairs={{0,126},{2,4},{4,2},{6,8},{8,6},{10,12},{12,10},{14,16},{16,14},{1... | collective-permute-start | bytes 1474568 | tf_op jit(solution)/shard_map/ppermute | solution.py:313
  19.6 26.1 %collective-permute-start.5 = (f32[8,128]{1,0:T(8,128)S(1)}, f32[8,128]{1,0:T(8,128)S(1)}, u32[]{:S(2)}, u32[]{:S(2)}) collective-permute-start(f32[8,128]{1,0:T(8,128)S(1)} %broadcast_in_dim.16), channel_id=1, source_target_pairs={{0,1},{1,0},{2,3},{3,2},{4,5},{5,4},{6,7},{7,6},{8,9},{9,8},{10,11... | collective-permute-start | bytes 12296 | tf_op jit(solution)/shard_map/ppermute | solution.py:310
  47.8 9.5 %collective-permute-start.6 = (f32[4,56,640]{2,1,0:T(8,128)S(1)}, f32[4,56,640]{2,1,0:T(8,128)}, u32[]{:S(2)}, u32[]{:S(2)}) collective-permute-start(f32[4,56,640]{2,1,0:T(8,128)S(1)} %shard_map.71.refs_0_.outer_ref), channel_id=1, source_target_pairs={{0,126},{2,4},{4,2},{6,8},{8,6},{10,12},{12,10},{14,16},{16,14},{1... | collective-permute-start | bytes 1720328 | tf_op jit(solution)/shard_map/ppermute | solution.py:324
  49.0 13.3 %collective-permute-start.2 = (f32[4,48,640]{2,1,0:T(8,128)S(1)}, f32[4,48,640]{2,1,0:T(8,128)}, u32[]{:S(2)}, u32[]{:S(2)}) collective-permute-start(f32[4,48,640]{2,1,0:T(8,128)S(1)} %shard_map.70.refs_1_.outer_ref), channel_id=1, source_target_pairs={{0,126},{2,4},{4,2},{6,8},{8,6},{10,12},{12,10},{14,16},{16,14},{1... | collective-permute-start | bytes 1474568 | tf_op jit(solution)/shard_map/ppermute | solution.py:324
  64.6 4.9 %collective-permute-start.7 = (f32[4,8,640]{2,1,0:T(8,128)S(1)}, f32[4,8,640]{2,1,0:T(8,128)S(1)}, u32[]{:S(2)}, u32[]{:S(2)}) collective-permute-start(f32[4,8,640]{2,1,0:T(8,128)S(1)} %get-tuple-element.32.own_ref), channel_id=1, source_target_pairs={{0,1},{1,0},{2,3},{3,2},{4,5},{5,4},{6,7},{7,6},{8,9},{9,8},{10,11... | collective-permute-start | bytes 245768 | tf_op jit(solution)/shard_map/ppermute | solution.py:351

commit v6 on v5

--- a/solution.py
+++ b/solution.py
@@ -217,23 +217,29 @@
         first, halo_ref, outer_ref, edge_ref, scaled_ref, weight_ref, coef_ref, inverse_ref, total_ref
     )
     low = low_half(total_ref.shape[1:])
+    tiles = total_ref.shape[2] // 128
     for c in range(REACH):
         outer, inner = total_ref[c] + earlier_ref[c], inner_ref[c]
         outer = outer + pltpu.roll(outer, SUB // 2, 0)
         inner = inner + pltpu.roll(inner, SUB // 2, 0)
-        logs_ref[c] = jnp.where(low, outer, inner)
-
-
-def merge_kernel(own_ref, other_ref, count_ref, mass_ref, coef_ref, merged_ref, payload_ref):
-    members, lat = mass_ref.shape[0], own_ref.shape[2]
-    scale = 1.0 / count_ref[...]
-    scale = jnp.broadcast_to(scale[:, :1], (SUB, lat))
-    level = jnp.zeros((SUB, lat), jnp.float32)
+        both = jnp.where(low, outer, inner)
+        for t in range(tiles):
+            logs_ref[rows_of(c * tiles + t), :] = both[:, t * 128 : (t + 1) * 128]
+    count = jnp.sum(weight_ref[...], axis=0, keepdims=True) * (1.0 / (SUB // 2))
+    logs_ref[rows_of(REACH * tiles), :] = jnp.broadcast_to(count, (SUB, 128))
+
+
+def merge_kernel(own_ref, other_ref, mass_ref, coef_ref, merged_ref, payload_ref):
+    members, tiles = mass_ref.shape[0], merged_ref.shape[2] // 128
+    both = lambda n: own_ref[rows_of(n), :] + other_ref[rows_of(n), :]
+    scale = 1.0 / both(REACH * tiles)
+    level = jnp.zeros((SUB, 128), jnp.float32)
     for c in range(REACH):
-        weighted = jnp.exp((own_ref[c] + other_ref[c]) * scale)
-        merged_ref[c] = weighted / coef_ref[AREA]
-        level = level + weighted
-    level = lane_fold(level)
+        for t in range(tiles):
+            span = slice(t * 128, (t + 1) * 128)
+            weighted = jnp.exp(both(c * tiles + t) * scale)
+            merged_ref[c, :, span] = weighted / coef_ref[AREA, :, span]
+            level = level + weighted
     level = level + pltpu.roll(level, SUB // 2, 0)
     spare = jnp.zeros((128 - members - SUB, 128), jnp.float32)
     table = jnp.concatenate([mass_ref[...], level, spare], axis=0)
@@ -306,13 +312,10 @@
     fields = fields.reshape(rows * lon, lat)
     weights = counts.astype(jnp.float32)
     weight_rows = jnp.broadcast_to(jnp.repeat(weights, levels)[:, None], (rows, 128))
-    count = jnp.broadcast_to(jnp.sum(weights), (SUB, 128))
-    count = count + lax.ppermute(count, "mem", [(0, 1), (1, 0)])
 
     inner, *outer = call(spread_kernel, (half, *parts), scaling, coef)
     outer_halo = [lax.ppermute(part, "tile", with_neighbour) for part in outer]
     inner_halo = lax.ppermute(inner, "tile", with_mate)
-    outer_halo[0], count = lax.optimization_barrier((outer_halo[0], count))
     v_inner, edges, filled, mass = call(
         smooth_inner_kernel, (half, edge, half, shape(rows, 128)), inner_halo, inner, fields, land_mask, coef, *outer
     )
@@ -337,7 +340,7 @@
     )
     inverse_last, logs = call(
         partial(last_return_kernel, firsts[1]),
-        (parts[1], packed),
+        (parts[1], shape((REACH * lat // 128 + 1) * SUB, 128)),
         v_outer_halo[1],
         v_outer[1],
         edges,
@@ -349,7 +352,7 @@
         scratch=[pltpu.VMEM((REACH, SUB, lat), jnp.float32)],
     )
     other = lax.ppermute(logs, "mem", [(0, 1), (1, 0)])
-    merged, payload = call(merge_kernel, (packed, shape(tiles, 1, 128)), logs, other, count, mass, coef)
+    merged, payload = call(merge_kernel, (packed, shape(tiles, 1, 128)), logs, other, mass, coef)
     got = lax.all_to_all(payload, "tile", split_axis=0, concat_axis=0)
     barycenter, updated = call(
         partial(finish_kernel, float(cells)),

time: 89.6 us -> 82.7 us (0.923)
  waiting for transfers between devices: 29.9 us -> 24.3 us
  starting transfers between devices: 14.2 us -> 16.3 us
  blocking collectives: 17 us -> 15.5 us
  other arithmetic: 1.25 us -> 0.01 us
    ppermute x1 -> x0, waiting for transfers between devices: 22.7 us -> none  [body(): count = count + lax.ppermute(count, 'mem', [(0, 1), (1, 0)])]
    ppermute x2, waiting for transfers between devices: 0.01 us -> 19.2 us  [body(): outer_halo = [lax.ppermute(part, 'tile', with_neighbour) for part in outer]]
    ppermute x1 -> x0, starting transfers between devices: 3.38 us -> none  [body(): count = count + lax.ppermute(count, 'mem', [(0, 1), (1, 0)])]
    ppermute x2, starting transfers between devices: 2.07 us -> 5.3 us  [body(): v_outer_halo.append(lax.ppermute(value, 'tile', with_neighbour))]
    ppermute x1, starting transfers between devices: 1.05 us -> 3.38 us  [body(): other = lax.ppermute(logs, 'mem', [(0, 1), (1, 0)])]
    ppermute x1, waiting for transfers between devices: 3.83 us -> 1.88 us  [body(): other = lax.ppermute(logs, 'mem', [(0, 1), (1, 0)])]
    all_to_all x1, blocking collectives: 17 us -> 15.5 us  [body(): got = lax.all_to_all(payload, 'tile', split_axis=0, concat_axis=0)]
  transfers between devices with their start and end apart: 8 -> 7, of which waited for: 5 -> 5; matrix products, arithmetic and copies ran while one was open for 2% -> 0% of each run, Pallas kernels for 19% -> 20%
where the time goes in v6:
time: 82.7 us; the launch traced here: 82.3 us
  waiting for transfers between devices  24.3 us (29%)
  Pallas kernels  21.8 us (26%)
  starting transfers between devices  16.3 us (20%)
  blocking collectives  15.5 us (19%)
  local copies, waits for them, and re-layouts  3.48 us (4%)
  between operations  0.89 us (1%)
    pallas_call x9, Pallas kernels, call(): pl.pallas_call(kernel, out_shape=outs, in_specs=[VMEM] * len(args), out_s...  21.8 us
    ppermute x2, waiting for transfers between devices, body(): outer_halo = [lax.ppermute(part, 'tile', with_neighbour) for part in outer]  19.2 us
    all_to_all x1, blocking collectives, body(): got = lax.all_to_all(payload, 'tile', split_axis=0, concat_axis=0)  15.5 us
    ppermute x2, starting transfers between devices, body(): v_outer_halo.append(lax.ppermute(value, 'tile', with_neighbour))  5.3 us
    ppermute x1, starting transfers between devices, body(): v_inner_halo = lax.ppermute(v_inner, 'tile', with_mate)  4.46 us
    ppermute x1, starting transfers between devices, body(): other = lax.ppermute(logs, 'mem', [(0, 1), (1, 0)])  3.38 us
    unnamed x12, local copies, waits for them, and re-layouts  3.23 us
    ppermute x2, waiting for transfers between devices, body(): v_outer_halo.append(lax.ppermute(value, 'tile', with_neighbour))  2.55 us
  transfers between devices with their start and end apart: 7, of which 5 were waited for; matrix products, arithmetic and copies ran while one was open for 0% of the time, Pallas kernels for 20%

profile of v6, /device:TPU:1, one launch (start us, length us, event | category | flops | bytes accessed | tf_op | source)
XLA Modules:
  0.0 82.3 jit_solution(4843067358640190625)
XLA Ops:
  0.6 0.0 copy-start
  0.6 0.9 %copy-done = f32[5,8,640]{2,1,0:T(8,128)S(1)} copy-done((f32[5,8,640]{2,1,0:T(8,128)S(1)}, f32[5,8,640]{2,1,0:T(8,128)}, u32[]{:S(2)}) %copy-start) | copy-done | bytes 102424
  1.5 0.0 copy-start.2
  1.5 1.6 %copy-done.2 = f32[26,4,8,640]{3,2,1,0:T(8,128)S(1)} copy-done((f32[26,4,8,640]{3,2,1,0:T(8,128)S(1)}, f32[26,4,8,640]{3,2,1,0:T(8,128)}, u32[]{:S(2)}) %copy-start.2) | copy-done | bytes 2129944
  3.1 0.0 copy-start.1
  3.1 0.0 copy-start.3
  3.1 0.5 shard_map.68
  3.6 1.5 %collective-permute-start.1 = (f32[4,104,640]{2,1,0:T(8,128)S(1)}, f32[4,104,640]{2,1,0:T(8,128)S(1)}, u32[]{:S(2)}, u32[]{:S(2)}) collective-permute-start(f32[4,104,640]{2,1,0:T(8,128)S(1)} %get-tuple-element.21.inner_ref.scaled_ref), channel_id=1, source_target_pairs={{0,2},{2,0},{4,6},{6,4},{8,10},{10,8},{12,14},{14,12},{16,18},{18,... | collective-permute-start | bytes 3194888 | tf_op jit(solution)/shard_map/ppermute | solution.py:318
  5.1 1.7 %collective-permute-start.4 = (f32[4,56,640]{2,1,0:T(8,128)S(1)}, f32[4,56,640]{2,1,0:T(8,128)S(1)}, u32[]{:S(2)}, u32[]{:S(2)}) collective-permute-start(f32[4,56,640]{2,1,0:T(8,128)S(1)} %get-tuple-element.22.refs_0_.outer_ref.scaled_ref), channel_id=1, source_target_pairs={{0,126},{2,4},{4,2},{6,8},{8,6},{10,12},{12,10},{14,16},{16,14},{1... | collective-permute-start | bytes 1720328 | tf_op jit(solution)/shard_map/ppermute | solution.py:317
  6.8 0.6 collective-permute-done.1.halo_ref
  7.4 0.0 copy-done.1
  7.4 0.0 copy-done.3
  7.4 0.0 copy-start.4
  7.4 0.7 copy-done.4
  8.1 5.8 %shard_map.69 = (f32[4,104,640]{2,1,0:T(8,128)}, f32[6,104,640]{2,1,0:T(8,128)S(1)}, f32[4,104,640]{2,1,0:T(8,128)S(1)}, f32[104,128]{1,0:T(8,128)S(1)}) custom-call(f32[4,104,640]{2,1,0:T(8,128)S(1)} %collective-permute-done.1.halo_ref, f32[4,104,640]{2,1,0:T(8,128)S(1)} %get-tuple-element.21.inner_ref.scaled_ref, f32[832,640]{1,0:T(8,128)S(1)} %bitcast.4, ...), custom_call_target="tpu_custom_call" | custom-call | tf_op jit(solution)/shard_map/pallas_call | solution.py:287
  13.9 4.5 %collective-permute-start.3 = (f32[4,104,640]{2,1,0:T(8,128)}, f32[4,104,640]{2,1,0:T(8,128)}, u32[]{:S(2)}, u32[]{:S(2)}) collective-permute-start(f32[4,104,640]{2,1,0:T(8,128)} %get-tuple-element.25.inner_ref), channel_id=1, source_target_pairs={{0,2},{2,0},{4,6},{6,4},{8,10},{10,8},{12,14},{14,12},{16,18},{18,... | collective-permute-start | bytes 3194888 | tf_op jit(solution)/shard_map/ppermute | solution.py:322
  18.4 0.0 collective-permute-start
  18.4 17.9 %collective-permute-done.4.halo_ref = f32[4,56,640]{2,1,0:T(8,128)S(1)} collective-permute-done((f32[4,56,640]{2,1,0:T(8,128)S(1)}, f32[4,56,640]{2,1,0:T(8,128)S(1)}, u32[]{:S(2)}, u32[]{:S(2)}) %collective-permute-start.4) | collective-permute-done | bytes 573472 | tf_op jit(solution)/shard_map/ppermute | solution.py:317
  36.3 1.3 %shard_map.71.refs_0_.outer_ref = f32[4,56,640]{2,1,0:T(8,128)S(1)} custom-call(f32[4,56,640]{2,1,0:T(8,128)S(1)} %collective-permute-done.4.halo_ref, f32[4,56,640]{2,1,0:T(8,128)S(1)} %get-tuple-element.22.refs_0_.outer_ref.scaled_ref, f32[6,104,640]{2,1,0:T(8,128)S(1)} %get-tuple-element.23.edge_ref, f32[4,104,640]{2,1,0:T(8,128)S(1)} %get-tuple-element.24.filled_ref, ...), custom_call_target="tpu_custom_call" | custom-call | tf_op jit(solution)/shard_map/pallas_call | solution.py:287
  37.6 0.0 copy-start.5
  37.6 2.6 %collective-permute-start.5 = (f32[4,56,640]{2,1,0:T(8,128)S(1)}, f32[4,56,640]{2,1,0:T(8,128)}, u32[]{:S(2)}, u32[]{:S(2)}) collective-permute-start(f32[4,56,640]{2,1,0:T(8,128)S(1)} %shard_map.71.refs_0_.outer_ref), channel_id=1, source_target_pairs={{0,126},{2,4},{4,2},{6,8},{8,6},{10,12},{12,10},{14,16},{16,14},{1... | collective-permute-start | bytes 1720328 | tf_op jit(solution)/shard_map/ppermute | solution.py:327
  40.2 1.4 %collective-permute-done.halo_ref = f32[4,48,640]{2,1,0:T(8,128)S(1)} collective-permute-done((f32[4,48,640]{2,1,0:T(8,128)S(1)}, f32[4,48,640]{2,1,0:T(8,128)S(1)}, u32[]{:S(2)}, u32[]{:S(2)}) %collective-permute-start) | collective-permute-done | bytes 491552 | tf_op jit(solution)/shard_map/ppermute | solution.py:317
  41.5 1.2 %shard_map.70.refs_1_.outer_ref = f32[4,48,640]{2,1,0:T(8,128)S(1)} custom-call(f32[4,48,640]{2,1,0:T(8,128)S(1)} %collective-permute-done.halo_ref, f32[4,48,640]{2,1,0:T(8,128)S(1)} %get-tuple-element.20.refs_1_.outer_ref.scaled_ref, f32[6,104,640]{2,1,0:T(8,128)S(1)} %get-tuple-element.23.edge_ref, f32[4,104,640]{2,1,0:T(8,128)S(1)} %get-tuple-element.24.filled_ref, ...), custom_call_target="tpu_custom_call" | custom-call | tf_op jit(solution)/shard_map/pallas_call | solution.py:287
  42.7 2.7 %collective-permute-start.2 = (f32[4,48,640]{2,1,0:T(8,128)S(1)}, f32[4,48,640]{2,1,0:T(8,128)}, u32[]{:S(2)}, u32[]{:S(2)}) collective-permute-start(f32[4,48,640]{2,1,0:T(8,128)S(1)} %shard_map.70.refs_1_.outer_ref), channel_id=1, source_target_pairs={{0,126},{2,4},{4,2},{6,8},{8,6},{10,12},{12,10},{14,16},{16,14},{1... | collective-permute-start | bytes 1474568 | tf_op jit(solution)/shard_map/ppermute | solution.py:327
  45.4 0.0 copy-done.5
  45.4 0.1 broadcast_in_dim.10
  45.5 0.1 broadcast_in_dim.11
  45.6 0.0 collective-permute-done.3.halo_ref
  45.6 0.1 broadcast_in_dim.12.weight_ref
  45.7 5.9 %shard_map.72 = (f32[4,104,640]{2,1,0:T(8,128)S(1)}, f32[6,104,640]{2,1,0:T(8,128)S(1)}, f32[4,8,640]{2,1,0:T(8,128)S(1)}) custom-call(f32[4,104,640]{2,1,0:T(8,128)} %collective-permute-done.3.halo_ref, f32[4,104,640]{2,1,0:T(8,128)} %get-tuple-element.25.inner_ref, f32[4,104,640]{2,1,0:T(8,128)S(1)} %get-tuple-element.21.inner_ref.scaled_ref, ...), custom_call_target="tpu_custom_call" | custom-call | tf_op jit(solution)/shard_map/pallas_call | solution.py:287
  51.6 0.0 collective-permute-done.5.halo_ref
  51.6 2.5 %shard_map.73 = (f32[4,56,640]{2,1,0:T(8,128)S(1)}, f32[4,8,640]{2,1,0:T(8,128)S(1)}) custom-call(f32[4,56,640]{2,1,0:T(8,128)} %collective-permute-done.5.halo_ref, f32[4,56,640]{2,1,0:T(8,128)S(1)} %shard_map.71.refs_0_.outer_ref, f32[6,104,640]{2,1,0:T(8,128)S(1)} %get-tuple-element.26.edge_ref, ...), custom_call_target="tpu_custom_call" | custom-call | tf_op jit(solution)/shard_map/pallas_call | solution.py:287
  54.1 2.5 %collective-permute-done.2.halo_ref = f32[4,48,640]{2,1,0:T(8,128)} collective-permute-done((f32[4,48,640]{2,1,0:T(8,128)S(1)}, f32[4,48,640]{2,1,0:T(8,128)}, u32[]{:S(2)}, u32[]{:S(2)}) %collective-permute-start.2) | collective-permute-done | bytes 491552 | tf_op jit(solution)/shard_map/ppermute | solution.py:327
  56.6 2.3 %shard_map.74 = (f32[4,48,640]{2,1,0:T(8,128)S(1)}, f32[168,128]{1,0:T(8,128)S(1)}) custom-call(f32[4,48,640]{2,1,0:T(8,128)} %collective-permute-done.2.halo_ref, f32[4,48,640]{2,1,0:T(8,128)S(1)} %shard_map.70.refs_1_.outer_ref, f32[6,104,640]{2,1,0:T(8,128)S(1)} %get-tuple-element.26.edge_ref, ...), custom_call_target="tpu_custom_call" | custom-call | tf_op jit(solution)/shard_map/pallas_call | solution.py:287
  58.9 3.4 %collective-permute-start.6 = (f32[168,128]{1,0:T(8,128)S(1)}, f32[168,128]{1,0:T(8,128)S(1)}, u32[]{:S(2)}, u32[]{:S(2)}) collective-permute-start(f32[168,128]{1,0:T(8,128)S(1)} %get-tuple-element.29.own_ref), channel_id=1, source_target_pairs={{0,1},{1,0},{2,3},{3,2},{4,5},{5,4},{6,7},{7,6},{8,9},{9,8},{10,11... | collective-permute-start | bytes 258056 | tf_op jit(solution)/shard_map/ppermute | solution.py:354
  62.3 1.9 %collective-permute-done.6.other_ref = f32[168,128]{1,0:T(8,128)S(1)} collective-permute-done((f32[168,128]{1,0:T(8,128)S(1)}, f32[168,128]{1,0:T(8,128)S(1)}, u32[]{:S(2)}, u32[]{:S(2)}) %collective-permute-start.6) | collective-permute-done | bytes 86048 | tf_op jit(solution)/shard_map/ppermute | solution.py:354
  64.1 0.1 shard_map.75
  64.3 15.5 %all_to_all.5.got_ref = f32[64,1,128]{2,1,0:T(1,128)S(1)} all-to-all(f32[64,1,128]{2,1,0:T(1,128)S(1)} %get-tuple-element.31), channel_id=1, replica_groups=mesh['tile'=64,'mem'=2] {'tile'}, dimensions={0} | all-to-all | bytes 65536 | tf_op jit(solution)/shard_map/all_to_all | solution.py:356
  79.8 2.3 %shard_map.76 = (f32[4,8,640]{2,1,0:T(8,128)}, f32[832,640]{1,0:T(8,128)}) custom-call(f32[64,1,128]{2,1,0:T(1,128)S(1)} %all_to_all.5.got_ref, f32[4,8,640]{2,1,0:T(8,128)S(1)} %get-tuple-element.32.merged_ref, f32[4,104,640]{2,1,0:T(8,128)S(1)} %get-tuple-element.33.inner_ref, f32[4,56,640]{2,1,0:T(8,128)S(1)} %get-tuple-element.34.refs_0_, ...), custom_call_target="tpu_custom_call" | custom-call | tf_op jit(solution)/shard_map/pallas_call | solution.py:287
  (1 shorter events, 0.0 us)
Async XLA Ops:
  0.6 0.9 %copy-start = (f32[5,8,640]{2,1,0:T(8,128)S(1)}, f32[5,8,640]{2,1,0:T(8,128)}, u32[]{:S(2)}) copy-start(f32[5,8,640]{2,1,0:T(8,128)} %constant.2.clone.coef_ref) | copy-start | bytes 307204
  1.5 1.6 %copy-start.2 = (f32[26,4,8,640]{3,2,1,0:T(8,128)S(1)}, f32[26,4,8,640]{3,2,1,0:T(8,128)}, u32[]{:S(2)}) copy-start(f32[26,4,8,640]{3,2,1,0:T(8,128)} %param.6) | copy-start | bytes 6389764
  3.1 4.3 %copy-start.1 = (f32[5,8,640]{2,1,0:T(8,128)S(1)}, f32[5,8,640]{2,1,0:T(8,128)}, u32[]{:S(2)}) copy-start(f32[5,8,640]{2,1,0:T(8,128)} %constant.2.clone.coef_ref) | copy-start | bytes 307204
  3.1 4.3 %copy-start.3 = (f32[26,4,8,640]{3,2,1,0:T(8,128)S(1)}, f32[26,4,8,640]{3,2,1,0:T(8,128)}, u32[]{:S(2)}) copy-start(f32[26,4,8,640]{3,2,1,0:T(8,128)} %param.5) | copy-start | bytes 6389764
  3.6 3.8 %collective-permute-start.1 = (f32[4,104,640]{2,1,0:T(8,128)S(1)}, f32[4,104,640]{2,1,0:T(8,128)S(1)}, u32[]{:S(2)}, u32[]{:S(2)}) collective-permute-start(f32[4,104,640]{2,1,0:T(8,128)S(1)} %get-tuple-element.21.inner_ref.scaled_ref), channel_id=1, source_target_pairs={{0,2},{2,0},{4,6},{6,4},{8,10},{10,8},{12,14},{14,12},{16,18},{18,... | collective-permute-start | bytes 3194888 | tf_op jit(solution)/shard_map/ppermute | solution.py:318
  5.1 31.2 %collective-permute-start.4 = (f32[4,56,640]{2,1,0:T(8,128)S(1)}, f32[4,56,640]{2,1,0:T(8,128)S(1)}, u32[]{:S(2)}, u32[]{:S(2)}) collective-permute-start(f32[4,56,640]{2,1,0:T(8,128)S(1)} %get-tuple-element.22.refs_0_.outer_ref.scaled_ref), channel_id=1, source_target_pairs={{0,126},{2,4},{4,2},{6,8},{8,6},{10,12},{12,10},{14,16},{16,14},{1... | collective-permute-start | bytes 1720328 | tf_op jit(solution)/shard_map/ppermute | solution.py:317
  7.4 0.7 copy-start.4
  13.9 31.7 %collective-permute-start.3 = (f32[4,104,640]{2,1,0:T(8,128)}, f32[4,104,640]{2,1,0:T(8,128)}, u32[]{:S(2)}, u32[]{:S(2)}) collective-permute-start(f32[4,104,640]{2,1,0:T(8,128)} %get-tuple-element.25.inner_ref), channel_id=1, source_target_pairs={{0,2},{2,0},{4,6},{6,4},{8,10},{10,8},{12,14},{14,12},{16,18},{18,... | collective-permute-start | bytes 3194888 | tf_op jit(solution)/shard_map/ppermute | solution.py:322
  18.4 23.2 %collective-permute-start = (f32[4,48,640]{2,1,0:T(8,128)S(1)}, f32[4,48,640]{2,1,0:T(8,128)S(1)}, u32[]{:S(2)}, u32[]{:S(2)}) collective-permute-start(f32[4,48,640]{2,1,0:T(8,128)S(1)} %get-tuple-element.20.refs_1_.outer_ref.scaled_ref), channel_id=1, source_target_pairs={{0,126},{2,4},{4,2},{6,8},{8,6},{10,12},{12,10},{14,16},{16,14},{1... | collective-permute-start | bytes 1474568 | tf_op jit(solution)/shard_map/ppermute | solution.py:317
  37.6 7.8 %copy-start.5 = (s32[26]{0:T(128)S(1)}, s32[26]{0:T(128)}, u32[]{:S(2)}) copy-start(s32[26]{0:T(128)} %param.7) | copy-start | bytes 316
  37.6 14.0 %collective-permute-start.5 = (f32[4,56,640]{2,1,0:T(8,128)S(1)}, f32[4,56,640]{2,1,0:T(8,128)}, u32[]{:S(2)}, u32[]{:S(2)}) collective-permute-start(f32[4,56,640]{2,1,0:T(8,128)S(1)} %shard_map.71.refs_0_.outer_ref), channel_id=1, source_target_pairs={{0,126},{2,4},{4,2},{6,8},{8,6},{10,12},{12,10},{14,16},{16,14},{1... | collective-permute-start | bytes 1720328 | tf_op jit(solution)/shard_map/ppermute | solution.py:327
  42.7 13.9 %collective-permute-start.2 = (f32[4,48,640]{2,1,0:T(8,128)S(1)}, f32[4,48,640]{2,1,0:T(8,128)}, u32[]{:S(2)}, u32[]{:S(2)}) collective-permute-start(f32[4,48,640]{2,1,0:T(8,128)S(1)} %shard_map.70.refs_1_.outer_ref), channel_id=1, source_target_pairs={{0,126},{2,4},{4,2},{6,8},{8,6},{10,12},{12,10},{14,16},{16,14},{1... | collective-permute-start | bytes 1474568 | tf_op jit(solution)/shard_map/ppermute | solution.py:327
  58.9 5.3 %collective-permute-start.6 = (f32[168,128]{1,0:T(8,128)S(1)}, f32[168,128]{1,0:T(8,128)S(1)}, u32[]{:S(2)}, u32[]{:S(2)}) collective-permute-start(f32[168,128]{1,0:T(8,128)S(1)} %get-tuple-element.29.own_ref), channel_id=1, source_target_pairs={{0,1},{1,0},{2,3},{3,2},{4,5},{5,4},{6,7},{7,6},{8,9},{9,8},{10,11... | collective-permute-start | bytes 258056 | tf_op jit(solution)/shard_map/ppermute | solution.py:354

commit v7 on v6

--- a/solution.py
+++ b/solution.py
@@ -47,8 +47,9 @@
 
 
 def chunk_groups(groups):
-    half = (groups + 1) // 2
-    return [half, groups - half]
+    last = max(1, groups // 6)
+    second = (groups - last) // 2
+    return [groups - last - second, second, last]
 
 
 class Chunked:
@@ -208,18 +209,16 @@
     weight_ref,
     coef_ref,
     inner_ref,
-    earlier_ref,
-    inverse_ref,
-    logs_ref,
-    total_ref,
+    *refs,
 ):
+    *earlier_refs, inverse_ref, logs_ref, total_ref = refs
     return_outer_kernel(
         first, halo_ref, outer_ref, edge_ref, scaled_ref, weight_ref, coef_ref, inverse_ref, total_ref
     )
     low = low_half(total_ref.shape[1:])
     tiles = total_ref.shape[2] // 128
     for c in range(REACH):
-        outer, inner = total_ref[c] + earlier_ref[c], inner_ref[c]
+        outer, inner = sum((ref[c] for ref in earlier_refs), total_ref[c]), inner_ref[c]
         outer = outer + pltpu.roll(outer, SUB // 2, 0)
         inner = inner + pltpu.roll(inner, SUB // 2, 0)
         both = jnp.where(low, outer, inner)
@@ -328,29 +327,26 @@
     inverse_inner, edges, inner_logs = call(
         return_inner_kernel, (half, edge, packed), v_inner_halo, v_inner, inner, weight_rows, coef, *v_outer
     )
-    inverse_first, first_logs = call(
-        partial(return_outer_kernel, firsts[0]),
-        (parts[0], packed),
-        v_outer_halo[0],
-        v_outer[0],
+    inverses, earlier = [inverse_inner], []
+    for n, first in enumerate(firsts[:-1]):
+        operands = v_outer_halo[n], v_outer[n], edges, outer[n], weight_rows, coef
+        inverse, partial_logs = call(partial(return_outer_kernel, first), (parts[n], packed), *operands)
+        inverses.append(inverse)
+        earlier.append(partial_logs)
+    inverse, logs = call(
+        partial(last_return_kernel, firsts[-1]),
+        (parts[-1], shape((REACH * lat // 128 + 1) * SUB, 128)),
+        v_outer_halo[-1],
+        v_outer[-1],
         edges,
-        outer[0],
-        weight_rows,
-        coef,
-    )
-    inverse_last, logs = call(
-        partial(last_return_kernel, firsts[1]),
-        (parts[1], shape((REACH * lat // 128 + 1) * SUB, 128)),
-        v_outer_halo[1],
-        v_outer[1],
-        edges,
-        outer[1],
+        outer[-1],
         weight_rows,
         coef,
         inner_logs,
-        first_logs,
+        *earlier,
         scratch=[pltpu.VMEM((REACH, SUB, lat), jnp.float32)],
     )
+    inverses.append(inverse)
     other = lax.ppermute(logs, "mem", [(0, 1), (1, 0)])
     merged, payload = call(merge_kernel, (packed, shape(tiles, 1, 128)), logs, other, mass, coef)
     got = lax.all_to_all(payload, "tile", split_axis=0, concat_axis=0)
@@ -359,9 +355,7 @@
         (shape(levels, lon, lat), shape(rows * lon, lat)),
         got,
         merged,
-        inverse_inner,
-        inverse_first,
-        inverse_last,
+        *inverses,
         scratch=[pltpu.VMEM((rows * lon, lat), jnp.float32), pltpu.SemaphoreType.DMA((rows // SUB,))],
         out_specs=(VMEM, HBM),
     )

time: 82.7 us -> 99.7 us (1.21)
  waiting for transfers between devices: 24.3 us -> 43.5 us
  starting transfers between devices: 16.3 us -> 12.5 us
  blocking collectives: 15.5 us -> 16.7 us
    ppermute x2 -> x3, waiting for transfers between devices: 19.2 us -> 39.3 us  [body(): outer_halo = [lax.ppermute(part, 'tile', with_neighbour) for part in outer]]
    ppermute x1, starting transfers between devices: 4.46 us -> 0.37 us  [body(): v_inner_halo = lax.ppermute(v_inner, 'tile', with_mate)]
    ppermute x2 -> x3, waiting for transfers between devices: 2.55 us -> 0.01 us  [body(): v_outer_halo.append(lax.ppermute(value, 'tile', with_neighbour))]
    ppermute x1, waiting for transfers between devices: 0.61 us -> 2.31 us  [body(): inner_halo = lax.ppermute(inner, 'tile', with_mate)]
    all_to_all x1, blocking collectives: 15.5 us -> 16.7 us  [body(): got = lax.all_to_all(payload, 'tile', split_axis=0, concat_axis=0)]
    pallas_call x9 -> x11, Pallas kernels: 21.8 us -> 22.2 us  [call(): pl.pallas_call(kernel, out_shape=outs, in_specs=[VMEM] * len(args), out_s...]
    ppermute x2 -> x3, starting transfers between devices: 5.3 us -> 5.41 us  [body(): v_outer_halo.append(lax.ppermute(value, 'tile', with_neighbour))]
  transfers between devices with their start and end apart: 7 -> 9, of which waited for: 5 -> 5; matrix products, arithmetic and copies ran while one was open for 0% -> 0% of each run, Pallas kernels for 20% -> 13%
where the time goes in v7:
time: 99.7 us; the launch traced here: 99.3 us
  waiting for transfers between devices  43.5 us (44%)
  Pallas kernels  22.2 us (22%)
  blocking collectives  16.7 us (17%)
  starting transfers between devices  12.5 us (13%)
  local copies, waits for them, and re-layouts  3.48 us (3%)
    ppermute x3, waiting for transfers between devices, body(): outer_halo = [lax.ppermute(part, 'tile', with_neighbour) for part in outer]  39.3 us
    pallas_call x11, Pallas kernels, call(): pl.pallas_call(kernel, out_shape=outs, in_specs=[VMEM] * len(args), out_s...  22.2 us
    all_to_all x1, blocking collectives, body(): got = lax.all_to_all(payload, 'tile', split_axis=0, concat_axis=0)  16.7 us
    ppermute x3, starting transfers between devices, body(): v_outer_halo.append(lax.ppermute(value, 'tile', with_neighbour))  5.41 us
    ppermute x1, starting transfers between devices, body(): other = lax.ppermute(logs, 'mem', [(0, 1), (1, 0)])  3.38 us
    unnamed x12, local copies, waits for them, and re-layouts  3.23 us
    ppermute x1, waiting for transfers between devices, body(): inner_halo = lax.ppermute(inner, 'tile', with_mate)  2.31 us
  transfers between devices with their start and end apart: 9, of which 5 were waited for; matrix products, arithmetic and copies ran while one was open for 0% of the time, Pallas kernels for 13%

profile of v7, /device:TPU:1, one launch (start us, length us, event | category | flops | bytes accessed | tf_op | source)
XLA Modules:
  0.0 99.3 jit_solution(3940260307976751618)
XLA Ops:
  0.6 0.0 copy-start
  0.6 0.9 copy-done
  1.5 0.0 copy-start.2
  1.5 1.6 %copy-done.2 = f32[26,4,8,640]{3,2,1,0:T(8,128)S(1)} copy-done((f32[26,4,8,640]{3,2,1,0:T(8,128)S(1)}, f32[26,4,8,640]{3,2,1,0:T(8,128)}, u32[]{:S(2)}) %copy-start.2) | copy-done | bytes 2129944
  3.1 0.0 copy-start.1
  3.1 0.0 copy-start.3
  3.1 0.5 shard_map.68
  3.6 1.5 %collective-permute-start.1 = (f32[4,104,640]{2,1,0:T(8,128)S(1)}, f32[4,104,640]{2,1,0:T(8,128)S(1)}, u32[]{:S(2)}, u32[]{:S(2)}) collective-permute-start(f32[4,104,640]{2,1,0:T(8,128)S(1)} %get-tuple-element.24.inner_ref.scaled_ref), channel_id=1, source_target_pairs={{0,2},{2,0},{4,6},{6,4},{8,10},{10,8},{12,14},{14,12},{16,18},{18,... | collective-permute-start | bytes 3194888 | tf_op jit(solution)/shard_map/ppermute | solution.py:317
  5.1 2.3 %collective-permute-done.1.halo_ref = f32[4,104,640]{2,1,0:T(8,128)S(1)} collective-permute-done((f32[4,104,640]{2,1,0:T(8,128)S(1)}, f32[4,104,640]{2,1,0:T(8,128)S(1)}, u32[]{:S(2)}, u32[]{:S(2)}) %collective-permute-start.1) | collective-permute-done | bytes 1064992 | tf_op jit(solution)/shard_map/ppermute | solution.py:317
  7.4 0.0 copy-done.1
  7.4 0.0 copy-done.3
  7.4 0.0 copy-start.4
  7.4 0.7 copy-done.4
  8.1 5.8 %shard_map.69 = (f32[4,104,640]{2,1,0:T(8,128)}, f32[6,104,640]{2,1,0:T(8,128)S(1)}, f32[4,104,640]{2,1,0:T(8,128)S(1)}, f32[104,128]{1,0:T(8,128)S(1)}) custom-call(f32[4,104,640]{2,1,0:T(8,128)S(1)} %collective-permute-done.1.halo_ref, f32[4,104,640]{2,1,0:T(8,128)S(1)} %get-tuple-element.24.inner_ref.scaled_ref, f32[832,640]{1,0:T(8,128)S(1)} %bitcast.4, ...), custom_call_target="tpu_custom_call" | custom-call | tf_op jit(solution)/shard_map/pallas_call | solution.py:286
  13.9 0.4 collective-permute-start.3
  14.3 1.7 %collective-permute-start.4 = (f32[4,48,640]{2,1,0:T(8,128)S(1)}, f32[4,48,640]{2,1,0:T(8,128)S(1)}, u32[]{:S(2)}, u32[]{:S(2)}) collective-permute-start(f32[4,48,640]{2,1,0:T(8,128)S(1)} %get-tuple-element.25.refs_0_.outer_ref.scaled_ref), channel_id=1, source_target_pairs={{0,126},{2,4},{4,2},{6,8},{8,6},{10,12},{12,10},{14,16},{16,14},{1... | collective-permute-start | bytes 1474568 | tf_op jit(solution)/shard_map/ppermute | solution.py:316
  16.0 0.0 collective-permute-start.5
  16.1 26.8 %collective-permute-done.4.halo_ref = f32[4,48,640]{2,1,0:T(8,128)S(1)} collective-permute-done((f32[4,48,640]{2,1,0:T(8,128)S(1)}, f32[4,48,640]{2,1,0:T(8,128)S(1)}, u32[]{:S(2)}, u32[]{:S(2)}) %collective-permute-start.4) | collective-permute-done | bytes 491552 | tf_op jit(solution)/shard_map/ppermute | solution.py:316
  42.9 1.2 %shard_map.71.refs_0_.outer_ref = f32[4,48,640]{2,1,0:T(8,128)S(1)} custom-call(f32[4,48,640]{2,1,0:T(8,128)S(1)} %collective-permute-done.4.halo_ref, f32[4,48,640]{2,1,0:T(8,128)S(1)} %get-tuple-element.25.refs_0_.outer_ref.scaled_ref, f32[6,104,640]{2,1,0:T(8,128)S(1)} %get-tuple-element.27.edge_ref, f32[4,104,640]{2,1,0:T(8,128)S(1)} %get-tuple-element.28.filled_ref, ...), custom_call_target="tpu_custom_call" | custom-call | tf_op jit(solution)/shard_map/pallas_call | solution.py:286
  44.1 2.6 %collective-permute-start.6 = (f32[4,48,640]{2,1,0:T(8,128)S(1)}, f32[4,48,640]{2,1,0:T(8,128)}, u32[]{:S(2)}, u32[]{:S(2)}) collective-permute-start(f32[4,48,640]{2,1,0:T(8,128)S(1)} %shard_map.71.refs_0_.outer_ref), channel_id=1, source_target_pairs={{0,126},{2,4},{4,2},{6,8},{8,6},{10,12},{12,10},{14,16},{16,14},{1... | collective-permute-start | bytes 1474568 | tf_op jit(solution)/shard_map/ppermute | solution.py:326
  46.6 2.4 %collective-permute-done.5.halo_ref = f32[4,40,640]{2,1,0:T(8,128)S(1)} collective-permute-done((f32[4,40,640]{2,1,0:T(8,128)S(1)}, f32[4,40,640]{2,1,0:T(8,128)S(1)}, u32[]{:S(2)}, u32[]{:S(2)}) %collective-permute-start.5) | collective-permute-done | bytes 409632 | tf_op jit(solution)/shard_map/ppermute | solution.py:316
  49.0 1.1 %shard_map.72.refs_1_.outer_ref = f32[4,40,640]{2,1,0:T(8,128)S(1)} custom-call(f32[4,40,640]{2,1,0:T(8,128)S(1)} %collective-permute-done.5.halo_ref, f32[4,40,640]{2,1,0:T(8,128)S(1)} %get-tuple-element.26.refs_1_.outer_ref.scaled_ref, f32[6,104,640]{2,1,0:T(8,128)S(1)} %get-tuple-element.27.edge_ref, f32[4,104,640]{2,1,0:T(8,128)S(1)} %get-tuple-element.28.filled_ref, ...), custom_call_target="tpu_custom_call" | custom-call | tf_op jit(solution)/shard_map/pallas_call | solution.py:286
  50.2 0.0 copy-start.5
  50.2 2.6 %collective-permute-start.7 = (f32[4,40,640]{2,1,0:T(8,128)S(1)}, f32[4,40,640]{2,1,0:T(8,128)}, u32[]{:S(2)}, u32[]{:S(2)}) collective-permute-start(f32[4,40,640]{2,1,0:T(8,128)S(1)} %shard_map.72.refs_1_.outer_ref), channel_id=1, source_target_pairs={{0,126},{2,4},{4,2},{6,8},{8,6},{10,12},{12,10},{14,16},{16,14},{1... | collective-permute-start | bytes 1228808 | tf_op jit(solution)/shard_map/ppermute | solution.py:326
  52.8 0.1 collective-permute-start
  52.8 10.0 %collective-permute-done.halo_ref = f32[4,16,640]{2,1,0:T(8,128)S(1)} collective-permute-done((f32[4,16,640]{2,1,0:T(8,128)S(1)}, f32[4,16,640]{2,1,0:T(8,128)S(1)}, u32[]{:S(2)}, u32[]{:S(2)}) %collective-permute-start) | collective-permute-done | bytes 163872 | tf_op jit(solution)/shard_map/ppermute | solution.py:316
  62.9 0.4 shard_map.70.refs_2_.outer_ref
  63.3 0.3 collective-permute-start.2
  63.6 0.0 copy-done.5
  63.6 0.1 broadcast_in_dim.10
  63.7 0.1 broadcast_in_dim.11
  63.8 0.0 collective-permute-done.3.halo_ref
  63.8 0.1 broadcast_in_dim.12.weight_ref
  63.9 5.9 %shard_map.73 = (f32[4,104,640]{2,1,0:T(8,128)S(1)}, f32[6,104,640]{2,1,0:T(8,128)S(1)}, f32[4,8,640]{2,1,0:T(8,128)S(1)}) custom-call(f32[4,104,640]{2,1,0:T(8,128)} %collective-permute-done.3.halo_ref, f32[4,104,640]{2,1,0:T(8,128)} %get-tuple-element.29.inner_ref, f32[4,104,640]{2,1,0:T(8,128)S(1)} %get-tuple-element.24.inner_ref.scaled_ref, ...), custom_call_target="tpu_custom_call" | custom-call | tf_op jit(solution)/shard_map/pallas_call | solution.py:286
  69.8 0.0 collective-permute-done.7.halo_ref
  69.8 2.2 %shard_map.75 = (f32[4,40,640]{2,1,0:T(8,128)S(1)}, f32[4,8,640]{2,1,0:T(8,128)S(1)}) custom-call(f32[4,40,640]{2,1,0:T(8,128)} %collective-permute-done.7.halo_ref, f32[4,40,640]{2,1,0:T(8,128)S(1)} %shard_map.72.refs_1_.outer_ref, f32[6,104,640]{2,1,0:T(8,128)S(1)} %get-tuple-element.30.edge_ref, ...), custom_call_target="tpu_custom_call" | custom-call | tf_op jit(solution)/shard_map/pallas_call | solution.py:286
  72.0 0.0 collective-permute-done.6.halo_ref
  72.0 2.2 %shard_map.74 = (f32[4,48,640]{2,1,0:T(8,128)S(1)}, f32[4,8,640]{2,1,0:T(8,128)S(1)}) custom-call(f32[4,48,640]{2,1,0:T(8,128)} %collective-permute-done.6.halo_ref, f32[4,48,640]{2,1,0:T(8,128)S(1)} %shard_map.71.refs_0_.outer_ref, f32[6,104,640]{2,1,0:T(8,128)S(1)} %get-tuple-element.30.edge_ref, ...), custom_call_target="tpu_custom_call" | custom-call | tf_op jit(solution)/shard_map/pallas_call | solution.py:286
  74.2 0.0 collective-permute-done.2.halo_ref
  74.2 0.5 shard_map.76
  74.7 3.4 %collective-permute-start.8 = (f32[168,128]{1,0:T(8,128)S(1)}, f32[168,128]{1,0:T(8,128)S(1)}, u32[]{:S(2)}, u32[]{:S(2)}) collective-permute-start(f32[168,128]{1,0:T(8,128)S(1)} %get-tuple-element.34.own_ref), channel_id=1, source_target_pairs={{0,1},{1,0},{2,3},{3,2},{4,5},{5,4},{6,7},{7,6},{8,9},{9,8},{10,11... | collective-permute-start | bytes 258056 | tf_op jit(solution)/shard_map/ppermute | solution.py:350
  78.1 1.9 %collective-permute-done.8.other_ref = f32[168,128]{1,0:T(8,128)S(1)} collective-permute-done((f32[168,128]{1,0:T(8,128)S(1)}, f32[168,128]{1,0:T(8,128)S(1)}, u32[]{:S(2)}, u32[]{:S(2)}) %collective-permute-start.8) | collective-permute-done | bytes 86048 | tf_op jit(solution)/shard_map/ppermute | solution.py:350
  80.0 0.1 shard_map.77
  80.1 16.7 %all_to_all.5.got_ref = f32[64,1,128]{2,1,0:T(1,128)S(1)} all-to-all(f32[64,1,128]{2,1,0:T(1,128)S(1)} %get-tuple-element.36), channel_id=1, replica_groups=mesh['tile'=64,'mem'=2] {'tile'}, dimensions={0} | all-to-all | bytes 65536 | tf_op jit(solution)/shard_map/all_to_all | solution.py:352
  96.8 2.3 %shard_map.78 = (f32[4,8,640]{2,1,0:T(8,128)}, f32[832,640]{1,0:T(8,128)}) custom-call(f32[64,1,128]{2,1,0:T(1,128)S(1)} %all_to_all.5.got_ref, f32[4,8,640]{2,1,0:T(8,128)S(1)} %get-tuple-element.37.merged_ref, f32[4,104,640]{2,1,0:T(8,128)S(1)} %get-tuple-element.38.inner_ref, f32[4,48,640]{2,1,0:T(8,128)S(1)} %get-tuple-element.39.refs_0_, ...), custom_call_target="tpu_custom_call" | custom-call | tf_op jit(solution)/shard_map/pallas_call | solution.py:286
  (1 shorter events, 0.0 us)
Async XLA Ops:
  0.6 0.9 copy-start
  1.5 1.6 %copy-start.2 = (f32[26,4,8,640]{3,2,1,0:T(8,128)S(1)}, f32[26,4,8,640]{3,2,1,0:T(8,128)}, u32[]{:S(2)}) copy-start(f32[26,4,8,640]{3,2,1,0:T(8,128)} %param.6) | copy-start | bytes 6389764
  3.1 4.3 %copy-start.1 = (f32[5,8,640]{2,1,0:T(8,128)S(1)}, f32[5,8,640]{2,1,0:T(8,128)}, u32[]{:S(2)}) copy-start(f32[5,8,640]{2,1,0:T(8,128)} %constant.2.clone.coef_ref) | copy-start | bytes 307204
  3.1 4.3 %copy-start.3 = (f32[26,4,8,640]{3,2,1,0:T(8,128)S(1)}, f32[26,4,8,640]{3,2,1,0:T(8,128)}, u32[]{:S(2)}) copy-start(f32[26,4,8,640]{3,2,1,0:T(8,128)} %param.5) | copy-start | bytes 6389764
  3.6 3.8 %collective-permute-start.1 = (f32[4,104,640]{2,1,0:T(8,128)S(1)}, f32[4,104,640]{2,1,0:T(8,128)S(1)}, u32[]{:S(2)}, u32[]{:S(2)}) collective-permute-start(f32[4,104,640]{2,1,0:T(8,128)S(1)} %get-tuple-element.24.inner_ref.scaled_ref), channel_id=1, source_target_pairs={{0,2},{2,0},{4,6},{6,4},{8,10},{10,8},{12,14},{14,12},{16,18},{18,... | collective-permute-start | bytes 3194888 | tf_op jit(solution)/shard_map/ppermute | solution.py:317
  7.4 0.7 copy-start.4
  13.9 49.9 %collective-permute-start.3 = (f32[4,104,640]{2,1,0:T(8,128)}, f32[4,104,640]{2,1,0:T(8,128)}, u32[]{:S(2)}, u32[]{:S(2)}) collective-permute-start(f32[4,104,640]{2,1,0:T(8,128)} %get-tuple-element.29.inner_ref), channel_id=1, source_target_pairs={{0,2},{2,0},{4,6},{6,4},{8,10},{10,8},{12,14},{14,12},{16,18},{18,... | collective-permute-start | bytes 3194888 | tf_op jit(solution)/shard_map/ppermute | solution.py:321
  14.3 28.6 %collective-permute-start.4 = (f32[4,48,640]{2,1,0:T(8,128)S(1)}, f32[4,48,640]{2,1,0:T(8,128)S(1)}, u32[]{:S(2)}, u32[]{:S(2)}) collective-permute-start(f32[4,48,640]{2,1,0:T(8,128)S(1)} %get-tuple-element.25.refs_0_.outer_ref.scaled_ref), channel_id=1, source_target_pairs={{0,126},{2,4},{4,2},{6,8},{8,6},{10,12},{12,10},{14,16},{16,14},{1... | collective-permute-start | bytes 1474568 | tf_op jit(solution)/shard_map/ppermute | solution.py:316
  16.0 33.0 %collective-permute-start.5 = (f32[4,40,640]{2,1,0:T(8,128)S(1)}, f32[4,40,640]{2,1,0:T(8,128)S(1)}, u32[]{:S(2)}, u32[]{:S(2)}) collective-permute-start(f32[4,40,640]{2,1,0:T(8,128)S(1)} %get-tuple-element.26.refs_1_.outer_ref.scaled_ref), channel_id=1, source_target_pairs={{0,126},{2,4},{4,2},{6,8},{8,6},{10,12},{12,10},{14,16},{16,14},{1... | collective-permute-start | bytes 1228808 | tf_op jit(solution)/shard_map/ppermute | solution.py:316
  44.1 27.9 %collective-permute-start.6 = (f32[4,48,640]{2,1,0:T(8,128)S(1)}, f32[4,48,640]{2,1,0:T(8,128)}, u32[]{:S(2)}, u32[]{:S(2)}) collective-permute-start(f32[4,48,640]{2,1,0:T(8,128)S(1)} %shard_map.71.refs_0_.outer_ref), channel_id=1, source_target_pairs={{0,126},{2,4},{4,2},{6,8},{8,6},{10,12},{12,10},{14,16},{16,14},{1... | collective-permute-start | bytes 1474568 | tf_op jit(solution)/shard_map/ppermute | solution.py:326
  50.2 13.5 %copy-start.5 = (s32[26]{0:T(128)S(1)}, s32[26]{0:T(128)}, u32[]{:S(2)}) copy-start(s32[26]{0:T(128)} %param.7) | copy-start | bytes 316
  50.2 19.6 %collective-permute-start.7 = (f32[4,40,640]{2,1,0:T(8,128)S(1)}, f32[4,40,640]{2,1,0:T(8,128)}, u32[]{:S(2)}, u32[]{:S(2)}) collective-permute-start(f32[4,40,640]{2,1,0:T(8,128)S(1)} %shard_map.72.refs_1_.outer_ref), channel_id=1, source_target_pairs={{0,126},{2,4},{4,2},{6,8},{8,6},{10,12},{12,10},{14,16},{16,14},{1... | collective-permute-start | bytes 1228808 | tf_op jit(solution)/shard_map/ppermute | solution.py:326
  52.8 10.1 %collective-permute-start = (f32[4,16,640]{2,1,0:T(8,128)S(1)}, f32[4,16,640]{2,1,0:T(8,128)S(1)}, u32[]{:S(2)}, u32[]{:S(2)}) collective-permute-start(f32[4,16,640]{2,1,0:T(8,128)S(1)} %get-tuple-element.23.refs_2_.outer_ref.scaled_ref), channel_id=1, source_target_pairs={{0,126},{2,4},{4,2},{6,8},{8,6},{10,12},{12,10},{14,16},{16,14},{1... | collective-permute-start | bytes 491528 | tf_op jit(solution)/shard_map/ppermute | solution.py:316
  63.3 10.9 %collective-permute-start.2 = (f32[4,16,640]{2,1,0:T(8,128)S(1)}, f32[4,16,640]{2,1,0:T(8,128)S(1)}, u32[]{:S(2)}, u32[]{:S(2)}) collective-permute-start(f32[4,16,640]{2,1,0:T(8,128)S(1)} %shard_map.70.refs_2_.outer_ref), channel_id=1, source_target_pairs={{0,126},{2,4},{4,2},{6,8},{8,6},{10,12},{12,10},{14,16},{16,14},{1... | collective-permute-start | bytes 491528 | tf_op jit(solution)/shard_map/ppermute | solution.py:326
  74.7 5.3 %collective-permute-start.8 = (f32[168,128]{1,0:T(8,128)S(1)}, f32[168,128]{1,0:T(8,128)S(1)}, u32[]{:S(2)}, u32[]{:S(2)}) collective-permute-start(f32[168,128]{1,0:T(8,128)S(1)} %get-tuple-element.34.own_ref), channel_id=1, source_target_pairs={{0,1},{1,0},{2,3},{3,2},{4,5},{5,4},{6,7},{7,6},{8,9},{9,8},{10,11... | collective-permute-start | bytes 258056 | tf_op jit(solution)/shard_map/ppermute | solution.py:350

commit v8 on v7

--- a/solution.py
+++ b/solution.py
@@ -47,9 +47,9 @@
 
 
 def chunk_groups(groups):
-    last = max(1, groups // 6)
-    second = (groups - last) // 2
-    return [groups - last - second, second, last]
+    half = (groups + 1) // 2
+    last = max(1, (groups - half) // 3)
+    return [[half], [groups - half - last, last]]
 
 
 class Chunked:
@@ -161,24 +161,25 @@
                 out_ref[c, rows_of(group), :] = filled[c + REACH] / smoothed[c]
 
 
-def smooth_outer_kernel(first, halo_ref, outer_ref, edge_ref, filled_ref, coef_ref, out_ref):
+def smooth_outer_kernel(first, halo_ref, outer_ref, edge_ref, filled_ref, coef_ref, *out_refs):
     last = first + outer_ref.shape[1] // SUB
+    out = Chunked(out_refs)
     for batch in batches(last, first):
         for group, smoothed in outer_half(batch, first, halo_ref, outer_ref, edge_ref, coef_ref):
-            for c in range(REACH):
-                out_ref[c, rows_of(group - first), :] = filled_ref[c, rows_of(group), :] / smoothed[c]
+            filled = stack_of(filled_ref, group)
+            out.put(group - first, [top / bottom for top, bottom in zip(filled, smoothed)])
 
 
 def low_half(shape):
     return lax.broadcasted_iota(jnp.int32, shape, 0) < SUB // 2
 
 
-def add_logs(group, held, result, scaled_ref, weight_ref, inverse_ref, total_ref):
-    lat = scaled_ref.shape[2]
+def add_logs(group, held, result, scaled, weight_ref, inverse_ref, total_ref):
+    lat = total_ref.shape[2]
     weight = jnp.broadcast_to(weight_ref[rows_of(group), :1], (SUB, lat))
     for c in range(REACH):
         inverse_ref[c, rows_of(held), :] = 1.0 / result[c]
-        total_ref[c] = total_ref[c] + weight * jnp.log(scaled_ref[c, rows_of(held), :] * result[c])
+        total_ref[c] = total_ref[c] + weight * jnp.log(scaled[c] * result[c])
 
 
 def return_inner_kernel(halo_ref, inner_ref, scaled_ref, weight_ref, coef_ref, *refs):
@@ -187,20 +188,22 @@
     total_ref[...] = jnp.zeros_like(total_ref)
     for batch in batches(groups):
         for group, result in inner_half(batch, halo_ref, inner_ref, outer_refs, coef_ref, edge_ref):
-            add_logs(group, group, result, scaled_ref, weight_ref, inverse_ref, total_ref)
+            add_logs(group, group, result, stack_of(scaled_ref, group), weight_ref, inverse_ref, total_ref)
 
 
 def return_outer_kernel(
-    first, halo_ref, outer_ref, edge_ref, scaled_ref, weight_ref, coef_ref, inverse_ref, total_ref
+    base, first, halo_ref, outer_ref, edge_ref, scaled_ref, weight_ref, coef_ref, inverse_ref, total_ref
 ):
     last = first + outer_ref.shape[1] // SUB
     total_ref[...] = jnp.zeros_like(total_ref)
     for batch in batches(last, first):
         for group, result in outer_half(batch, first, halo_ref, outer_ref, edge_ref, coef_ref):
-            add_logs(group, group - first, result, scaled_ref, weight_ref, inverse_ref, total_ref)
+            scaled = stack_of(scaled_ref, group - base)
+            add_logs(group, group - first, result, scaled, weight_ref, inverse_ref, total_ref)
 
 
 def last_return_kernel(
+    base,
     first,
     halo_ref,
     outer_ref,
@@ -213,7 +216,7 @@
 ):
     *earlier_refs, inverse_ref, logs_ref, total_ref = refs
     return_outer_kernel(
-        first, halo_ref, outer_ref, edge_ref, scaled_ref, weight_ref, coef_ref, inverse_ref, total_ref
+        base, first, halo_ref, outer_ref, edge_ref, scaled_ref, weight_ref, coef_ref, inverse_ref, total_ref
     )
     low = low_half(total_ref.shape[1:])
     tiles = total_ref.shape[2] // 128
@@ -302,8 +305,8 @@
     edge = shape(2 * REACH - 2, rows, lat)
     packed = shape(REACH, SUB, lat)
     chunks = chunk_groups(rows // SUB)
-    firsts = [sum(chunks[:n]) for n in range(len(chunks))]
-    parts = [shape(REACH, n * SUB, lat) for n in chunks]
+    bases = [sum(map(sum, chunks[:n])) for n in range(len(chunks))]
+    parts = [shape(REACH, sum(own) * SUB, lat) for own in chunks]
     coef = jnp.asarray(coefficients(lat))
     with_mate = [(i, i ^ 1) for i in range(tiles)]
     with_neighbour = [(i, (i + (1 if i % 2 else -1)) % tiles) for i in range(tiles)]
@@ -319,34 +322,33 @@
         smooth_inner_kernel, (half, edge, half, shape(rows, 128)), inner_halo, inner, fields, land_mask, coef, *outer
     )
     v_inner_halo = lax.ppermute(v_inner, "tile", with_mate)
-    v_outer, v_outer_halo = [], []
-    for first, part, halo, own in zip(firsts, parts, outer_halo, outer):
-        (value,) = call(partial(smooth_outer_kernel, first), (part,), halo, own, edges, filled, coef)
-        v_outer.append(value)
-        v_outer_halo.append(lax.ppermute(value, "tile", with_neighbour))
+    v_outer, v_outer_halo, places = [], [], []
+    for base, sizes, halo, own in zip(bases, chunks, outer_halo, outer):
+        outs = tuple(shape(REACH, size * SUB, lat) for size in sizes)
+        values = call(partial(smooth_outer_kernel, base), outs, halo, own, edges, filled, coef)
+        v_outer += values
+        v_outer_halo += [lax.ppermute(value, "tile", with_neighbour) for value in values]
+        places += [(base, base + sum(sizes[:n]), own) for n in range(len(sizes))]
     inverse_inner, edges, inner_logs = call(
         return_inner_kernel, (half, edge, packed), v_inner_halo, v_inner, inner, weight_rows, coef, *v_outer
     )
     inverses, earlier = [inverse_inner], []
-    for n, first in enumerate(firsts[:-1]):
-        operands = v_outer_halo[n], v_outer[n], edges, outer[n], weight_rows, coef
-        inverse, partial_logs = call(partial(return_outer_kernel, first), (parts[n], packed), *operands)
+    for n, (base, first, own) in enumerate(places):
+        operands = v_outer_halo[n], v_outer[n], edges, own, weight_rows, coef
+        part = shape(*v_outer[n].shape)
+        if n < len(places) - 1:
+            inverse, logs = call(partial(return_outer_kernel, base, first), (part, packed), *operands)
+            earlier.append(logs)
+        else:
+            inverse, logs = call(
+                partial(last_return_kernel, base, first),
+                (part, shape((REACH * lat // 128 + 1) * SUB, 128)),
+                *operands,
+                inner_logs,
+                *earlier,
+                scratch=[pltpu.VMEM((REACH, SUB, lat), jnp.float32)],
+            )
         inverses.append(inverse)
-        earlier.append(partial_logs)
-    inverse, logs = call(
-        partial(last_return_kernel, firsts[-1]),
-        (parts[-1], shape((REACH * lat // 128 + 1) * SUB, 128)),
-        v_outer_halo[-1],
-        v_outer[-1],
-        edges,
-        outer[-1],
-        weight_rows,
-        coef,
-        inner_logs,
-        *earlier,
-        scratch=[pltpu.VMEM((REACH, SUB, lat), jnp.float32)],
-    )
-    inverses.append(inverse)
     other = lax.ppermute(logs, "mem", [(0, 1), (1, 0)])
     merged, payload = call(merge_kernel, (packed, shape(tiles, 1, 128)), logs, other, mass, coef)
     got = lax.all_to_all(payload, "tile", split_axis=0, concat_axis=0)

time: 99.7 us -> 83.4 us (0.84)
  waiting for transfers between devices: 43.5 us -> 24.9 us
  starting transfers between devices: 12.5 us -> 16.4 us
  blocking collectives: 16.7 us -> 15.6 us
    ppermute x3 -> x2, waiting for transfers between devices: 39.3 us -> 19.2 us  [body(): outer_halo = [lax.ppermute(part, 'tile', with_neighbour) for part in outer]]
    ppermute x1, starting transfers between devices: 0.37 us -> 4.46 us  [body(): v_inner_halo = lax.ppermute(v_inner, 'tile', with_mate)]
    ppermute x3, waiting for transfers between devices: 0.01 us -> 3.18 us  [body(): lax.ppermute(value, 'tile', with_neighbour)]
    ppermute x1, waiting for transfers between devices: 2.31 us -> 0.61 us  [body(): inner_halo = lax.ppermute(inner, 'tile', with_mate)]
    all_to_all x1, blocking collectives: 16.7 us -> 15.6 us  [body(): got = lax.all_to_all(payload, 'tile', split_axis=0, concat_axis=0)]
    pallas_call x11 -> x10, Pallas kernels: 22.2 us -> 21.8 us  [call(): pl.pallas_call(kernel, out_shape=outs, in_specs=[VMEM] * len(args), out_s...]
  transfers between devices with their start and end apart: 9 -> 8, of which waited for: 5 -> 5; matrix products, arithmetic and copies ran while one was open for 0% -> 0% of each run, Pallas kernels for 13% -> 22%
where the time goes in v8:
time: 83.4 us; the launch traced here: 83 us
  waiting for transfers between devices  24.9 us (30%)
  Pallas kernels  21.8 us (26%)
  starting transfers between devices  16.4 us (20%)
  blocking collectives  15.6 us (19%)
  local copies, waits for them, and re-layouts  3.48 us (4%)
  between operations  0.9 us (1%)
    pallas_call x10, Pallas kernels, call(): pl.pallas_call(kernel, out_shape=outs, in_specs=[VMEM] * len(args), out_s...  21.8 us
    ppermute x2, waiting for transfers between devices, body(): outer_halo = [lax.ppermute(part, 'tile', with_neighbour) for part in outer]  19.2 us
    all_to_all x1, blocking collectives, body(): got = lax.all_to_all(payload, 'tile', split_axis=0, concat_axis=0)  15.6 us
    ppermute x3, starting transfers between devices, body(): lax.ppermute(value, 'tile', with_neighbour)  5.39 us
    ppermute x1, starting transfers between devices, body(): v_inner_halo = lax.ppermute(v_inner, 'tile', with_mate)  4.46 us
    ppermute x1, starting transfers between devices, body(): other = lax.ppermute(logs, 'mem', [(0, 1), (1, 0)])  3.3 us
    unnamed x12, local copies, waits for them, and re-layouts  3.23 us
    ppermute x3, waiting for transfers between devices, body(): lax.ppermute(value, 'tile', with_neighbour)  3.18 us
  transfers between devices with their start and end apart: 8, of which 5 were waited for; matrix products, arithmetic and copies ran while one was open for 0% of the time, Pallas kernels for 22%

profile of v8, /device:TPU:1, one launch (start us, length us, event | category | flops | bytes accessed | tf_op | source)
XLA Modules:
  0.0 83.0 jit_solution(4619570842223618459)
XLA Ops:
  0.6 0.0 copy-start
  0.6 0.9 %copy-done = f32[5,8,640]{2,1,0:T(8,128)S(1)} copy-done((f32[5,8,640]{2,1,0:T(8,128)S(1)}, f32[5,8,640]{2,1,0:T(8,128)}, u32[]{:S(2)}) %copy-start) | copy-done | bytes 102424
  1.5 0.0 copy-start.2
  1.5 1.6 %copy-done.2 = f32[26,4,8,640]{3,2,1,0:T(8,128)S(1)} copy-done((f32[26,4,8,640]{3,2,1,0:T(8,128)S(1)}, f32[26,4,8,640]{3,2,1,0:T(8,128)}, u32[]{:S(2)}) %copy-start.2) | copy-done | bytes 2129944
  3.1 0.0 copy-start.1
  3.1 0.0 copy-start.3
  3.1 0.5 shard_map.68
  3.6 1.5 %collective-permute-start.1 = (f32[4,104,640]{2,1,0:T(8,128)S(1)}, f32[4,104,640]{2,1,0:T(8,128)S(1)}, u32[]{:S(2)}, u32[]{:S(2)}) collective-permute-start(f32[4,104,640]{2,1,0:T(8,128)S(1)} %get-tuple-element.25.inner_ref.scaled_ref), channel_id=1, source_target_pairs={{0,2},{2,0},{4,6},{6,4},{8,10},{10,8},{12,14},{14,12},{16,18},{18,... | collective-permute-start | bytes 3194888 | tf_op jit(solution)/shard_map/ppermute | solution.py:320
  5.1 1.7 %collective-permute-start.4 = (f32[4,56,640]{2,1,0:T(8,128)S(1)}, f32[4,56,640]{2,1,0:T(8,128)S(1)}, u32[]{:S(2)}, u32[]{:S(2)}) collective-permute-start(f32[4,56,640]{2,1,0:T(8,128)S(1)} %get-tuple-element.26.refs_0_.outer_ref.scaled_ref), channel_id=1, source_target_pairs={{0,126},{2,4},{4,2},{6,8},{8,6},{10,12},{12,10},{14,16},{16,14},{1... | collective-permute-start | bytes 1720328 | tf_op jit(solution)/shard_map/ppermute | solution.py:319
  6.8 0.6 collective-permute-done.1.halo_ref
  7.4 0.0 copy-done.1
  7.4 0.0 copy-done.3
  7.4 0.0 copy-start.4
  7.4 0.7 copy-done.4
  8.1 5.8 %shard_map.69 = (f32[4,104,640]{2,1,0:T(8,128)}, f32[6,104,640]{2,1,0:T(8,128)S(1)}, f32[4,104,640]{2,1,0:T(8,128)S(1)}, f32[104,128]{1,0:T(8,128)S(1)}) custom-call(f32[4,104,640]{2,1,0:T(8,128)S(1)} %collective-permute-done.1.halo_ref, f32[4,104,640]{2,1,0:T(8,128)S(1)} %get-tuple-element.25.inner_ref.scaled_ref, f32[832,640]{1,0:T(8,128)S(1)} %bitcast.4, ...), custom_call_target="tpu_custom_call" | custom-call | tf_op jit(solution)/shard_map/pallas_call | solution.py:289
  13.9 4.5 %collective-permute-start.3 = (f32[4,104,640]{2,1,0:T(8,128)}, f32[4,104,640]{2,1,0:T(8,128)}, u32[]{:S(2)}, u32[]{:S(2)}) collective-permute-start(f32[4,104,640]{2,1,0:T(8,128)} %get-tuple-element.30.inner_ref), channel_id=1, source_target_pairs={{0,2},{2,0},{4,6},{6,4},{8,10},{10,8},{12,14},{14,12},{16,18},{18,... | collective-permute-start | bytes 3194888 | tf_op jit(solution)/shard_map/ppermute | solution.py:324
  18.4 0.0 collective-permute-start
  18.4 17.9 %collective-permute-done.4.halo_ref = f32[4,56,640]{2,1,0:T(8,128)S(1)} collective-permute-done((f32[4,56,640]{2,1,0:T(8,128)S(1)}, f32[4,56,640]{2,1,0:T(8,128)S(1)}, u32[]{:S(2)}, u32[]{:S(2)}) %collective-permute-start.4) | collective-permute-done | bytes 573472 | tf_op jit(solution)/shard_map/ppermute | solution.py:319
  36.3 1.3 %shard_map.71.refs_0_.outer_ref = f32[4,56,640]{2,1,0:T(8,128)S(1)} custom-call(f32[4,56,640]{2,1,0:T(8,128)S(1)} %collective-permute-done.4.halo_ref, f32[4,56,640]{2,1,0:T(8,128)S(1)} %get-tuple-element.26.refs_0_.outer_ref.scaled_ref, f32[6,104,640]{2,1,0:T(8,128)S(1)} %get-tuple-element.27.edge_ref, f32[4,104,640]{2,1,0:T(8,128)S(1)} %get-tuple-element.28.filled_ref, ...), custom_call_target="tpu_custom_call" | custom-call | tf_op jit(solution)/shard_map/pallas_call | solution.py:289
  37.6 0.0 copy-start.5
  37.6 2.6 %collective-permute-start.5 = (f32[4,56,640]{2,1,0:T(8,128)S(1)}, f32[4,56,640]{2,1,0:T(8,128)}, u32[]{:S(2)}, u32[]{:S(2)}) collective-permute-start(f32[4,56,640]{2,1,0:T(8,128)S(1)} %shard_map.71.refs_0_.outer_ref), channel_id=1, source_target_pairs={{0,126},{2,4},{4,2},{6,8},{8,6},{10,12},{12,10},{14,16},{16,14},{1... | collective-permute-start | bytes 1720328 | tf_op jit(solution)/shard_map/ppermute | solution.py:330
  40.2 1.4 %collective-permute-done.halo_ref = f32[4,48,640]{2,1,0:T(8,128)S(1)} collective-permute-done((f32[4,48,640]{2,1,0:T(8,128)S(1)}, f32[4,48,640]{2,1,0:T(8,128)S(1)}, u32[]{:S(2)}, u32[]{:S(2)}) %collective-permute-start) | collective-permute-done | bytes 491552 | tf_op jit(solution)/shard_map/ppermute | solution.py:319
  41.5 1.2 %shard_map.70 = (f32[4,32,640]{2,1,0:T(8,128)S(1)}, f32[4,16,640]{2,1,0:T(8,128)S(1)}) custom-call(f32[4,48,640]{2,1,0:T(8,128)S(1)} %collective-permute-done.halo_ref, f32[4,48,640]{2,1,0:T(8,128)S(1)} %get-tuple-element.24.refs_1_.outer_ref.scaled_ref, f32[6,104,640]{2,1,0:T(8,128)S(1)} %get-tuple-element.27.edge_ref, ...), custom_call_target="tpu_custom_call" | custom-call | tf_op jit(solution)/shard_map/pallas_call | solution.py:289
  42.7 2.6 %collective-permute-start.6 = (f32[4,32,640]{2,1,0:T(8,128)S(1)}, f32[4,32,640]{2,1,0:T(8,128)}, u32[]{:S(2)}, u32[]{:S(2)}) collective-permute-start(f32[4,32,640]{2,1,0:T(8,128)S(1)} %get-tuple-element.31.refs_1_.outer_ref), channel_id=1, source_target_pairs={{0,126},{2,4},{4,2},{6,8},{8,6},{10,12},{12,10},{14,16},{16,14},{1... | collective-permute-start | bytes 983048 | tf_op jit(solution)/shard_map/ppermute | solution.py:330
  45.3 0.3 collective-permute-start.2
  45.5 0.0 copy-done.5
  45.5 0.1 broadcast_in_dim.10
  45.6 0.1 broadcast_in_dim.11
  45.7 0.0 collective-permute-done.3.halo_ref
  45.7 0.1 broadcast_in_dim.12.weight_ref
  45.8 5.9 %shard_map.72 = (f32[4,104,640]{2,1,0:T(8,128)S(1)}, f32[6,104,640]{2,1,0:T(8,128)S(1)}, f32[4,8,640]{2,1,0:T(8,128)S(1)}) custom-call(f32[4,104,640]{2,1,0:T(8,128)} %collective-permute-done.3.halo_ref, f32[4,104,640]{2,1,0:T(8,128)} %get-tuple-element.30.inner_ref, f32[4,104,640]{2,1,0:T(8,128)S(1)} %get-tuple-element.25.inner_ref.scaled_ref, ...), custom_call_target="tpu_custom_call" | custom-call | tf_op jit(solution)/shard_map/pallas_call | solution.py:289
  51.7 3.2 %collective-permute-done.6.halo_ref = f32[4,32,640]{2,1,0:T(8,128)} collective-permute-done((f32[4,32,640]{2,1,0:T(8,128)S(1)}, f32[4,32,640]{2,1,0:T(8,128)}, u32[]{:S(2)}, u32[]{:S(2)}) %collective-permute-start.6) | collective-permute-done | bytes 327712 | tf_op jit(solution)/shard_map/ppermute | solution.py:330
  54.9 1.8 %shard_map.74 = (f32[4,32,640]{2,1,0:T(8,128)S(1)}, f32[4,8,640]{2,1,0:T(8,128)S(1)}) custom-call(f32[4,32,640]{2,1,0:T(8,128)} %collective-permute-done.6.halo_ref, f32[4,32,640]{2,1,0:T(8,128)S(1)} %get-tuple-element.31.refs_1_.outer_ref, f32[6,104,640]{2,1,0:T(8,128)S(1)} %get-tuple-element.32.edge_ref, ...), custom_call_target="tpu_custom_call" | custom-call | tf_op jit(solution)/shard_map/pallas_call | solution.py:289
  56.7 0.0 collective-permute-done.5.halo_ref
  56.7 2.5 %shard_map.73 = (f32[4,56,640]{2,1,0:T(8,128)S(1)}, f32[4,8,640]{2,1,0:T(8,128)S(1)}) custom-call(f32[4,56,640]{2,1,0:T(8,128)} %collective-permute-done.5.halo_ref, f32[4,56,640]{2,1,0:T(8,128)S(1)} %shard_map.71.refs_0_.outer_ref, f32[6,104,640]{2,1,0:T(8,128)S(1)} %get-tuple-element.32.edge_ref, ...), custom_call_target="tpu_custom_call" | custom-call | tf_op jit(solution)/shard_map/pallas_call | solution.py:289
  59.1 0.0 collective-permute-done.2.halo_ref
  59.2 0.5 shard_map.75
  59.6 3.3 %collective-permute-start.7 = (f32[168,128]{1,0:T(8,128)S(1)}, f32[168,128]{1,0:T(8,128)S(1)}, u32[]{:S(2)}, u32[]{:S(2)}) collective-permute-start(f32[168,128]{1,0:T(8,128)S(1)} %get-tuple-element.36.own_ref), channel_id=1, source_target_pairs={{0,1},{1,0},{2,3},{3,2},{4,5},{5,4},{6,7},{7,6},{8,9},{9,8},{10,11... | collective-permute-start | bytes 258056 | tf_op jit(solution)/shard_map/ppermute | solution.py:352
  62.9 1.9 %collective-permute-done.7.other_ref = f32[168,128]{1,0:T(8,128)S(1)} collective-permute-done((f32[168,128]{1,0:T(8,128)S(1)}, f32[168,128]{1,0:T(8,128)S(1)}, u32[]{:S(2)}, u32[]{:S(2)}) %collective-permute-start.7) | collective-permute-done | bytes 86048 | tf_op jit(solution)/shard_map/ppermute | solution.py:352
  64.8 0.1 shard_map.76
  65.0 15.6 %all_to_all.5.got_ref = f32[64,1,128]{2,1,0:T(1,128)S(1)} all-to-all(f32[64,1,128]{2,1,0:T(1,128)S(1)} %get-tuple-element.38), channel_id=1, replica_groups=mesh['tile'=64,'mem'=2] {'tile'}, dimensions={0} | all-to-all | bytes 65536 | tf_op jit(solution)/shard_map/all_to_all | solution.py:354
  80.5 2.3 %shard_map.77 = (f32[4,8,640]{2,1,0:T(8,128)}, f32[832,640]{1,0:T(8,128)}) custom-call(f32[64,1,128]{2,1,0:T(1,128)S(1)} %all_to_all.5.got_ref, f32[4,8,640]{2,1,0:T(8,128)S(1)} %get-tuple-element.39.merged_ref, f32[4,104,640]{2,1,0:T(8,128)S(1)} %get-tuple-element.40.inner_ref, f32[4,56,640]{2,1,0:T(8,128)S(1)} %get-tuple-element.41.refs_0_, ...), custom_call_target="tpu_custom_call" | custom-call | tf_op jit(solution)/shard_map/pallas_call | solution.py:289
  (1 shorter events, 0.0 us)
Async XLA Ops:
  0.6 0.9 %copy-start = (f32[5,8,640]{2,1,0:T(8,128)S(1)}, f32[5,8,640]{2,1,0:T(8,128)}, u32[]{:S(2)}) copy-start(f32[5,8,640]{2,1,0:T(8,128)} %constant.2.clone.coef_ref) | copy-start | bytes 307204
  1.5 1.6 %copy-start.2 = (f32[26,4,8,640]{3,2,1,0:T(8,128)S(1)}, f32[26,4,8,640]{3,2,1,0:T(8,128)}, u32[]{:S(2)}) copy-start(f32[26,4,8,640]{3,2,1,0:T(8,128)} %param.6) | copy-start | bytes 6389764
  3.1 4.3 %copy-start.1 = (f32[5,8,640]{2,1,0:T(8,128)S(1)}, f32[5,8,640]{2,1,0:T(8,128)}, u32[]{:S(2)}) copy-start(f32[5,8,640]{2,1,0:T(8,128)} %constant.2.clone.coef_ref) | copy-start | bytes 307204
  3.1 4.3 %copy-start.3 = (f32[26,4,8,640]{3,2,1,0:T(8,128)S(1)}, f32[26,4,8,640]{3,2,1,0:T(8,128)}, u32[]{:S(2)}) copy-start(f32[26,4,8,640]{3,2,1,0:T(8,128)} %param.5) | copy-start | bytes 6389764
  3.6 3.8 %collective-permute-start.1 = (f32[4,104,640]{2,1,0:T(8,128)S(1)}, f32[4,104,640]{2,1,0:T(8,128)S(1)}, u32[]{:S(2)}, u32[]{:S(2)}) collective-permute-start(f32[4,104,640]{2,1,0:T(8,128)S(1)} %get-tuple-element.25.inner_ref.scaled_ref), channel_id=1, source_target_pairs={{0,2},{2,0},{4,6},{6,4},{8,10},{10,8},{12,14},{14,12},{16,18},{18,... | collective-permute-start | bytes 3194888 | tf_op jit(solution)/shard_map/ppermute | solution.py:320
  5.1 31.2 %collective-permute-start.4 = (f32[4,56,640]{2,1,0:T(8,128)S(1)}, f32[4,56,640]{2,1,0:T(8,128)S(1)}, u32[]{:S(2)}, u32[]{:S(2)}) collective-permute-start(f32[4,56,640]{2,1,0:T(8,128)S(1)} %get-tuple-element.26.refs_0_.outer_ref.scaled_ref), channel_id=1, source_target_pairs={{0,126},{2,4},{4,2},{6,8},{8,6},{10,12},{12,10},{14,16},{16,14},{1... | collective-permute-start | bytes 1720328 | tf_op jit(solution)/shard_map/ppermute | solution.py:319
  7.4 0.7 copy-start.4
  13.9 31.8 %collective-permute-start.3 = (f32[4,104,640]{2,1,0:T(8,128)}, f32[4,104,640]{2,1,0:T(8,128)}, u32[]{:S(2)}, u32[]{:S(2)}) collective-permute-start(f32[4,104,640]{2,1,0:T(8,128)} %get-tuple-element.30.inner_ref), channel_id=1, source_target_pairs={{0,2},{2,0},{4,6},{6,4},{8,10},{10,8},{12,14},{14,12},{16,18},{18,... | collective-permute-start | bytes 3194888 | tf_op jit(solution)/shard_map/ppermute | solution.py:324
  18.4 23.2 %collective-permute-start = (f32[4,48,640]{2,1,0:T(8,128)S(1)}, f32[4,48,640]{2,1,0:T(8,128)S(1)}, u32[]{:S(2)}, u32[]{:S(2)}) collective-permute-start(f32[4,48,640]{2,1,0:T(8,128)S(1)} %get-tuple-element.24.refs_1_.outer_ref.scaled_ref), channel_id=1, source_target_pairs={{0,126},{2,4},{4,2},{6,8},{8,6},{10,12},{12,10},{14,16},{16,14},{1... | collective-permute-start | bytes 1474568 | tf_op jit(solution)/shard_map/ppermute | solution.py:319
  37.6 7.9 %copy-start.5 = (s32[26]{0:T(128)S(1)}, s32[26]{0:T(128)}, u32[]{:S(2)}) copy-start(s32[26]{0:T(128)} %param.7) | copy-start | bytes 316
  37.6 19.1 %collective-permute-start.5 = (f32[4,56,640]{2,1,0:T(8,128)S(1)}, f32[4,56,640]{2,1,0:T(8,128)}, u32[]{:S(2)}, u32[]{:S(2)}) collective-permute-start(f32[4,56,640]{2,1,0:T(8,128)S(1)} %shard_map.71.refs_0_.outer_ref), channel_id=1, source_target_pairs={{0,126},{2,4},{4,2},{6,8},{8,6},{10,12},{12,10},{14,16},{16,14},{1... | collective-permute-start | bytes 1720328 | tf_op jit(solution)/shard_map/ppermute | solution.py:330
  42.7 12.2 %collective-permute-start.6 = (f32[4,32,640]{2,1,0:T(8,128)S(1)}, f32[4,32,640]{2,1,0:T(8,128)}, u32[]{:S(2)}, u32[]{:S(2)}) collective-permute-start(f32[4,32,640]{2,1,0:T(8,128)S(1)} %get-tuple-element.31.refs_1_.outer_ref), channel_id=1, source_target_pairs={{0,126},{2,4},{4,2},{6,8},{8,6},{10,12},{12,10},{14,16},{16,14},{1... | collective-permute-start | bytes 983048 | tf_op jit(solution)/shard_map/ppermute | solution.py:330
  45.3 13.9 %collective-permute-start.2 = (f32[4,16,640]{2,1,0:T(8,128)S(1)}, f32[4,16,640]{2,1,0:T(8,128)S(1)}, u32[]{:S(2)}, u32[]{:S(2)}) collective-permute-start(f32[4,16,640]{2,1,0:T(8,128)S(1)} %get-tuple-element.29.refs_2_.outer_ref), channel_id=1, source_target_pairs={{0,126},{2,4},{4,2},{6,8},{8,6},{10,12},{12,10},{14,16},{16,14},{1... | collective-permute-start | bytes 491528 | tf_op jit(solution)/shard_map/ppermute | solution.py:330
  59.6 5.2 %collective-permute-start.7 = (f32[168,128]{1,0:T(8,128)S(1)}, f32[168,128]{1,0:T(8,128)S(1)}, u32[]{:S(2)}, u32[]{:S(2)}) collective-permute-start(f32[168,128]{1,0:T(8,128)S(1)} %get-tuple-element.36.own_ref), channel_id=1, source_target_pairs={{0,1},{1,0},{2,3},{3,2},{4,5},{5,4},{6,7},{7,6},{8,9},{9,8},{10,11... | collective-permute-start | bytes 258056 | tf_op jit(solution)/shard_map/ppermute | solution.py:352

commit v9 on v8

--- a/solution.py
+++ b/solution.py
@@ -321,11 +321,14 @@
     v_inner, edges, filled, mass = call(
         smooth_inner_kernel, (half, edge, half, shape(rows, 128)), inner_halo, inner, fields, land_mask, coef, *outer
     )
-    v_inner_halo = lax.ppermute(v_inner, "tile", with_mate)
     v_outer, v_outer_halo, places = [], [], []
     for base, sizes, halo, own in zip(bases, chunks, outer_halo, outer):
         outs = tuple(shape(REACH, size * SUB, lat) for size in sizes)
         values = call(partial(smooth_outer_kernel, base), outs, halo, own, edges, filled, coef)
+        if not v_outer:
+            v_inner, *values = lax.optimization_barrier((v_inner, *values))
+            v_inner_halo = lax.ppermute(v_inner, "tile", with_mate)
+            v_inner_halo, *values = lax.optimization_barrier((v_inner_halo, *values))
         v_outer += values
         v_outer_halo += [lax.ppermute(value, "tile", with_neighbour) for value in values]
         places += [(base, base + sum(sizes[:n]), own) for n in range(len(sizes))]
@@ -334,6 +337,8 @@
     )
     inverses, earlier = [inverse_inner], []
     for n, (base, first, own) in enumerate(places):
+        if earlier:
+            v_outer_halo[n], earlier[-1] = lax.optimization_barrier((v_outer_halo[n], earlier[-1]))
         operands = v_outer_halo[n], v_outer[n], edges, own, weight_rows, coef
         part = shape(*v_outer[n].shape)
         if n < len(places) - 1:

time: 83.4 us -> 87.3 us (1.047)
  waiting for transfers between devices: 24.9 us -> 29.7 us
  local copies, waits for them, and re-layouts: 3.48 us -> 6.93 us
  starting transfers between devices: 16.4 us -> 13 us
  Pallas kernels: 21.8 us -> 19.2 us
  blocking collectives: 15.6 us -> 17.1 us
    ppermute x2, waiting for transfers between devices: 19.2 us -> 26.3 us  [body(): outer_halo = [lax.ppermute(part, 'tile', with_neighbour) for part in outer]]
    ppermute x1, starting transfers between devices: 4.46 us -> 0.09 us  [body(): v_inner_halo = lax.ppermute(v_inner, 'tile', with_mate)]
    unnamed x12 -> x20, local copies, waits for them, and re-layouts: 3.23 us -> 6.68 us
    ppermute x3, waiting for transfers between devices: 3.18 us -> 0.01 us  [body(): lax.ppermute(value, 'tile', with_neighbour)]
    pallas_call x10, Pallas kernels: 21.8 us -> 19.2 us  [call(): pl.pallas_call(kernel, out_shape=outs, in_specs=[VMEM] * len(args), out_s...]
    ppermute x2, starting transfers between devices: 1.7 us -> 3.48 us  [body(): outer_halo = [lax.ppermute(part, 'tile', with_neighbour) for part in outer]]
    all_to_all x1, blocking collectives: 15.6 us -> 17.1 us  [body(): got = lax.all_to_all(payload, 'tile', split_axis=0, concat_axis=0)]
    ppermute x1, waiting for transfers between devices: 0.01 us -> 0.89 us  [body(): v_inner_halo = lax.ppermute(v_inner, 'tile', with_mate)]
  transfers between devices with their start and end apart: 8 -> 8, of which waited for: 5 -> 5; matrix products, arithmetic and copies ran while one was open for 0% -> 0% of each run, Pallas kernels for 22% -> 17%
where the time goes in v9:
time: 87.3 us; the launch traced here: 86.9 us
  waiting for transfers between devices  29.7 us (34%)
  Pallas kernels  19.2 us (22%)
  blocking collectives  17.1 us (20%)
  starting transfers between devices  13 us (15%)
  local copies, waits for them, and re-layouts  6.93 us (8%)
  between operations  0.94 us (1%)
    ppermute x2, waiting for transfers between devices, body(): outer_halo = [lax.ppermute(part, 'tile', with_neighbour) for part in outer]  26.3 us
    pallas_call x10, Pallas kernels, call(): pl.pallas_call(kernel, out_shape=outs, in_specs=[VMEM] * len(args), out_s...  19.2 us
    all_to_all x1, blocking collectives, body(): got = lax.all_to_all(payload, 'tile', split_axis=0, concat_axis=0)  17.1 us
    unnamed x20, local copies, waits for them, and re-layouts  6.68 us
    ppermute x3, starting transfers between devices, body(): lax.ppermute(value, 'tile', with_neighbour)  4.53 us
    ppermute x2, starting transfers between devices, body(): outer_halo = [lax.ppermute(part, 'tile', with_neighbour) for part in outer]  3.48 us
    ppermute x1, starting transfers between devices, body(): other = lax.ppermute(logs, 'mem', [(0, 1), (1, 0)])  3.38 us
    ppermute x1, waiting for transfers between devices, body(): other = lax.ppermute(logs, 'mem', [(0, 1), (1, 0)])  1.88 us
  transfers between devices with their start and end apart: 8, of which 5 were waited for; matrix products, arithmetic and copies ran while one was open for 0% of the time, Pallas kernels for 17%

profile of v9, /device:TPU:1, one launch (start us, length us, event | category | flops | bytes accessed | tf_op | source)
XLA Modules:
  0.0 86.9 jit_solution(10417472579110700711)
XLA Ops:
  0.6 0.0 copy-start
  0.6 0.9 %copy-done = f32[5,8,640]{2,1,0:T(8,128)S(1)} copy-done((f32[5,8,640]{2,1,0:T(8,128)S(1)}, f32[5,8,640]{2,1,0:T(8,128)}, u32[]{:S(2)}) %copy-start) | copy-done | bytes 102424
  1.5 0.0 copy-start.2
  1.5 1.6 %copy-done.2 = f32[26,4,8,640]{3,2,1,0:T(8,128)S(1)} copy-done((f32[26,4,8,640]{3,2,1,0:T(8,128)S(1)}, f32[26,4,8,640]{3,2,1,0:T(8,128)}, u32[]{:S(2)}) %copy-start.2) | copy-done | bytes 2129944
  3.1 0.0 copy-start.1
  3.1 0.0 copy-start.3
  3.1 0.5 shard_map.68
  3.6 1.5 %collective-permute-start.1 = (f32[4,104,640]{2,1,0:T(8,128)S(1)}, f32[4,104,640]{2,1,0:T(8,128)S(1)}, u32[]{:S(2)}, u32[]{:S(2)}) collective-permute-start(f32[4,104,640]{2,1,0:T(8,128)S(1)} %get-tuple-element.33.inner_ref.scaled_ref), channel_id=1, source_target_pairs={{0,2},{2,0},{4,6},{6,4},{8,10},{10,8},{12,14},{14,12},{16,18},{18,... | collective-permute-start | bytes 3194888 | tf_op jit(solution)/shard_map/ppermute | solution.py:320
  5.1 1.7 %collective-permute-start.4 = (f32[4,56,640]{2,1,0:T(8,128)S(1)}, f32[4,56,640]{2,1,0:T(8,128)S(1)}, u32[]{:S(2)}, u32[]{:S(2)}) collective-permute-start(f32[4,56,640]{2,1,0:T(8,128)S(1)} %get-tuple-element.34.refs_0_.outer_ref.scaled_ref), channel_id=1, source_target_pairs={{0,126},{2,4},{4,2},{6,8},{8,6},{10,12},{12,10},{14,16},{16,14},{1... | collective-permute-start | bytes 1720328 | tf_op jit(solution)/shard_map/ppermute | solution.py:319
  6.8 0.6 collective-permute-done.1.halo_ref
  7.4 0.0 copy-done.1
  7.4 0.0 copy-done.3
  7.4 0.0 copy-start.8
  7.4 0.7 copy-done.8
  8.1 4.8 %shard_map.69 = (f32[4,104,640]{2,1,0:T(8,128)S(1)}, f32[6,104,640]{2,1,0:T(8,128)S(1)}, f32[4,104,640]{2,1,0:T(8,128)S(1)}, f32[104,128]{1,0:T(8,128)S(1)}) custom-call(f32[4,104,640]{2,1,0:T(8,128)S(1)} %collective-permute-done.1.halo_ref, f32[4,104,640]{2,1,0:T(8,128)S(1)} %get-tuple-element.33.inner_ref.scaled_ref, f32[832,640]{1,0:T(8,128)S(1)} %bitcast.4, ...), custom_call_target="tpu_custom_call" | custom-call | tf_op jit(solution)/shard_map/pallas_call | solution.py:289
  12.9 0.0 copy-start.4
  12.9 7.4 %collective-permute-done.4.halo_ref = f32[4,56,640]{2,1,0:T(8,128)S(1)} collective-permute-done((f32[4,56,640]{2,1,0:T(8,128)S(1)}, f32[4,56,640]{2,1,0:T(8,128)S(1)}, u32[]{:S(2)}, u32[]{:S(2)}) %collective-permute-start.4) | collective-permute-done | bytes 573472 | tf_op jit(solution)/shard_map/ppermute | solution.py:319
  20.4 1.3 %shard_map.71.refs_0_.outer_ref = f32[4,56,640]{2,1,0:T(8,128)S(1)} custom-call(f32[4,56,640]{2,1,0:T(8,128)S(1)} %collective-permute-done.4.halo_ref, f32[4,56,640]{2,1,0:T(8,128)S(1)} %get-tuple-element.34.refs_0_.outer_ref.scaled_ref, f32[6,104,640]{2,1,0:T(8,128)S(1)} %get-tuple-element.35.edge_ref, f32[4,104,640]{2,1,0:T(8,128)S(1)} %get-tuple-element.36.filled_ref, ...), custom_call_target="tpu_custom_call" | custom-call | tf_op jit(solution)/shard_map/pallas_call | solution.py:289
  21.7 0.0 copy-done.4
  21.7 0.0 copy-start.9
  21.7 0.1 collective-permute-start.5
  21.8 1.8 %collective-permute-start = (f32[4,48,640]{2,1,0:T(8,128)S(1)}, f32[4,48,640]{2,1,0:T(8,128)S(1)}, u32[]{:S(2)}, u32[]{:S(2)}) collective-permute-start(f32[4,48,640]{2,1,0:T(8,128)S(1)} %get-tuple-element.32.refs_1_.outer_ref.scaled_ref), channel_id=1, source_target_pairs={{0,126},{2,4},{4,2},{6,8},{8,6},{10,12},{12,10},{14,16},{16,14},{1... | collective-permute-start | bytes 1474568 | tf_op jit(solution)/shard_map/ppermute | solution.py:319
  23.6 0.9 %collective-permute-done.5.halo_ref = f32[4,104,640]{2,1,0:T(8,128)S(1)} collective-permute-done((f32[4,104,640]{2,1,0:T(8,128)S(1)}, f32[4,104,640]{2,1,0:T(8,128)S(1)}, u32[]{:S(2)}, u32[]{:S(2)}) %collective-permute-start.5) | collective-permute-done | bytes 1064992 | tf_op jit(solution)/shard_map/ppermute | solution.py:330
  24.5 0.0 copy-start.6
  24.5 1.0 %copy-done.6 = f32[4,104,640]{2,1,0:T(8,128)} copy-done((f32[4,104,640]{2,1,0:T(8,128)}, f32[4,104,640]{2,1,0:T(8,128)S(1)}, u32[]{:S(2)}) %copy-start.6) | copy-done | bytes 1064984
  25.5 1.7 %collective-permute-start.6 = (f32[4,56,640]{2,1,0:T(8,128)S(1)}, f32[4,56,640]{2,1,0:T(8,128)}, u32[]{:S(2)}, u32[]{:S(2)}) collective-permute-start(f32[4,56,640]{2,1,0:T(8,128)S(1)} %shard_map.71.refs_0_.outer_ref), channel_id=1, source_target_pairs={{0,126},{2,4},{4,2},{6,8},{8,6},{10,12},{12,10},{14,16},{16,14},{1... | collective-permute-start | bytes 1720328 | tf_op jit(solution)/shard_map/ppermute | solution.py:333
  27.2 18.9 %collective-permute-done.halo_ref = f32[4,48,640]{2,1,0:T(8,128)S(1)} collective-permute-done((f32[4,48,640]{2,1,0:T(8,128)S(1)}, f32[4,48,640]{2,1,0:T(8,128)S(1)}, u32[]{:S(2)}, u32[]{:S(2)}) %collective-permute-start) | collective-permute-done | bytes 491552 | tf_op jit(solution)/shard_map/ppermute | solution.py:319
  46.0 1.2 %shard_map.70 = (f32[4,32,640]{2,1,0:T(8,128)S(1)}, f32[4,16,640]{2,1,0:T(8,128)S(1)}) custom-call(f32[4,48,640]{2,1,0:T(8,128)S(1)} %collective-permute-done.halo_ref, f32[4,48,640]{2,1,0:T(8,128)S(1)} %get-tuple-element.32.refs_1_.outer_ref.scaled_ref, f32[6,104,640]{2,1,0:T(8,128)S(1)} %get-tuple-element.35.edge_ref, ...), custom_call_target="tpu_custom_call" | custom-call | tf_op jit(solution)/shard_map/pallas_call | solution.py:289
  47.2 2.6 %collective-permute-start.3 = (f32[4,32,640]{2,1,0:T(8,128)S(1)}, f32[4,32,640]{2,1,0:T(8,128)}, u32[]{:S(2)}, u32[]{:S(2)}) collective-permute-start(f32[4,32,640]{2,1,0:T(8,128)S(1)} %get-tuple-element.38.refs_1_.outer_ref), channel_id=1, source_target_pairs={{0,126},{2,4},{4,2},{6,8},{8,6},{10,12},{12,10},{14,16},{16,14},{1... | collective-permute-start | bytes 983048 | tf_op jit(solution)/shard_map/ppermute | solution.py:333
  49.8 0.3 collective-permute-start.2
  50.0 0.0 copy-done.9
  50.1 0.1 broadcast_in_dim.10
  50.1 0.1 broadcast_in_dim.11
  50.2 0.1 broadcast_in_dim.12.weight_ref
  50.3 0.0 copy-start.5
  50.3 1.2 %copy-done.5 = f32[4,104,640]{2,1,0:T(8,128)S(1)} copy-done((f32[4,104,640]{2,1,0:T(8,128)S(1)}, f32[4,104,640]{2,1,0:T(8,128)}, u32[]{:S(2)}) %copy-start.5) | copy-done | bytes 1064984
  51.6 0.0 copy-start.7
  51.6 1.2 %copy-done.7 = f32[4,104,640]{2,1,0:T(8,128)S(1)} copy-done((f32[4,104,640]{2,1,0:T(8,128)S(1)}, f32[4,104,640]{2,1,0:T(8,128)}, u32[]{:S(2)}) %copy-start.7) | copy-done | bytes 1064984
  52.8 4.3 %shard_map.72 = (f32[4,104,640]{2,1,0:T(8,128)S(1)}, f32[6,104,640]{2,1,0:T(8,128)S(1)}, f32[4,8,640]{2,1,0:T(8,128)S(1)}) custom-call(f32[4,104,640]{2,1,0:T(8,128)S(1)} %copy-done.7, f32[4,104,640]{2,1,0:T(8,128)S(1)} %copy-done.5, f32[4,104,640]{2,1,0:T(8,128)S(1)} %get-tuple-element.33.inner_ref.scaled_ref, f32[104,128]{1,0:T(8,128)S(1)} %broadcast_in_dim.12.weight_ref, ...), custom_call_target="tpu_custom_call" | custom-call | tf_op jit(solution)/shard_map/pallas_call | solution.py:289
  57.1 0.0 collective-permute-done.6.halo_ref
  57.1 2.5 %shard_map.73 = (f32[4,56,640]{2,1,0:T(8,128)S(1)}, f32[4,8,640]{2,1,0:T(8,128)S(1)}) custom-call(f32[4,56,640]{2,1,0:T(8,128)} %collective-permute-done.6.halo_ref, f32[4,56,640]{2,1,0:T(8,128)S(1)} %shard_map.71.refs_0_.outer_ref, f32[6,104,640]{2,1,0:T(8,128)S(1)} %get-tuple-element.44.edge_ref, ...), custom_call_target="tpu_custom_call" | custom-call | tf_op jit(solution)/shard_map/pallas_call | solution.py:289
  59.6 0.0 collective-permute-done.3.halo_ref
  59.6 1.8 %shard_map.74 = (f32[4,32,640]{2,1,0:T(8,128)S(1)}, f32[4,8,640]{2,1,0:T(8,128)S(1)}) custom-call(f32[4,32,640]{2,1,0:T(8,128)} %collective-permute-done.3.halo_ref, f32[4,32,640]{2,1,0:T(8,128)S(1)} %get-tuple-element.38.refs_1_.outer_ref, f32[6,104,640]{2,1,0:T(8,128)S(1)} %get-tuple-element.44.edge_ref, ...), custom_call_target="tpu_custom_call" | custom-call | tf_op jit(solution)/shard_map/pallas_call | solution.py:289
  61.4 0.0 collective-permute-done.2.halo_ref
  61.4 0.5 shard_map.75
  61.9 3.4 %collective-permute-start.7 = (f32[168,128]{1,0:T(8,128)S(1)}, f32[168,128]{1,0:T(8,128)S(1)}, u32[]{:S(2)}, u32[]{:S(2)}) collective-permute-start(f32[168,128]{1,0:T(8,128)S(1)} %get-tuple-element.52.own_ref), channel_id=1, source_target_pairs={{0,1},{1,0},{2,3},{3,2},{4,5},{5,4},{6,7},{7,6},{8,9},{9,8},{10,11... | collective-permute-start | bytes 258056 | tf_op jit(solution)/shard_map/ppermute | solution.py:357
  65.3 1.9 %collective-permute-done.7.other_ref = f32[168,128]{1,0:T(8,128)S(1)} collective-permute-done((f32[168,128]{1,0:T(8,128)S(1)}, f32[168,128]{1,0:T(8,128)S(1)}, u32[]{:S(2)}, u32[]{:S(2)}) %collective-permute-start.7) | collective-permute-done | bytes 86048 | tf_op jit(solution)/shard_map/ppermute | solution.py:357
  67.1 0.1 shard_map.76
  67.3 17.1 %all_to_all.5.got_ref = f32[64,1,128]{2,1,0:T(1,128)S(1)} all-to-all(f32[64,1,128]{2,1,0:T(1,128)S(1)} %get-tuple-element.54), channel_id=1, replica_groups=mesh['tile'=64,'mem'=2] {'tile'}, dimensions={0} | all-to-all | bytes 65536 | tf_op jit(solution)/shard_map/all_to_all | solution.py:359
  84.4 2.3 %shard_map.77 = (f32[4,8,640]{2,1,0:T(8,128)}, f32[832,640]{1,0:T(8,128)}) custom-call(f32[64,1,128]{2,1,0:T(1,128)S(1)} %all_to_all.5.got_ref, f32[4,8,640]{2,1,0:T(8,128)S(1)} %get-tuple-element.55.merged_ref, f32[4,104,640]{2,1,0:T(8,128)S(1)} %get-tuple-element.56.inner_ref, f32[4,56,640]{2,1,0:T(8,128)S(1)} %get-tuple-element.57.refs_0_, ...), custom_call_target="tpu_custom_call" | custom-call | tf_op jit(solution)/shard_map/pallas_call | solution.py:289
  (1 shorter events, 0.0 us)
Async XLA Ops:
  0.6 0.9 %copy-start = (f32[5,8,640]{2,1,0:T(8,128)S(1)}, f32[5,8,640]{2,1,0:T(8,128)}, u32[]{:S(2)}) copy-start(f32[5,8,640]{2,1,0:T(8,128)} %constant.2.clone.coef_ref) | copy-start | bytes 307204
  1.5 1.6 %copy-start.2 = (f32[26,4,8,640]{3,2,1,0:T(8,128)S(1)}, f32[26,4,8,640]{3,2,1,0:T(8,128)}, u32[]{:S(2)}) copy-start(f32[26,4,8,640]{3,2,1,0:T(8,128)} %param.6) | copy-start | bytes 6389764
  3.1 4.3 %copy-start.1 = (f32[5,8,640]{2,1,0:T(8,128)S(1)}, f32[5,8,640]{2,1,0:T(8,128)}, u32[]{:S(2)}) copy-start(f32[5,8,640]{2,1,0:T(8,128)} %constant.2.clone.coef_ref) | copy-start | bytes 307204
  3.1 4.3 %copy-start.3 = (f32[26,4,8,640]{3,2,1,0:T(8,128)S(1)}, f32[26,4,8,640]{3,2,1,0:T(8,128)}, u32[]{:S(2)}) copy-start(f32[26,4,8,640]{3,2,1,0:T(8,128)} %param.5) | copy-start | bytes 6389764
  3.6 3.8 %collective-permute-start.1 = (f32[4,104,640]{2,1,0:T(8,128)S(1)}, f32[4,104,640]{2,1,0:T(8,128)S(1)}, u32[]{:S(2)}, u32[]{:S(2)}) collective-permute-start(f32[4,104,640]{2,1,0:T(8,128)S(1)} %get-tuple-element.33.inner_ref.scaled_ref), channel_id=1, source_target_pairs={{0,2},{2,0},{4,6},{6,4},{8,10},{10,8},{12,14},{14,12},{16,18},{18,... | collective-permute-start | bytes 3194888 | tf_op jit(solution)/shard_map/ppermute | solution.py:320
  5.1 15.3 %collective-permute-start.4 = (f32[4,56,640]{2,1,0:T(8,128)S(1)}, f32[4,56,640]{2,1,0:T(8,128)S(1)}, u32[]{:S(2)}, u32[]{:S(2)}) collective-permute-start(f32[4,56,640]{2,1,0:T(8,128)S(1)} %get-tuple-element.34.refs_0_.outer_ref.scaled_ref), channel_id=1, source_target_pairs={{0,126},{2,4},{4,2},{6,8},{8,6},{10,12},{12,10},{14,16},{16,14},{1... | collective-permute-start | bytes 1720328 | tf_op jit(solution)/shard_map/ppermute | solution.py:319
  7.4 0.7 copy-start.8
  12.9 8.8 %copy-start.4 = (f32[4,104,640]{2,1,0:T(8,128)}, f32[4,104,640]{2,1,0:T(8,128)S(1)}, u32[]{:S(2)}) copy-start(f32[4,104,640]{2,1,0:T(8,128)S(1)} %get-tuple-element.40.inner_ref) | copy-start | bytes 3194884
  21.7 28.3 %copy-start.9 = (s32[26]{0:T(128)S(1)}, s32[26]{0:T(128)}, u32[]{:S(2)}) copy-start(s32[26]{0:T(128)} %param.7) | copy-start | bytes 316
  21.7 2.8 %collective-permute-start.5 = (f32[4,104,640]{2,1,0:T(8,128)S(1)}, f32[4,104,640]{2,1,0:T(8,128)S(1)}, u32[]{:S(2)}, u32[]{:S(2)}) collective-permute-start(f32[4,104,640]{2,1,0:T(8,128)S(1)} %get-tuple-element.40.inner_ref), channel_id=1, source_target_pairs={{0,2},{2,0},{4,6},{6,4},{8,10},{10,8},{12,14},{14,12},{16,18},{18,... | collective-permute-start | bytes 3194888 | tf_op jit(solution)/shard_map/ppermute | solution.py:330
  21.8 24.2 %collective-permute-start = (f32[4,48,640]{2,1,0:T(8,128)S(1)}, f32[4,48,640]{2,1,0:T(8,128)S(1)}, u32[]{:S(2)}, u32[]{:S(2)}) collective-permute-start(f32[4,48,640]{2,1,0:T(8,128)S(1)} %get-tuple-element.32.refs_1_.outer_ref.scaled_ref), channel_id=1, source_target_pairs={{0,126},{2,4},{4,2},{6,8},{8,6},{10,12},{12,10},{14,16},{16,14},{1... | collective-permute-start | bytes 1474568 | tf_op jit(solution)/shard_map/ppermute | solution.py:319
  24.5 1.0 %copy-start.6 = (f32[4,104,640]{2,1,0:T(8,128)}, f32[4,104,640]{2,1,0:T(8,128)S(1)}, u32[]{:S(2)}) copy-start(f32[4,104,640]{2,1,0:T(8,128)S(1)} %collective-permute-done.5.halo_ref) | copy-start | bytes 3194884
  25.5 31.6 %collective-permute-start.6 = (f32[4,56,640]{2,1,0:T(8,128)S(1)}, f32[4,56,640]{2,1,0:T(8,128)}, u32[]{:S(2)}, u32[]{:S(2)}) collective-permute-start(f32[4,56,640]{2,1,0:T(8,128)S(1)} %shard_map.71.refs_0_.outer_ref), channel_id=1, source_target_pairs={{0,126},{2,4},{4,2},{6,8},{8,6},{10,12},{12,10},{14,16},{16,14},{1... | collective-permute-start | bytes 1720328 | tf_op jit(solution)/shard_map/ppermute | solution.py:333
  47.2 12.4 %collective-permute-start.3 = (f32[4,32,640]{2,1,0:T(8,128)S(1)}, f32[4,32,640]{2,1,0:T(8,128)}, u32[]{:S(2)}, u32[]{:S(2)}) collective-permute-start(f32[4,32,640]{2,1,0:T(8,128)S(1)} %get-tuple-element.38.refs_1_.outer_ref), channel_id=1, source_target_pairs={{0,126},{2,4},{4,2},{6,8},{8,6},{10,12},{12,10},{14,16},{16,14},{1... | collective-permute-start | bytes 983048 | tf_op jit(solution)/shard_map/ppermute | solution.py:333
  49.8 11.6 %collective-permute-start.2 = (f32[4,16,640]{2,1,0:T(8,128)S(1)}, f32[4,16,640]{2,1,0:T(8,128)S(1)}, u32[]{:S(2)}, u32[]{:S(2)}) collective-permute-start(f32[4,16,640]{2,1,0:T(8,128)S(1)} %get-tuple-element.37.refs_2_.outer_ref), channel_id=1, source_target_pairs={{0,126},{2,4},{4,2},{6,8},{8,6},{10,12},{12,10},{14,16},{16,14},{1... | collective-permute-start | bytes 491528 | tf_op jit(solution)/shard_map/ppermute | solution.py:333
  50.3 1.2 %copy-start.5 = (f32[4,104,640]{2,1,0:T(8,128)S(1)}, f32[4,104,640]{2,1,0:T(8,128)}, u32[]{:S(2)}) copy-start(f32[4,104,640]{2,1,0:T(8,128)} %copy-done.4) | copy-start | bytes 3194884
  51.6 1.2 %copy-start.7 = (f32[4,104,640]{2,1,0:T(8,128)S(1)}, f32[4,104,640]{2,1,0:T(8,128)}, u32[]{:S(2)}) copy-start(f32[4,104,640]{2,1,0:T(8,128)} %copy-done.6) | copy-start | bytes 3194884
  61.9 5.3 %collective-permute-start.7 = (f32[168,128]{1,0:T(8,128)S(1)}, f32[168,128]{1,0:T(8,128)S(1)}, u32[]{:S(2)}, u32[]{:S(2)}) collective-permute-start(f32[168,128]{1,0:T(8,128)S(1)} %get-tuple-element.52.own_ref), channel_id=1, source_target_pairs={{0,1},{1,0},{2,3},{3,2},{4,5},{5,4},{6,7},{7,6},{8,9},{9,8},{10,11... | collective-permute-start | bytes 258056 | tf_op jit(solution)/shard_map/ppermute | solution.py:357

commit v10 on v8

--- a/solution.py
+++ b/solution.py
@@ -322,10 +322,14 @@
         smooth_inner_kernel, (half, edge, half, shape(rows, 128)), inner_halo, inner, fields, land_mask, coef, *outer
     )
     v_inner_halo = lax.ppermute(v_inner, "tile", with_mate)
+    weight_rows, outer_halo[-1] = lax.optimization_barrier((weight_rows, outer_halo[-1]))
+    weight_rows = lax.ppermute(weight_rows, "tile", with_mate)
     v_outer, v_outer_halo, places = [], [], []
     for base, sizes, halo, own in zip(bases, chunks, outer_halo, outer):
         outs = tuple(shape(REACH, size * SUB, lat) for size in sizes)
         values = call(partial(smooth_outer_kernel, base), outs, halo, own, edges, filled, coef)
+        if not v_outer:
+            weight_rows, *values = lax.optimization_barrier((weight_rows, *values))
         v_outer += values
         v_outer_halo += [lax.ppermute(value, "tile", with_neighbour) for value in values]
         places += [(base, base + sum(sizes[:n]), own) for n in range(len(sizes))]
@@ -334,6 +338,8 @@
     )
     inverses, earlier = [inverse_inner], []
     for n, (base, first, own) in enumerate(places):
+        if earlier:
+            v_outer_halo[n], earlier[-1] = lax.optimization_barrier((v_outer_halo[n], earlier[-1]))
         operands = v_outer_halo[n], v_outer[n], edges, own, weight_rows, coef
         part = shape(*v_outer[n].shape)
         if n < len(places) - 1:

time: 83.4 us -> 86.7 us (1.040)
  local copies, waits for them, and re-layouts: 3.48 us -> 5.71 us
  waiting for transfers between devices: 24.9 us -> 26.8 us
  blocking collectives: 15.6 us -> 17 us
  starting transfers between devices: 16.4 us -> 15.2 us
  Pallas kernels: 21.8 us -> 20.7 us
    ppermute x3, waiting for transfers between devices: 3.18 us -> 13 us  [body(): lax.ppermute(value, 'tile', with_neighbour)]
    ppermute x2, waiting for transfers between devices: 19.2 us -> 11.4 us  [body(): outer_halo = [lax.ppermute(part, 'tile', with_neighbour) for part in outer]]
    unnamed x12 -> x22, local copies, waits for them, and re-layouts: 3.23 us -> 5.46 us
    ppermute x3, starting transfers between devices: 5.39 us -> 3.6 us  [body(): lax.ppermute(value, 'tile', with_neighbour)]
    all_to_all x1, blocking collectives: 15.6 us -> 17 us  [body(): got = lax.all_to_all(payload, 'tile', split_axis=0, concat_axis=0)]
    pallas_call x10, Pallas kernels: 21.8 us -> 20.7 us  [call(): pl.pallas_call(kernel, out_shape=outs, in_specs=[VMEM] * len(args), out_s...]
  transfers between devices with their start and end apart: 8 -> 9, of which waited for: 5 -> 6; matrix products, arithmetic and copies ran while one was open for 0% -> 0% of each run, Pallas kernels for 22% -> 20%
where the time goes in v10:
time: 86.7 us; the launch traced here: 86.3 us
  waiting for transfers between devices  26.8 us (31%)
  Pallas kernels  20.7 us (24%)
  blocking collectives  17 us (20%)
  starting transfers between devices  15.2 us (18%)
  local copies, waits for them, and re-layouts  5.71 us (7%)
  between operations  0.92 us (1%)
    pallas_call x10, Pallas kernels, call(): pl.pallas_call(kernel, out_shape=outs, in_specs=[VMEM] * len(args), out_s...  20.7 us
    all_to_all x1, blocking collectives, body(): got = lax.all_to_all(payload, 'tile', split_axis=0, concat_axis=0)  17 us
    ppermute x3, waiting for transfers between devices, body(): lax.ppermute(value, 'tile', with_neighbour)  13 us
    ppermute x2, waiting for transfers between devices, body(): outer_halo = [lax.ppermute(part, 'tile', with_neighbour) for part in outer]  11.4 us
    unnamed x22, local copies, waits for them, and re-layouts  5.46 us
    ppermute x1, starting transfers between devices, body(): v_inner_halo = lax.ppermute(v_inner, 'tile', with_mate)  4.49 us
    ppermute x1, starting transfers between devices, body(): other = lax.ppermute(logs, 'mem', [(0, 1), (1, 0)])  3.76 us
    ppermute x3, starting transfers between devices, body(): lax.ppermute(value, 'tile', with_neighbour)  3.6 us
  transfers between devices with their start and end apart: 9, of which 6 were waited for; matrix products, arithmetic and copies ran while one was open for 0% of the time, Pallas kernels for 20%

profile of v10, /device:TPU:1, one launch (start us, length us, event | category | flops | bytes accessed | tf_op | source)
XLA Modules:
  0.0 86.3 jit_solution(14434143714846950454)
XLA Ops:
  0.6 0.0 copy-start
  0.6 0.9 %copy-done = f32[5,8,640]{2,1,0:T(8,128)S(1)} copy-done((f32[5,8,640]{2,1,0:T(8,128)S(1)}, f32[5,8,640]{2,1,0:T(8,128)}, u32[]{:S(2)}) %copy-start) | copy-done | bytes 102424
  1.5 0.0 copy-start.7
  1.5 1.6 %copy-done.7 = f32[26,4,8,640]{3,2,1,0:T(8,128)S(1)} copy-done((f32[26,4,8,640]{3,2,1,0:T(8,128)S(1)}, f32[26,4,8,640]{3,2,1,0:T(8,128)}, u32[]{:S(2)}) %copy-start.7) | copy-done | bytes 2129944
  3.1 0.0 copy-start.1
  3.1 0.0 copy-start.8
  3.1 0.5 shard_map.68
  3.6 0.0 copy-start.5
  3.6 1.5 %collective-permute-start.1 = (f32[4,104,640]{2,1,0:T(8,128)S(1)}, f32[4,104,640]{2,1,0:T(8,128)S(1)}, u32[]{:S(2)}, u32[]{:S(2)}) collective-permute-start(f32[4,104,640]{2,1,0:T(8,128)S(1)} %get-tuple-element.34.inner_ref.scaled_ref), channel_id=1, source_target_pairs={{0,2},{2,0},{4,6},{6,4},{8,10},{10,8},{12,14},{14,12},{16,18},{18,... | collective-permute-start | bytes 3194888 | tf_op jit(solution)/shard_map/ppermute | solution.py:320
  5.1 1.7 %collective-permute-start.5 = (f32[4,56,640]{2,1,0:T(8,128)S(1)}, f32[4,56,640]{2,1,0:T(8,128)S(1)}, u32[]{:S(2)}, u32[]{:S(2)}) collective-permute-start(f32[4,56,640]{2,1,0:T(8,128)S(1)} %get-tuple-element.35.refs_0_.outer_ref.scaled_ref), channel_id=1, source_target_pairs={{0,126},{2,4},{4,2},{6,8},{8,6},{10,12},{12,10},{14,16},{16,14},{1... | collective-permute-start | bytes 1720328 | tf_op jit(solution)/shard_map/ppermute | solution.py:319
  6.8 0.1 collective-permute-start
  6.9 0.5 collective-permute-done.1.halo_ref
  7.4 0.0 copy-done.1
  7.4 0.0 copy-done.8
  7.4 0.0 copy-start.9
  7.4 0.7 copy-done.9
  8.1 0.0 copy-start.10
  8.1 5.8 %shard_map.69 = (f32[4,104,640]{2,1,0:T(8,128)}, f32[6,104,640]{2,1,0:T(8,128)S(1)}, f32[4,104,640]{2,1,0:T(8,128)S(1)}, f32[104,128]{1,0:T(8,128)S(1)}) custom-call(f32[4,104,640]{2,1,0:T(8,128)S(1)} %collective-permute-done.1.halo_ref, f32[4,104,640]{2,1,0:T(8,128)S(1)} %get-tuple-element.34.inner_ref.scaled_ref, f32[832,640]{1,0:T(8,128)S(1)} %bitcast.4, ...), custom_call_target="tpu_custom_call" | custom-call | tf_op jit(solution)/shard_map/pallas_call | solution.py:289
  13.9 0.0 copy-done.5
  13.9 0.0 copy-start.2
  13.9 1.0 %copy-done.2 = f32[4,104,640]{2,1,0:T(8,128)} copy-done((f32[4,104,640]{2,1,0:T(8,128)}, f32[4,104,640]{2,1,0:T(8,128)S(1)}, u32[]{:S(2)}) %copy-start.2) | copy-done | bytes 1064984
  14.9 4.5 %collective-permute-start.7 = (f32[4,104,640]{2,1,0:T(8,128)}, f32[4,104,640]{2,1,0:T(8,128)}, u32[]{:S(2)}, u32[]{:S(2)}) collective-permute-start(f32[4,104,640]{2,1,0:T(8,128)} %get-tuple-element.42.inner_ref), channel_id=1, source_target_pairs={{0,2},{2,0},{4,6},{6,4},{8,10},{10,8},{12,14},{14,12},{16,18},{18,... | collective-permute-start | bytes 3194888 | tf_op jit(solution)/shard_map/ppermute | solution.py:324
  19.4 0.0 copy-done.10
  19.4 0.1 broadcast_in_dim.10
  19.5 0.1 broadcast_in_dim.11
  19.6 11.4 %collective-permute-done.halo_ref = f32[4,48,640]{2,1,0:T(8,128)} collective-permute-done((f32[4,48,640]{2,1,0:T(8,128)S(1)}, f32[4,48,640]{2,1,0:T(8,128)}, u32[]{:S(2)}, u32[]{:S(2)}) %collective-permute-start) | collective-permute-done | bytes 491552 | tf_op jit(solution)/shard_map/ppermute | solution.py:319
  31.0 0.1 broadcast_in_dim.12
  31.1 0.0 collective-permute-start.4
  31.1 0.0 collective-permute-done.5.halo_ref
  31.1 0.0 copy-start.3
  31.1 1.2 %copy-done.3 = f32[4,104,640]{2,1,0:T(8,128)S(1)} copy-done((f32[4,104,640]{2,1,0:T(8,128)S(1)}, f32[4,104,640]{2,1,0:T(8,128)}, u32[]{:S(2)}) %copy-start.3) | copy-done | bytes 1064984
  32.4 0.0 copy-start.4
  32.4 1.3 %shard_map.71.refs_0_.outer_ref = f32[4,56,640]{2,1,0:T(8,128)S(1)} custom-call(f32[4,56,640]{2,1,0:T(8,128)S(1)} %collective-permute-done.5.halo_ref, f32[4,56,640]{2,1,0:T(8,128)S(1)} %get-tuple-element.35.refs_0_.outer_ref.scaled_ref, f32[6,104,640]{2,1,0:T(8,128)S(1)} %get-tuple-element.36.edge_ref, f32[4,104,640]{2,1,0:T(8,128)S(1)} %copy-done.3, ...), custom_call_target="tpu_custom_call" | custom-call | tf_op jit(solution)/shard_map/pallas_call | solution.py:289
  33.7 0.0 copy-start.6
  33.7 0.0 collective-permute-done.4.weight_ref
  33.7 1.8 %collective-permute-start.6 = (f32[4,56,640]{2,1,0:T(8,128)S(1)}, f32[4,56,640]{2,1,0:T(8,128)S(1)}, u32[]{:S(2)}, u32[]{:S(2)}) collective-permute-start(f32[4,56,640]{2,1,0:T(8,128)S(1)} %shard_map.71.refs_0_.outer_ref), channel_id=1, source_target_pairs={{0,126},{2,4},{4,2},{6,8},{8,6},{10,12},{12,10},{14,16},{16,14},{1... | collective-permute-start | bytes 1720328 | tf_op jit(solution)/shard_map/ppermute | solution.py:334
  35.5 0.0 copy-done.4
  35.5 2.2 %shard_map.70 = (f32[4,32,640]{2,1,0:T(8,128)S(1)}, f32[4,16,640]{2,1,0:T(8,128)S(1)}) custom-call(f32[4,48,640]{2,1,0:T(8,128)} %collective-permute-done.halo_ref, f32[4,48,640]{2,1,0:T(8,128)S(1)} %get-tuple-element.32.refs_1_.outer_ref.scaled_ref, f32[6,104,640]{2,1,0:T(8,128)S(1)} %get-tuple-element.36.edge_ref, f32[4,104,640]{2,1,0:T(8,128)S(1)} %copy-done.4, ...), custom_call_target="tpu_custom_call" | custom-call | tf_op jit(solution)/shard_map/pallas_call | solution.py:289
  37.7 0.2 collective-permute-start.3
  37.9 1.6 %collective-permute-start.2 = (f32[4,16,640]{2,1,0:T(8,128)S(1)}, f32[4,16,640]{2,1,0:T(8,128)S(1)}, u32[]{:S(2)}, u32[]{:S(2)}) collective-permute-start(f32[4,16,640]{2,1,0:T(8,128)S(1)} %get-tuple-element.38.refs_2_.outer_ref), channel_id=1, source_target_pairs={{0,126},{2,4},{4,2},{6,8},{8,6},{10,12},{12,10},{14,16},{16,14},{1... | collective-permute-start | bytes 491528 | tf_op jit(solution)/shard_map/ppermute | solution.py:334
  39.6 0.0 collective-permute-done.7.halo_ref
  39.6 0.0 copy-done.6
  39.6 5.8 %shard_map.72 = (f32[4,104,640]{2,1,0:T(8,128)S(1)}, f32[6,104,640]{2,1,0:T(8,128)S(1)}, f32[4,8,640]{2,1,0:T(8,128)S(1)}) custom-call(f32[4,104,640]{2,1,0:T(8,128)} %collective-permute-done.7.halo_ref, f32[4,104,640]{2,1,0:T(8,128)} %get-tuple-element.42.inner_ref, f32[4,104,640]{2,1,0:T(8,128)S(1)} %copy-done.6, ...), custom_call_target="tpu_custom_call" | custom-call | tf_op jit(solution)/shard_map/pallas_call | solution.py:289
  45.4 8.2 %collective-permute-done.6.halo_ref = f32[4,56,640]{2,1,0:T(8,128)S(1)} collective-permute-done((f32[4,56,640]{2,1,0:T(8,128)S(1)}, f32[4,56,640]{2,1,0:T(8,128)S(1)}, u32[]{:S(2)}, u32[]{:S(2)}) %collective-permute-start.6) | collective-permute-done | bytes 573472 | tf_op jit(solution)/shard_map/ppermute | solution.py:334
  53.6 1.4 %shard_map.73 = (f32[4,56,640]{2,1,0:T(8,128)S(1)}, f32[4,8,640]{2,1,0:T(8,128)S(1)}) custom-call(f32[4,56,640]{2,1,0:T(8,128)S(1)} %collective-permute-done.6.halo_ref, f32[4,56,640]{2,1,0:T(8,128)S(1)} %shard_map.71.refs_0_.outer_ref, f32[6,104,640]{2,1,0:T(8,128)S(1)} %get-tuple-element.44.edge_ref, ...), custom_call_target="tpu_custom_call" | custom-call | tf_op jit(solution)/shard_map/pallas_call | solution.py:289
  55.0 3.8 %collective-permute-done.3.halo_ref = f32[4,32,640]{2,1,0:T(8,128)S(1)} collective-permute-done((f32[4,32,640]{2,1,0:T(8,128)S(1)}, f32[4,32,640]{2,1,0:T(8,128)S(1)}, u32[]{:S(2)}, u32[]{:S(2)}) %collective-permute-start.3) | collective-permute-done | bytes 327712 | tf_op jit(solution)/shard_map/ppermute | solution.py:334
  58.8 0.8 shard_map.74
  59.6 0.9 %collective-permute-done.2.halo_ref = f32[4,16,640]{2,1,0:T(8,128)S(1)} collective-permute-done((f32[4,16,640]{2,1,0:T(8,128)S(1)}, f32[4,16,640]{2,1,0:T(8,128)S(1)}, u32[]{:S(2)}, u32[]{:S(2)}) %collective-permute-start.2) | collective-permute-done | bytes 163872 | tf_op jit(solution)/shard_map/ppermute | solution.py:334
  60.6 0.5 shard_map.75
  61.0 3.8 %collective-permute-start.8 = (f32[168,128]{1,0:T(8,128)S(1)}, f32[168,128]{1,0:T(8,128)S(1)}, u32[]{:S(2)}, u32[]{:S(2)}) collective-permute-start(f32[168,128]{1,0:T(8,128)S(1)} %get-tuple-element.52.own_ref), channel_id=1, source_target_pairs={{0,1},{1,0},{2,3},{3,2},{4,5},{5,4},{6,7},{7,6},{8,9},{9,8},{10,11... | collective-permute-start | bytes 258056 | tf_op jit(solution)/shard_map/ppermute | solution.py:358
  64.8 1.9 %collective-permute-done.8.other_ref = f32[168,128]{1,0:T(8,128)S(1)} collective-permute-done((f32[168,128]{1,0:T(8,128)S(1)}, f32[168,128]{1,0:T(8,128)S(1)}, u32[]{:S(2)}, u32[]{:S(2)}) %collective-permute-start.8) | collective-permute-done | bytes 86048 | tf_op jit(solution)/shard_map/ppermute | solution.py:358
  66.7 0.1 shard_map.76
  66.8 17.0 %all_to_all.5.got_ref = f32[64,1,128]{2,1,0:T(1,128)S(1)} all-to-all(f32[64,1,128]{2,1,0:T(1,128)S(1)} %get-tuple-element.54), channel_id=1, replica_groups=mesh['tile'=64,'mem'=2] {'tile'}, dimensions={0} | all-to-all | bytes 65536 | tf_op jit(solution)/shard_map/all_to_all | solution.py:360
  83.8 2.3 %shard_map.77 = (f32[4,8,640]{2,1,0:T(8,128)}, f32[832,640]{1,0:T(8,128)}) custom-call(f32[64,1,128]{2,1,0:T(1,128)S(1)} %all_to_all.5.got_ref, f32[4,8,640]{2,1,0:T(8,128)S(1)} %get-tuple-element.55.merged_ref, f32[4,104,640]{2,1,0:T(8,128)S(1)} %get-tuple-element.56.inner_ref, f32[4,56,640]{2,1,0:T(8,128)S(1)} %get-tuple-element.57.refs_0_, ...), custom_call_target="tpu_custom_call" | custom-call | tf_op jit(solution)/shard_map/pallas_call | solution.py:289
  (1 shorter events, 0.0 us)
Async XLA Ops:
  0.6 0.9 %copy-start = (f32[5,8,640]{2,1,0:T(8,128)S(1)}, f32[5,8,640]{2,1,0:T(8,128)}, u32[]{:S(2)}) copy-start(f32[5,8,640]{2,1,0:T(8,128)} %constant.2.clone.coef_ref) | copy-start | bytes 307204
  1.5 1.6 %copy-start.7 = (f32[26,4,8,640]{3,2,1,0:T(8,128)S(1)}, f32[26,4,8,640]{3,2,1,0:T(8,128)}, u32[]{:S(2)}) copy-start(f32[26,4,8,640]{3,2,1,0:T(8,128)} %param.6) | copy-start | bytes 6389764
  3.1 4.3 %copy-start.1 = (f32[5,8,640]{2,1,0:T(8,128)S(1)}, f32[5,8,640]{2,1,0:T(8,128)}, u32[]{:S(2)}) copy-start(f32[5,8,640]{2,1,0:T(8,128)} %constant.2.clone.coef_ref) | copy-start | bytes 307204
  3.1 4.3 %copy-start.8 = (f32[26,4,8,640]{3,2,1,0:T(8,128)S(1)}, f32[26,4,8,640]{3,2,1,0:T(8,128)}, u32[]{:S(2)}) copy-start(f32[26,4,8,640]{3,2,1,0:T(8,128)} %param.5) | copy-start | bytes 6389764
  3.6 10.3 %copy-start.5 = (f32[4,104,640]{2,1,0:T(8,128)}, f32[4,104,640]{2,1,0:T(8,128)S(1)}, u32[]{:S(2)}) copy-start(f32[4,104,640]{2,1,0:T(8,128)S(1)} %get-tuple-element.34.inner_ref.scaled_ref) | copy-start | bytes 3194884
  3.6 3.8 %collective-permute-start.1 = (f32[4,104,640]{2,1,0:T(8,128)S(1)}, f32[4,104,640]{2,1,0:T(8,128)S(1)}, u32[]{:S(2)}, u32[]{:S(2)}) collective-permute-start(f32[4,104,640]{2,1,0:T(8,128)S(1)} %get-tuple-element.34.inner_ref.scaled_ref), channel_id=1, source_target_pairs={{0,2},{2,0},{4,6},{6,4},{8,10},{10,8},{12,14},{14,12},{16,18},{18,... | collective-permute-start | bytes 3194888 | tf_op jit(solution)/shard_map/ppermute | solution.py:320
  5.1 26.0 %collective-permute-start.5 = (f32[4,56,640]{2,1,0:T(8,128)S(1)}, f32[4,56,640]{2,1,0:T(8,128)S(1)}, u32[]{:S(2)}, u32[]{:S(2)}) collective-permute-start(f32[4,56,640]{2,1,0:T(8,128)S(1)} %get-tuple-element.35.refs_0_.outer_ref.scaled_ref), channel_id=1, source_target_pairs={{0,126},{2,4},{4,2},{6,8},{8,6},{10,12},{12,10},{14,16},{16,14},{1... | collective-permute-start | bytes 1720328 | tf_op jit(solution)/shard_map/ppermute | solution.py:319
  6.8 24.2 %collective-permute-start = (f32[4,48,640]{2,1,0:T(8,128)S(1)}, f32[4,48,640]{2,1,0:T(8,128)}, u32[]{:S(2)}, u32[]{:S(2)}) collective-permute-start(f32[4,48,640]{2,1,0:T(8,128)S(1)} %get-tuple-element.32.refs_1_.outer_ref.scaled_ref), channel_id=1, source_target_pairs={{0,126},{2,4},{4,2},{6,8},{8,6},{10,12},{12,10},{14,16},{16,14},{1... | collective-permute-start | bytes 1474568 | tf_op jit(solution)/shard_map/ppermute | solution.py:319
  7.4 0.7 copy-start.9
  8.1 11.3 %copy-start.10 = (s32[26]{0:T(128)S(1)}, s32[26]{0:T(128)}, u32[]{:S(2)}) copy-start(s32[26]{0:T(128)} %param.7) | copy-start | bytes 316
  13.9 1.0 %copy-start.2 = (f32[4,104,640]{2,1,0:T(8,128)}, f32[4,104,640]{2,1,0:T(8,128)S(1)}, u32[]{:S(2)}) copy-start(f32[4,104,640]{2,1,0:T(8,128)S(1)} %get-tuple-element.37.filled_ref) | copy-start | bytes 3194884
  14.9 24.6 %collective-permute-start.7 = (f32[4,104,640]{2,1,0:T(8,128)}, f32[4,104,640]{2,1,0:T(8,128)}, u32[]{:S(2)}, u32[]{:S(2)}) collective-permute-start(f32[4,104,640]{2,1,0:T(8,128)} %get-tuple-element.42.inner_ref), channel_id=1, source_target_pairs={{0,2},{2,0},{4,6},{6,4},{8,10},{10,8},{12,14},{14,12},{16,18},{18,... | collective-permute-start | bytes 3194888 | tf_op jit(solution)/shard_map/ppermute | solution.py:324
  31.1 2.7 %collective-permute-start.4 = (f32[104,128]{1,0:T(8,128)S(1)}, f32[104,128]{1,0:T(8,128)S(1)}, u32[]{:S(2)}, u32[]{:S(2)}) collective-permute-start(f32[104,128]{1,0:T(8,128)S(1)} %broadcast_in_dim.12), channel_id=1, source_target_pairs={{0,2},{2,0},{4,6},{6,4},{8,10},{10,8},{12,14},{14,12},{16,18},{18,... | collective-permute-start | bytes 159752 | tf_op jit(solution)/shard_map/ppermute | solution.py:326
  31.1 1.2 %copy-start.3 = (f32[4,104,640]{2,1,0:T(8,128)S(1)}, f32[4,104,640]{2,1,0:T(8,128)}, u32[]{:S(2)}) copy-start(f32[4,104,640]{2,1,0:T(8,128)} %copy-done.2) | copy-start | bytes 3194884
  32.4 3.2 %copy-start.4 = (f32[4,104,640]{2,1,0:T(8,128)S(1)}, f32[4,104,640]{2,1,0:T(8,128)}, u32[]{:S(2)}) copy-start(f32[4,104,640]{2,1,0:T(8,128)} %copy-done.2) | copy-start | bytes 3194884
  33.7 5.8 %copy-start.6 = (f32[4,104,640]{2,1,0:T(8,128)S(1)}, f32[4,104,640]{2,1,0:T(8,128)}, u32[]{:S(2)}) copy-start(f32[4,104,640]{2,1,0:T(8,128)} %copy-done.5) | copy-start | bytes 3194884
  33.7 19.8 %collective-permute-start.6 = (f32[4,56,640]{2,1,0:T(8,128)S(1)}, f32[4,56,640]{2,1,0:T(8,128)S(1)}, u32[]{:S(2)}, u32[]{:S(2)}) collective-permute-start(f32[4,56,640]{2,1,0:T(8,128)S(1)} %shard_map.71.refs_0_.outer_ref), channel_id=1, source_target_pairs={{0,126},{2,4},{4,2},{6,8},{8,6},{10,12},{12,10},{14,16},{16,14},{1... | collective-permute-start | bytes 1720328 | tf_op jit(solution)/shard_map/ppermute | solution.py:334
  37.7 21.1 %collective-permute-start.3 = (f32[4,32,640]{2,1,0:T(8,128)S(1)}, f32[4,32,640]{2,1,0:T(8,128)S(1)}, u32[]{:S(2)}, u32[]{:S(2)}) collective-permute-start(f32[4,32,640]{2,1,0:T(8,128)S(1)} %get-tuple-element.39.refs_1_.outer_ref), channel_id=1, source_target_pairs={{0,126},{2,4},{4,2},{6,8},{8,6},{10,12},{12,10},{14,16},{16,14},{1... | collective-permute-start | bytes 983048 | tf_op jit(solution)/shard_map/ppermute | solution.py:334
  37.9 22.6 %collective-permute-start.2 = (f32[4,16,640]{2,1,0:T(8,128)S(1)}, f32[4,16,640]{2,1,0:T(8,128)S(1)}, u32[]{:S(2)}, u32[]{:S(2)}) collective-permute-start(f32[4,16,640]{2,1,0:T(8,128)S(1)} %get-tuple-element.38.refs_2_.outer_ref), channel_id=1, source_target_pairs={{0,126},{2,4},{4,2},{6,8},{8,6},{10,12},{12,10},{14,16},{16,14},{1... | collective-permute-start | bytes 491528 | tf_op jit(solution)/shard_map/ppermute | solution.py:334
  61.0 5.6 %collective-permute-start.8 = (f32[168,128]{1,0:T(8,128)S(1)}, f32[168,128]{1,0:T(8,128)S(1)}, u32[]{:S(2)}, u32[]{:S(2)}) collective-permute-start(f32[168,128]{1,0:T(8,128)S(1)} %get-tuple-element.52.own_ref), channel_id=1, source_target_pairs={{0,1},{1,0},{2,3},{3,2},{4,5},{5,4},{6,7},{7,6},{8,9},{9,8},{10,11... | collective-permute-start | bytes 258056 | tf_op jit(solution)/shard_map/ppermute | solution.py:358

commit v11 on v8

--- a/solution.py
+++ b/solution.py
@@ -30,7 +30,7 @@
     return np.ascontiguousarray(np.broadcast_to(rows[:, None, :], (5, SUB, lat_cells)))
 
 
-def params(mib=20):
+def params(mib=12):
     return pltpu.CompilerParams(vmem_limit_bytes=mib * 2**20)
 
 
@@ -334,6 +334,8 @@
     )
     inverses, earlier = [inverse_inner], []
     for n, (base, first, own) in enumerate(places):
+        if earlier:
+            v_outer_halo[n], earlier[-1] = lax.optimization_barrier((v_outer_halo[n], earlier[-1]))
         operands = v_outer_halo[n], v_outer[n], edges, own, weight_rows, coef
         part = shape(*v_outer[n].shape)
         if n < len(places) - 1:

time: 83.4 us -> 82.3 us (0.987)
  waiting for transfers between devices: 24.9 us -> 22.4 us
  blocking collectives: 15.6 us -> 16.9 us
    ppermute x3, waiting for transfers between devices: 3.18 us -> 0.71 us  [body(): lax.ppermute(value, 'tile', with_neighbour)]
    all_to_all x1, blocking collectives: 15.6 us -> 16.9 us  [body(): got = lax.all_to_all(payload, 'tile', split_axis=0, concat_axis=0)]
where the time goes in v11:
time: 82.3 us; the launch traced here: 81.9 us
  waiting for transfers between devices  22.4 us (27%)
  Pallas kernels  21.8 us (26%)
  blocking collectives  16.9 us (21%)
  starting transfers between devices  16.4 us (20%)
  local copies, waits for them, and re-layouts  3.48 us (4%)
  between operations  0.9 us (1%)
    pallas_call x10, Pallas kernels, call(): pl.pallas_call(kernel, out_shape=outs, in_specs=[VMEM] * len(args), out_s...  21.8 us
    ppermute x2, waiting for transfers between devices, body(): outer_halo = [lax.ppermute(part, 'tile', with_neighbour) for part in outer]  19.2 us
    all_to_all x1, blocking collectives, body(): got = lax.all_to_all(payload, 'tile', split_axis=0, concat_axis=0)  16.9 us
    ppermute x3, starting transfers between devices, body(): lax.ppermute(value, 'tile', with_neighbour)  5.39 us
    ppermute x1, starting transfers between devices, body(): v_inner_halo = lax.ppermute(v_inner, 'tile', with_mate)  4.46 us
    ppermute x1, starting transfers between devices, body(): other = lax.ppermute(logs, 'mem', [(0, 1), (1, 0)])  3.3 us
    unnamed x12, local copies, waits for them, and re-layouts  3.23 us
    ppermute x1, waiting for transfers between devices, body(): other = lax.ppermute(logs, 'mem', [(0, 1), (1, 0)])  1.88 us
  transfers between devices with their start and end apart: 8, of which 5 were waited for; matrix products, arithmetic and copies ran while one was open for 0% of the time, Pallas kernels for 22%

profile of v11, /device:TPU:1, one launch (start us, length us, event | category | flops | bytes accessed | tf_op | source)
XLA Modules:
  0.0 81.9 jit_solution(13716615306407996091)
XLA Ops:
  0.6 0.0 copy-start
  0.6 0.9 %copy-done = f32[5,8,640]{2,1,0:T(8,128)S(1)} copy-done((f32[5,8,640]{2,1,0:T(8,128)S(1)}, f32[5,8,640]{2,1,0:T(8,128)}, u32[]{:S(2)}) %copy-start) | copy-done | bytes 102424
  1.5 0.0 copy-start.2
  1.5 1.6 %copy-done.2 = f32[26,4,8,640]{3,2,1,0:T(8,128)S(1)} copy-done((f32[26,4,8,640]{3,2,1,0:T(8,128)S(1)}, f32[26,4,8,640]{3,2,1,0:T(8,128)}, u32[]{:S(2)}) %copy-start.2) | copy-done | bytes 2129944
  3.1 0.0 copy-start.1
  3.1 0.0 copy-start.3
  3.1 0.5 shard_map.68
  3.6 1.5 %collective-permute-start.1 = (f32[4,104,640]{2,1,0:T(8,128)S(1)}, f32[4,104,640]{2,1,0:T(8,128)S(1)}, u32[]{:S(2)}, u32[]{:S(2)}) collective-permute-start(f32[4,104,640]{2,1,0:T(8,128)S(1)} %get-tuple-element.29.inner_ref.scaled_ref), channel_id=1, source_target_pairs={{0,2},{2,0},{4,6},{6,4},{8,10},{10,8},{12,14},{14,12},{16,18},{18,... | collective-permute-start | bytes 3194888 | tf_op jit(solution)/shard_map/ppermute | solution.py:320
  5.1 1.7 %collective-permute-start.4 = (f32[4,56,640]{2,1,0:T(8,128)S(1)}, f32[4,56,640]{2,1,0:T(8,128)S(1)}, u32[]{:S(2)}, u32[]{:S(2)}) collective-permute-start(f32[4,56,640]{2,1,0:T(8,128)S(1)} %get-tuple-element.30.refs_0_.outer_ref.scaled_ref), channel_id=1, source_target_pairs={{0,126},{2,4},{4,2},{6,8},{8,6},{10,12},{12,10},{14,16},{16,14},{1... | collective-permute-start | bytes 1720328 | tf_op jit(solution)/shard_map/ppermute | solution.py:319
  6.8 0.6 collective-permute-done.1.halo_ref
  7.4 0.0 copy-done.1
  7.4 0.0 copy-done.3
  7.4 0.0 copy-start.4
  7.4 0.7 copy-done.4
  8.1 5.8 %shard_map.69 = (f32[4,104,640]{2,1,0:T(8,128)}, f32[6,104,640]{2,1,0:T(8,128)S(1)}, f32[4,104,640]{2,1,0:T(8,128)S(1)}, f32[104,128]{1,0:T(8,128)S(1)}) custom-call(f32[4,104,640]{2,1,0:T(8,128)S(1)} %collective-permute-done.1.halo_ref, f32[4,104,640]{2,1,0:T(8,128)S(1)} %get-tuple-element.29.inner_ref.scaled_ref, f32[832,640]{1,0:T(8,128)S(1)} %bitcast.4, ...), custom_call_target="tpu_custom_call" | custom-call | tf_op jit(solution)/shard_map/pallas_call | solution.py:289
  13.9 4.5 %collective-permute-start.6 = (f32[4,104,640]{2,1,0:T(8,128)}, f32[4,104,640]{2,1,0:T(8,128)}, u32[]{:S(2)}, u32[]{:S(2)}) collective-permute-start(f32[4,104,640]{2,1,0:T(8,128)} %get-tuple-element.35.inner_ref), channel_id=1, source_target_pairs={{0,2},{2,0},{4,6},{6,4},{8,10},{10,8},{12,14},{14,12},{16,18},{18,... | collective-permute-start | bytes 3194888 | tf_op jit(solution)/shard_map/ppermute | solution.py:324
  18.4 0.0 collective-permute-start
  18.4 17.9 %collective-permute-done.4.halo_ref = f32[4,56,640]{2,1,0:T(8,128)S(1)} collective-permute-done((f32[4,56,640]{2,1,0:T(8,128)S(1)}, f32[4,56,640]{2,1,0:T(8,128)S(1)}, u32[]{:S(2)}, u32[]{:S(2)}) %collective-permute-start.4) | collective-permute-done | bytes 573472 | tf_op jit(solution)/shard_map/ppermute | solution.py:319
  36.3 1.3 %shard_map.71.refs_0_.outer_ref = f32[4,56,640]{2,1,0:T(8,128)S(1)} custom-call(f32[4,56,640]{2,1,0:T(8,128)S(1)} %collective-permute-done.4.halo_ref, f32[4,56,640]{2,1,0:T(8,128)S(1)} %get-tuple-element.30.refs_0_.outer_ref.scaled_ref, f32[6,104,640]{2,1,0:T(8,128)S(1)} %get-tuple-element.31.edge_ref, f32[4,104,640]{2,1,0:T(8,128)S(1)} %get-tuple-element.32.filled_ref, ...), custom_call_target="tpu_custom_call" | custom-call | tf_op jit(solution)/shard_map/pallas_call | solution.py:289
  37.6 0.0 copy-start.5
  37.6 2.6 %collective-permute-start.5 = (f32[4,56,640]{2,1,0:T(8,128)S(1)}, f32[4,56,640]{2,1,0:T(8,128)}, u32[]{:S(2)}, u32[]{:S(2)}) collective-permute-start(f32[4,56,640]{2,1,0:T(8,128)S(1)} %shard_map.71.refs_0_.outer_ref), channel_id=1, source_target_pairs={{0,126},{2,4},{4,2},{6,8},{8,6},{10,12},{12,10},{14,16},{16,14},{1... | collective-permute-start | bytes 1720328 | tf_op jit(solution)/shard_map/ppermute | solution.py:330
  40.2 1.4 %collective-permute-done.halo_ref = f32[4,48,640]{2,1,0:T(8,128)S(1)} collective-permute-done((f32[4,48,640]{2,1,0:T(8,128)S(1)}, f32[4,48,640]{2,1,0:T(8,128)S(1)}, u32[]{:S(2)}, u32[]{:S(2)}) %collective-permute-start) | collective-permute-done | bytes 491552 | tf_op jit(solution)/shard_map/ppermute | solution.py:319
  41.5 1.2 %shard_map.70 = (f32[4,32,640]{2,1,0:T(8,128)S(1)}, f32[4,16,640]{2,1,0:T(8,128)S(1)}) custom-call(f32[4,48,640]{2,1,0:T(8,128)S(1)} %collective-permute-done.halo_ref, f32[4,48,640]{2,1,0:T(8,128)S(1)} %get-tuple-element.28.refs_1_.outer_ref.scaled_ref, f32[6,104,640]{2,1,0:T(8,128)S(1)} %get-tuple-element.31.edge_ref, ...), custom_call_target="tpu_custom_call" | custom-call | tf_op jit(solution)/shard_map/pallas_call | solution.py:289
  42.7 2.6 %collective-permute-start.3 = (f32[4,32,640]{2,1,0:T(8,128)S(1)}, f32[4,32,640]{2,1,0:T(8,128)}, u32[]{:S(2)}, u32[]{:S(2)}) collective-permute-start(f32[4,32,640]{2,1,0:T(8,128)S(1)} %get-tuple-element.34.refs_1_.outer_ref), channel_id=1, source_target_pairs={{0,126},{2,4},{4,2},{6,8},{8,6},{10,12},{12,10},{14,16},{16,14},{1... | collective-permute-start | bytes 983048 | tf_op jit(solution)/shard_map/ppermute | solution.py:330
  45.3 0.3 collective-permute-start.2
  45.5 0.0 copy-done.5
  45.5 0.1 broadcast_in_dim.10
  45.6 0.1 broadcast_in_dim.11
  45.7 0.0 collective-permute-done.6.halo_ref
  45.7 0.1 broadcast_in_dim.12.weight_ref
  45.8 5.9 %shard_map.72 = (f32[4,104,640]{2,1,0:T(8,128)S(1)}, f32[6,104,640]{2,1,0:T(8,128)S(1)}, f32[4,8,640]{2,1,0:T(8,128)S(1)}) custom-call(f32[4,104,640]{2,1,0:T(8,128)} %collective-permute-done.6.halo_ref, f32[4,104,640]{2,1,0:T(8,128)} %get-tuple-element.35.inner_ref, f32[4,104,640]{2,1,0:T(8,128)S(1)} %get-tuple-element.29.inner_ref.scaled_ref, ...), custom_call_target="tpu_custom_call" | custom-call | tf_op jit(solution)/shard_map/pallas_call | solution.py:289
  51.7 0.0 collective-permute-done.5.halo_ref
  51.7 2.5 %shard_map.73 = (f32[4,56,640]{2,1,0:T(8,128)S(1)}, f32[4,8,640]{2,1,0:T(8,128)S(1)}) custom-call(f32[4,56,640]{2,1,0:T(8,128)} %collective-permute-done.5.halo_ref, f32[4,56,640]{2,1,0:T(8,128)S(1)} %shard_map.71.refs_0_.outer_ref, f32[6,104,640]{2,1,0:T(8,128)S(1)} %get-tuple-element.36.edge_ref, ...), custom_call_target="tpu_custom_call" | custom-call | tf_op jit(solution)/shard_map/pallas_call | solution.py:289
  54.2 0.7 collective-permute-done.3.halo_ref
  54.9 1.8 %shard_map.74 = (f32[4,32,640]{2,1,0:T(8,128)S(1)}, f32[4,8,640]{2,1,0:T(8,128)S(1)}) custom-call(f32[4,32,640]{2,1,0:T(8,128)} %collective-permute-done.3.halo_ref, f32[4,32,640]{2,1,0:T(8,128)S(1)} %get-tuple-element.34.refs_1_.outer_ref, f32[6,104,640]{2,1,0:T(8,128)S(1)} %get-tuple-element.36.edge_ref, ...), custom_call_target="tpu_custom_call" | custom-call | tf_op jit(solution)/shard_map/pallas_call | solution.py:289
  56.7 0.0 collective-permute-done.2.halo_ref
  56.7 0.5 shard_map.75
  57.2 3.3 %collective-permute-start.7 = (f32[168,128]{1,0:T(8,128)S(1)}, f32[168,128]{1,0:T(8,128)S(1)}, u32[]{:S(2)}, u32[]{:S(2)}) collective-permute-start(f32[168,128]{1,0:T(8,128)S(1)} %get-tuple-element.44.own_ref), channel_id=1, source_target_pairs={{0,1},{1,0},{2,3},{3,2},{4,5},{5,4},{6,7},{7,6},{8,9},{9,8},{10,11... | collective-permute-start | bytes 258056 | tf_op jit(solution)/shard_map/ppermute | solution.py:354
  60.5 1.9 %collective-permute-done.7.other_ref = f32[168,128]{1,0:T(8,128)S(1)} collective-permute-done((f32[168,128]{1,0:T(8,128)S(1)}, f32[168,128]{1,0:T(8,128)S(1)}, u32[]{:S(2)}, u32[]{:S(2)}) %collective-permute-start.7) | collective-permute-done | bytes 86048 | tf_op jit(solution)/shard_map/ppermute | solution.py:354
  62.3 0.1 shard_map.76
  62.5 16.9 %all_to_all.5.got_ref = f32[64,1,128]{2,1,0:T(1,128)S(1)} all-to-all(f32[64,1,128]{2,1,0:T(1,128)S(1)} %get-tuple-element.46), channel_id=1, replica_groups=mesh['tile'=64,'mem'=2] {'tile'}, dimensions={0} | all-to-all | bytes 65536 | tf_op jit(solution)/shard_map/all_to_all | solution.py:356
  79.4 2.3 %shard_map.77 = (f32[4,8,640]{2,1,0:T(8,128)}, f32[832,640]{1,0:T(8,128)}) custom-call(f32[64,1,128]{2,1,0:T(1,128)S(1)} %all_to_all.5.got_ref, f32[4,8,640]{2,1,0:T(8,128)S(1)} %get-tuple-element.47.merged_ref, f32[4,104,640]{2,1,0:T(8,128)S(1)} %get-tuple-element.48.inner_ref, f32[4,56,640]{2,1,0:T(8,128)S(1)} %get-tuple-element.49.refs_0_, ...), custom_call_target="tpu_custom_call" | custom-call | tf_op jit(solution)/shard_map/pallas_call | solution.py:289
  (1 shorter events, 0.0 us)
Async XLA Ops:
  0.6 0.9 %copy-start = (f32[5,8,640]{2,1,0:T(8,128)S(1)}, f32[5,8,640]{2,1,0:T(8,128)}, u32[]{:S(2)}) copy-start(f32[5,8,640]{2,1,0:T(8,128)} %constant.2.clone.coef_ref) | copy-start | bytes 307204
  1.5 1.6 %copy-start.2 = (f32[26,4,8,640]{3,2,1,0:T(8,128)S(1)}, f32[26,4,8,640]{3,2,1,0:T(8,128)}, u32[]{:S(2)}) copy-start(f32[26,4,8,640]{3,2,1,0:T(8,128)} %param.6) | copy-start | bytes 6389764
  3.1 4.3 %copy-start.1 = (f32[5,8,640]{2,1,0:T(8,128)S(1)}, f32[5,8,640]{2,1,0:T(8,128)}, u32[]{:S(2)}) copy-start(f32[5,8,640]{2,1,0:T(8,128)} %constant.2.clone.coef_ref) | copy-start | bytes 307204
  3.1 4.3 %copy-start.3 = (f32[26,4,8,640]{3,2,1,0:T(8,128)S(1)}, f32[26,4,8,640]{3,2,1,0:T(8,128)}, u32[]{:S(2)}) copy-start(f32[26,4,8,640]{3,2,1,0:T(8,128)} %param.5) | copy-start | bytes 6389764
  3.6 3.8 %collective-permute-start.1 = (f32[4,104,640]{2,1,0:T(8,128)S(1)}, f32[4,104,640]{2,1,0:T(8,128)S(1)}, u32[]{:S(2)}, u32[]{:S(2)}) collective-permute-start(f32[4,104,640]{2,1,0:T(8,128)S(1)} %get-tuple-element.29.inner_ref.scaled_ref), channel_id=1, source_target_pairs={{0,2},{2,0},{4,6},{6,4},{8,10},{10,8},{12,14},{14,12},{16,18},{18,... | collective-permute-start | bytes 3194888 | tf_op jit(solution)/shard_map/ppermute | solution.py:320
  5.1 31.2 %collective-permute-start.4 = (f32[4,56,640]{2,1,0:T(8,128)S(1)}, f32[4,56,640]{2,1,0:T(8,128)S(1)}, u32[]{:S(2)}, u32[]{:S(2)}) collective-permute-start(f32[4,56,640]{2,1,0:T(8,128)S(1)} %get-tuple-element.30.refs_0_.outer_ref.scaled_ref), channel_id=1, source_target_pairs={{0,126},{2,4},{4,2},{6,8},{8,6},{10,12},{12,10},{14,16},{16,14},{1... | collective-permute-start | bytes 1720328 | tf_op jit(solution)/shard_map/ppermute | solution.py:319
  7.4 0.7 copy-start.4
  13.9 31.8 %collective-permute-start.6 = (f32[4,104,640]{2,1,0:T(8,128)}, f32[4,104,640]{2,1,0:T(8,128)}, u32[]{:S(2)}, u32[]{:S(2)}) collective-permute-start(f32[4,104,640]{2,1,0:T(8,128)} %get-tuple-element.35.inner_ref), channel_id=1, source_target_pairs={{0,2},{2,0},{4,6},{6,4},{8,10},{10,8},{12,14},{14,12},{16,18},{18,... | collective-permute-start | bytes 3194888 | tf_op jit(solution)/shard_map/ppermute | solution.py:324
  18.4 23.2 %collective-permute-start = (f32[4,48,640]{2,1,0:T(8,128)S(1)}, f32[4,48,640]{2,1,0:T(8,128)S(1)}, u32[]{:S(2)}, u32[]{:S(2)}) collective-permute-start(f32[4,48,640]{2,1,0:T(8,128)S(1)} %get-tuple-element.28.refs_1_.outer_ref.scaled_ref), channel_id=1, source_target_pairs={{0,126},{2,4},{4,2},{6,8},{8,6},{10,12},{12,10},{14,16},{16,14},{1... | collective-permute-start | bytes 1474568 | tf_op jit(solution)/shard_map/ppermute | solution.py:319
  37.6 7.9 %copy-start.5 = (s32[26]{0:T(128)S(1)}, s32[26]{0:T(128)}, u32[]{:S(2)}) copy-start(s32[26]{0:T(128)} %param.7) | copy-start | bytes 316
  37.6 14.1 %collective-permute-start.5 = (f32[4,56,640]{2,1,0:T(8,128)S(1)}, f32[4,56,640]{2,1,0:T(8,128)}, u32[]{:S(2)}, u32[]{:S(2)}) collective-permute-start(f32[4,56,640]{2,1,0:T(8,128)S(1)} %shard_map.71.refs_0_.outer_ref), channel_id=1, source_target_pairs={{0,126},{2,4},{4,2},{6,8},{8,6},{10,12},{12,10},{14,16},{16,14},{1... | collective-permute-start | bytes 1720328 | tf_op jit(solution)/shard_map/ppermute | solution.py:330
  42.7 12.2 %collective-permute-start.3 = (f32[4,32,640]{2,1,0:T(8,128)S(1)}, f32[4,32,640]{2,1,0:T(8,128)}, u32[]{:S(2)}, u32[]{:S(2)}) collective-permute-start(f32[4,32,640]{2,1,0:T(8,128)S(1)} %get-tuple-element.34.refs_1_.outer_ref), channel_id=1, source_target_pairs={{0,126},{2,4},{4,2},{6,8},{8,6},{10,12},{12,10},{14,16},{16,14},{1... | collective-permute-start | bytes 983048 | tf_op jit(solution)/shard_map/ppermute | solution.py:330
  45.3 11.4 %collective-permute-start.2 = (f32[4,16,640]{2,1,0:T(8,128)S(1)}, f32[4,16,640]{2,1,0:T(8,128)S(1)}, u32[]{:S(2)}, u32[]{:S(2)}) collective-permute-start(f32[4,16,640]{2,1,0:T(8,128)S(1)} %get-tuple-element.33.refs_2_.outer_ref), channel_id=1, source_target_pairs={{0,126},{2,4},{4,2},{6,8},{8,6},{10,12},{12,10},{14,16},{16,14},{1... | collective-permute-start | bytes 491528 | tf_op jit(solution)/shard_map/ppermute | solution.py:330
  57.2 5.2 %collective-permute-start.7 = (f32[168,128]{1,0:T(8,128)S(1)}, f32[168,128]{1,0:T(8,128)S(1)}, u32[]{:S(2)}, u32[]{:S(2)}) collective-permute-start(f32[168,128]{1,0:T(8,128)S(1)} %get-tuple-element.44.own_ref), channel_id=1, source_target_pairs={{0,1},{1,0},{2,3},{3,2},{4,5},{5,4},{6,7},{7,6},{8,9},{9,8},{10,11... | collective-permute-start | bytes 258056 | tf_op jit(solution)/shard_map/ppermute | solution.py:354

commit v12 on v11

--- a/solution.py
+++ b/solution.py
@@ -13,6 +13,7 @@
 REACH = 4
 SUB = 8
 VMEM = pl.BlockSpec(memory_space=pltpu.VMEM)
+SMEM = pl.BlockSpec(memory_space=pltpu.SMEM)
 HBM = pl.BlockSpec(memory_space=pl.ANY)
 AREA, ZONAL, NORTH, SOUTH, CENTER = range(5)
 
@@ -176,7 +177,8 @@
 
 def add_logs(group, held, result, scaled, weight_ref, inverse_ref, total_ref):
     lat = total_ref.shape[2]
-    weight = jnp.broadcast_to(weight_ref[rows_of(group), :1], (SUB, lat))
+    first, second = (weight_ref[2 * group + n].astype(jnp.float32) for n in range(2))
+    weight = jnp.where(low_half((SUB, lat)), first, second)
     for c in range(REACH):
         inverse_ref[c, rows_of(held), :] = 1.0 / result[c]
         total_ref[c] = total_ref[c] + weight * jnp.log(scaled[c] * result[c])
@@ -227,8 +229,8 @@
         both = jnp.where(low, outer, inner)
         for t in range(tiles):
             logs_ref[rows_of(c * tiles + t), :] = both[:, t * 128 : (t + 1) * 128]
-    count = jnp.sum(weight_ref[...], axis=0, keepdims=True) * (1.0 / (SUB // 2))
-    logs_ref[rows_of(REACH * tiles), :] = jnp.broadcast_to(count, (SUB, 128))
+    count = sum(weight_ref[m] for m in range(weight_ref.shape[0])).astype(jnp.float32)
+    logs_ref[rows_of(REACH * tiles), :] = jnp.full((SUB, 128), count)
 
 
 def merge_kernel(own_ref, other_ref, mass_ref, coef_ref, merged_ref, payload_ref):
@@ -289,7 +291,7 @@
     return pl.pallas_call(
         kernel,
         out_shape=outs,
-        in_specs=[VMEM] * len(args),
+        in_specs=[SMEM if arg.ndim == 1 else VMEM for arg in args],
         out_specs=out_specs or (VMEM,) * len(outs),
         scratch_shapes=scratch,
         compiler_params=params(),
@@ -312,8 +314,6 @@
     with_neighbour = [(i, (i + (1 if i % 2 else -1)) % tiles) for i in range(tiles)]
     scaling = scaling.reshape(rows * lon, lat)
     fields = fields.reshape(rows * lon, lat)
-    weights = counts.astype(jnp.float32)
-    weight_rows = jnp.broadcast_to(jnp.repeat(weights, levels)[:, None], (rows, 128))
 
     inner, *outer = call(spread_kernel, (half, *parts), scaling, coef)
     outer_halo = [lax.ppermute(part, "tile", with_neighbour) for part in outer]
@@ -330,13 +330,13 @@
         v_outer_halo += [lax.ppermute(value, "tile", with_neighbour) for value in values]
         places += [(base, base + sum(sizes[:n]), own) for n in range(len(sizes))]
     inverse_inner, edges, inner_logs = call(
-        return_inner_kernel, (half, edge, packed), v_inner_halo, v_inner, inner, weight_rows, coef, *v_outer
+        return_inner_kernel, (half, edge, packed), v_inner_halo, v_inner, inner, counts, coef, *v_outer
     )
     inverses, earlier = [inverse_inner], []
     for n, (base, first, own) in enumerate(places):
         if earlier:
             v_outer_halo[n], earlier[-1] = lax.optimization_barrier((v_outer_halo[n], earlier[-1]))
-        operands = v_outer_halo[n], v_outer[n], edges, own, weight_rows, coef
+        operands = v_outer_halo[n], v_outer[n], edges, own, counts, coef
         part = shape(*v_outer[n].shape)
         if n < len(places) - 1:
             inverse, logs = call(partial(return_outer_kernel, base, first), (part, packed), *operands)

time: 82.3 us -> 81.2 us (0.987)
  Pallas kernels: 21.8 us -> 19.6 us
  waiting for transfers between devices: 22.4 us -> 24.3 us
    pallas_call x10, Pallas kernels: 21.8 us -> 19.6 us  [call(): pl.pallas_call(kernel, out_shape=outs, in_specs=[SMEM if arg.ndim == 1 el...]
    ppermute x3, waiting for transfers between devices: 0.71 us -> 1.91 us  [body(): lax.ppermute(value, 'tile', with_neighbour)]
  transfers between devices with their start and end apart: 8 -> 8, of which waited for: 5 -> 6; matrix products, arithmetic and copies ran while one was open for 0% -> 0% of each run, Pallas kernels for 22% -> 19%
where the time goes in v12:
time: 81.2 us; the launch traced here: 80.9 us
  waiting for transfers between devices  24.3 us (30%)
  Pallas kernels  19.6 us (24%)
  starting transfers between devices  16.5 us (20%)
  blocking collectives  16.3 us (20%)
  local copies, waits for them, and re-layouts  3.23 us (4%)
  between operations  0.89 us (1%)
    ppermute x2, waiting for transfers between devices, body(): outer_halo = [lax.ppermute(part, 'tile', with_neighbour) for part in outer]  19.9 us
    pallas_call x10, Pallas kernels, call(): pl.pallas_call(kernel, out_shape=outs, in_specs=[SMEM if arg.ndim == 1 el...  19.6 us
    all_to_all x1, blocking collectives, body(): got = lax.all_to_all(payload, 'tile', split_axis=0, concat_axis=0)  16.3 us
    ppermute x3, starting transfers between devices, body(): lax.ppermute(value, 'tile', with_neighbour)  5.39 us
    ppermute x1, starting transfers between devices, body(): v_inner_halo = lax.ppermute(v_inner, 'tile', with_mate)  4.54 us
    ppermute x1, starting transfers between devices, body(): other = lax.ppermute(logs, 'mem', [(0, 1), (1, 0)])  3.38 us
    unnamed x12, local copies, waits for them, and re-layouts  3.23 us
    ppermute x3, waiting for transfers between devices, body(): lax.ppermute(value, 'tile', with_neighbour)  1.91 us
  transfers between devices with their start and end apart: 8, of which 6 were waited for; matrix products, arithmetic and copies ran while one was open for 0% of the time, Pallas kernels for 19%

profile of v12, /device:TPU:1, one launch (start us, length us, event | category | flops | bytes accessed | tf_op | source)
XLA Modules:
  0.0 80.9 jit_solution(8862416833124475933)
XLA Ops:
  0.6 0.0 copy-start
  0.6 0.9 %copy-done = f32[5,8,640]{2,1,0:T(8,128)S(1)} copy-done((f32[5,8,640]{2,1,0:T(8,128)S(1)}, f32[5,8,640]{2,1,0:T(8,128)}, u32[]{:S(2)}) %copy-start) | copy-done | bytes 102424
  1.5 0.0 copy-start.2
  1.5 1.6 %copy-done.2 = f32[26,4,8,640]{3,2,1,0:T(8,128)S(1)} copy-done((f32[26,4,8,640]{3,2,1,0:T(8,128)S(1)}, f32[26,4,8,640]{3,2,1,0:T(8,128)}, u32[]{:S(2)}) %copy-start.2) | copy-done | bytes 2129944
  3.1 0.0 copy-start.1
  3.1 0.0 copy-start.3
  3.1 0.5 shard_map.68
  3.6 1.5 %collective-permute-start.1 = (f32[4,104,640]{2,1,0:T(8,128)S(1)}, f32[4,104,640]{2,1,0:T(8,128)S(1)}, u32[]{:S(2)}, u32[]{:S(2)}) collective-permute-start(f32[4,104,640]{2,1,0:T(8,128)S(1)} %get-tuple-element.29.inner_ref.scaled_ref), channel_id=1, source_target_pairs={{0,2},{2,0},{4,6},{6,4},{8,10},{10,8},{12,14},{14,12},{16,18},{18,... | collective-permute-start | bytes 3194888 | tf_op jit(solution)/shard_map/ppermute | solution.py:320
  5.1 1.7 %collective-permute-start.4 = (f32[4,56,640]{2,1,0:T(8,128)S(1)}, f32[4,56,640]{2,1,0:T(8,128)S(1)}, u32[]{:S(2)}, u32[]{:S(2)}) collective-permute-start(f32[4,56,640]{2,1,0:T(8,128)S(1)} %get-tuple-element.30.refs_0_.outer_ref.scaled_ref), channel_id=1, source_target_pairs={{0,126},{2,4},{4,2},{6,8},{8,6},{10,12},{12,10},{14,16},{16,14},{1... | collective-permute-start | bytes 1720328 | tf_op jit(solution)/shard_map/ppermute | solution.py:319
  6.8 0.6 collective-permute-done.1.halo_ref
  7.4 0.0 copy-done.1
  7.4 0.0 copy-done.3
  7.4 0.0 copy-start.4
  7.4 0.7 copy-done.4
  8.1 5.0 %shard_map.69 = (f32[4,104,640]{2,1,0:T(8,128)S(1)}, f32[6,104,640]{2,1,0:T(8,128)S(1)}, f32[4,104,640]{2,1,0:T(8,128)S(1)}, f32[104,128]{1,0:T(8,128)S(1)}) custom-call(f32[4,104,640]{2,1,0:T(8,128)S(1)} %collective-permute-done.1.halo_ref, f32[4,104,640]{2,1,0:T(8,128)S(1)} %get-tuple-element.29.inner_ref.scaled_ref, f32[832,640]{1,0:T(8,128)S(1)} %bitcast.4, ...), custom_call_target="tpu_custom_call" | custom-call | tf_op jit(solution)/shard_map/pallas_call | solution.py:291
  13.1 4.5 %collective-permute-start.6 = (f32[4,104,640]{2,1,0:T(8,128)S(1)}, f32[4,104,640]{2,1,0:T(8,128)S(1)}, u32[]{:S(2)}, u32[]{:S(2)}) collective-permute-start(f32[4,104,640]{2,1,0:T(8,128)S(1)} %get-tuple-element.35.inner_ref), channel_id=1, source_target_pairs={{0,2},{2,0},{4,6},{6,4},{8,10},{10,8},{12,14},{14,12},{16,18},{18,... | collective-permute-start | bytes 3194888 | tf_op jit(solution)/shard_map/ppermute | solution.py:324
  17.6 0.0 collective-permute-start
  17.6 18.6 %collective-permute-done.4.halo_ref = f32[4,56,640]{2,1,0:T(8,128)S(1)} collective-permute-done((f32[4,56,640]{2,1,0:T(8,128)S(1)}, f32[4,56,640]{2,1,0:T(8,128)S(1)}, u32[]{:S(2)}, u32[]{:S(2)}) %collective-permute-start.4) | collective-permute-done | bytes 573472 | tf_op jit(solution)/shard_map/ppermute | solution.py:319
  36.3 1.4 %shard_map.71.refs_0_.outer_ref = f32[4,56,640]{2,1,0:T(8,128)S(1)} custom-call(f32[4,56,640]{2,1,0:T(8,128)S(1)} %collective-permute-done.4.halo_ref, f32[4,56,640]{2,1,0:T(8,128)S(1)} %get-tuple-element.30.refs_0_.outer_ref.scaled_ref, f32[6,104,640]{2,1,0:T(8,128)S(1)} %get-tuple-element.31.edge_ref, f32[4,104,640]{2,1,0:T(8,128)S(1)} %get-tuple-element.32.filled_ref, ...), custom_call_target="tpu_custom_call" | custom-call | tf_op jit(solution)/shard_map/pallas_call | solution.py:291
  37.6 0.0 copy-start.5
  37.7 2.6 %collective-permute-start.5 = (f32[4,56,640]{2,1,0:T(8,128)S(1)}, f32[4,56,640]{2,1,0:T(8,128)S(1)}, u32[]{:S(2)}, u32[]{:S(2)}) collective-permute-start(f32[4,56,640]{2,1,0:T(8,128)S(1)} %shard_map.71.refs_0_.outer_ref), channel_id=1, source_target_pairs={{0,126},{2,4},{4,2},{6,8},{8,6},{10,12},{12,10},{14,16},{16,14},{1... | collective-permute-start | bytes 1720328 | tf_op jit(solution)/shard_map/ppermute | solution.py:330
  40.2 1.3 %collective-permute-done.halo_ref = f32[4,48,640]{2,1,0:T(8,128)S(1)} collective-permute-done((f32[4,48,640]{2,1,0:T(8,128)S(1)}, f32[4,48,640]{2,1,0:T(8,128)S(1)}, u32[]{:S(2)}, u32[]{:S(2)}) %collective-permute-start) | collective-permute-done | bytes 491552 | tf_op jit(solution)/shard_map/ppermute | solution.py:319
  41.5 1.2 %shard_map.70 = (f32[4,32,640]{2,1,0:T(8,128)S(1)}, f32[4,16,640]{2,1,0:T(8,128)S(1)}) custom-call(f32[4,48,640]{2,1,0:T(8,128)S(1)} %collective-permute-done.halo_ref, f32[4,48,640]{2,1,0:T(8,128)S(1)} %get-tuple-element.28.refs_1_.outer_ref.scaled_ref, f32[6,104,640]{2,1,0:T(8,128)S(1)} %get-tuple-element.31.edge_ref, ...), custom_call_target="tpu_custom_call" | custom-call | tf_op jit(solution)/shard_map/pallas_call | solution.py:291
  42.7 2.6 %collective-permute-start.3 = (f32[4,32,640]{2,1,0:T(8,128)S(1)}, f32[4,32,640]{2,1,0:T(8,128)S(1)}, u32[]{:S(2)}, u32[]{:S(2)}) collective-permute-start(f32[4,32,640]{2,1,0:T(8,128)S(1)} %get-tuple-element.34.refs_1_.outer_ref), channel_id=1, source_target_pairs={{0,126},{2,4},{4,2},{6,8},{8,6},{10,12},{12,10},{14,16},{16,14},{1... | collective-permute-start | bytes 983048 | tf_op jit(solution)/shard_map/ppermute | solution.py:330
  45.3 0.3 collective-permute-start.2
  45.6 0.0 collective-permute-done.6.halo_ref
  45.6 0.0 copy-done.5
  45.6 4.9 %shard_map.72 = (f32[4,104,640]{2,1,0:T(8,128)S(1)}, f32[6,104,640]{2,1,0:T(8,128)S(1)}, f32[4,8,640]{2,1,0:T(8,128)S(1)}) custom-call(f32[4,104,640]{2,1,0:T(8,128)S(1)} %collective-permute-done.6.halo_ref, f32[4,104,640]{2,1,0:T(8,128)S(1)} %get-tuple-element.35.inner_ref, f32[4,104,640]{2,1,0:T(8,128)S(1)} %get-tuple-element.29.inner_ref.scaled_ref, ...), custom_call_target="tpu_custom_call" | custom-call | tf_op jit(solution)/shard_map/pallas_call | solution.py:291
  50.5 0.0 collective-permute-done.5.halo_ref
  50.5 1.9 %shard_map.73 = (f32[4,56,640]{2,1,0:T(8,128)S(1)}, f32[4,8,640]{2,1,0:T(8,128)S(1)}) custom-call(f32[4,56,640]{2,1,0:T(8,128)S(1)} %collective-permute-done.5.halo_ref, f32[4,56,640]{2,1,0:T(8,128)S(1)} %shard_map.71.refs_0_.outer_ref, f32[6,104,640]{2,1,0:T(8,128)S(1)} %get-tuple-element.36.edge_ref, ...), custom_call_target="tpu_custom_call" | custom-call | tf_op jit(solution)/shard_map/pallas_call | solution.py:291
  52.4 1.5 %collective-permute-done.3.halo_ref = f32[4,32,640]{2,1,0:T(8,128)S(1)} collective-permute-done((f32[4,32,640]{2,1,0:T(8,128)S(1)}, f32[4,32,640]{2,1,0:T(8,128)S(1)}, u32[]{:S(2)}, u32[]{:S(2)}) %collective-permute-start.3) | collective-permute-done | bytes 327712 | tf_op jit(solution)/shard_map/ppermute | solution.py:330
  53.9 1.4 %shard_map.74 = (f32[4,32,640]{2,1,0:T(8,128)S(1)}, f32[4,8,640]{2,1,0:T(8,128)S(1)}) custom-call(f32[4,32,640]{2,1,0:T(8,128)S(1)} %collective-permute-done.3.halo_ref, f32[4,32,640]{2,1,0:T(8,128)S(1)} %get-tuple-element.34.refs_1_.outer_ref, f32[6,104,640]{2,1,0:T(8,128)S(1)} %get-tuple-element.36.edge_ref, ...), custom_call_target="tpu_custom_call" | custom-call | tf_op jit(solution)/shard_map/pallas_call | solution.py:291
  55.3 0.4 collective-permute-done.2.halo_ref
  55.7 1.0 %shard_map.75 = (f32[4,16,640]{2,1,0:T(8,128)S(1)}, f32[168,128]{1,0:T(8,128)S(1)}) custom-call(f32[4,16,640]{2,1,0:T(8,128)S(1)} %collective-permute-done.2.halo_ref, f32[4,16,640]{2,1,0:T(8,128)S(1)} %get-tuple-element.33.refs_2_.outer_ref, f32[6,104,640]{2,1,0:T(8,128)S(1)} %get-tuple-element.36.edge_ref, ...), custom_call_target="tpu_custom_call" | custom-call | tf_op jit(solution)/shard_map/pallas_call | solution.py:291
  56.7 3.4 %collective-permute-start.7 = (f32[168,128]{1,0:T(8,128)S(1)}, f32[168,128]{1,0:T(8,128)S(1)}, u32[]{:S(2)}, u32[]{:S(2)}) collective-permute-start(f32[168,128]{1,0:T(8,128)S(1)} %get-tuple-element.44.own_ref), channel_id=1, source_target_pairs={{0,1},{1,0},{2,3},{3,2},{4,5},{5,4},{6,7},{7,6},{8,9},{9,8},{10,11... | collective-permute-start | bytes 258056 | tf_op jit(solution)/shard_map/ppermute | solution.py:354
  60.1 1.9 %collective-permute-done.7.other_ref = f32[168,128]{1,0:T(8,128)S(1)} collective-permute-done((f32[168,128]{1,0:T(8,128)S(1)}, f32[168,128]{1,0:T(8,128)S(1)}, u32[]{:S(2)}, u32[]{:S(2)}) %collective-permute-start.7) | collective-permute-done | bytes 86048 | tf_op jit(solution)/shard_map/ppermute | solution.py:354
  62.0 0.1 shard_map.76
  62.1 16.3 %all_to_all.5.got_ref = f32[64,1,128]{2,1,0:T(1,128)S(1)} all-to-all(f32[64,1,128]{2,1,0:T(1,128)S(1)} %get-tuple-element.46), channel_id=1, replica_groups=mesh['tile'=64,'mem'=2] {'tile'}, dimensions={0} | all-to-all | bytes 65536 | tf_op jit(solution)/shard_map/all_to_all | solution.py:356
  78.4 2.3 %shard_map.77 = (f32[4,8,640]{2,1,0:T(8,128)}, f32[832,640]{1,0:T(8,128)}) custom-call(f32[64,1,128]{2,1,0:T(1,128)S(1)} %all_to_all.5.got_ref, f32[4,8,640]{2,1,0:T(8,128)S(1)} %get-tuple-element.47.merged_ref, f32[4,104,640]{2,1,0:T(8,128)S(1)} %get-tuple-element.48.inner_ref, f32[4,56,640]{2,1,0:T(8,128)S(1)} %get-tuple-element.49.refs_0_, ...), custom_call_target="tpu_custom_call" | custom-call | tf_op jit(solution)/shard_map/pallas_call | solution.py:291
Async XLA Ops:
  0.6 0.9 %copy-start = (f32[5,8,640]{2,1,0:T(8,128)S(1)}, f32[5,8,640]{2,1,0:T(8,128)}, u32[]{:S(2)}) copy-start(f32[5,8,640]{2,1,0:T(8,128)} %constant.2.clone.coef_ref) | copy-start | bytes 307204
  1.5 1.6 %copy-start.2 = (f32[26,4,8,640]{3,2,1,0:T(8,128)S(1)}, f32[26,4,8,640]{3,2,1,0:T(8,128)}, u32[]{:S(2)}) copy-start(f32[26,4,8,640]{3,2,1,0:T(8,128)} %param.6) | copy-start | bytes 6389764
  3.1 4.3 %copy-start.1 = (f32[5,8,640]{2,1,0:T(8,128)S(1)}, f32[5,8,640]{2,1,0:T(8,128)}, u32[]{:S(2)}) copy-start(f32[5,8,640]{2,1,0:T(8,128)} %constant.2.clone.coef_ref) | copy-start | bytes 307204
  3.1 4.3 %copy-start.3 = (f32[26,4,8,640]{3,2,1,0:T(8,128)S(1)}, f32[26,4,8,640]{3,2,1,0:T(8,128)}, u32[]{:S(2)}) copy-start(f32[26,4,8,640]{3,2,1,0:T(8,128)} %param.5) | copy-start | bytes 6389764
  3.6 3.8 %collective-permute-start.1 = (f32[4,104,640]{2,1,0:T(8,128)S(1)}, f32[4,104,640]{2,1,0:T(8,128)S(1)}, u32[]{:S(2)}, u32[]{:S(2)}) collective-permute-start(f32[4,104,640]{2,1,0:T(8,128)S(1)} %get-tuple-element.29.inner_ref.scaled_ref), channel_id=1, source_target_pairs={{0,2},{2,0},{4,6},{6,4},{8,10},{10,8},{12,14},{14,12},{16,18},{18,... | collective-permute-start | bytes 3194888 | tf_op jit(solution)/shard_map/ppermute | solution.py:320
  5.1 31.2 %collective-permute-start.4 = (f32[4,56,640]{2,1,0:T(8,128)S(1)}, f32[4,56,640]{2,1,0:T(8,128)S(1)}, u32[]{:S(2)}, u32[]{:S(2)}) collective-permute-start(f32[4,56,640]{2,1,0:T(8,128)S(1)} %get-tuple-element.30.refs_0_.outer_ref.scaled_ref), channel_id=1, source_target_pairs={{0,126},{2,4},{4,2},{6,8},{8,6},{10,12},{12,10},{14,16},{16,14},{1... | collective-permute-start | bytes 1720328 | tf_op jit(solution)/shard_map/ppermute | solution.py:319
  7.4 0.7 copy-start.4
  13.1 32.5 %collective-permute-start.6 = (f32[4,104,640]{2,1,0:T(8,128)S(1)}, f32[4,104,640]{2,1,0:T(8,128)S(1)}, u32[]{:S(2)}, u32[]{:S(2)}) collective-permute-start(f32[4,104,640]{2,1,0:T(8,128)S(1)} %get-tuple-element.35.inner_ref), channel_id=1, source_target_pairs={{0,2},{2,0},{4,6},{6,4},{8,10},{10,8},{12,14},{14,12},{16,18},{18,... | collective-permute-start | bytes 3194888 | tf_op jit(solution)/shard_map/ppermute | solution.py:324
  17.6 23.9 %collective-permute-start = (f32[4,48,640]{2,1,0:T(8,128)S(1)}, f32[4,48,640]{2,1,0:T(8,128)S(1)}, u32[]{:S(2)}, u32[]{:S(2)}) collective-permute-start(f32[4,48,640]{2,1,0:T(8,128)S(1)} %get-tuple-element.28.refs_1_.outer_ref.scaled_ref), channel_id=1, source_target_pairs={{0,126},{2,4},{4,2},{6,8},{8,6},{10,12},{12,10},{14,16},{16,14},{1... | collective-permute-start | bytes 1474568 | tf_op jit(solution)/shard_map/ppermute | solution.py:319
  37.6 7.9 %copy-start.5 = (s32[26]{0:T(128)S(1)}, s32[26]{0:T(128)}, u32[]{:S(2)}) copy-start(s32[26]{0:T(128)} %weight_ref.7) | copy-start | bytes 316
  37.7 12.8 %collective-permute-start.5 = (f32[4,56,640]{2,1,0:T(8,128)S(1)}, f32[4,56,640]{2,1,0:T(8,128)S(1)}, u32[]{:S(2)}, u32[]{:S(2)}) collective-permute-start(f32[4,56,640]{2,1,0:T(8,128)S(1)} %shard_map.71.refs_0_.outer_ref), channel_id=1, source_target_pairs={{0,126},{2,4},{4,2},{6,8},{8,6},{10,12},{12,10},{14,16},{16,14},{1... | collective-permute-start | bytes 1720328 | tf_op jit(solution)/shard_map/ppermute | solution.py:330
  42.7 11.2 %collective-permute-start.3 = (f32[4,32,640]{2,1,0:T(8,128)S(1)}, f32[4,32,640]{2,1,0:T(8,128)S(1)}, u32[]{:S(2)}, u32[]{:S(2)}) collective-permute-start(f32[4,32,640]{2,1,0:T(8,128)S(1)} %get-tuple-element.34.refs_1_.outer_ref), channel_id=1, source_target_pairs={{0,126},{2,4},{4,2},{6,8},{8,6},{10,12},{12,10},{14,16},{16,14},{1... | collective-permute-start | bytes 983048 | tf_op jit(solution)/shard_map/ppermute | solution.py:330
  45.3 10.4 %collective-permute-start.2 = (f32[4,16,640]{2,1,0:T(8,128)S(1)}, f32[4,16,640]{2,1,0:T(8,128)S(1)}, u32[]{:S(2)}, u32[]{:S(2)}) collective-permute-start(f32[4,16,640]{2,1,0:T(8,128)S(1)} %get-tuple-element.33.refs_2_.outer_ref), channel_id=1, source_target_pairs={{0,126},{2,4},{4,2},{6,8},{8,6},{10,12},{12,10},{14,16},{16,14},{1... | collective-permute-start | bytes 491528 | tf_op jit(solution)/shard_map/ppermute | solution.py:330
  56.7 5.3 %collective-permute-start.7 = (f32[168,128]{1,0:T(8,128)S(1)}, f32[168,128]{1,0:T(8,128)S(1)}, u32[]{:S(2)}, u32[]{:S(2)}) collective-permute-start(f32[168,128]{1,0:T(8,128)S(1)} %get-tuple-element.44.own_ref), channel_id=1, source_target_pairs={{0,1},{1,0},{2,3},{3,2},{4,5},{5,4},{6,7},{7,6},{8,9},{9,8},{10,11... | collective-permute-start | bytes 258056 | tf_op jit(solution)/shard_map/ppermute | solution.py:354

commit v13 on v12

--- a/solution.py
+++ b/solution.py
@@ -90,6 +90,10 @@
     return [jnp.where(odd, columns[last - c], columns[c]) for c in range(len(columns))]
 
 
+def low_half(shape):
+    return lax.broadcasted_iota(jnp.int32, shape, 0) < SUB // 2
+
+
 def spread_kernel(scaling_ref, coef_ref, inner_ref, *outer_refs):
     groups, lat = inner_ref.shape[1] // SUB, inner_ref.shape[2]
     odd = odd_core()
@@ -143,11 +147,17 @@
 
 
 def smooth_inner_kernel(
-    halo_ref, inner_ref, fields_ref, mask_ref, coef_ref, *refs
+    halo_ref, inner_ref, fields_ref, mask_ref, count_ref, coef_ref, *refs
 ):
-    *outer_refs, out_ref, edge_ref, filled_ref, mass_ref = refs
+    *outer_refs, out_ref, edge_ref, filled_ref, mass_ref, weight_ref = refs
     groups, lat = inner_ref.shape[1] // SUB, inner_ref.shape[2]
     odd = odd_core()
+    low = low_half((SUB, 128))
+    for group in range(groups):
+        first, second = (count_ref[2 * group + n].astype(jnp.float32) for n in range(2))
+        weight_ref[rows_of(group), :] = jnp.where(low, first, second)
+    count = sum(count_ref[m] for m in range(2 * groups)).astype(jnp.float32)
+    weight_ref[rows_of(groups), :] = jnp.full((SUB, 128), count)
     for batch in batches(groups):
         for group, smoothed in inner_half(batch, halo_ref, inner_ref, outer_refs, coef_ref, edge_ref):
             fields = by_longitude(fields_ref[block_of(group), :], lat)
@@ -171,14 +181,9 @@
             out.put(group - first, [top / bottom for top, bottom in zip(filled, smoothed)])
 
 
-def low_half(shape):
-    return lax.broadcasted_iota(jnp.int32, shape, 0) < SUB // 2
-
-
 def add_logs(group, held, result, scaled, weight_ref, inverse_ref, total_ref):
     lat = total_ref.shape[2]
-    first, second = (weight_ref[2 * group + n].astype(jnp.float32) for n in range(2))
-    weight = jnp.where(low_half((SUB, lat)), first, second)
+    weight = jnp.concatenate([weight_ref[rows_of(group), :]] * (lat // 128), axis=1)
     for c in range(REACH):
         inverse_ref[c, rows_of(held), :] = 1.0 / result[c]
         total_ref[c] = total_ref[c] + weight * jnp.log(scaled[c] * result[c])
@@ -229,8 +234,7 @@
         both = jnp.where(low, outer, inner)
         for t in range(tiles):
             logs_ref[rows_of(c * tiles + t), :] = both[:, t * 128 : (t + 1) * 128]
-    count = sum(weight_ref[m] for m in range(weight_ref.shape[0])).astype(jnp.float32)
-    logs_ref[rows_of(REACH * tiles), :] = jnp.full((SUB, 128), count)
+    logs_ref[rows_of(REACH * tiles), :] = weight_ref[rows_of(weight_ref.shape[0] // SUB - 1), :]
 
 
 def merge_kernel(own_ref, other_ref, mass_ref, coef_ref, merged_ref, payload_ref):
@@ -318,8 +322,17 @@
     inner, *outer = call(spread_kernel, (half, *parts), scaling, coef)
     outer_halo = [lax.ppermute(part, "tile", with_neighbour) for part in outer]
     inner_halo = lax.ppermute(inner, "tile", with_mate)
-    v_inner, edges, filled, mass = call(
-        smooth_inner_kernel, (half, edge, half, shape(rows, 128)), inner_halo, inner, fields, land_mask, coef, *outer
+    fields, inner = lax.optimization_barrier((fields, inner))
+    v_inner, edges, filled, mass, weights = call(
+        smooth_inner_kernel,
+        (half, edge, half, shape(rows, 128), shape(rows + SUB, 128)),
+        inner_halo,
+        inner,
+        fields,
+        land_mask,
+        counts,
+        coef,
+        *outer,
     )
     v_inner_halo = lax.ppermute(v_inner, "tile", with_mate)
     v_outer, v_outer_halo, places = [], [], []
@@ -330,13 +343,13 @@
         v_outer_halo += [lax.ppermute(value, "tile", with_neighbour) for value in values]
         places += [(base, base + sum(sizes[:n]), own) for n in range(len(sizes))]
     inverse_inner, edges, inner_logs = call(
-        return_inner_kernel, (half, edge, packed), v_inner_halo, v_inner, inner, counts, coef, *v_outer
+        return_inner_kernel, (half, edge, packed), v_inner_halo, v_inner, inner, weights, coef, *v_outer
     )
     inverses, earlier = [inverse_inner], []
     for n, (base, first, own) in enumerate(places):
         if earlier:
             v_outer_halo[n], earlier[-1] = lax.optimization_barrier((v_outer_halo[n], earlier[-1]))
-        operands = v_outer_halo[n], v_outer[n], edges, own, counts, coef
+        operands = v_outer_halo[n], v_outer[n], edges, own, weights, coef
         part = shape(*v_outer[n].shape)
         if n < len(places) - 1:
             inverse, logs = call(partial(return_outer_kernel, base, first), (part, packed), *operands)

time: 81.2 us -> 80.6 us (level)
  Pallas kernels: 19.6 us -> 17.7 us
  waiting for transfers between devices: 24.3 us -> 26.2 us
    ppermute x3, waiting for transfers between devices: 1.91 us -> 4.08 us  [body(): lax.ppermute(value, 'tile', with_neighbour)]
    pallas_call x10, Pallas kernels: 19.6 us -> 17.7 us  [call(): pl.pallas_call(kernel, out_shape=outs, in_specs=[SMEM if arg.ndim == 1 el...]
  transfers between devices with their start and end apart: 8 -> 8, of which waited for: 6 -> 7; matrix products, arithmetic and copies ran while one was open for 0% -> 0% of each run, Pallas kernels for 19% -> 18%
where the time goes in v13:
time: 80.6 us; the launch traced here: 80.4 us
  waiting for transfers between devices  26.2 us (33%)
  Pallas kernels  17.7 us (22%)
  blocking collectives  16.3 us (20%)
  starting transfers between devices  16.2 us (20%)
  local copies, waits for them, and re-layouts  3.22 us (4%)
  between operations  0.88 us (1%)
    ppermute x2, waiting for transfers between devices, body(): outer_halo = [lax.ppermute(part, 'tile', with_neighbour) for part in outer]  19.6 us
    pallas_call x10, Pallas kernels, call(): pl.pallas_call(kernel, out_shape=outs, in_specs=[SMEM if arg.ndim == 1 el...  17.7 us
    all_to_all x1, blocking collectives, body(): got = lax.all_to_all(payload, 'tile', split_axis=0, concat_axis=0)  16.3 us
    ppermute x3, starting transfers between devices, body(): lax.ppermute(value, 'tile', with_neighbour)  5.39 us
    ppermute x1, starting transfers between devices, body(): v_inner_halo = lax.ppermute(v_inner, 'tile', with_mate)  4.54 us
    ppermute x3, waiting for transfers between devices, body(): lax.ppermute(value, 'tile', with_neighbour)  4.08 us
    unnamed x12, local copies, waits for them, and re-layouts  3.22 us
    ppermute x1, starting transfers between devices, body(): other = lax.ppermute(logs, 'mem', [(0, 1), (1, 0)])  3.02 us
  transfers between devices with their start and end apart: 8, of which 7 were waited for; matrix products, arithmetic and copies ran while one was open for 0% of the time, Pallas kernels for 18%

profile of v13, /device:TPU:1, one launch (start us, length us, event | category | flops | bytes accessed | tf_op | source)
XLA Modules:
  0.0 80.4 jit_solution(57749461339496404)
XLA Ops:
  0.6 0.0 copy-start
  0.6 0.9 %copy-done = f32[5,8,640]{2,1,0:T(8,128)S(1)} copy-done((f32[5,8,640]{2,1,0:T(8,128)S(1)}, f32[5,8,640]{2,1,0:T(8,128)}, u32[]{:S(2)}) %copy-start) | copy-done | bytes 102424
  1.5 0.0 copy-start.2
  1.5 1.6 %copy-done.2 = f32[26,4,8,640]{3,2,1,0:T(8,128)S(1)} copy-done((f32[26,4,8,640]{3,2,1,0:T(8,128)S(1)}, f32[26,4,8,640]{3,2,1,0:T(8,128)}, u32[]{:S(2)}) %copy-start.2) | copy-done | bytes 2129944
  3.1 0.0 copy-start.1
  3.1 0.0 copy-start.3
  3.1 0.0 copy-start.5
  3.1 0.5 shard_map.68
  3.6 1.5 %collective-permute-start.1 = (f32[4,104,640]{2,1,0:T(8,128)S(1)}, f32[4,104,640]{2,1,0:T(8,128)S(1)}, u32[]{:S(2)}, u32[]{:S(2)}) collective-permute-start(f32[4,104,640]{2,1,0:T(8,128)S(1)} %get-tuple-element.33.inner_ref.scaled_ref), channel_id=1, source_target_pairs={{0,2},{2,0},{4,6},{6,4},{8,10},{10,8},{12,14},{14,12},{16,18},{18,... | collective-permute-start | bytes 3194888 | tf_op jit(solution)/shard_map/ppermute | solution.py:324
  5.1 1.7 %collective-permute-start.4 = (f32[4,56,640]{2,1,0:T(8,128)S(1)}, f32[4,56,640]{2,1,0:T(8,128)S(1)}, u32[]{:S(2)}, u32[]{:S(2)}) collective-permute-start(f32[4,56,640]{2,1,0:T(8,128)S(1)} %get-tuple-element.35.refs_0_.outer_ref.scaled_ref), channel_id=1, source_target_pairs={{0,126},{2,4},{4,2},{6,8},{8,6},{10,12},{12,10},{14,16},{16,14},{1... | collective-permute-start | bytes 1720328 | tf_op jit(solution)/shard_map/ppermute | solution.py:323
  6.8 0.6 collective-permute-done.1.halo_ref
  7.4 0.0 copy-done.1
  7.4 0.0 copy-done.3
  7.4 0.0 copy-done.5
  7.4 0.0 copy-start.4
  7.4 0.7 copy-done.4
  8.1 5.4 %shard_map.69 = (f32[4,104,640]{2,1,0:T(8,128)S(1)}, f32[6,104,640]{2,1,0:T(8,128)S(1)}, f32[4,104,640]{2,1,0:T(8,128)S(1)}, f32[104,128]{1,0:T(8,128)S(1)}, f32[112,128]{1,0:T(8,128)S(1)}) custom-call(f32[4,104,640]{2,1,0:T(8,128)S(1)} %collective-permute-done.1.halo_ref, f32[4,104,640]{2,1,0:T(8,128)S(1)} %get-tuple-element.33.inner_ref.scaled_ref, ...), custom_call_target="tpu_custom_call" | custom-call | tf_op jit(solution)/shard_map/pallas_call | solution.py:295
  13.5 4.5 %collective-permute-start.6 = (f32[4,104,640]{2,1,0:T(8,128)S(1)}, f32[4,104,640]{2,1,0:T(8,128)S(1)}, u32[]{:S(2)}, u32[]{:S(2)}) collective-permute-start(f32[4,104,640]{2,1,0:T(8,128)S(1)} %get-tuple-element.40.inner_ref), channel_id=1, source_target_pairs={{0,2},{2,0},{4,6},{6,4},{8,10},{10,8},{12,14},{14,12},{16,18},{18,... | collective-permute-start | bytes 3194888 | tf_op jit(solution)/shard_map/ppermute | solution.py:337
  18.0 0.0 collective-permute-start
  18.1 18.2 %collective-permute-done.4.halo_ref = f32[4,56,640]{2,1,0:T(8,128)S(1)} collective-permute-done((f32[4,56,640]{2,1,0:T(8,128)S(1)}, f32[4,56,640]{2,1,0:T(8,128)S(1)}, u32[]{:S(2)}, u32[]{:S(2)}) %collective-permute-start.4) | collective-permute-done | bytes 573472 | tf_op jit(solution)/shard_map/ppermute | solution.py:323
  36.3 1.3 %shard_map.71.refs_0_.outer_ref = f32[4,56,640]{2,1,0:T(8,128)S(1)} custom-call(f32[4,56,640]{2,1,0:T(8,128)S(1)} %collective-permute-done.4.halo_ref, f32[4,56,640]{2,1,0:T(8,128)S(1)} %get-tuple-element.35.refs_0_.outer_ref.scaled_ref, f32[6,104,640]{2,1,0:T(8,128)S(1)} %get-tuple-element.36.edge_ref, f32[4,104,640]{2,1,0:T(8,128)S(1)} %get-tuple-element.37.filled_ref, ...), custom_call_target="tpu_custom_call" | custom-call | tf_op jit(solution)/shard_map/pallas_call | solution.py:295
  37.6 2.6 %collective-permute-start.5 = (f32[4,56,640]{2,1,0:T(8,128)S(1)}, f32[4,56,640]{2,1,0:T(8,128)S(1)}, u32[]{:S(2)}, u32[]{:S(2)}) collective-permute-start(f32[4,56,640]{2,1,0:T(8,128)S(1)} %shard_map.71.refs_0_.outer_ref), channel_id=1, source_target_pairs={{0,126},{2,4},{4,2},{6,8},{8,6},{10,12},{12,10},{14,16},{16,14},{1... | collective-permute-start | bytes 1720328 | tf_op jit(solution)/shard_map/ppermute | solution.py:343
  40.2 1.3 %collective-permute-done.halo_ref = f32[4,48,640]{2,1,0:T(8,128)S(1)} collective-permute-done((f32[4,48,640]{2,1,0:T(8,128)S(1)}, f32[4,48,640]{2,1,0:T(8,128)S(1)}, u32[]{:S(2)}, u32[]{:S(2)}) %collective-permute-start) | collective-permute-done | bytes 491552 | tf_op jit(solution)/shard_map/ppermute | solution.py:323
  41.5 1.2 %shard_map.70 = (f32[4,32,640]{2,1,0:T(8,128)S(1)}, f32[4,16,640]{2,1,0:T(8,128)S(1)}) custom-call(f32[4,48,640]{2,1,0:T(8,128)S(1)} %collective-permute-done.halo_ref, f32[4,48,640]{2,1,0:T(8,128)S(1)} %get-tuple-element.31.refs_1_.outer_ref.scaled_ref, f32[6,104,640]{2,1,0:T(8,128)S(1)} %get-tuple-element.36.edge_ref, ...), custom_call_target="tpu_custom_call" | custom-call | tf_op jit(solution)/shard_map/pallas_call | solution.py:295
  42.7 2.6 %collective-permute-start.3 = (f32[4,32,640]{2,1,0:T(8,128)S(1)}, f32[4,32,640]{2,1,0:T(8,128)S(1)}, u32[]{:S(2)}, u32[]{:S(2)}) collective-permute-start(f32[4,32,640]{2,1,0:T(8,128)S(1)} %get-tuple-element.39.refs_1_.outer_ref), channel_id=1, source_target_pairs={{0,126},{2,4},{4,2},{6,8},{8,6},{10,12},{12,10},{14,16},{16,14},{1... | collective-permute-start | bytes 983048 | tf_op jit(solution)/shard_map/ppermute | solution.py:343
  45.3 0.3 collective-permute-start.2
  45.5 0.0 collective-permute-done.6.halo_ref
  45.5 4.3 %shard_map.72 = (f32[4,104,640]{2,1,0:T(8,128)S(1)}, f32[6,104,640]{2,1,0:T(8,128)S(1)}, f32[4,8,640]{2,1,0:T(8,128)S(1)}) custom-call(f32[4,104,640]{2,1,0:T(8,128)S(1)} %collective-permute-done.6.halo_ref, f32[4,104,640]{2,1,0:T(8,128)S(1)} %get-tuple-element.40.inner_ref, f32[4,104,640]{2,1,0:T(8,128)S(1)} %get-tuple-element.33.inner_ref.scaled_ref, ...), custom_call_target="tpu_custom_call" | custom-call | tf_op jit(solution)/shard_map/pallas_call | solution.py:295
  49.8 1.3 %collective-permute-done.5.halo_ref = f32[4,56,640]{2,1,0:T(8,128)S(1)} collective-permute-done((f32[4,56,640]{2,1,0:T(8,128)S(1)}, f32[4,56,640]{2,1,0:T(8,128)S(1)}, u32[]{:S(2)}, u32[]{:S(2)}) %collective-permute-start.5) | collective-permute-done | bytes 573472 | tf_op jit(solution)/shard_map/ppermute | solution.py:343
  51.1 1.4 %shard_map.73 = (f32[4,56,640]{2,1,0:T(8,128)S(1)}, f32[4,8,640]{2,1,0:T(8,128)S(1)}) custom-call(f32[4,56,640]{2,1,0:T(8,128)S(1)} %collective-permute-done.5.halo_ref, f32[4,56,640]{2,1,0:T(8,128)S(1)} %shard_map.71.refs_0_.outer_ref, f32[6,104,640]{2,1,0:T(8,128)S(1)} %get-tuple-element.42.edge_ref, ...), custom_call_target="tpu_custom_call" | custom-call | tf_op jit(solution)/shard_map/pallas_call | solution.py:295
  52.5 1.8 %collective-permute-done.3.halo_ref = f32[4,32,640]{2,1,0:T(8,128)S(1)} collective-permute-done((f32[4,32,640]{2,1,0:T(8,128)S(1)}, f32[4,32,640]{2,1,0:T(8,128)S(1)}, u32[]{:S(2)}, u32[]{:S(2)}) %collective-permute-start.3) | collective-permute-done | bytes 327712 | tf_op jit(solution)/shard_map/ppermute | solution.py:343
  54.3 0.8 %shard_map.74 = (f32[4,32,640]{2,1,0:T(8,128)S(1)}, f32[4,8,640]{2,1,0:T(8,128)S(1)}) custom-call(f32[4,32,640]{2,1,0:T(8,128)S(1)} %collective-permute-done.3.halo_ref, f32[4,32,640]{2,1,0:T(8,128)S(1)} %get-tuple-element.39.refs_1_.outer_ref, f32[6,104,640]{2,1,0:T(8,128)S(1)} %get-tuple-element.42.edge_ref, ...), custom_call_target="tpu_custom_call" | custom-call | tf_op jit(solution)/shard_map/pallas_call | solution.py:295
  55.2 0.9 %collective-permute-done.2.halo_ref = f32[4,16,640]{2,1,0:T(8,128)S(1)} collective-permute-done((f32[4,16,640]{2,1,0:T(8,128)S(1)}, f32[4,16,640]{2,1,0:T(8,128)S(1)}, u32[]{:S(2)}, u32[]{:S(2)}) %collective-permute-start.2) | collective-permute-done | bytes 163872 | tf_op jit(solution)/shard_map/ppermute | solution.py:343
  56.1 0.5 shard_map.75
  56.6 3.0 %collective-permute-start.7 = (f32[168,128]{1,0:T(8,128)S(1)}, f32[168,128]{1,0:T(8,128)S(1)}, u32[]{:S(2)}, u32[]{:S(2)}) collective-permute-start(f32[168,128]{1,0:T(8,128)S(1)} %get-tuple-element.50.own_ref), channel_id=1, source_target_pairs={{0,1},{1,0},{2,3},{3,2},{4,5},{5,4},{6,7},{7,6},{8,9},{9,8},{10,11... | collective-permute-start | bytes 258056 | tf_op jit(solution)/shard_map/ppermute | solution.py:367
  59.6 1.9 %collective-permute-done.7.other_ref = f32[168,128]{1,0:T(8,128)S(1)} collective-permute-done((f32[168,128]{1,0:T(8,128)S(1)}, f32[168,128]{1,0:T(8,128)S(1)}, u32[]{:S(2)}, u32[]{:S(2)}) %collective-permute-start.7) | collective-permute-done | bytes 86048 | tf_op jit(solution)/shard_map/ppermute | solution.py:367
  61.5 0.1 shard_map.76
  61.6 16.3 %all_to_all.5.got_ref = f32[64,1,128]{2,1,0:T(1,128)S(1)} all-to-all(f32[64,1,128]{2,1,0:T(1,128)S(1)} %get-tuple-element.52), channel_id=1, replica_groups=mesh['tile'=64,'mem'=2] {'tile'}, dimensions={0} | all-to-all | bytes 65536 | tf_op jit(solution)/shard_map/all_to_all | solution.py:369
  77.9 2.3 %shard_map.77 = (f32[4,8,640]{2,1,0:T(8,128)}, f32[832,640]{1,0:T(8,128)}) custom-call(f32[64,1,128]{2,1,0:T(1,128)S(1)} %all_to_all.5.got_ref, f32[4,8,640]{2,1,0:T(8,128)S(1)} %get-tuple-element.53.merged_ref, f32[4,104,640]{2,1,0:T(8,128)S(1)} %get-tuple-element.54.inner_ref, f32[4,56,640]{2,1,0:T(8,128)S(1)} %get-tuple-element.55.refs_0_, ...), custom_call_target="tpu_custom_call" | custom-call | tf_op jit(solution)/shard_map/pallas_call | solution.py:295
Async XLA Ops:
  0.6 0.9 %copy-start = (f32[5,8,640]{2,1,0:T(8,128)S(1)}, f32[5,8,640]{2,1,0:T(8,128)}, u32[]{:S(2)}) copy-start(f32[5,8,640]{2,1,0:T(8,128)} %constant.2.clone.coef_ref) | copy-start | bytes 307204
  1.5 1.6 %copy-start.2 = (f32[26,4,8,640]{3,2,1,0:T(8,128)S(1)}, f32[26,4,8,640]{3,2,1,0:T(8,128)}, u32[]{:S(2)}) copy-start(f32[26,4,8,640]{3,2,1,0:T(8,128)} %param.6) | copy-start | bytes 6389764
  3.1 4.3 %copy-start.1 = (f32[5,8,640]{2,1,0:T(8,128)S(1)}, f32[5,8,640]{2,1,0:T(8,128)}, u32[]{:S(2)}) copy-start(f32[5,8,640]{2,1,0:T(8,128)} %constant.2.clone.coef_ref) | copy-start | bytes 307204
  3.1 4.3 %copy-start.3 = (f32[26,4,8,640]{3,2,1,0:T(8,128)S(1)}, f32[26,4,8,640]{3,2,1,0:T(8,128)}, u32[]{:S(2)}) copy-start(f32[26,4,8,640]{3,2,1,0:T(8,128)} %param.5) | copy-start | bytes 6389764
  3.1 4.3 %copy-start.5 = (s32[26]{0:T(128)S(1)}, s32[26]{0:T(128)}, u32[]{:S(2)}) copy-start(s32[26]{0:T(128)} %count_ref.1) | copy-start | bytes 316
  3.6 3.8 %collective-permute-start.1 = (f32[4,104,640]{2,1,0:T(8,128)S(1)}, f32[4,104,640]{2,1,0:T(8,128)S(1)}, u32[]{:S(2)}, u32[]{:S(2)}) collective-permute-start(f32[4,104,640]{2,1,0:T(8,128)S(1)} %get-tuple-element.33.inner_ref.scaled_ref), channel_id=1, source_target_pairs={{0,2},{2,0},{4,6},{6,4},{8,10},{10,8},{12,14},{14,12},{16,18},{18,... | collective-permute-start | bytes 3194888 | tf_op jit(solution)/shard_map/ppermute | solution.py:324
  5.1 31.2 %collective-permute-start.4 = (f32[4,56,640]{2,1,0:T(8,128)S(1)}, f32[4,56,640]{2,1,0:T(8,128)S(1)}, u32[]{:S(2)}, u32[]{:S(2)}) collective-permute-start(f32[4,56,640]{2,1,0:T(8,128)S(1)} %get-tuple-element.35.refs_0_.outer_ref.scaled_ref), channel_id=1, source_target_pairs={{0,126},{2,4},{4,2},{6,8},{8,6},{10,12},{12,10},{14,16},{16,14},{1... | collective-permute-start | bytes 1720328 | tf_op jit(solution)/shard_map/ppermute | solution.py:323
  7.4 0.7 copy-start.4
  13.5 32.0 %collective-permute-start.6 = (f32[4,104,640]{2,1,0:T(8,128)S(1)}, f32[4,104,640]{2,1,0:T(8,128)S(1)}, u32[]{:S(2)}, u32[]{:S(2)}) collective-permute-start(f32[4,104,640]{2,1,0:T(8,128)S(1)} %get-tuple-element.40.inner_ref), channel_id=1, source_target_pairs={{0,2},{2,0},{4,6},{6,4},{8,10},{10,8},{12,14},{14,12},{16,18},{18,... | collective-permute-start | bytes 3194888 | tf_op jit(solution)/shard_map/ppermute | solution.py:337
  18.0 23.5 %collective-permute-start = (f32[4,48,640]{2,1,0:T(8,128)S(1)}, f32[4,48,640]{2,1,0:T(8,128)S(1)}, u32[]{:S(2)}, u32[]{:S(2)}) collective-permute-start(f32[4,48,640]{2,1,0:T(8,128)S(1)} %get-tuple-element.31.refs_1_.outer_ref.scaled_ref), channel_id=1, source_target_pairs={{0,126},{2,4},{4,2},{6,8},{8,6},{10,12},{12,10},{14,16},{16,14},{1... | collective-permute-start | bytes 1474568 | tf_op jit(solution)/shard_map/ppermute | solution.py:323
  37.6 13.5 %collective-permute-start.5 = (f32[4,56,640]{2,1,0:T(8,128)S(1)}, f32[4,56,640]{2,1,0:T(8,128)S(1)}, u32[]{:S(2)}, u32[]{:S(2)}) collective-permute-start(f32[4,56,640]{2,1,0:T(8,128)S(1)} %shard_map.71.refs_0_.outer_ref), channel_id=1, source_target_pairs={{0,126},{2,4},{4,2},{6,8},{8,6},{10,12},{12,10},{14,16},{16,14},{1... | collective-permute-start | bytes 1720328 | tf_op jit(solution)/shard_map/ppermute | solution.py:343
  42.7 11.6 %collective-permute-start.3 = (f32[4,32,640]{2,1,0:T(8,128)S(1)}, f32[4,32,640]{2,1,0:T(8,128)S(1)}, u32[]{:S(2)}, u32[]{:S(2)}) collective-permute-start(f32[4,32,640]{2,1,0:T(8,128)S(1)} %get-tuple-element.39.refs_1_.outer_ref), channel_id=1, source_target_pairs={{0,126},{2,4},{4,2},{6,8},{8,6},{10,12},{12,10},{14,16},{16,14},{1... | collective-permute-start | bytes 983048 | tf_op jit(solution)/shard_map/ppermute | solution.py:343
  45.3 10.8 %collective-permute-start.2 = (f32[4,16,640]{2,1,0:T(8,128)S(1)}, f32[4,16,640]{2,1,0:T(8,128)S(1)}, u32[]{:S(2)}, u32[]{:S(2)}) collective-permute-start(f32[4,16,640]{2,1,0:T(8,128)S(1)} %get-tuple-element.38.refs_2_.outer_ref), channel_id=1, source_target_pairs={{0,126},{2,4},{4,2},{6,8},{8,6},{10,12},{12,10},{14,16},{16,14},{1... | collective-permute-start | bytes 491528 | tf_op jit(solution)/shard_map/ppermute | solution.py:343
  56.6 4.9 %collective-permute-start.7 = (f32[168,128]{1,0:T(8,128)S(1)}, f32[168,128]{1,0:T(8,128)S(1)}, u32[]{:S(2)}, u32[]{:S(2)}) collective-permute-start(f32[168,128]{1,0:T(8,128)S(1)} %get-tuple-element.50.own_ref), channel_id=1, source_target_pairs={{0,1},{1,0},{2,3},{3,2},{4,5},{5,4},{6,7},{7,6},{8,9},{9,8},{10,11... | collective-permute-start | bytes 258056 | tf_op jit(solution)/shard_map/ppermute | solution.py:367

commit v14 on v13

--- a/solution.py
+++ b/solution.py
@@ -94,13 +94,12 @@
     return lax.broadcasted_iota(jnp.int32, shape, 0) < SUB // 2
 
 
-def spread_kernel(scaling_ref, coef_ref, inner_ref, *outer_refs):
+def spread_kernel(scaling_ref, inner_ref, *outer_refs):
     groups, lat = inner_ref.shape[1] // SUB, inner_ref.shape[2]
     odd = odd_core()
     outer = Chunked(outer_refs)
     for group in range(groups):
         columns = from_outside(by_longitude(scaling_ref[block_of(group), :], lat), odd)
-        columns = [column * coef_ref[AREA] for column in columns]
         outer.put(group, columns[:REACH])
         for c in range(REACH):
             inner_ref[c, rows_of(group), :] = columns[c + REACH]
@@ -125,9 +124,18 @@
     ]
 
 
-def inner_half(batch, halo_ref, inner_ref, outer_refs, coef_ref, edge_ref):
+def unit(values, coef_ref):
+    return values
+
+
+def by_area(values, coef_ref):
+    return [value * coef_ref[AREA] for value in values]
+
+
+def inner_half(batch, halo_ref, inner_ref, outer_refs, coef_ref, edge_ref, weigh=unit):
     outer = Chunked(outer_refs)
     columns = [outer.stack(g) + stack_of(inner_ref, g) + stack_of(halo_ref, g, (3, 2, 1, 0)) for g in batch]
+    columns = [weigh(own, coef_ref) for own in columns]
     for s in range(REACH):
         columns = [diffuse(own, coef_ref) for own in columns]
         if s < REACH - 1:
@@ -137,8 +145,9 @@
     return zip(batch, columns)
 
 
-def outer_half(batch, first, halo_ref, outer_ref, edge_ref, coef_ref):
+def outer_half(batch, first, halo_ref, outer_ref, edge_ref, coef_ref, weigh=unit):
     columns = [stack_of(halo_ref, g - first, (3, 2, 1, 0)) + stack_of(outer_ref, g - first, (0, 1)) for g in batch]
+    columns = [weigh(own, coef_ref) for own in columns]
     for s in range(REACH):
         columns = [diffuse(own, coef_ref) for own in columns]
         if s < REACH - 1:
@@ -159,7 +168,9 @@
     count = sum(count_ref[m] for m in range(2 * groups)).astype(jnp.float32)
     weight_ref[rows_of(groups), :] = jnp.full((SUB, 128), count)
     for batch in batches(groups):
-        for group, smoothed in inner_half(batch, halo_ref, inner_ref, outer_refs, coef_ref, edge_ref):
+        for group, smoothed in inner_half(
+            batch, halo_ref, inner_ref, outer_refs, coef_ref, edge_ref, by_area
+        ):
             fields = by_longitude(fields_ref[block_of(group), :], lat)
             filled = []
             for c in range(2 * REACH):
@@ -176,7 +187,7 @@
     last = first + outer_ref.shape[1] // SUB
     out = Chunked(out_refs)
     for batch in batches(last, first):
-        for group, smoothed in outer_half(batch, first, halo_ref, outer_ref, edge_ref, coef_ref):
+        for group, smoothed in outer_half(batch, first, halo_ref, outer_ref, edge_ref, coef_ref, by_area):
             filled = stack_of(filled_ref, group)
             out.put(group - first, [top / bottom for top, bottom in zip(filled, smoothed)])
 
@@ -245,9 +256,9 @@
     for c in range(REACH):
         for t in range(tiles):
             span = slice(t * 128, (t + 1) * 128)
-            weighted = jnp.exp(both(c * tiles + t) * scale)
-            merged_ref[c, :, span] = weighted / coef_ref[AREA, :, span]
-            level = level + weighted
+            merged = jnp.exp(both(c * tiles + t) * scale)
+            merged_ref[c, :, span] = merged
+            level = level + merged * coef_ref[AREA, :, span]
     level = level + pltpu.roll(level, SUB // 2, 0)
     spare = jnp.zeros((128 - members - SUB, 128), jnp.float32)
     table = jnp.concatenate([mass_ref[...], level, spare], axis=0)
@@ -255,36 +266,47 @@
     payload_ref[...] = jnp.broadcast_to(row[None], payload_ref.shape)
 
 
-def finish_kernel(cells, got_ref, merged_ref, inner_ref, *refs):
-    *outer_refs, bary_ref, updated_ref, staged_ref, sem = refs
+def ratio_kernel(merged_ref, inner_ref, *refs):
+    *outer_refs, ratio_ref, field_ref = refs
     members, lat = inner_ref.shape[1:]
-    groups = members // SUB
     odd = odd_core()
-    total = jnp.sum(got_ref[...], axis=0)
-    table = jnp.broadcast_to(total, (128, 128)).T
-    level = table[members : members + SUB, :]
     low = low_half((SUB, lat))
-    wide = lambda v: jnp.concatenate([v] * (lat // 128), axis=1)
-    inverse = wide(cells / level)
     outer, inner = [], []
     for c in range(REACH):
-        both = merged_ref[c] * inverse
+        both = merged_ref[c]
         swapped = pltpu.roll(both, SUB // 2, 0)
         outer.append(jnp.where(low, both, swapped))
         inner.append(jnp.where(low, swapped, both))
-    bary = from_outside(outer + inner, odd)
-    bary_ref[...] = jnp.swapaxes(jnp.stack(bary), 0, 1)[: SUB // 2]
+    merged = from_outside(outer + inner, odd)
+    field_ref[...] = jnp.swapaxes(jnp.stack(merged), 0, 1)[: SUB // 2]
+    for group in range(members // SUB):
+        quotients = Chunked(outer_refs).stack(group) + stack_of(inner_ref, group)
+        out = [m * quotient for m, quotient in zip(merged, from_outside(quotients, odd))]
+        ratio_ref[block_of(group), :] = jnp.swapaxes(jnp.stack(out), 0, 1).reshape(SUB * SUB, lat)
+
+
+def finish_kernel(cells, got_ref, ratio_ref, field_ref, bary_ref, updated_ref, factor_ref, staged_ref, sem):
+    lat = ratio_ref.shape[1]
+    groups = ratio_ref.shape[0] // (SUB * SUB)
+    members = groups * SUB
+    total = jnp.sum(got_ref[...], axis=0)
+    factor_ref[...] = jnp.broadcast_to(total, (128, 128)).T
+    level = 1.0 / factor_ref[members : members + SUB, :]
     for group in range(groups):
-        rows = slice(group * SUB, (group + 1) * SUB)
-        factor = wide(table[rows, :] / cells)
-        quotients = Chunked(outer_refs).stack(group) + stack_of(inner_ref, group)
-        out = [b * factor * quotient for b, quotient in zip(bary, from_outside(quotients, odd))]
-        span = pl.ds(group * SUB * SUB, SUB * SUB)
-        staged_ref[span, :] = jnp.swapaxes(jnp.stack(out), 0, 1).reshape(SUB * SUB, lat)
-        pltpu.make_async_copy(staged_ref.at[span, :], updated_ref.at[span, :], sem.at[group]).start()
+        factor_ref[rows_of(group), :] = factor_ref[rows_of(group), :] * level
+    factor_ref[members : members + SUB, :] = level * cells
+    wide = lambda n: jnp.concatenate([jnp.broadcast_to(factor_ref[n : n + 1, :], (SUB, 128))] * (lat // 128), axis=1)
+    copies = []
     for group in range(groups):
-        span = pl.ds(group * SUB * SUB, SUB * SUB)
-        pltpu.make_async_copy(staged_ref.at[span, :], updated_ref.at[span, :], sem.at[group]).wait()
+        for n in range(group * SUB, (group + 1) * SUB):
+            staged_ref[rows_of(n), :] = ratio_ref[rows_of(n), :] * wide(n)
+        span = block_of(group)
+        copies.append(pltpu.make_async_copy(staged_ref.at[span, :], updated_ref.at[span, :], sem.at[group]))
+        copies[-1].start()
+    for n in range(SUB // 2):
+        bary_ref[n] = field_ref[n] * wide(members + n)
+    for copy in copies:
+        copy.wait()
 
 
 def shape(*dims):
@@ -319,7 +341,7 @@
     scaling = scaling.reshape(rows * lon, lat)
     fields = fields.reshape(rows * lon, lat)
 
-    inner, *outer = call(spread_kernel, (half, *parts), scaling, coef)
+    inner, *outer = call(spread_kernel, (half, *parts), scaling)
     outer_halo = [lax.ppermute(part, "tile", with_neighbour) for part in outer]
     inner_halo = lax.ppermute(inner, "tile", with_mate)
     fields, inner = lax.optimization_barrier((fields, inner))
@@ -366,14 +388,19 @@
         inverses.append(inverse)
     other = lax.ppermute(logs, "mem", [(0, 1), (1, 0)])
     merged, payload = call(merge_kernel, (packed, shape(tiles, 1, 128)), logs, other, mass, coef)
+    ratio, field = call(ratio_kernel, (shape(rows * lon, lat), shape(levels, lon, lat)), merged, *inverses)
     got = lax.all_to_all(payload, "tile", split_axis=0, concat_axis=0)
     barycenter, updated = call(
         partial(finish_kernel, float(cells)),
         (shape(levels, lon, lat), shape(rows * lon, lat)),
         got,
-        merged,
-        *inverses,
-        scratch=[pltpu.VMEM((rows * lon, lat), jnp.float32), pltpu.SemaphoreType.DMA((rows // SUB,))],
+        ratio,
+        field,
+        scratch=[
+            pltpu.VMEM((128, 128), jnp.float32),
+            pltpu.VMEM((rows * lon, lat), jnp.float32),
+            pltpu.SemaphoreType.DMA((rows // SUB,)),
+        ],
         out_specs=(VMEM, HBM),
     )
     return barycenter, updated.reshape(members, levels, lon, lat)

time: 80.6 us -> 82.2 us (1.020)
  blocking collectives: 16.3 us -> 0 us
  starting transfers between devices: 16.2 us -> 24.2 us
  local copies, waits for them, and re-layouts: 3.22 us -> 8.25 us
  waiting for transfers between devices: 26.2 us -> 29.8 us
  Pallas kernels: 17.7 us -> 18.7 us
    all_to_all x1 -> x0, blocking collectives: 16.3 us -> none  [body(): got = lax.all_to_all(payload, 'tile', split_axis=0, concat_axis=0)]
    all_to_all x0 -> x1, starting transfers between devices: none -> 7.98 us  [body(): got = lax.all_to_all(payload, 'tile', split_axis=0, concat_axis=0)]
    unnamed x12 -> x26, local copies, waits for them, and re-layouts: 3.22 us -> 8.25 us
    all_to_all x0 -> x1, waiting for transfers between devices: none -> 3.66 us  [body(): got = lax.all_to_all(payload, 'tile', split_axis=0, concat_axis=0)]
    pallas_call x10 -> x11, Pallas kernels: 17.7 us -> 18.7 us  [call(): pl.pallas_call(kernel, out_shape=outs, in_specs=[SMEM if arg.ndim == 1 el...]
  transfers between devices with their start and end apart: 8 -> 9, of which waited for: 7 -> 8; matrix products, arithmetic and copies ran while one was open for 0% -> 0% of each run, Pallas kernels for 18% -> 18%
where the time goes in v14:
time: 82.2 us; the launch traced here: 81.8 us
  waiting for transfers between devices  29.8 us (36%)
  starting transfers between devices  24.2 us (29%)
  Pallas kernels  18.7 us (23%)
  local copies, waits for them, and re-layouts  8.25 us (10%)
  between operations  0.94 us (1%)
    ppermute x2, waiting for transfers between devices, body(): outer_halo = [lax.ppermute(part, 'tile', with_neighbour) for part in outer]  18.9 us
    pallas_call x11, Pallas kernels, call(): pl.pallas_call(kernel, out_shape=outs, in_specs=[SMEM if arg.ndim == 1 el...  18.7 us
    unnamed x26, local copies, waits for them, and re-layouts  8.25 us
    all_to_all x1, starting transfers between devices, body(): got = lax.all_to_all(payload, 'tile', split_axis=0, concat_axis=0)  7.98 us
    ppermute x3, starting transfers between devices, body(): lax.ppermute(value, 'tile', with_neighbour)  5.39 us
    ppermute x3, waiting for transfers between devices, body(): lax.ppermute(value, 'tile', with_neighbour)  4.77 us
    ppermute x1, starting transfers between devices, body(): v_inner_halo = lax.ppermute(v_inner, 'tile', with_mate)  4.54 us
    all_to_all x1, waiting for transfers between devices, body(): got = lax.all_to_all(payload, 'tile', split_axis=0, concat_axis=0)  3.66 us
  transfers between devices with their start and end apart: 9, of which 8 were waited for; matrix products, arithmetic and copies ran while one was open for 0% of the time, Pallas kernels for 18%

profile of v14, /device:TPU:1, one launch (start us, length us, event | category | flops | bytes accessed | tf_op | source)
XLA Modules:
  0.0 81.8 jit_solution(8488707882064895123)
XLA Ops:
  0.6 0.0 copy-start
  0.6 0.0 copy-start.1
  0.7 1.6 %copy-done.1 = f32[26,4,8,640]{3,2,1,0:T(8,128)S(1)} copy-done((f32[26,4,8,640]{3,2,1,0:T(8,128)S(1)}, f32[26,4,8,640]{3,2,1,0:T(8,128)}, u32[]{:S(2)}) %copy-start.1) | copy-done | bytes 2129944
  2.3 0.0 copy-start.11
  2.3 0.0 copy-start.12
  2.3 0.4 shard_map.68
  2.7 1.5 %collective-permute-start.1 = (f32[4,104,640]{2,1,0:T(8,128)S(1)}, f32[4,104,640]{2,1,0:T(8,128)S(1)}, u32[]{:S(2)}, u32[]{:S(2)}) collective-permute-start(f32[4,104,640]{2,1,0:T(8,128)S(1)} %get-tuple-element.35.inner_ref.scaled_ref), channel_id=1, source_target_pairs={{0,2},{2,0},{4,6},{6,4},{8,10},{10,8},{12,14},{14,12},{16,18},{18,... | collective-permute-start | bytes 3194888 | tf_op jit(solution)/shard_map/ppermute | solution.py:346
  4.2 1.7 %collective-permute-start.4 = (f32[4,56,640]{2,1,0:T(8,128)S(1)}, f32[4,56,640]{2,1,0:T(8,128)S(1)}, u32[]{:S(2)}, u32[]{:S(2)}) collective-permute-start(f32[4,56,640]{2,1,0:T(8,128)S(1)} %get-tuple-element.37.refs_0_.outer_ref.scaled_ref), channel_id=1, source_target_pairs={{0,126},{2,4},{4,2},{6,8},{8,6},{10,12},{12,10},{14,16},{16,14},{1... | collective-permute-start | bytes 1720328 | tf_op jit(solution)/shard_map/ppermute | solution.py:345
  5.9 0.6 collective-permute-done.1.halo_ref
  6.5 0.0 copy-done
  6.5 0.0 copy-done.11
  6.5 0.0 copy-done.12
  6.5 0.0 copy-start.2
  6.5 1.6 %copy-done.2 = f32[26,4,8,640]{3,2,1,0:T(8,128)S(1)} copy-done((f32[26,4,8,640]{3,2,1,0:T(8,128)S(1)}, f32[26,4,8,640]{3,2,1,0:T(8,128)}, u32[]{:S(2)}) %copy-start.2) | copy-done | bytes 2129944
  8.1 5.2 %shard_map.69 = (f32[4,104,640]{2,1,0:T(8,128)S(1)}, f32[6,104,640]{2,1,0:T(8,128)S(1)}, f32[4,104,640]{2,1,0:T(8,128)S(1)}, f32[104,128]{1,0:T(8,128)S(1)}, f32[112,128]{1,0:T(8,128)S(1)}) custom-call(f32[4,104,640]{2,1,0:T(8,128)S(1)} %collective-permute-done.1.halo_ref, f32[4,104,640]{2,1,0:T(8,128)S(1)} %get-tuple-element.35.inner_ref.scaled_ref, ...), custom_call_target="tpu_custom_call" | custom-call | tf_op jit(solution)/shard_map/pallas_call | solution.py:317
  13.3 4.5 %collective-permute-start.6 = (f32[4,104,640]{2,1,0:T(8,128)S(1)}, f32[4,104,640]{2,1,0:T(8,128)S(1)}, u32[]{:S(2)}, u32[]{:S(2)}) collective-permute-start(f32[4,104,640]{2,1,0:T(8,128)S(1)} %get-tuple-element.42.inner_ref), channel_id=1, source_target_pairs={{0,2},{2,0},{4,6},{6,4},{8,10},{10,8},{12,14},{14,12},{16,18},{18,... | collective-permute-start | bytes 3194888 | tf_op jit(solution)/shard_map/ppermute | solution.py:359
  17.9 0.0 collective-permute-start
  17.9 17.5 %collective-permute-done.4.halo_ref = f32[4,56,640]{2,1,0:T(8,128)S(1)} collective-permute-done((f32[4,56,640]{2,1,0:T(8,128)S(1)}, f32[4,56,640]{2,1,0:T(8,128)S(1)}, u32[]{:S(2)}, u32[]{:S(2)}) %collective-permute-start.4) | collective-permute-done | bytes 573472 | tf_op jit(solution)/shard_map/ppermute | solution.py:345
  35.3 1.3 %shard_map.71.refs_0_.outer_ref = f32[4,56,640]{2,1,0:T(8,128)S(1)} custom-call(f32[4,56,640]{2,1,0:T(8,128)S(1)} %collective-permute-done.4.halo_ref, f32[4,56,640]{2,1,0:T(8,128)S(1)} %get-tuple-element.37.refs_0_.outer_ref.scaled_ref, f32[6,104,640]{2,1,0:T(8,128)S(1)} %get-tuple-element.38.edge_ref, f32[4,104,640]{2,1,0:T(8,128)S(1)} %get-tuple-element.39.filled_ref, ...), custom_call_target="tpu_custom_call" | custom-call | tf_op jit(solution)/shard_map/pallas_call | solution.py:317
  36.7 2.6 %collective-permute-start.5 = (f32[4,56,640]{2,1,0:T(8,128)S(1)}, f32[4,56,640]{2,1,0:T(8,128)S(1)}, u32[]{:S(2)}, u32[]{:S(2)}) collective-permute-start(f32[4,56,640]{2,1,0:T(8,128)S(1)} %shard_map.71.refs_0_.outer_ref), channel_id=1, source_target_pairs={{0,126},{2,4},{4,2},{6,8},{8,6},{10,12},{12,10},{14,16},{16,14},{1... | collective-permute-start | bytes 1720328 | tf_op jit(solution)/shard_map/ppermute | solution.py:365
  39.2 1.4 %collective-permute-done.halo_ref = f32[4,48,640]{2,1,0:T(8,128)S(1)} collective-permute-done((f32[4,48,640]{2,1,0:T(8,128)S(1)}, f32[4,48,640]{2,1,0:T(8,128)S(1)}, u32[]{:S(2)}, u32[]{:S(2)}) %collective-permute-start) | collective-permute-done | bytes 491552 | tf_op jit(solution)/shard_map/ppermute | solution.py:345
  40.6 1.2 %shard_map.70 = (f32[4,32,640]{2,1,0:T(8,128)S(1)}, f32[4,16,640]{2,1,0:T(8,128)S(1)}) custom-call(f32[4,48,640]{2,1,0:T(8,128)S(1)} %collective-permute-done.halo_ref, f32[4,48,640]{2,1,0:T(8,128)S(1)} %get-tuple-element.33.refs_1_.outer_ref.scaled_ref, f32[6,104,640]{2,1,0:T(8,128)S(1)} %get-tuple-element.38.edge_ref, ...), custom_call_target="tpu_custom_call" | custom-call | tf_op jit(solution)/shard_map/pallas_call | solution.py:317
  41.8 2.6 %collective-permute-start.3 = (f32[4,32,640]{2,1,0:T(8,128)S(1)}, f32[4,32,640]{2,1,0:T(8,128)S(1)}, u32[]{:S(2)}, u32[]{:S(2)}) collective-permute-start(f32[4,32,640]{2,1,0:T(8,128)S(1)} %get-tuple-element.41.refs_1_.outer_ref), channel_id=1, source_target_pairs={{0,126},{2,4},{4,2},{6,8},{8,6},{10,12},{12,10},{14,16},{16,14},{1... | collective-permute-start | bytes 983048 | tf_op jit(solution)/shard_map/ppermute | solution.py:365
  44.3 0.3 collective-permute-start.2
  44.6 0.0 collective-permute-done.6.halo_ref
  44.6 4.3 %shard_map.72 = (f32[4,104,640]{2,1,0:T(8,128)S(1)}, f32[6,104,640]{2,1,0:T(8,128)S(1)}, f32[4,8,640]{2,1,0:T(8,128)S(1)}) custom-call(f32[4,104,640]{2,1,0:T(8,128)S(1)} %collective-permute-done.6.halo_ref, f32[4,104,640]{2,1,0:T(8,128)S(1)} %get-tuple-element.42.inner_ref, f32[4,104,640]{2,1,0:T(8,128)S(1)} %get-tuple-element.35.inner_ref.scaled_ref, ...), custom_call_target="tpu_custom_call" | custom-call | tf_op jit(solution)/shard_map/pallas_call | solution.py:317
  48.9 2.0 %collective-permute-done.5.halo_ref = f32[4,56,640]{2,1,0:T(8,128)S(1)} collective-permute-done((f32[4,56,640]{2,1,0:T(8,128)S(1)}, f32[4,56,640]{2,1,0:T(8,128)S(1)}, u32[]{:S(2)}, u32[]{:S(2)}) %collective-permute-start.5) | collective-permute-done | bytes 573472 | tf_op jit(solution)/shard_map/ppermute | solution.py:365
  50.9 1.4 %shard_map.73 = (f32[4,56,640]{2,1,0:T(8,128)S(1)}, f32[4,8,640]{2,1,0:T(8,128)S(1)}) custom-call(f32[4,56,640]{2,1,0:T(8,128)S(1)} %collective-permute-done.5.halo_ref, f32[4,56,640]{2,1,0:T(8,128)S(1)} %shard_map.71.refs_0_.outer_ref, f32[6,104,640]{2,1,0:T(8,128)S(1)} %get-tuple-element.44.edge_ref, ...), custom_call_target="tpu_custom_call" | custom-call | tf_op jit(solution)/shard_map/pallas_call | solution.py:317
  52.3 0.0 copy-start.3
  52.3 1.8 %collective-permute-done.3.halo_ref = f32[4,32,640]{2,1,0:T(8,128)S(1)} collective-permute-done((f32[4,32,640]{2,1,0:T(8,128)S(1)}, f32[4,32,640]{2,1,0:T(8,128)S(1)}, u32[]{:S(2)}, u32[]{:S(2)}) %collective-permute-start.3) | collective-permute-done | bytes 327712 | tf_op jit(solution)/shard_map/ppermute | solution.py:365
  54.1 0.8 shard_map.74
  55.0 0.9 %collective-permute-done.2.halo_ref = f32[4,16,640]{2,1,0:T(8,128)S(1)} collective-permute-done((f32[4,16,640]{2,1,0:T(8,128)S(1)}, f32[4,16,640]{2,1,0:T(8,128)S(1)}, u32[]{:S(2)}, u32[]{:S(2)}) %collective-permute-start.2) | collective-permute-done | bytes 163872 | tf_op jit(solution)/shard_map/ppermute | solution.py:365
  55.9 0.5 shard_map.75
  56.4 0.0 copy-done.3
  56.4 0.0 copy-start.5
  56.4 3.0 %collective-permute-start.7 = (f32[168,128]{1,0:T(8,128)S(1)}, f32[168,128]{1,0:T(8,128)S(1)}, u32[]{:S(2)}, u32[]{:S(2)}) collective-permute-start(f32[168,128]{1,0:T(8,128)S(1)} %get-tuple-element.52.own_ref), channel_id=1, source_target_pairs={{0,1},{1,0},{2,3},{3,2},{4,5},{5,4},{6,7},{7,6},{8,9},{9,8},{10,11... | collective-permute-start | bytes 258056 | tf_op jit(solution)/shard_map/ppermute | solution.py:389
  59.4 1.9 %collective-permute-done.7.other_ref = f32[168,128]{1,0:T(8,128)S(1)} collective-permute-done((f32[168,128]{1,0:T(8,128)S(1)}, f32[168,128]{1,0:T(8,128)S(1)}, u32[]{:S(2)}, u32[]{:S(2)}) %collective-permute-start.7) | collective-permute-done | bytes 86048 | tf_op jit(solution)/shard_map/ppermute | solution.py:389
  61.3 0.7 shard_map.76
  62.1 0.0 copy-done.5
  62.1 0.0 copy-start.7
  62.1 0.6 copy-done.7
  62.7 8.0 %all-to-all-start = ((f32[64,1,128]{2,1,0:T(1,128)}), f32[64,1,128]{2,1,0:T(1,128)S(1)}, u32[]{:S(2)}, u32[]{:S(2)}) async-start(f32[64,1,128]{2,1,0:T(1,128)} %get-tuple-element.54), calls=%async_computation | async-start | bytes 65536 | tf_op jit(solution)/shard_map/all_to_all | solution.py:392
  70.7 0.0 copy-start.4
  70.7 1.1 %copy-done.4 = f32[4,56,640]{2,1,0:T(8,128)S(1)} copy-done((f32[4,56,640]{2,1,0:T(8,128)S(1)}, f32[4,56,640]{2,1,0:T(8,128)}, u32[]{:S(2)}) %copy-start.4) | copy-done | bytes 573464
  71.8 0.0 copy-start.6
  71.8 0.9 %copy-done.6 = f32[4,16,640]{2,1,0:T(8,128)S(1)} copy-done((f32[4,16,640]{2,1,0:T(8,128)S(1)}, f32[4,16,640]{2,1,0:T(8,128)}, u32[]{:S(2)}) %copy-start.6) | copy-done | bytes 163864
  72.7 0.0 copy-start.8
  72.7 0.9 %copy-done.8 = f32[4,8,640]{2,1,0:T(8,128)S(1)} copy-done((f32[4,8,640]{2,1,0:T(8,128)S(1)}, f32[4,8,640]{2,1,0:T(8,128)}, u32[]{:S(2)}) %copy-start.8) | copy-done | bytes 81944
  73.6 0.6 shard_map.77
  74.1 0.0 copy-start.9
  74.1 0.6 copy-done.9
  74.8 3.7 %all-to-all-done.got_ref = f32[64,1,128]{2,1,0:T(1,128)S(1)} async-done(((f32[64,1,128]{2,1,0:T(1,128)}), f32[64,1,128]{2,1,0:T(1,128)S(1)}, u32[]{:S(2)}, u32[]{:S(2)}) %all-to-all-start) | async-done | bytes 32800 | tf_op jit(solution)/shard_map/all_to_all | solution.py:392
  78.4 0.0 copy-start.10
  78.4 0.9 %copy-done.10 = f32[4,8,640]{2,1,0:T(8,128)S(1)} copy-done((f32[4,8,640]{2,1,0:T(8,128)S(1)}, f32[4,8,640]{2,1,0:T(8,128)}, u32[]{:S(2)}) %copy-start.10) | copy-done | bytes 81944
  79.3 2.4 %shard_map.78 = (f32[4,8,640]{2,1,0:T(8,128)}, f32[832,640]{1,0:T(8,128)}) custom-call(f32[64,1,128]{2,1,0:T(1,128)S(1)} %all-to-all-done.got_ref, f32[832,640]{1,0:T(8,128)S(1)} %get-tuple-element.60.ratio_ref, f32[4,8,640]{2,1,0:T(8,128)S(1)} %copy-done.10), custom_call_target="tpu_custom_call" | custom-call | tf_op jit(solution)/shard_map/pallas_call | solution.py:317
Async XLA Ops:
  0.6 5.9 %copy-start = (f32[5,8,640]{2,1,0:T(8,128)S(1)}, f32[5,8,640]{2,1,0:T(8,128)}, u32[]{:S(2)}) copy-start(f32[5,8,640]{2,1,0:T(8,128)} %constant.2.clone.coef_ref) | copy-start | bytes 307204
  0.6 1.6 %copy-start.1 = (f32[26,4,8,640]{3,2,1,0:T(8,128)S(1)}, f32[26,4,8,640]{3,2,1,0:T(8,128)}, u32[]{:S(2)}) copy-start(f32[26,4,8,640]{3,2,1,0:T(8,128)} %param.6) | copy-start | bytes 6389764
  2.3 4.2 %copy-start.11 = (s32[8,640]{1,0:T(8,128)S(1)}, s32[8,640]{1,0:T(8,128)}, u32[]{:S(2)}) copy-start(s32[8,640]{1,0:T(8,128)} %mask_ref.1) | copy-start | bytes 61444
  2.3 4.2 %copy-start.12 = (s32[26]{0:T(128)S(1)}, s32[26]{0:T(128)}, u32[]{:S(2)}) copy-start(s32[26]{0:T(128)} %count_ref.1) | copy-start | bytes 316
  2.7 3.8 %collective-permute-start.1 = (f32[4,104,640]{2,1,0:T(8,128)S(1)}, f32[4,104,640]{2,1,0:T(8,128)S(1)}, u32[]{:S(2)}, u32[]{:S(2)}) collective-permute-start(f32[4,104,640]{2,1,0:T(8,128)S(1)} %get-tuple-element.35.inner_ref.scaled_ref), channel_id=1, source_target_pairs={{0,2},{2,0},{4,6},{6,4},{8,10},{10,8},{12,14},{14,12},{16,18},{18,... | collective-permute-start | bytes 3194888 | tf_op jit(solution)/shard_map/ppermute | solution.py:346
  4.2 31.2 %collective-permute-start.4 = (f32[4,56,640]{2,1,0:T(8,128)S(1)}, f32[4,56,640]{2,1,0:T(8,128)S(1)}, u32[]{:S(2)}, u32[]{:S(2)}) collective-permute-start(f32[4,56,640]{2,1,0:T(8,128)S(1)} %get-tuple-element.37.refs_0_.outer_ref.scaled_ref), channel_id=1, source_target_pairs={{0,126},{2,4},{4,2},{6,8},{8,6},{10,12},{12,10},{14,16},{16,14},{1... | collective-permute-start | bytes 1720328 | tf_op jit(solution)/shard_map/ppermute | solution.py:345
  6.5 1.6 %copy-start.2 = (f32[26,4,8,640]{3,2,1,0:T(8,128)S(1)}, f32[26,4,8,640]{3,2,1,0:T(8,128)}, u32[]{:S(2)}) copy-start(f32[26,4,8,640]{3,2,1,0:T(8,128)} %param.5) | copy-start | bytes 6389764
  13.3 31.3 %collective-permute-start.6 = (f32[4,104,640]{2,1,0:T(8,128)S(1)}, f32[4,104,640]{2,1,0:T(8,128)S(1)}, u32[]{:S(2)}, u32[]{:S(2)}) collective-permute-start(f32[4,104,640]{2,1,0:T(8,128)S(1)} %get-tuple-element.42.inner_ref), channel_id=1, source_target_pairs={{0,2},{2,0},{4,6},{6,4},{8,10},{10,8},{12,14},{14,12},{16,18},{18,... | collective-permute-start | bytes 3194888 | tf_op jit(solution)/shard_map/ppermute | solution.py:359
  17.9 22.7 %collective-permute-start = (f32[4,48,640]{2,1,0:T(8,128)S(1)}, f32[4,48,640]{2,1,0:T(8,128)S(1)}, u32[]{:S(2)}, u32[]{:S(2)}) collective-permute-start(f32[4,48,640]{2,1,0:T(8,128)S(1)} %get-tuple-element.33.refs_1_.outer_ref.scaled_ref), channel_id=1, source_target_pairs={{0,126},{2,4},{4,2},{6,8},{8,6},{10,12},{12,10},{14,16},{16,14},{1... | collective-permute-start | bytes 1474568 | tf_op jit(solution)/shard_map/ppermute | solution.py:345
  36.7 14.3 %collective-permute-start.5 = (f32[4,56,640]{2,1,0:T(8,128)S(1)}, f32[4,56,640]{2,1,0:T(8,128)S(1)}, u32[]{:S(2)}, u32[]{:S(2)}) collective-permute-start(f32[4,56,640]{2,1,0:T(8,128)S(1)} %shard_map.71.refs_0_.outer_ref), channel_id=1, source_target_pairs={{0,126},{2,4},{4,2},{6,8},{8,6},{10,12},{12,10},{14,16},{16,14},{1... | collective-permute-start | bytes 1720328 | tf_op jit(solution)/shard_map/ppermute | solution.py:365
  41.8 12.4 %collective-permute-start.3 = (f32[4,32,640]{2,1,0:T(8,128)S(1)}, f32[4,32,640]{2,1,0:T(8,128)S(1)}, u32[]{:S(2)}, u32[]{:S(2)}) collective-permute-start(f32[4,32,640]{2,1,0:T(8,128)S(1)} %get-tuple-element.41.refs_1_.outer_ref), channel_id=1, source_target_pairs={{0,126},{2,4},{4,2},{6,8},{8,6},{10,12},{12,10},{14,16},{16,14},{1... | collective-permute-start | bytes 983048 | tf_op jit(solution)/shard_map/ppermute | solution.py:365
  44.3 11.6 %collective-permute-start.2 = (f32[4,16,640]{2,1,0:T(8,128)S(1)}, f32[4,16,640]{2,1,0:T(8,128)S(1)}, u32[]{:S(2)}, u32[]{:S(2)}) collective-permute-start(f32[4,16,640]{2,1,0:T(8,128)S(1)} %get-tuple-element.40.refs_2_.outer_ref), channel_id=1, source_target_pairs={{0,126},{2,4},{4,2},{6,8},{8,6},{10,12},{12,10},{14,16},{16,14},{1... | collective-permute-start | bytes 491528 | tf_op jit(solution)/shard_map/ppermute | solution.py:365
  52.3 4.1 %copy-start.3 = (f32[4,56,640]{2,1,0:T(8,128)}, f32[4,56,640]{2,1,0:T(8,128)S(1)}, u32[]{:S(2)}) copy-start(f32[4,56,640]{2,1,0:T(8,128)S(1)} %get-tuple-element.57.refs_0_) | copy-start | bytes 1720324
  56.4 5.7 %copy-start.5 = (f32[4,16,640]{2,1,0:T(8,128)}, f32[4,16,640]{2,1,0:T(8,128)S(1)}, u32[]{:S(2)}) copy-start(f32[4,16,640]{2,1,0:T(8,128)S(1)} %get-tuple-element.59.refs_2_) | copy-start | bytes 491524
  56.4 4.9 %collective-permute-start.7 = (f32[168,128]{1,0:T(8,128)S(1)}, f32[168,128]{1,0:T(8,128)S(1)}, u32[]{:S(2)}, u32[]{:S(2)}) collective-permute-start(f32[168,128]{1,0:T(8,128)S(1)} %get-tuple-element.52.own_ref), channel_id=1, source_target_pairs={{0,1},{1,0},{2,3},{3,2},{4,5},{5,4},{6,7},{7,6},{8,9},{9,8},{10,11... | collective-permute-start | bytes 258056 | tf_op jit(solution)/shard_map/ppermute | solution.py:389
  62.1 0.6 copy-start.7
  62.7 15.7 %all-to-all-start = ((f32[64,1,128]{2,1,0:T(1,128)}), f32[64,1,128]{2,1,0:T(1,128)S(1)}, u32[]{:S(2)}, u32[]{:S(2)}) async-start(f32[64,1,128]{2,1,0:T(1,128)} %get-tuple-element.54), calls=%async_computation | async-start | bytes 65536 | tf_op jit(solution)/shard_map/all_to_all | solution.py:392
  70.7 1.1 %copy-start.4 = (f32[4,56,640]{2,1,0:T(8,128)S(1)}, f32[4,56,640]{2,1,0:T(8,128)}, u32[]{:S(2)}) copy-start(f32[4,56,640]{2,1,0:T(8,128)} %copy-done.3) | copy-start | bytes 1720324
  71.8 0.9 %copy-start.6 = (f32[4,16,640]{2,1,0:T(8,128)S(1)}, f32[4,16,640]{2,1,0:T(8,128)}, u32[]{:S(2)}) copy-start(f32[4,16,640]{2,1,0:T(8,128)} %copy-done.5) | copy-start | bytes 491524
  72.7 0.9 %copy-start.8 = (f32[4,8,640]{2,1,0:T(8,128)S(1)}, f32[4,8,640]{2,1,0:T(8,128)}, u32[]{:S(2)}) copy-start(f32[4,8,640]{2,1,0:T(8,128)} %copy-done.7) | copy-start | bytes 245764
  74.1 0.6 copy-start.9
  78.4 0.9 %copy-start.10 = (f32[4,8,640]{2,1,0:T(8,128)S(1)}, f32[4,8,640]{2,1,0:T(8,128)}, u32[]{:S(2)}) copy-start(f32[4,8,640]{2,1,0:T(8,128)} %copy-done.9) | copy-start | bytes 245764

commit v15 on v13

--- a/solution.py
+++ b/solution.py
@@ -94,13 +94,12 @@
     return lax.broadcasted_iota(jnp.int32, shape, 0) < SUB // 2
 
 
-def spread_kernel(scaling_ref, coef_ref, inner_ref, *outer_refs):
+def spread_kernel(scaling_ref, inner_ref, *outer_refs):
     groups, lat = inner_ref.shape[1] // SUB, inner_ref.shape[2]
     odd = odd_core()
     outer = Chunked(outer_refs)
     for group in range(groups):
         columns = from_outside(by_longitude(scaling_ref[block_of(group), :], lat), odd)
-        columns = [column * coef_ref[AREA] for column in columns]
         outer.put(group, columns[:REACH])
         for c in range(REACH):
             inner_ref[c, rows_of(group), :] = columns[c + REACH]
@@ -125,9 +124,18 @@
     ]
 
 
-def inner_half(batch, halo_ref, inner_ref, outer_refs, coef_ref, edge_ref):
+def unit(values, coef_ref):
+    return values
+
+
+def by_area(values, coef_ref):
+    return [value * coef_ref[AREA] for value in values]
+
+
+def inner_half(batch, halo_ref, inner_ref, outer_refs, coef_ref, edge_ref, weigh=unit):
     outer = Chunked(outer_refs)
     columns = [outer.stack(g) + stack_of(inner_ref, g) + stack_of(halo_ref, g, (3, 2, 1, 0)) for g in batch]
+    columns = [weigh(own, coef_ref) for own in columns]
     for s in range(REACH):
         columns = [diffuse(own, coef_ref) for own in columns]
         if s < REACH - 1:
@@ -137,8 +145,9 @@
     return zip(batch, columns)
 
 
-def outer_half(batch, first, halo_ref, outer_ref, edge_ref, coef_ref):
+def outer_half(batch, first, halo_ref, outer_ref, edge_ref, coef_ref, weigh=unit):
     columns = [stack_of(halo_ref, g - first, (3, 2, 1, 0)) + stack_of(outer_ref, g - first, (0, 1)) for g in batch]
+    columns = [weigh(own, coef_ref) for own in columns]
     for s in range(REACH):
         columns = [diffuse(own, coef_ref) for own in columns]
         if s < REACH - 1:
@@ -159,7 +168,9 @@
     count = sum(count_ref[m] for m in range(2 * groups)).astype(jnp.float32)
     weight_ref[rows_of(groups), :] = jnp.full((SUB, 128), count)
     for batch in batches(groups):
-        for group, smoothed in inner_half(batch, halo_ref, inner_ref, outer_refs, coef_ref, edge_ref):
+        for group, smoothed in inner_half(
+            batch, halo_ref, inner_ref, outer_refs, coef_ref, edge_ref, by_area
+        ):
             fields = by_longitude(fields_ref[block_of(group), :], lat)
             filled = []
             for c in range(2 * REACH):
@@ -176,7 +187,7 @@
     last = first + outer_ref.shape[1] // SUB
     out = Chunked(out_refs)
     for batch in batches(last, first):
-        for group, smoothed in outer_half(batch, first, halo_ref, outer_ref, edge_ref, coef_ref):
+        for group, smoothed in outer_half(batch, first, halo_ref, outer_ref, edge_ref, coef_ref, by_area):
             filled = stack_of(filled_ref, group)
             out.put(group - first, [top / bottom for top, bottom in zip(filled, smoothed)])
 
@@ -245,9 +256,9 @@
     for c in range(REACH):
         for t in range(tiles):
             span = slice(t * 128, (t + 1) * 128)
-            weighted = jnp.exp(both(c * tiles + t) * scale)
-            merged_ref[c, :, span] = weighted / coef_ref[AREA, :, span]
-            level = level + weighted
+            merged = jnp.exp(both(c * tiles + t) * scale)
+            merged_ref[c, :, span] = merged
+            level = level + merged * coef_ref[AREA, :, span]
     level = level + pltpu.roll(level, SUB // 2, 0)
     spare = jnp.zeros((128 - members - SUB, 128), jnp.float32)
     table = jnp.concatenate([mass_ref[...], level, spare], axis=0)
@@ -319,7 +330,7 @@
     scaling = scaling.reshape(rows * lon, lat)
     fields = fields.reshape(rows * lon, lat)
 
-    inner, *outer = call(spread_kernel, (half, *parts), scaling, coef)
+    inner, *outer = call(spread_kernel, (half, *parts), scaling)
     outer_halo = [lax.ppermute(part, "tile", with_neighbour) for part in outer]
     inner_halo = lax.ppermute(inner, "tile", with_mate)
     fields, inner = lax.optimization_barrier((fields, inner))

time: 80.6 us -> 79.6 us (0.988)
    unnamed x12 -> x10, local copies, waits for them, and re-layouts: 3.22 us -> 3.2 us
where the time goes in v15:
time: 79.6 us; the launch traced here: 79.4 us
  waiting for transfers between devices  26.1 us (33%)
  Pallas kernels  17.5 us (22%)
  starting transfers between devices  16.2 us (20%)
  blocking collectives  15.5 us (19%)
  local copies, waits for them, and re-layouts  3.2 us (4%)
  between operations  0.88 us (1%)
    ppermute x2, waiting for transfers between devices, body(): outer_halo = [lax.ppermute(part, 'tile', with_neighbour) for part in outer]  18.9 us
    pallas_call x10, Pallas kernels, call(): pl.pallas_call(kernel, out_shape=outs, in_specs=[SMEM if arg.ndim == 1 el...  17.5 us
    all_to_all x1, blocking collectives, body(): got = lax.all_to_all(payload, 'tile', split_axis=0, concat_axis=0)  15.5 us
    ppermute x3, starting transfers between devices, body(): lax.ppermute(value, 'tile', with_neighbour)  5.39 us
    ppermute x3, waiting for transfers between devices, body(): lax.ppermute(value, 'tile', with_neighbour)  4.78 us
    ppermute x1, starting transfers between devices, body(): v_inner_halo = lax.ppermute(v_inner, 'tile', with_mate)  4.54 us
    unnamed x10, local copies, waits for them, and re-layouts  3.2 us
    ppermute x1, starting transfers between devices, body(): other = lax.ppermute(logs, 'mem', [(0, 1), (1, 0)])  3.03 us
  transfers between devices with their start and end apart: 8, of which 7 were waited for; matrix products, arithmetic and copies ran while one was open for 0% of the time, Pallas kernels for 18%

profile of v15, /device:TPU:1, one launch (start us, length us, event | category | flops | bytes accessed | tf_op | source)
XLA Modules:
  0.0 79.4 jit_solution(3637523485702252442)
XLA Ops:
  0.6 0.0 copy-start.1
  0.6 1.6 %copy-done.1 = f32[26,4,8,640]{3,2,1,0:T(8,128)S(1)} copy-done((f32[26,4,8,640]{3,2,1,0:T(8,128)S(1)}, f32[26,4,8,640]{3,2,1,0:T(8,128)}, u32[]{:S(2)}) %copy-start.1) | copy-done | bytes 2129944
  2.2 0.0 copy-start
  2.2 0.0 copy-start.3
  2.2 0.0 copy-start.4
  2.2 0.4 shard_map.68
  2.6 1.5 %collective-permute-start.1 = (f32[4,104,640]{2,1,0:T(8,128)S(1)}, f32[4,104,640]{2,1,0:T(8,128)S(1)}, u32[]{:S(2)}, u32[]{:S(2)}) collective-permute-start(f32[4,104,640]{2,1,0:T(8,128)S(1)} %get-tuple-element.33.inner_ref.scaled_ref), channel_id=1, source_target_pairs={{0,2},{2,0},{4,6},{6,4},{8,10},{10,8},{12,14},{14,12},{16,18},{18,... | collective-permute-start | bytes 3194888 | tf_op jit(solution)/shard_map/ppermute | solution.py:335
  4.1 1.7 %collective-permute-start.4 = (f32[4,56,640]{2,1,0:T(8,128)S(1)}, f32[4,56,640]{2,1,0:T(8,128)S(1)}, u32[]{:S(2)}, u32[]{:S(2)}) collective-permute-start(f32[4,56,640]{2,1,0:T(8,128)S(1)} %get-tuple-element.35.refs_0_.outer_ref.scaled_ref), channel_id=1, source_target_pairs={{0,126},{2,4},{4,2},{6,8},{8,6},{10,12},{12,10},{14,16},{16,14},{1... | collective-permute-start | bytes 1720328 | tf_op jit(solution)/shard_map/ppermute | solution.py:334
  5.8 0.6 collective-permute-done.1.halo_ref
  6.4 0.0 copy-done
  6.4 0.0 copy-done.3
  6.4 0.0 copy-done.4
  6.4 0.0 copy-start.2
  6.5 1.6 %copy-done.2 = f32[26,4,8,640]{3,2,1,0:T(8,128)S(1)} copy-done((f32[26,4,8,640]{3,2,1,0:T(8,128)S(1)}, f32[26,4,8,640]{3,2,1,0:T(8,128)}, u32[]{:S(2)}) %copy-start.2) | copy-done | bytes 2129944
  8.0 5.2 %shard_map.69 = (f32[4,104,640]{2,1,0:T(8,128)S(1)}, f32[6,104,640]{2,1,0:T(8,128)S(1)}, f32[4,104,640]{2,1,0:T(8,128)S(1)}, f32[104,128]{1,0:T(8,128)S(1)}, f32[112,128]{1,0:T(8,128)S(1)}) custom-call(f32[4,104,640]{2,1,0:T(8,128)S(1)} %collective-permute-done.1.halo_ref, f32[4,104,640]{2,1,0:T(8,128)S(1)} %get-tuple-element.33.inner_ref.scaled_ref, ...), custom_call_target="tpu_custom_call" | custom-call | tf_op jit(solution)/shard_map/pallas_call | solution.py:306
  13.3 4.5 %collective-permute-start.6 = (f32[4,104,640]{2,1,0:T(8,128)S(1)}, f32[4,104,640]{2,1,0:T(8,128)S(1)}, u32[]{:S(2)}, u32[]{:S(2)}) collective-permute-start(f32[4,104,640]{2,1,0:T(8,128)S(1)} %get-tuple-element.40.inner_ref), channel_id=1, source_target_pairs={{0,2},{2,0},{4,6},{6,4},{8,10},{10,8},{12,14},{14,12},{16,18},{18,... | collective-permute-start | bytes 3194888 | tf_op jit(solution)/shard_map/ppermute | solution.py:348
  17.8 0.0 collective-permute-start
  17.8 17.5 %collective-permute-done.4.halo_ref = f32[4,56,640]{2,1,0:T(8,128)S(1)} collective-permute-done((f32[4,56,640]{2,1,0:T(8,128)S(1)}, f32[4,56,640]{2,1,0:T(8,128)S(1)}, u32[]{:S(2)}, u32[]{:S(2)}) %collective-permute-start.4) | collective-permute-done | bytes 573472 | tf_op jit(solution)/shard_map/ppermute | solution.py:334
  35.3 1.3 %shard_map.71.refs_0_.outer_ref = f32[4,56,640]{2,1,0:T(8,128)S(1)} custom-call(f32[4,56,640]{2,1,0:T(8,128)S(1)} %collective-permute-done.4.halo_ref, f32[4,56,640]{2,1,0:T(8,128)S(1)} %get-tuple-element.35.refs_0_.outer_ref.scaled_ref, f32[6,104,640]{2,1,0:T(8,128)S(1)} %get-tuple-element.36.edge_ref, f32[4,104,640]{2,1,0:T(8,128)S(1)} %get-tuple-element.37.filled_ref, ...), custom_call_target="tpu_custom_call" | custom-call | tf_op jit(solution)/shard_map/pallas_call | solution.py:306
  36.6 2.6 %collective-permute-start.5 = (f32[4,56,640]{2,1,0:T(8,128)S(1)}, f32[4,56,640]{2,1,0:T(8,128)S(1)}, u32[]{:S(2)}, u32[]{:S(2)}) collective-permute-start(f32[4,56,640]{2,1,0:T(8,128)S(1)} %shard_map.71.refs_0_.outer_ref), channel_id=1, source_target_pairs={{0,126},{2,4},{4,2},{6,8},{8,6},{10,12},{12,10},{14,16},{16,14},{1... | collective-permute-start | bytes 1720328 | tf_op jit(solution)/shard_map/ppermute | solution.py:354
  39.2 1.4 %collective-permute-done.halo_ref = f32[4,48,640]{2,1,0:T(8,128)S(1)} collective-permute-done((f32[4,48,640]{2,1,0:T(8,128)S(1)}, f32[4,48,640]{2,1,0:T(8,128)S(1)}, u32[]{:S(2)}, u32[]{:S(2)}) %collective-permute-start) | collective-permute-done | bytes 491552 | tf_op jit(solution)/shard_map/ppermute | solution.py:334
  40.6 1.2 %shard_map.70 = (f32[4,32,640]{2,1,0:T(8,128)S(1)}, f32[4,16,640]{2,1,0:T(8,128)S(1)}) custom-call(f32[4,48,640]{2,1,0:T(8,128)S(1)} %collective-permute-done.halo_ref, f32[4,48,640]{2,1,0:T(8,128)S(1)} %get-tuple-element.31.refs_1_.outer_ref.scaled_ref, f32[6,104,640]{2,1,0:T(8,128)S(1)} %get-tuple-element.36.edge_ref, ...), custom_call_target="tpu_custom_call" | custom-call | tf_op jit(solution)/shard_map/pallas_call | solution.py:306
  41.7 2.6 %collective-permute-start.3 = (f32[4,32,640]{2,1,0:T(8,128)S(1)}, f32[4,32,640]{2,1,0:T(8,128)S(1)}, u32[]{:S(2)}, u32[]{:S(2)}) collective-permute-start(f32[4,32,640]{2,1,0:T(8,128)S(1)} %get-tuple-element.39.refs_1_.outer_ref), channel_id=1, source_target_pairs={{0,126},{2,4},{4,2},{6,8},{8,6},{10,12},{12,10},{14,16},{16,14},{1... | collective-permute-start | bytes 983048 | tf_op jit(solution)/shard_map/ppermute | solution.py:354
  44.3 0.3 collective-permute-start.2
  44.6 0.0 collective-permute-done.6.halo_ref
  44.6 4.3 %shard_map.72 = (f32[4,104,640]{2,1,0:T(8,128)S(1)}, f32[6,104,640]{2,1,0:T(8,128)S(1)}, f32[4,8,640]{2,1,0:T(8,128)S(1)}) custom-call(f32[4,104,640]{2,1,0:T(8,128)S(1)} %collective-permute-done.6.halo_ref, f32[4,104,640]{2,1,0:T(8,128)S(1)} %get-tuple-element.40.inner_ref, f32[4,104,640]{2,1,0:T(8,128)S(1)} %get-tuple-element.33.inner_ref.scaled_ref, ...), custom_call_target="tpu_custom_call" | custom-call | tf_op jit(solution)/shard_map/pallas_call | solution.py:306
  48.9 2.0 %collective-permute-done.5.halo_ref = f32[4,56,640]{2,1,0:T(8,128)S(1)} collective-permute-done((f32[4,56,640]{2,1,0:T(8,128)S(1)}, f32[4,56,640]{2,1,0:T(8,128)S(1)}, u32[]{:S(2)}, u32[]{:S(2)}) %collective-permute-start.5) | collective-permute-done | bytes 573472 | tf_op jit(solution)/shard_map/ppermute | solution.py:354
  50.9 1.4 %shard_map.73 = (f32[4,56,640]{2,1,0:T(8,128)S(1)}, f32[4,8,640]{2,1,0:T(8,128)S(1)}) custom-call(f32[4,56,640]{2,1,0:T(8,128)S(1)} %collective-permute-done.5.halo_ref, f32[4,56,640]{2,1,0:T(8,128)S(1)} %shard_map.71.refs_0_.outer_ref, f32[6,104,640]{2,1,0:T(8,128)S(1)} %get-tuple-element.42.edge_ref, ...), custom_call_target="tpu_custom_call" | custom-call | tf_op jit(solution)/shard_map/pallas_call | solution.py:306
  52.2 1.9 %collective-permute-done.3.halo_ref = f32[4,32,640]{2,1,0:T(8,128)S(1)} collective-permute-done((f32[4,32,640]{2,1,0:T(8,128)S(1)}, f32[4,32,640]{2,1,0:T(8,128)S(1)}, u32[]{:S(2)}, u32[]{:S(2)}) %collective-permute-start.3) | collective-permute-done | bytes 327712 | tf_op jit(solution)/shard_map/ppermute | solution.py:354
  54.1 0.8 %shard_map.74 = (f32[4,32,640]{2,1,0:T(8,128)S(1)}, f32[4,8,640]{2,1,0:T(8,128)S(1)}) custom-call(f32[4,32,640]{2,1,0:T(8,128)S(1)} %collective-permute-done.3.halo_ref, f32[4,32,640]{2,1,0:T(8,128)S(1)} %get-tuple-element.39.refs_1_.outer_ref, f32[6,104,640]{2,1,0:T(8,128)S(1)} %get-tuple-element.42.edge_ref, ...), custom_call_target="tpu_custom_call" | custom-call | tf_op jit(solution)/shard_map/pallas_call | solution.py:306
  54.9 0.9 %collective-permute-done.2.halo_ref = f32[4,16,640]{2,1,0:T(8,128)S(1)} collective-permute-done((f32[4,16,640]{2,1,0:T(8,128)S(1)}, f32[4,16,640]{2,1,0:T(8,128)S(1)}, u32[]{:S(2)}, u32[]{:S(2)}) %collective-permute-start.2) | collective-permute-done | bytes 163872 | tf_op jit(solution)/shard_map/ppermute | solution.py:354
  55.9 0.5 shard_map.75
  56.3 3.0 %collective-permute-start.7 = (f32[168,128]{1,0:T(8,128)S(1)}, f32[168,128]{1,0:T(8,128)S(1)}, u32[]{:S(2)}, u32[]{:S(2)}) collective-permute-start(f32[168,128]{1,0:T(8,128)S(1)} %get-tuple-element.50.own_ref), channel_id=1, source_target_pairs={{0,1},{1,0},{2,3},{3,2},{4,5},{5,4},{6,7},{7,6},{8,9},{9,8},{10,11... | collective-permute-start | bytes 258056 | tf_op jit(solution)/shard_map/ppermute | solution.py:378
  59.4 1.9 %collective-permute-done.7.other_ref = f32[168,128]{1,0:T(8,128)S(1)} collective-permute-done((f32[168,128]{1,0:T(8,128)S(1)}, f32[168,128]{1,0:T(8,128)S(1)}, u32[]{:S(2)}, u32[]{:S(2)}) %collective-permute-start.7) | collective-permute-done | bytes 86048 | tf_op jit(solution)/shard_map/ppermute | solution.py:378
  61.3 0.1 shard_map.76
  61.4 15.5 %all_to_all.5.got_ref = f32[64,1,128]{2,1,0:T(1,128)S(1)} all-to-all(f32[64,1,128]{2,1,0:T(1,128)S(1)} %get-tuple-element.52), channel_id=1, replica_groups=mesh['tile'=64,'mem'=2] {'tile'}, dimensions={0} | all-to-all | bytes 65536 | tf_op jit(solution)/shard_map/all_to_all | solution.py:380
  76.9 2.3 %shard_map.77 = (f32[4,8,640]{2,1,0:T(8,128)}, f32[832,640]{1,0:T(8,128)}) custom-call(f32[64,1,128]{2,1,0:T(1,128)S(1)} %all_to_all.5.got_ref, f32[4,8,640]{2,1,0:T(8,128)S(1)} %get-tuple-element.53.merged_ref, f32[4,104,640]{2,1,0:T(8,128)S(1)} %get-tuple-element.54.inner_ref, f32[4,56,640]{2,1,0:T(8,128)S(1)} %get-tuple-element.55.refs_0_, ...), custom_call_target="tpu_custom_call" | custom-call | tf_op jit(solution)/shard_map/pallas_call | solution.py:306
Async XLA Ops:
  0.6 1.6 %copy-start.1 = (f32[26,4,8,640]{3,2,1,0:T(8,128)S(1)}, f32[26,4,8,640]{3,2,1,0:T(8,128)}, u32[]{:S(2)}) copy-start(f32[26,4,8,640]{3,2,1,0:T(8,128)} %param.6) | copy-start | bytes 6389764
  2.2 4.2 %copy-start = (f32[5,8,640]{2,1,0:T(8,128)S(1)}, f32[5,8,640]{2,1,0:T(8,128)}, u32[]{:S(2)}) copy-start(f32[5,8,640]{2,1,0:T(8,128)} %constant.2.clone.coef_ref) | copy-start | bytes 307204
  2.2 4.2 %copy-start.3 = (s32[8,640]{1,0:T(8,128)S(1)}, s32[8,640]{1,0:T(8,128)}, u32[]{:S(2)}) copy-start(s32[8,640]{1,0:T(8,128)} %mask_ref.1) | copy-start | bytes 61444
  2.2 4.2 %copy-start.4 = (s32[26]{0:T(128)S(1)}, s32[26]{0:T(128)}, u32[]{:S(2)}) copy-start(s32[26]{0:T(128)} %count_ref.1) | copy-start | bytes 316
  2.6 3.8 %collective-permute-start.1 = (f32[4,104,640]{2,1,0:T(8,128)S(1)}, f32[4,104,640]{2,1,0:T(8,128)S(1)}, u32[]{:S(2)}, u32[]{:S(2)}) collective-permute-start(f32[4,104,640]{2,1,0:T(8,128)S(1)} %get-tuple-element.33.inner_ref.scaled_ref), channel_id=1, source_target_pairs={{0,2},{2,0},{4,6},{6,4},{8,10},{10,8},{12,14},{14,12},{16,18},{18,... | collective-permute-start | bytes 3194888 | tf_op jit(solution)/shard_map/ppermute | solution.py:335
  4.1 31.2 %collective-permute-start.4 = (f32[4,56,640]{2,1,0:T(8,128)S(1)}, f32[4,56,640]{2,1,0:T(8,128)S(1)}, u32[]{:S(2)}, u32[]{:S(2)}) collective-permute-start(f32[4,56,640]{2,1,0:T(8,128)S(1)} %get-tuple-element.35.refs_0_.outer_ref.scaled_ref), channel_id=1, source_target_pairs={{0,126},{2,4},{4,2},{6,8},{8,6},{10,12},{12,10},{14,16},{16,14},{1... | collective-permute-start | bytes 1720328 | tf_op jit(solution)/shard_map/ppermute | solution.py:334
  6.4 1.6 %copy-start.2 = (f32[26,4,8,640]{3,2,1,0:T(8,128)S(1)}, f32[26,4,8,640]{3,2,1,0:T(8,128)}, u32[]{:S(2)}) copy-start(f32[26,4,8,640]{3,2,1,0:T(8,128)} %param.5) | copy-start | bytes 6389764
  13.3 31.3 %collective-permute-start.6 = (f32[4,104,640]{2,1,0:T(8,128)S(1)}, f32[4,104,640]{2,1,0:T(8,128)S(1)}, u32[]{:S(2)}, u32[]{:S(2)}) collective-permute-start(f32[4,104,640]{2,1,0:T(8,128)S(1)} %get-tuple-element.40.inner_ref), channel_id=1, source_target_pairs={{0,2},{2,0},{4,6},{6,4},{8,10},{10,8},{12,14},{14,12},{16,18},{18,... | collective-permute-start | bytes 3194888 | tf_op jit(solution)/shard_map/ppermute | solution.py:348
  17.8 22.7 %collective-permute-start = (f32[4,48,640]{2,1,0:T(8,128)S(1)}, f32[4,48,640]{2,1,0:T(8,128)S(1)}, u32[]{:S(2)}, u32[]{:S(2)}) collective-permute-start(f32[4,48,640]{2,1,0:T(8,128)S(1)} %get-tuple-element.31.refs_1_.outer_ref.scaled_ref), channel_id=1, source_target_pairs={{0,126},{2,4},{4,2},{6,8},{8,6},{10,12},{12,10},{14,16},{16,14},{1... | collective-permute-start | bytes 1474568 | tf_op jit(solution)/shard_map/ppermute | solution.py:334
  36.6 14.3 %collective-permute-start.5 = (f32[4,56,640]{2,1,0:T(8,128)S(1)}, f32[4,56,640]{2,1,0:T(8,128)S(1)}, u32[]{:S(2)}, u32[]{:S(2)}) collective-permute-start(f32[4,56,640]{2,1,0:T(8,128)S(1)} %shard_map.71.refs_0_.outer_ref), channel_id=1, source_target_pairs={{0,126},{2,4},{4,2},{6,8},{8,6},{10,12},{12,10},{14,16},{16,14},{1... | collective-permute-start | bytes 1720328 | tf_op jit(solution)/shard_map/ppermute | solution.py:354
  41.7 12.4 %collective-permute-start.3 = (f32[4,32,640]{2,1,0:T(8,128)S(1)}, f32[4,32,640]{2,1,0:T(8,128)S(1)}, u32[]{:S(2)}, u32[]{:S(2)}) collective-permute-start(f32[4,32,640]{2,1,0:T(8,128)S(1)} %get-tuple-element.39.refs_1_.outer_ref), channel_id=1, source_target_pairs={{0,126},{2,4},{4,2},{6,8},{8,6},{10,12},{12,10},{14,16},{16,14},{1... | collective-permute-start | bytes 983048 | tf_op jit(solution)/shard_map/ppermute | solution.py:354
  44.3 11.6 %collective-permute-start.2 = (f32[4,16,640]{2,1,0:T(8,128)S(1)}, f32[4,16,640]{2,1,0:T(8,128)S(1)}, u32[]{:S(2)}, u32[]{:S(2)}) collective-permute-start(f32[4,16,640]{2,1,0:T(8,128)S(1)} %get-tuple-element.38.refs_2_.outer_ref), channel_id=1, source_target_pairs={{0,126},{2,4},{4,2},{6,8},{8,6},{10,12},{12,10},{14,16},{16,14},{1... | collective-permute-start | bytes 491528 | tf_op jit(solution)/shard_map/ppermute | solution.py:354
  56.3 4.9 %collective-permute-start.7 = (f32[168,128]{1,0:T(8,128)S(1)}, f32[168,128]{1,0:T(8,128)S(1)}, u32[]{:S(2)}, u32[]{:S(2)}) collective-permute-start(f32[168,128]{1,0:T(8,128)S(1)} %get-tuple-element.50.own_ref), channel_id=1, source_target_pairs={{0,1},{1,0},{2,3},{3,2},{4,5},{5,4},{6,7},{7,6},{8,9},{9,8},{10,11... | collective-permute-start | bytes 258056 | tf_op jit(solution)/shard_map/ppermute | solution.py:378

commit v16 on v15

--- a/solution.py
+++ b/solution.py
@@ -267,7 +267,7 @@
 
 
 def finish_kernel(cells, got_ref, merged_ref, inner_ref, *refs):
-    *outer_refs, bary_ref, updated_ref, staged_ref, sem = refs
+    *outer_refs, bary_ref, updated_ref, field_ref, staged_ref, field_sem, sem = refs
     members, lat = inner_ref.shape[1:]
     groups = members // SUB
     odd = odd_core()
@@ -284,18 +284,20 @@
         outer.append(jnp.where(low, both, swapped))
         inner.append(jnp.where(low, swapped, both))
     bary = from_outside(outer + inner, odd)
-    bary_ref[...] = jnp.swapaxes(jnp.stack(bary), 0, 1)[: SUB // 2]
+    field_ref[...] = jnp.swapaxes(jnp.stack(bary), 0, 1)[: SUB // 2]
+    copies = [pltpu.make_async_copy(field_ref, bary_ref, field_sem)]
+    copies[0].start()
     for group in range(groups):
         rows = slice(group * SUB, (group + 1) * SUB)
         factor = wide(table[rows, :] / cells)
         quotients = Chunked(outer_refs).stack(group) + stack_of(inner_ref, group)
         out = [b * factor * quotient for b, quotient in zip(bary, from_outside(quotients, odd))]
-        span = pl.ds(group * SUB * SUB, SUB * SUB)
+        span = block_of(group)
         staged_ref[span, :] = jnp.swapaxes(jnp.stack(out), 0, 1).reshape(SUB * SUB, lat)
-        pltpu.make_async_copy(staged_ref.at[span, :], updated_ref.at[span, :], sem.at[group]).start()
-    for group in range(groups):
-        span = pl.ds(group * SUB * SUB, SUB * SUB)
-        pltpu.make_async_copy(staged_ref.at[span, :], updated_ref.at[span, :], sem.at[group]).wait()
+        copies.append(pltpu.make_async_copy(staged_ref.at[span, :], updated_ref.at[span, :], sem.at[group]))
+        copies[-1].start()
+    for copy in copies:
+        copy.wait()
 
 
 def shape(*dims):
@@ -384,8 +386,13 @@
         got,
         merged,
         *inverses,
-        scratch=[pltpu.VMEM((rows * lon, lat), jnp.float32), pltpu.SemaphoreType.DMA((rows // SUB,))],
-        out_specs=(VMEM, HBM),
+        scratch=[
+            pltpu.VMEM((levels, lon, lat), jnp.float32),
+            pltpu.VMEM((rows * lon, lat), jnp.float32),
+            pltpu.SemaphoreType.DMA,
+            pltpu.SemaphoreType.DMA((rows // SUB,)),
+        ],
+        out_specs=(HBM, HBM),
     )
     return barycenter, updated.reshape(members, levels, lon, lat)
 

time: 79.6 us -> 79 us (level)
  no operation moved by 1% of the time
where the time goes in v16:
time: 79 us; the launch traced here: 78.8 us
  waiting for transfers between devices  26.1 us (33%)
  Pallas kernels  16.9 us (21%)
  starting transfers between devices  16.2 us (21%)
  blocking collectives  15.5 us (20%)
  local copies, waits for them, and re-layouts  3.2 us (4%)
  between operations  0.88 us (1%)
    ppermute x2, waiting for transfers between devices, body(): outer_halo = [lax.ppermute(part, 'tile', with_neighbour) for part in outer]  18.9 us
    pallas_call x10, Pallas kernels, call(): pl.pallas_call(kernel, out_shape=outs, in_specs=[SMEM if arg.ndim == 1 el...  16.9 us
    all_to_all x1, blocking collectives, body(): got = lax.all_to_all(payload, 'tile', split_axis=0, concat_axis=0)  15.5 us
    ppermute x3, starting transfers between devices, body(): lax.ppermute(value, 'tile', with_neighbour)  5.39 us
    ppermute x3, waiting for transfers between devices, body(): lax.ppermute(value, 'tile', with_neighbour)  4.78 us
    ppermute x1, starting transfers between devices, body(): v_inner_halo = lax.ppermute(v_inner, 'tile', with_mate)  4.54 us
    unnamed x10, local copies, waits for them, and re-layouts  3.2 us
    ppermute x1, starting transfers between devices, body(): other = lax.ppermute(logs, 'mem', [(0, 1), (1, 0)])  3.03 us
  transfers between devices with their start and end apart: 8, of which 7 were waited for; matrix products, arithmetic and copies ran while one was open for 0% of the time, Pallas kernels for 18%

profile of v16, /device:TPU:1, one launch (start us, length us, event | category | flops | bytes accessed | tf_op | source)
XLA Modules:
  0.0 78.8 jit_solution(9007189532563888326)
XLA Ops:
  0.6 0.0 copy-start.1
  0.6 1.6 %copy-done.1 = f32[26,4,8,640]{3,2,1,0:T(8,128)S(1)} copy-done((f32[26,4,8,640]{3,2,1,0:T(8,128)S(1)}, f32[26,4,8,640]{3,2,1,0:T(8,128)}, u32[]{:S(2)}) %copy-start.1) | copy-done | bytes 2129944
  2.2 0.0 copy-start
  2.2 0.0 copy-start.3
  2.2 0.0 copy-start.4
  2.2 0.4 shard_map.68
  2.6 1.5 %collective-permute-start.1 = (f32[4,104,640]{2,1,0:T(8,128)S(1)}, f32[4,104,640]{2,1,0:T(8,128)S(1)}, u32[]{:S(2)}, u32[]{:S(2)}) collective-permute-start(f32[4,104,640]{2,1,0:T(8,128)S(1)} %get-tuple-element.33.inner_ref.scaled_ref), channel_id=1, source_target_pairs={{0,2},{2,0},{4,6},{6,4},{8,10},{10,8},{12,14},{14,12},{16,18},{18,... | collective-permute-start | bytes 3194888 | tf_op jit(solution)/shard_map/ppermute | solution.py:337
  4.1 1.7 %collective-permute-start.4 = (f32[4,56,640]{2,1,0:T(8,128)S(1)}, f32[4,56,640]{2,1,0:T(8,128)S(1)}, u32[]{:S(2)}, u32[]{:S(2)}) collective-permute-start(f32[4,56,640]{2,1,0:T(8,128)S(1)} %get-tuple-element.35.refs_0_.outer_ref.scaled_ref), channel_id=1, source_target_pairs={{0,126},{2,4},{4,2},{6,8},{8,6},{10,12},{12,10},{14,16},{16,14},{1... | collective-permute-start | bytes 1720328 | tf_op jit(solution)/shard_map/ppermute | solution.py:336
  5.8 0.6 collective-permute-done.1.halo_ref
  6.4 0.0 copy-done
  6.4 0.0 copy-done.3
  6.4 0.0 copy-done.4
  6.4 0.0 copy-start.2
  6.5 1.6 %copy-done.2 = f32[26,4,8,640]{3,2,1,0:T(8,128)S(1)} copy-done((f32[26,4,8,640]{3,2,1,0:T(8,128)S(1)}, f32[26,4,8,640]{3,2,1,0:T(8,128)}, u32[]{:S(2)}) %copy-start.2) | copy-done | bytes 2129944
  8.0 5.2 %shard_map.69 = (f32[4,104,640]{2,1,0:T(8,128)S(1)}, f32[6,104,640]{2,1,0:T(8,128)S(1)}, f32[4,104,640]{2,1,0:T(8,128)S(1)}, f32[104,128]{1,0:T(8,128)S(1)}, f32[112,128]{1,0:T(8,128)S(1)}) custom-call(f32[4,104,640]{2,1,0:T(8,128)S(1)} %collective-permute-done.1.halo_ref, f32[4,104,640]{2,1,0:T(8,128)S(1)} %get-tuple-element.33.inner_ref.scaled_ref, ...), custom_call_target="tpu_custom_call" | custom-call | tf_op jit(solution)/shard_map/pallas_call | solution.py:308
  13.3 4.5 %collective-permute-start.6 = (f32[4,104,640]{2,1,0:T(8,128)S(1)}, f32[4,104,640]{2,1,0:T(8,128)S(1)}, u32[]{:S(2)}, u32[]{:S(2)}) collective-permute-start(f32[4,104,640]{2,1,0:T(8,128)S(1)} %get-tuple-element.40.inner_ref), channel_id=1, source_target_pairs={{0,2},{2,0},{4,6},{6,4},{8,10},{10,8},{12,14},{14,12},{16,18},{18,... | collective-permute-start | bytes 3194888 | tf_op jit(solution)/shard_map/ppermute | solution.py:350
  17.8 0.0 collective-permute-start
  17.8 17.5 %collective-permute-done.4.halo_ref = f32[4,56,640]{2,1,0:T(8,128)S(1)} collective-permute-done((f32[4,56,640]{2,1,0:T(8,128)S(1)}, f32[4,56,640]{2,1,0:T(8,128)S(1)}, u32[]{:S(2)}, u32[]{:S(2)}) %collective-permute-start.4) | collective-permute-done | bytes 573472 | tf_op jit(solution)/shard_map/ppermute | solution.py:336
  35.3 1.3 %shard_map.71.refs_0_.outer_ref = f32[4,56,640]{2,1,0:T(8,128)S(1)} custom-call(f32[4,56,640]{2,1,0:T(8,128)S(1)} %collective-permute-done.4.halo_ref, f32[4,56,640]{2,1,0:T(8,128)S(1)} %get-tuple-element.35.refs_0_.outer_ref.scaled_ref, f32[6,104,640]{2,1,0:T(8,128)S(1)} %get-tuple-element.36.edge_ref, f32[4,104,640]{2,1,0:T(8,128)S(1)} %get-tuple-element.37.filled_ref, ...), custom_call_target="tpu_custom_call" | custom-call | tf_op jit(solution)/shard_map/pallas_call | solution.py:308
  36.6 2.6 %collective-permute-start.5 = (f32[4,56,640]{2,1,0:T(8,128)S(1)}, f32[4,56,640]{2,1,0:T(8,128)S(1)}, u32[]{:S(2)}, u32[]{:S(2)}) collective-permute-start(f32[4,56,640]{2,1,0:T(8,128)S(1)} %shard_map.71.refs_0_.outer_ref), channel_id=1, source_target_pairs={{0,126},{2,4},{4,2},{6,8},{8,6},{10,12},{12,10},{14,16},{16,14},{1... | collective-permute-start | bytes 1720328 | tf_op jit(solution)/shard_map/ppermute | solution.py:356
  39.2 1.4 %collective-permute-done.halo_ref = f32[4,48,640]{2,1,0:T(8,128)S(1)} collective-permute-done((f32[4,48,640]{2,1,0:T(8,128)S(1)}, f32[4,48,640]{2,1,0:T(8,128)S(1)}, u32[]{:S(2)}, u32[]{:S(2)}) %collective-permute-start) | collective-permute-done | bytes 491552 | tf_op jit(solution)/shard_map/ppermute | solution.py:336
  40.6 1.2 %shard_map.70 = (f32[4,32,640]{2,1,0:T(8,128)S(1)}, f32[4,16,640]{2,1,0:T(8,128)S(1)}) custom-call(f32[4,48,640]{2,1,0:T(8,128)S(1)} %collective-permute-done.halo_ref, f32[4,48,640]{2,1,0:T(8,128)S(1)} %get-tuple-element.31.refs_1_.outer_ref.scaled_ref, f32[6,104,640]{2,1,0:T(8,128)S(1)} %get-tuple-element.36.edge_ref, ...), custom_call_target="tpu_custom_call" | custom-call | tf_op jit(solution)/shard_map/pallas_call | solution.py:308
  41.7 2.6 %collective-permute-start.3 = (f32[4,32,640]{2,1,0:T(8,128)S(1)}, f32[4,32,640]{2,1,0:T(8,128)S(1)}, u32[]{:S(2)}, u32[]{:S(2)}) collective-permute-start(f32[4,32,640]{2,1,0:T(8,128)S(1)} %get-tuple-element.39.refs_1_.outer_ref), channel_id=1, source_target_pairs={{0,126},{2,4},{4,2},{6,8},{8,6},{10,12},{12,10},{14,16},{16,14},{1... | collective-permute-start | bytes 983048 | tf_op jit(solution)/shard_map/ppermute | solution.py:356
  44.3 0.3 collective-permute-start.2
  44.6 0.0 collective-permute-done.6.halo_ref
  44.6 4.3 %shard_map.72 = (f32[4,104,640]{2,1,0:T(8,128)S(1)}, f32[6,104,640]{2,1,0:T(8,128)S(1)}, f32[4,8,640]{2,1,0:T(8,128)S(1)}) custom-call(f32[4,104,640]{2,1,0:T(8,128)S(1)} %collective-permute-done.6.halo_ref, f32[4,104,640]{2,1,0:T(8,128)S(1)} %get-tuple-element.40.inner_ref, f32[4,104,640]{2,1,0:T(8,128)S(1)} %get-tuple-element.33.inner_ref.scaled_ref, ...), custom_call_target="tpu_custom_call" | custom-call | tf_op jit(solution)/shard_map/pallas_call | solution.py:308
  48.9 2.0 %collective-permute-done.5.halo_ref = f32[4,56,640]{2,1,0:T(8,128)S(1)} collective-permute-done((f32[4,56,640]{2,1,0:T(8,128)S(1)}, f32[4,56,640]{2,1,0:T(8,128)S(1)}, u32[]{:S(2)}, u32[]{:S(2)}) %collective-permute-start.5) | collective-permute-done | bytes 573472 | tf_op jit(solution)/shard_map/ppermute | solution.py:356
  50.9 1.4 %shard_map.73 = (f32[4,56,640]{2,1,0:T(8,128)S(1)}, f32[4,8,640]{2,1,0:T(8,128)S(1)}) custom-call(f32[4,56,640]{2,1,0:T(8,128)S(1)} %collective-permute-done.5.halo_ref, f32[4,56,640]{2,1,0:T(8,128)S(1)} %shard_map.71.refs_0_.outer_ref, f32[6,104,640]{2,1,0:T(8,128)S(1)} %get-tuple-element.42.edge_ref, ...), custom_call_target="tpu_custom_call" | custom-call | tf_op jit(solution)/shard_map/pallas_call | solution.py:308
  52.2 1.9 %collective-permute-done.3.halo_ref = f32[4,32,640]{2,1,0:T(8,128)S(1)} collective-permute-done((f32[4,32,640]{2,1,0:T(8,128)S(1)}, f32[4,32,640]{2,1,0:T(8,128)S(1)}, u32[]{:S(2)}, u32[]{:S(2)}) %collective-permute-start.3) | collective-permute-done | bytes 327712 | tf_op jit(solution)/shard_map/ppermute | solution.py:356
  54.1 0.8 %shard_map.74 = (f32[4,32,640]{2,1,0:T(8,128)S(1)}, f32[4,8,640]{2,1,0:T(8,128)S(1)}) custom-call(f32[4,32,640]{2,1,0:T(8,128)S(1)} %collective-permute-done.3.halo_ref, f32[4,32,640]{2,1,0:T(8,128)S(1)} %get-tuple-element.39.refs_1_.outer_ref, f32[6,104,640]{2,1,0:T(8,128)S(1)} %get-tuple-element.42.edge_ref, ...), custom_call_target="tpu_custom_call" | custom-call | tf_op jit(solution)/shard_map/pallas_call | solution.py:308
  54.9 0.9 %collective-permute-done.2.halo_ref = f32[4,16,640]{2,1,0:T(8,128)S(1)} collective-permute-done((f32[4,16,640]{2,1,0:T(8,128)S(1)}, f32[4,16,640]{2,1,0:T(8,128)S(1)}, u32[]{:S(2)}, u32[]{:S(2)}) %collective-permute-start.2) | collective-permute-done | bytes 163872 | tf_op jit(solution)/shard_map/ppermute | solution.py:356
  55.9 0.5 shard_map.75
  56.3 3.0 %collective-permute-start.7 = (f32[168,128]{1,0:T(8,128)S(1)}, f32[168,128]{1,0:T(8,128)S(1)}, u32[]{:S(2)}, u32[]{:S(2)}) collective-permute-start(f32[168,128]{1,0:T(8,128)S(1)} %get-tuple-element.50.own_ref), channel_id=1, source_target_pairs={{0,1},{1,0},{2,3},{3,2},{4,5},{5,4},{6,7},{7,6},{8,9},{9,8},{10,11... | collective-permute-start | bytes 258056 | tf_op jit(solution)/shard_map/ppermute | solution.py:380
  59.4 1.9 %collective-permute-done.7.other_ref = f32[168,128]{1,0:T(8,128)S(1)} collective-permute-done((f32[168,128]{1,0:T(8,128)S(1)}, f32[168,128]{1,0:T(8,128)S(1)}, u32[]{:S(2)}, u32[]{:S(2)}) %collective-permute-start.7) | collective-permute-done | bytes 86048 | tf_op jit(solution)/shard_map/ppermute | solution.py:380
  61.3 0.1 shard_map.76
  61.4 15.5 %all_to_all.5.got_ref = f32[64,1,128]{2,1,0:T(1,128)S(1)} all-to-all(f32[64,1,128]{2,1,0:T(1,128)S(1)} %get-tuple-element.52), channel_id=1, replica_groups=mesh['tile'=64,'mem'=2] {'tile'}, dimensions={0} | all-to-all | bytes 65536 | tf_op jit(solution)/shard_map/all_to_all | solution.py:382
  76.9 1.7 %shard_map.77 = (f32[4,8,640]{2,1,0:T(8,128)}, f32[832,640]{1,0:T(8,128)}) custom-call(f32[64,1,128]{2,1,0:T(1,128)S(1)} %all_to_all.5.got_ref, f32[4,8,640]{2,1,0:T(8,128)S(1)} %get-tuple-element.53.merged_ref, f32[4,104,640]{2,1,0:T(8,128)S(1)} %get-tuple-element.54.inner_ref, f32[4,56,640]{2,1,0:T(8,128)S(1)} %get-tuple-element.55.refs_0_, ...), custom_call_target="tpu_custom_call" | custom-call | tf_op jit(solution)/shard_map/pallas_call | solution.py:308
Async XLA Ops:
  0.6 1.6 %copy-start.1 = (f32[26,4,8,640]{3,2,1,0:T(8,128)S(1)}, f32[26,4,8,640]{3,2,1,0:T(8,128)}, u32[]{:S(2)}) copy-start(f32[26,4,8,640]{3,2,1,0:T(8,128)} %param.6) | copy-start | bytes 6389764
  2.2 4.2 %copy-start = (f32[5,8,640]{2,1,0:T(8,128)S(1)}, f32[5,8,640]{2,1,0:T(8,128)}, u32[]{:S(2)}) copy-start(f32[5,8,640]{2,1,0:T(8,128)} %constant.2.clone.coef_ref) | copy-start | bytes 307204
  2.2 4.2 %copy-start.3 = (s32[8,640]{1,0:T(8,128)S(1)}, s32[8,640]{1,0:T(8,128)}, u32[]{:S(2)}) copy-start(s32[8,640]{1,0:T(8,128)} %mask_ref.1) | copy-start | bytes 61444
  2.2 4.2 %copy-start.4 = (s32[26]{0:T(128)S(1)}, s32[26]{0:T(128)}, u32[]{:S(2)}) copy-start(s32[26]{0:T(128)} %count_ref.1) | copy-start | bytes 316
  2.6 3.8 %collective-permute-start.1 = (f32[4,104,640]{2,1,0:T(8,128)S(1)}, f32[4,104,640]{2,1,0:T(8,128)S(1)}, u32[]{:S(2)}, u32[]{:S(2)}) collective-permute-start(f32[4,104,640]{2,1,0:T(8,128)S(1)} %get-tuple-element.33.inner_ref.scaled_ref), channel_id=1, source_target_pairs={{0,2},{2,0},{4,6},{6,4},{8,10},{10,8},{12,14},{14,12},{16,18},{18,... | collective-permute-start | bytes 3194888 | tf_op jit(solution)/shard_map/ppermute | solution.py:337
  4.1 31.2 %collective-permute-start.4 = (f32[4,56,640]{2,1,0:T(8,128)S(1)}, f32[4,56,640]{2,1,0:T(8,128)S(1)}, u32[]{:S(2)}, u32[]{:S(2)}) collective-permute-start(f32[4,56,640]{2,1,0:T(8,128)S(1)} %get-tuple-element.35.refs_0_.outer_ref.scaled_ref), channel_id=1, source_target_pairs={{0,126},{2,4},{4,2},{6,8},{8,6},{10,12},{12,10},{14,16},{16,14},{1... | collective-permute-start | bytes 1720328 | tf_op jit(solution)/shard_map/ppermute | solution.py:336
  6.4 1.6 %copy-start.2 = (f32[26,4,8,640]{3,2,1,0:T(8,128)S(1)}, f32[26,4,8,640]{3,2,1,0:T(8,128)}, u32[]{:S(2)}) copy-start(f32[26,4,8,640]{3,2,1,0:T(8,128)} %param.5) | copy-start | bytes 6389764
  13.3 31.3 %collective-permute-start.6 = (f32[4,104,640]{2,1,0:T(8,128)S(1)}, f32[4,104,640]{2,1,0:T(8,128)S(1)}, u32[]{:S(2)}, u32[]{:S(2)}) collective-permute-start(f32[4,104,640]{2,1,0:T(8,128)S(1)} %get-tuple-element.40.inner_ref), channel_id=1, source_target_pairs={{0,2},{2,0},{4,6},{6,4},{8,10},{10,8},{12,14},{14,12},{16,18},{18,... | collective-permute-start | bytes 3194888 | tf_op jit(solution)/shard_map/ppermute | solution.py:350
  17.8 22.7 %collective-permute-start = (f32[4,48,640]{2,1,0:T(8,128)S(1)}, f32[4,48,640]{2,1,0:T(8,128)S(1)}, u32[]{:S(2)}, u32[]{:S(2)}) collective-permute-start(f32[4,48,640]{2,1,0:T(8,128)S(1)} %get-tuple-element.31.refs_1_.outer_ref.scaled_ref), channel_id=1, source_target_pairs={{0,126},{2,4},{4,2},{6,8},{8,6},{10,12},{12,10},{14,16},{16,14},{1... | collective-permute-start | bytes 1474568 | tf_op jit(solution)/shard_map/ppermute | solution.py:336
  36.6 14.3 %collective-permute-start.5 = (f32[4,56,640]{2,1,0:T(8,128)S(1)}, f32[4,56,640]{2,1,0:T(8,128)S(1)}, u32[]{:S(2)}, u32[]{:S(2)}) collective-permute-start(f32[4,56,640]{2,1,0:T(8,128)S(1)} %shard_map.71.refs_0_.outer_ref), channel_id=1, source_target_pairs={{0,126},{2,4},{4,2},{6,8},{8,6},{10,12},{12,10},{14,16},{16,14},{1... | collective-permute-start | bytes 1720328 | tf_op jit(solution)/shard_map/ppermute | solution.py:356
  41.7 12.4 %collective-permute-start.3 = (f32[4,32,640]{2,1,0:T(8,128)S(1)}, f32[4,32,640]{2,1,0:T(8,128)S(1)}, u32[]{:S(2)}, u32[]{:S(2)}) collective-permute-start(f32[4,32,640]{2,1,0:T(8,128)S(1)} %get-tuple-element.39.refs_1_.outer_ref), channel_id=1, source_target_pairs={{0,126},{2,4},{4,2},{6,8},{8,6},{10,12},{12,10},{14,16},{16,14},{1... | collective-permute-start | bytes 983048 | tf_op jit(solution)/shard_map/ppermute | solution.py:356
  44.3 11.6 %collective-permute-start.2 = (f32[4,16,640]{2,1,0:T(8,128)S(1)}, f32[4,16,640]{2,1,0:T(8,128)S(1)}, u32[]{:S(2)}, u32[]{:S(2)}) collective-permute-start(f32[4,16,640]{2,1,0:T(8,128)S(1)} %get-tuple-element.38.refs_2_.outer_ref), channel_id=1, source_target_pairs={{0,126},{2,4},{4,2},{6,8},{8,6},{10,12},{12,10},{14,16},{16,14},{1... | collective-permute-start | bytes 491528 | tf_op jit(solution)/shard_map/ppermute | solution.py:356
  56.3 4.9 %collective-permute-start.7 = (f32[168,128]{1,0:T(8,128)S(1)}, f32[168,128]{1,0:T(8,128)S(1)}, u32[]{:S(2)}, u32[]{:S(2)}) collective-permute-start(f32[168,128]{1,0:T(8,128)S(1)} %get-tuple-element.50.own_ref), channel_id=1, source_target_pairs={{0,1},{1,0},{2,3},{3,2},{4,5},{5,4},{6,7},{7,6},{8,9},{9,8},{10,11... | collective-permute-start | bytes 258056 | tf_op jit(solution)/shard_map/ppermute | solution.py:380

commit v17 on v16

--- a/solution.py
+++ b/solution.py
@@ -31,7 +31,7 @@
     return np.ascontiguousarray(np.broadcast_to(rows[:, None, :], (5, SUB, lat_cells)))
 
 
-def params(mib=12):
+def params(mib):
     return pltpu.CompilerParams(vmem_limit_bytes=mib * 2**20)
 
 
@@ -94,12 +94,20 @@
     return lax.broadcasted_iota(jnp.int32, shape, 0) < SUB // 2
 
 
-def spread_kernel(scaling_ref, inner_ref, *outer_refs):
+def spread_kernel(scaling_ref, inner_ref, *refs):
+    *outer_refs, staged_ref, sem = refs
     groups, lat = inner_ref.shape[1] // SUB, inner_ref.shape[2]
     odd = odd_core()
     outer = Chunked(outer_refs)
+    copies = [
+        pltpu.make_async_copy(scaling_ref.at[block_of(g), :], staged_ref.at[block_of(g), :], sem.at[g])
+        for g in range(groups)
+    ]
+    for copy in copies:
+        copy.start()
     for group in range(groups):
-        columns = from_outside(by_longitude(scaling_ref[block_of(group), :], lat), odd)
+        copies[group].wait()
+        columns = from_outside(by_longitude(staged_ref[block_of(group), :], lat), odd)
         outer.put(group, columns[:REACH])
         for c in range(REACH):
             inner_ref[c, rows_of(group), :] = columns[c + REACH]
@@ -304,14 +312,14 @@
     return jax.ShapeDtypeStruct(dims, jnp.float32)
 
 
-def call(kernel, outs, *args, scratch=(), out_specs=None):
+def call(kernel, outs, *args, scratch=(), in_specs=None, out_specs=None, mib=12):
     return pl.pallas_call(
         kernel,
         out_shape=outs,
-        in_specs=[SMEM if arg.ndim == 1 else VMEM for arg in args],
+        in_specs=in_specs or [SMEM if arg.ndim == 1 else VMEM for arg in args],
         out_specs=out_specs or (VMEM,) * len(outs),
         scratch_shapes=scratch,
-        compiler_params=params(),
+        compiler_params=params(mib),
     )(*args)
 
 
@@ -332,7 +340,14 @@
     scaling = scaling.reshape(rows * lon, lat)
     fields = fields.reshape(rows * lon, lat)
 
-    inner, *outer = call(spread_kernel, (half, *parts), scaling)
+    inner, *outer = call(
+        spread_kernel,
+        (half, *parts),
+        scaling,
+        in_specs=[HBM],
+        scratch=[pltpu.VMEM((rows * lon, lat), jnp.float32), pltpu.SemaphoreType.DMA((rows // SUB,))],
+        mib=51,
+    )
     outer_halo = [lax.ppermute(part, "tile", with_neighbour) for part in outer]
     inner_halo = lax.ppermute(inner, "tile", with_mate)
     fields, inner = lax.optimization_barrier((fields, inner))

time: 79 us -> 78.9 us (level)
  local copies, waits for them, and re-layouts: 3.2 us -> 1.61 us
  Pallas kernels: 16.9 us -> 18.2 us
    unnamed x10 -> x8, local copies, waits for them, and re-layouts: 3.2 us -> 1.61 us
    pallas_call x10, Pallas kernels: 16.9 us -> 18.2 us  [call(): pl.pallas_call(kernel, out_shape=outs, in_specs=in_specs or [SMEM if arg....]
where the time goes in v17:
time: 78.9 us; the launch traced here: 78.7 us
  waiting for transfers between devices  26.2 us (33%)
  Pallas kernels  18.2 us (23%)
  starting transfers between devices  16.2 us (21%)
  blocking collectives  15.5 us (20%)
  local copies, waits for them, and re-layouts  1.61 us (2%)
  between operations  0.9 us (1%)
    ppermute x2, waiting for transfers between devices, body(): outer_halo = [lax.ppermute(part, 'tile', with_neighbour) for part in outer]  18.8 us
    pallas_call x10, Pallas kernels, call(): pl.pallas_call(kernel, out_shape=outs, in_specs=in_specs or [SMEM if arg....  18.2 us
    all_to_all x1, blocking collectives, body(): got = lax.all_to_all(payload, 'tile', split_axis=0, concat_axis=0)  15.5 us
    ppermute x3, starting transfers between devices, body(): lax.ppermute(value, 'tile', with_neighbour)  5.39 us
    ppermute x3, waiting for transfers between devices, body(): lax.ppermute(value, 'tile', with_neighbour)  4.89 us
    ppermute x1, starting transfers between devices, body(): v_inner_halo = lax.ppermute(v_inner, 'tile', with_mate)  4.54 us
    ppermute x1, starting transfers between devices, body(): other = lax.ppermute(logs, 'mem', [(0, 1), (1, 0)])  3.03 us
    ppermute x1, waiting for transfers between devices, body(): other = lax.ppermute(logs, 'mem', [(0, 1), (1, 0)])  1.89 us
  transfers between devices with their start and end apart: 8, of which 7 were waited for; matrix products, arithmetic and copies ran while one was open for 0% of the time, Pallas kernels for 18%

profile of v17, /device:TPU:1, one launch (start us, length us, event | category | flops | bytes accessed | tf_op | source)
XLA Modules:
  0.0 78.7 jit_solution(3211091113140641282)
XLA Ops:
  0.6 0.0 copy-start
  0.6 0.0 copy-start.2
  0.7 0.0 copy-start.3
  0.7 1.8 %shard_map.68 = (f32[4,104,640]{2,1,0:T(8,128)S(1)}, f32[4,56,640]{2,1,0:T(8,128)S(1)}, f32[4,48,640]{2,1,0:T(8,128)S(1)}) custom-call(f32[832,640]{1,0:T(8,128)} %bitcast.4), custom_call_target="tpu_custom_call" | custom-call | tf_op jit(solution)/shard_map/pallas_call | solution.py:316
  2.5 1.5 %collective-permute-start.1 = (f32[4,104,640]{2,1,0:T(8,128)S(1)}, f32[4,104,640]{2,1,0:T(8,128)S(1)}, u32[]{:S(2)}, u32[]{:S(2)}) collective-permute-start(f32[4,104,640]{2,1,0:T(8,128)S(1)} %get-tuple-element.33.inner_ref.scaled_ref), channel_id=1, source_target_pairs={{0,2},{2,0},{4,6},{6,4},{8,10},{10,8},{12,14},{14,12},{16,18},{18,... | collective-permute-start | bytes 3194888 | tf_op jit(solution)/shard_map/ppermute | solution.py:352
  4.0 1.7 %collective-permute-start.4 = (f32[4,56,640]{2,1,0:T(8,128)S(1)}, f32[4,56,640]{2,1,0:T(8,128)S(1)}, u32[]{:S(2)}, u32[]{:S(2)}) collective-permute-start(f32[4,56,640]{2,1,0:T(8,128)S(1)} %get-tuple-element.35.refs_0_.outer_ref.scaled_ref), channel_id=1, source_target_pairs={{0,126},{2,4},{4,2},{6,8},{8,6},{10,12},{12,10},{14,16},{16,14},{1... | collective-permute-start | bytes 1720328 | tf_op jit(solution)/shard_map/ppermute | solution.py:351
  5.7 0.6 collective-permute-done.1.halo_ref
  6.3 0.0 copy-done
  6.3 0.0 copy-done.2
  6.3 0.0 copy-done.3
  6.3 0.0 copy-start.1
  6.3 1.6 %copy-done.1 = f32[26,4,8,640]{3,2,1,0:T(8,128)S(1)} copy-done((f32[26,4,8,640]{3,2,1,0:T(8,128)S(1)}, f32[26,4,8,640]{3,2,1,0:T(8,128)}, u32[]{:S(2)}) %copy-start.1) | copy-done | bytes 2129944
  7.9 5.2 %shard_map.69 = (f32[4,104,640]{2,1,0:T(8,128)S(1)}, f32[6,104,640]{2,1,0:T(8,128)S(1)}, f32[4,104,640]{2,1,0:T(8,128)S(1)}, f32[104,128]{1,0:T(8,128)S(1)}, f32[112,128]{1,0:T(8,128)S(1)}) custom-call(f32[4,104,640]{2,1,0:T(8,128)S(1)} %collective-permute-done.1.halo_ref, f32[4,104,640]{2,1,0:T(8,128)S(1)} %get-tuple-element.33.inner_ref.scaled_ref, ...), custom_call_target="tpu_custom_call" | custom-call | tf_op jit(solution)/shard_map/pallas_call | solution.py:316
  13.1 4.5 %collective-permute-start.6 = (f32[4,104,640]{2,1,0:T(8,128)S(1)}, f32[4,104,640]{2,1,0:T(8,128)S(1)}, u32[]{:S(2)}, u32[]{:S(2)}) collective-permute-start(f32[4,104,640]{2,1,0:T(8,128)S(1)} %get-tuple-element.40.inner_ref), channel_id=1, source_target_pairs={{0,2},{2,0},{4,6},{6,4},{8,10},{10,8},{12,14},{14,12},{16,18},{18,... | collective-permute-start | bytes 3194888 | tf_op jit(solution)/shard_map/ppermute | solution.py:365
  17.7 0.0 collective-permute-start
  17.7 17.5 %collective-permute-done.4.halo_ref = f32[4,56,640]{2,1,0:T(8,128)S(1)} collective-permute-done((f32[4,56,640]{2,1,0:T(8,128)S(1)}, f32[4,56,640]{2,1,0:T(8,128)S(1)}, u32[]{:S(2)}, u32[]{:S(2)}) %collective-permute-start.4) | collective-permute-done | bytes 573472 | tf_op jit(solution)/shard_map/ppermute | solution.py:351
  35.2 1.3 %shard_map.71.refs_0_.outer_ref = f32[4,56,640]{2,1,0:T(8,128)S(1)} custom-call(f32[4,56,640]{2,1,0:T(8,128)S(1)} %collective-permute-done.4.halo_ref, f32[4,56,640]{2,1,0:T(8,128)S(1)} %get-tuple-element.35.refs_0_.outer_ref.scaled_ref, f32[6,104,640]{2,1,0:T(8,128)S(1)} %get-tuple-element.36.edge_ref, f32[4,104,640]{2,1,0:T(8,128)S(1)} %get-tuple-element.37.filled_ref, ...), custom_call_target="tpu_custom_call" | custom-call | tf_op jit(solution)/shard_map/pallas_call | solution.py:316
  36.5 2.6 %collective-permute-start.5 = (f32[4,56,640]{2,1,0:T(8,128)S(1)}, f32[4,56,640]{2,1,0:T(8,128)S(1)}, u32[]{:S(2)}, u32[]{:S(2)}) collective-permute-start(f32[4,56,640]{2,1,0:T(8,128)S(1)} %shard_map.71.refs_0_.outer_ref), channel_id=1, source_target_pairs={{0,126},{2,4},{4,2},{6,8},{8,6},{10,12},{12,10},{14,16},{16,14},{1... | collective-permute-start | bytes 1720328 | tf_op jit(solution)/shard_map/ppermute | solution.py:371
  39.1 1.4 %collective-permute-done.halo_ref = f32[4,48,640]{2,1,0:T(8,128)S(1)} collective-permute-done((f32[4,48,640]{2,1,0:T(8,128)S(1)}, f32[4,48,640]{2,1,0:T(8,128)S(1)}, u32[]{:S(2)}, u32[]{:S(2)}) %collective-permute-start) | collective-permute-done | bytes 491552 | tf_op jit(solution)/shard_map/ppermute | solution.py:351
  40.4 1.2 %shard_map.70 = (f32[4,32,640]{2,1,0:T(8,128)S(1)}, f32[4,16,640]{2,1,0:T(8,128)S(1)}) custom-call(f32[4,48,640]{2,1,0:T(8,128)S(1)} %collective-permute-done.halo_ref, f32[4,48,640]{2,1,0:T(8,128)S(1)} %get-tuple-element.31.refs_1_.outer_ref.scaled_ref, f32[6,104,640]{2,1,0:T(8,128)S(1)} %get-tuple-element.36.edge_ref, ...), custom_call_target="tpu_custom_call" | custom-call | tf_op jit(solution)/shard_map/pallas_call | solution.py:316
  41.6 2.6 %collective-permute-start.3 = (f32[4,32,640]{2,1,0:T(8,128)S(1)}, f32[4,32,640]{2,1,0:T(8,128)S(1)}, u32[]{:S(2)}, u32[]{:S(2)}) collective-permute-start(f32[4,32,640]{2,1,0:T(8,128)S(1)} %get-tuple-element.39.refs_1_.outer_ref), channel_id=1, source_target_pairs={{0,126},{2,4},{4,2},{6,8},{8,6},{10,12},{12,10},{14,16},{16,14},{1... | collective-permute-start | bytes 983048 | tf_op jit(solution)/shard_map/ppermute | solution.py:371
  44.2 0.3 collective-permute-start.2
  44.4 0.0 collective-permute-done.6.halo_ref
  44.4 4.2 %shard_map.72 = (f32[4,104,640]{2,1,0:T(8,128)S(1)}, f32[6,104,640]{2,1,0:T(8,128)S(1)}, f32[4,8,640]{2,1,0:T(8,128)S(1)}) custom-call(f32[4,104,640]{2,1,0:T(8,128)S(1)} %collective-permute-done.6.halo_ref, f32[4,104,640]{2,1,0:T(8,128)S(1)} %get-tuple-element.40.inner_ref, f32[4,104,640]{2,1,0:T(8,128)S(1)} %get-tuple-element.33.inner_ref.scaled_ref, ...), custom_call_target="tpu_custom_call" | custom-call | tf_op jit(solution)/shard_map/pallas_call | solution.py:316
  48.7 2.1 %collective-permute-done.5.halo_ref = f32[4,56,640]{2,1,0:T(8,128)S(1)} collective-permute-done((f32[4,56,640]{2,1,0:T(8,128)S(1)}, f32[4,56,640]{2,1,0:T(8,128)S(1)}, u32[]{:S(2)}, u32[]{:S(2)}) %collective-permute-start.5) | collective-permute-done | bytes 573472 | tf_op jit(solution)/shard_map/ppermute | solution.py:371
  50.8 1.3 %shard_map.73 = (f32[4,56,640]{2,1,0:T(8,128)S(1)}, f32[4,8,640]{2,1,0:T(8,128)S(1)}) custom-call(f32[4,56,640]{2,1,0:T(8,128)S(1)} %collective-permute-done.5.halo_ref, f32[4,56,640]{2,1,0:T(8,128)S(1)} %shard_map.71.refs_0_.outer_ref, f32[6,104,640]{2,1,0:T(8,128)S(1)} %get-tuple-element.42.edge_ref, ...), custom_call_target="tpu_custom_call" | custom-call | tf_op jit(solution)/shard_map/pallas_call | solution.py:316
  52.1 1.9 %collective-permute-done.3.halo_ref = f32[4,32,640]{2,1,0:T(8,128)S(1)} collective-permute-done((f32[4,32,640]{2,1,0:T(8,128)S(1)}, f32[4,32,640]{2,1,0:T(8,128)S(1)}, u32[]{:S(2)}, u32[]{:S(2)}) %collective-permute-start.3) | collective-permute-done | bytes 327712 | tf_op jit(solution)/shard_map/ppermute | solution.py:371
  54.0 0.8 %shard_map.74 = (f32[4,32,640]{2,1,0:T(8,128)S(1)}, f32[4,8,640]{2,1,0:T(8,128)S(1)}) custom-call(f32[4,32,640]{2,1,0:T(8,128)S(1)} %collective-permute-done.3.halo_ref, f32[4,32,640]{2,1,0:T(8,128)S(1)} %get-tuple-element.39.refs_1_.outer_ref, f32[6,104,640]{2,1,0:T(8,128)S(1)} %get-tuple-element.42.edge_ref, ...), custom_call_target="tpu_custom_call" | custom-call | tf_op jit(solution)/shard_map/pallas_call | solution.py:316
  54.8 0.9 %collective-permute-done.2.halo_ref = f32[4,16,640]{2,1,0:T(8,128)S(1)} collective-permute-done((f32[4,16,640]{2,1,0:T(8,128)S(1)}, f32[4,16,640]{2,1,0:T(8,128)S(1)}, u32[]{:S(2)}, u32[]{:S(2)}) %collective-permute-start.2) | collective-permute-done | bytes 163872 | tf_op jit(solution)/shard_map/ppermute | solution.py:371
  55.7 0.5 shard_map.75
  56.2 3.0 %collective-permute-start.7 = (f32[168,128]{1,0:T(8,128)S(1)}, f32[168,128]{1,0:T(8,128)S(1)}, u32[]{:S(2)}, u32[]{:S(2)}) collective-permute-start(f32[168,128]{1,0:T(8,128)S(1)} %get-tuple-element.50.own_ref), channel_id=1, source_target_pairs={{0,1},{1,0},{2,3},{3,2},{4,5},{5,4},{6,7},{7,6},{8,9},{9,8},{10,11... | collective-permute-start | bytes 258056 | tf_op jit(solution)/shard_map/ppermute | solution.py:395
  59.2 1.9 %collective-permute-done.7.other_ref = f32[168,128]{1,0:T(8,128)S(1)} collective-permute-done((f32[168,128]{1,0:T(8,128)S(1)}, f32[168,128]{1,0:T(8,128)S(1)}, u32[]{:S(2)}, u32[]{:S(2)}) %collective-permute-start.7) | collective-permute-done | bytes 86048 | tf_op jit(solution)/shard_map/ppermute | solution.py:395
  61.1 0.1 shard_map.76
  61.3 15.5 %all_to_all.5.got_ref = f32[64,1,128]{2,1,0:T(1,128)S(1)} all-to-all(f32[64,1,128]{2,1,0:T(1,128)S(1)} %get-tuple-element.52), channel_id=1, replica_groups=mesh['tile'=64,'mem'=2] {'tile'}, dimensions={0} | all-to-all | bytes 65536 | tf_op jit(solution)/shard_map/all_to_all | solution.py:397
  76.8 1.7 %shard_map.77 = (f32[4,8,640]{2,1,0:T(8,128)}, f32[832,640]{1,0:T(8,128)}) custom-call(f32[64,1,128]{2,1,0:T(1,128)S(1)} %all_to_all.5.got_ref, f32[4,8,640]{2,1,0:T(8,128)S(1)} %get-tuple-element.53.merged_ref, f32[4,104,640]{2,1,0:T(8,128)S(1)} %get-tuple-element.54.inner_ref, f32[4,56,640]{2,1,0:T(8,128)S(1)} %get-tuple-element.55.refs_0_, ...), custom_call_target="tpu_custom_call" | custom-call | tf_op jit(solution)/shard_map/pallas_call | solution.py:316
Async XLA Ops:
  0.6 5.7 %copy-start = (f32[5,8,640]{2,1,0:T(8,128)S(1)}, f32[5,8,640]{2,1,0:T(8,128)}, u32[]{:S(2)}) copy-start(f32[5,8,640]{2,1,0:T(8,128)} %constant.2.clone.coef_ref) | copy-start | bytes 307204
  0.6 5.7 %copy-start.2 = (s32[8,640]{1,0:T(8,128)S(1)}, s32[8,640]{1,0:T(8,128)}, u32[]{:S(2)}) copy-start(s32[8,640]{1,0:T(8,128)} %mask_ref.1) | copy-start | bytes 61444
  0.7 5.7 %copy-start.3 = (s32[26]{0:T(128)S(1)}, s32[26]{0:T(128)}, u32[]{:S(2)}) copy-start(s32[26]{0:T(128)} %count_ref.1) | copy-start | bytes 316
  2.5 3.8 %collective-permute-start.1 = (f32[4,104,640]{2,1,0:T(8,128)S(1)}, f32[4,104,640]{2,1,0:T(8,128)S(1)}, u32[]{:S(2)}, u32[]{:S(2)}) collective-permute-start(f32[4,104,640]{2,1,0:T(8,128)S(1)} %get-tuple-element.33.inner_ref.scaled_ref), channel_id=1, source_target_pairs={{0,2},{2,0},{4,6},{6,4},{8,10},{10,8},{12,14},{14,12},{16,18},{18,... | collective-permute-start | bytes 3194888 | tf_op jit(solution)/shard_map/ppermute | solution.py:352
  4.0 31.2 %collective-permute-start.4 = (f32[4,56,640]{2,1,0:T(8,128)S(1)}, f32[4,56,640]{2,1,0:T(8,128)S(1)}, u32[]{:S(2)}, u32[]{:S(2)}) collective-permute-start(f32[4,56,640]{2,1,0:T(8,128)S(1)} %get-tuple-element.35.refs_0_.outer_ref.scaled_ref), channel_id=1, source_target_pairs={{0,126},{2,4},{4,2},{6,8},{8,6},{10,12},{12,10},{14,16},{16,14},{1... | collective-permute-start | bytes 1720328 | tf_op jit(solution)/shard_map/ppermute | solution.py:351
  6.3 1.6 %copy-start.1 = (f32[26,4,8,640]{3,2,1,0:T(8,128)S(1)}, f32[26,4,8,640]{3,2,1,0:T(8,128)}, u32[]{:S(2)}) copy-start(f32[26,4,8,640]{3,2,1,0:T(8,128)} %param.5) | copy-start | bytes 6389764
  13.1 31.3 %collective-permute-start.6 = (f32[4,104,640]{2,1,0:T(8,128)S(1)}, f32[4,104,640]{2,1,0:T(8,128)S(1)}, u32[]{:S(2)}, u32[]{:S(2)}) collective-permute-start(f32[4,104,640]{2,1,0:T(8,128)S(1)} %get-tuple-element.40.inner_ref), channel_id=1, source_target_pairs={{0,2},{2,0},{4,6},{6,4},{8,10},{10,8},{12,14},{14,12},{16,18},{18,... | collective-permute-start | bytes 3194888 | tf_op jit(solution)/shard_map/ppermute | solution.py:365
  17.7 22.7 %collective-permute-start = (f32[4,48,640]{2,1,0:T(8,128)S(1)}, f32[4,48,640]{2,1,0:T(8,128)S(1)}, u32[]{:S(2)}, u32[]{:S(2)}) collective-permute-start(f32[4,48,640]{2,1,0:T(8,128)S(1)} %get-tuple-element.31.refs_1_.outer_ref.scaled_ref), channel_id=1, source_target_pairs={{0,126},{2,4},{4,2},{6,8},{8,6},{10,12},{12,10},{14,16},{16,14},{1... | collective-permute-start | bytes 1474568 | tf_op jit(solution)/shard_map/ppermute | solution.py:351
  36.5 14.3 %collective-permute-start.5 = (f32[4,56,640]{2,1,0:T(8,128)S(1)}, f32[4,56,640]{2,1,0:T(8,128)S(1)}, u32[]{:S(2)}, u32[]{:S(2)}) collective-permute-start(f32[4,56,640]{2,1,0:T(8,128)S(1)} %shard_map.71.refs_0_.outer_ref), channel_id=1, source_target_pairs={{0,126},{2,4},{4,2},{6,8},{8,6},{10,12},{12,10},{14,16},{16,14},{1... | collective-permute-start | bytes 1720328 | tf_op jit(solution)/shard_map/ppermute | solution.py:371
  41.6 12.4 %collective-permute-start.3 = (f32[4,32,640]{2,1,0:T(8,128)S(1)}, f32[4,32,640]{2,1,0:T(8,128)S(1)}, u32[]{:S(2)}, u32[]{:S(2)}) collective-permute-start(f32[4,32,640]{2,1,0:T(8,128)S(1)} %get-tuple-element.39.refs_1_.outer_ref), channel_id=1, source_target_pairs={{0,126},{2,4},{4,2},{6,8},{8,6},{10,12},{12,10},{14,16},{16,14},{1... | collective-permute-start | bytes 983048 | tf_op jit(solution)/shard_map/ppermute | solution.py:371
  44.2 11.6 %collective-permute-start.2 = (f32[4,16,640]{2,1,0:T(8,128)S(1)}, f32[4,16,640]{2,1,0:T(8,128)S(1)}, u32[]{:S(2)}, u32[]{:S(2)}) collective-permute-start(f32[4,16,640]{2,1,0:T(8,128)S(1)} %get-tuple-element.38.refs_2_.outer_ref), channel_id=1, source_target_pairs={{0,126},{2,4},{4,2},{6,8},{8,6},{10,12},{12,10},{14,16},{16,14},{1... | collective-permute-start | bytes 491528 | tf_op jit(solution)/shard_map/ppermute | solution.py:371
  56.2 4.9 %collective-permute-start.7 = (f32[168,128]{1,0:T(8,128)S(1)}, f32[168,128]{1,0:T(8,128)S(1)}, u32[]{:S(2)}, u32[]{:S(2)}) collective-permute-start(f32[168,128]{1,0:T(8,128)S(1)} %get-tuple-element.50.own_ref), channel_id=1, source_target_pairs={{0,1},{1,0},{2,3},{3,2},{4,5},{5,4},{6,7},{7,6},{8,9},{9,8},{10,11... | collective-permute-start | bytes 258056 | tf_op jit(solution)/shard_map/ppermute | solution.py:395

commit v18 on v16

--- a/solution.py
+++ b/solution.py
@@ -48,9 +48,8 @@
 
 
 def chunk_groups(groups):
-    half = (groups + 1) // 2
-    last = max(1, (groups - half) // 3)
-    return [[half], [groups - half - last, last]]
+    first = (groups * 3 + 2) // 5
+    return [[first], [groups - first - 1, 1]]
 
 
 class Chunked:

time: 79 us -> 78.9 us (level)
  waiting for transfers between devices: 26.1 us -> 24 us
  blocking collectives: 15.5 us -> 17 us
    ppermute x3, waiting for transfers between devices: 4.78 us -> 2.88 us  [body(): lax.ppermute(value, 'tile', with_neighbour)]
    all_to_all x1, blocking collectives: 15.5 us -> 17 us  [body(): got = lax.all_to_all(payload, 'tile', split_axis=0, concat_axis=0)]
where the time goes in v18:
time: 78.9 us; the launch traced here: 78.7 us
  waiting for transfers between devices  24 us (30%)
  Pallas kernels  17.1 us (22%)
  blocking collectives  17 us (22%)
  starting transfers between devices  16.5 us (21%)
  local copies, waits for them, and re-layouts  3.2 us (4%)
  between operations  0.88 us (1%)
    ppermute x2, waiting for transfers between devices, body(): outer_halo = [lax.ppermute(part, 'tile', with_neighbour) for part in outer]  18.7 us
    pallas_call x10, Pallas kernels, call(): pl.pallas_call(kernel, out_shape=outs, in_specs=[SMEM if arg.ndim == 1 el...  17.1 us
    all_to_all x1, blocking collectives, body(): got = lax.all_to_all(payload, 'tile', split_axis=0, concat_axis=0)  17 us
    ppermute x3, starting transfers between devices, body(): lax.ppermute(value, 'tile', with_neighbour)  5.39 us
    ppermute x1, starting transfers between devices, body(): v_inner_halo = lax.ppermute(v_inner, 'tile', with_mate)  4.54 us
    ppermute x1, starting transfers between devices, body(): other = lax.ppermute(logs, 'mem', [(0, 1), (1, 0)])  3.37 us
    unnamed x10, local copies, waits for them, and re-layouts  3.2 us
    ppermute x3, waiting for transfers between devices, body(): lax.ppermute(value, 'tile', with_neighbour)  2.88 us
  transfers between devices with their start and end apart: 8, of which 7 were waited for; matrix products, arithmetic and copies ran while one was open for 0% of the time, Pallas kernels for 18%

profile of v18, /device:TPU:1, one launch (start us, length us, event | category | flops | bytes accessed | tf_op | source)
XLA Modules:
  0.0 78.7 jit_solution(3441048736002976341)
XLA Ops:
  0.6 0.0 copy-start.1
  0.6 1.6 %copy-done.1 = f32[26,4,8,640]{3,2,1,0:T(8,128)S(1)} copy-done((f32[26,4,8,640]{3,2,1,0:T(8,128)S(1)}, f32[26,4,8,640]{3,2,1,0:T(8,128)}, u32[]{:S(2)}) %copy-start.1) | copy-done | bytes 2129944
  2.2 0.0 copy-start
  2.2 0.0 copy-start.3
  2.2 0.0 copy-start.4
  2.2 0.4 shard_map.68
  2.6 1.5 %collective-permute-start.1 = (f32[4,104,640]{2,1,0:T(8,128)S(1)}, f32[4,104,640]{2,1,0:T(8,128)S(1)}, u32[]{:S(2)}, u32[]{:S(2)}) collective-permute-start(f32[4,104,640]{2,1,0:T(8,128)S(1)} %get-tuple-element.33.inner_ref.scaled_ref), channel_id=1, source_target_pairs={{0,2},{2,0},{4,6},{6,4},{8,10},{10,8},{12,14},{14,12},{16,18},{18,... | collective-permute-start | bytes 3194888 | tf_op jit(solution)/shard_map/ppermute | solution.py:336
  4.1 1.7 %collective-permute-start.4 = (f32[4,64,640]{2,1,0:T(8,128)S(1)}, f32[4,64,640]{2,1,0:T(8,128)S(1)}, u32[]{:S(2)}, u32[]{:S(2)}) collective-permute-start(f32[4,64,640]{2,1,0:T(8,128)S(1)} %get-tuple-element.35.refs_0_.outer_ref.scaled_ref), channel_id=1, source_target_pairs={{0,126},{2,4},{4,2},{6,8},{8,6},{10,12},{12,10},{14,16},{16,14},{1... | collective-permute-start | bytes 1966088 | tf_op jit(solution)/shard_map/ppermute | solution.py:335
  5.8 0.6 collective-permute-done.1.halo_ref
  6.4 0.0 copy-done
  6.4 0.0 copy-done.3
  6.4 0.0 copy-done.4
  6.4 0.0 copy-start.2
  6.5 1.6 %copy-done.2 = f32[26,4,8,640]{3,2,1,0:T(8,128)S(1)} copy-done((f32[26,4,8,640]{3,2,1,0:T(8,128)S(1)}, f32[26,4,8,640]{3,2,1,0:T(8,128)}, u32[]{:S(2)}) %copy-start.2) | copy-done | bytes 2129944
  8.0 5.2 %shard_map.69 = (f32[4,104,640]{2,1,0:T(8,128)S(1)}, f32[6,104,640]{2,1,0:T(8,128)S(1)}, f32[4,104,640]{2,1,0:T(8,128)S(1)}, f32[104,128]{1,0:T(8,128)S(1)}, f32[112,128]{1,0:T(8,128)S(1)}) custom-call(f32[4,104,640]{2,1,0:T(8,128)S(1)} %collective-permute-done.1.halo_ref, f32[4,104,640]{2,1,0:T(8,128)S(1)} %get-tuple-element.33.inner_ref.scaled_ref, ...), custom_call_target="tpu_custom_call" | custom-call | tf_op jit(solution)/shard_map/pallas_call | solution.py:307
  13.3 4.5 %collective-permute-start.6 = (f32[4,104,640]{2,1,0:T(8,128)S(1)}, f32[4,104,640]{2,1,0:T(8,128)S(1)}, u32[]{:S(2)}, u32[]{:S(2)}) collective-permute-start(f32[4,104,640]{2,1,0:T(8,128)S(1)} %get-tuple-element.40.inner_ref), channel_id=1, source_target_pairs={{0,2},{2,0},{4,6},{6,4},{8,10},{10,8},{12,14},{14,12},{16,18},{18,... | collective-permute-start | bytes 3194888 | tf_op jit(solution)/shard_map/ppermute | solution.py:349
  17.8 0.0 collective-permute-start
  17.8 18.4 %collective-permute-done.4.halo_ref = f32[4,64,640]{2,1,0:T(8,128)S(1)} collective-permute-done((f32[4,64,640]{2,1,0:T(8,128)S(1)}, f32[4,64,640]{2,1,0:T(8,128)S(1)}, u32[]{:S(2)}, u32[]{:S(2)}) %collective-permute-start.4) | collective-permute-done | bytes 655392 | tf_op jit(solution)/shard_map/ppermute | solution.py:335
  36.2 1.5 %shard_map.71.refs_0_.outer_ref = f32[4,64,640]{2,1,0:T(8,128)S(1)} custom-call(f32[4,64,640]{2,1,0:T(8,128)S(1)} %collective-permute-done.4.halo_ref, f32[4,64,640]{2,1,0:T(8,128)S(1)} %get-tuple-element.35.refs_0_.outer_ref.scaled_ref, f32[6,104,640]{2,1,0:T(8,128)S(1)} %get-tuple-element.36.edge_ref, f32[4,104,640]{2,1,0:T(8,128)S(1)} %get-tuple-element.37.filled_ref, ...), custom_call_target="tpu_custom_call" | custom-call | tf_op jit(solution)/shard_map/pallas_call | solution.py:307
  37.7 2.6 %collective-permute-start.5 = (f32[4,64,640]{2,1,0:T(8,128)S(1)}, f32[4,64,640]{2,1,0:T(8,128)S(1)}, u32[]{:S(2)}, u32[]{:S(2)}) collective-permute-start(f32[4,64,640]{2,1,0:T(8,128)S(1)} %shard_map.71.refs_0_.outer_ref), channel_id=1, source_target_pairs={{0,126},{2,4},{4,2},{6,8},{8,6},{10,12},{12,10},{14,16},{16,14},{1... | collective-permute-start | bytes 1966088 | tf_op jit(solution)/shard_map/ppermute | solution.py:355
  40.3 0.3 collective-permute-done.halo_ref
  40.6 1.1 %shard_map.70 = (f32[4,32,640]{2,1,0:T(8,128)S(1)}, f32[4,8,640]{2,1,0:T(8,128)S(1)}) custom-call(f32[4,40,640]{2,1,0:T(8,128)S(1)} %collective-permute-done.halo_ref, f32[4,40,640]{2,1,0:T(8,128)S(1)} %get-tuple-element.31.refs_1_.outer_ref.scaled_ref, f32[6,104,640]{2,1,0:T(8,128)S(1)} %get-tuple-element.36.edge_ref, ...), custom_call_target="tpu_custom_call" | custom-call | tf_op jit(solution)/shard_map/pallas_call | solution.py:307
  41.7 2.6 %collective-permute-start.3 = (f32[4,32,640]{2,1,0:T(8,128)S(1)}, f32[4,32,640]{2,1,0:T(8,128)S(1)}, u32[]{:S(2)}, u32[]{:S(2)}) collective-permute-start(f32[4,32,640]{2,1,0:T(8,128)S(1)} %get-tuple-element.39.refs_1_.outer_ref), channel_id=1, source_target_pairs={{0,126},{2,4},{4,2},{6,8},{8,6},{10,12},{12,10},{14,16},{16,14},{1... | collective-permute-start | bytes 983048 | tf_op jit(solution)/shard_map/ppermute | solution.py:355
  44.3 0.3 collective-permute-start.2
  44.5 0.0 collective-permute-done.6.halo_ref
  44.6 4.3 %shard_map.72 = (f32[4,104,640]{2,1,0:T(8,128)S(1)}, f32[6,104,640]{2,1,0:T(8,128)S(1)}, f32[4,8,640]{2,1,0:T(8,128)S(1)}) custom-call(f32[4,104,640]{2,1,0:T(8,128)S(1)} %collective-permute-done.6.halo_ref, f32[4,104,640]{2,1,0:T(8,128)S(1)} %get-tuple-element.40.inner_ref, f32[4,104,640]{2,1,0:T(8,128)S(1)} %get-tuple-element.33.inner_ref.scaled_ref, ...), custom_call_target="tpu_custom_call" | custom-call | tf_op jit(solution)/shard_map/pallas_call | solution.py:307
  48.8 1.1 %collective-permute-done.5.halo_ref = f32[4,64,640]{2,1,0:T(8,128)S(1)} collective-permute-done((f32[4,64,640]{2,1,0:T(8,128)S(1)}, f32[4,64,640]{2,1,0:T(8,128)S(1)}, u32[]{:S(2)}, u32[]{:S(2)}) %collective-permute-start.5) | collective-permute-done | bytes 655392 | tf_op jit(solution)/shard_map/ppermute | solution.py:355
  50.0 1.5 %shard_map.73 = (f32[4,64,640]{2,1,0:T(8,128)S(1)}, f32[4,8,640]{2,1,0:T(8,128)S(1)}) custom-call(f32[4,64,640]{2,1,0:T(8,128)S(1)} %collective-permute-done.5.halo_ref, f32[4,64,640]{2,1,0:T(8,128)S(1)} %shard_map.71.refs_0_.outer_ref, f32[6,104,640]{2,1,0:T(8,128)S(1)} %get-tuple-element.42.edge_ref, ...), custom_call_target="tpu_custom_call" | custom-call | tf_op jit(solution)/shard_map/pallas_call | solution.py:307
  51.5 1.7 %collective-permute-done.3.halo_ref = f32[4,32,640]{2,1,0:T(8,128)S(1)} collective-permute-done((f32[4,32,640]{2,1,0:T(8,128)S(1)}, f32[4,32,640]{2,1,0:T(8,128)S(1)}, u32[]{:S(2)}, u32[]{:S(2)}) %collective-permute-start.3) | collective-permute-done | bytes 327712 | tf_op jit(solution)/shard_map/ppermute | solution.py:355
  53.2 0.8 %shard_map.74 = (f32[4,32,640]{2,1,0:T(8,128)S(1)}, f32[4,8,640]{2,1,0:T(8,128)S(1)}) custom-call(f32[4,32,640]{2,1,0:T(8,128)S(1)} %collective-permute-done.3.halo_ref, f32[4,32,640]{2,1,0:T(8,128)S(1)} %get-tuple-element.39.refs_1_.outer_ref, f32[6,104,640]{2,1,0:T(8,128)S(1)} %get-tuple-element.42.edge_ref, ...), custom_call_target="tpu_custom_call" | custom-call | tf_op jit(solution)/shard_map/pallas_call | solution.py:307
  54.0 0.1 collective-permute-done.2.halo_ref
  54.1 0.4 shard_map.75
  54.5 3.4 %collective-permute-start.7 = (f32[168,128]{1,0:T(8,128)S(1)}, f32[168,128]{1,0:T(8,128)S(1)}, u32[]{:S(2)}, u32[]{:S(2)}) collective-permute-start(f32[168,128]{1,0:T(8,128)S(1)} %get-tuple-element.50.own_ref), channel_id=1, source_target_pairs={{0,1},{1,0},{2,3},{3,2},{4,5},{5,4},{6,7},{7,6},{8,9},{9,8},{10,11... | collective-permute-start | bytes 258056 | tf_op jit(solution)/shard_map/ppermute | solution.py:379
  57.8 1.9 %collective-permute-done.7.other_ref = f32[168,128]{1,0:T(8,128)S(1)} collective-permute-done((f32[168,128]{1,0:T(8,128)S(1)}, f32[168,128]{1,0:T(8,128)S(1)}, u32[]{:S(2)}, u32[]{:S(2)}) %collective-permute-start.7) | collective-permute-done | bytes 86048 | tf_op jit(solution)/shard_map/ppermute | solution.py:379
  59.7 0.1 shard_map.76
  59.9 17.0 %all_to_all.5.got_ref = f32[64,1,128]{2,1,0:T(1,128)S(1)} all-to-all(f32[64,1,128]{2,1,0:T(1,128)S(1)} %get-tuple-element.52), channel_id=1, replica_groups=mesh['tile'=64,'mem'=2] {'tile'}, dimensions={0} | all-to-all | bytes 65536 | tf_op jit(solution)/shard_map/all_to_all | solution.py:381
  76.9 1.7 %shard_map.77 = (f32[4,8,640]{2,1,0:T(8,128)}, f32[832,640]{1,0:T(8,128)}) custom-call(f32[64,1,128]{2,1,0:T(1,128)S(1)} %all_to_all.5.got_ref, f32[4,8,640]{2,1,0:T(8,128)S(1)} %get-tuple-element.53.merged_ref, f32[4,104,640]{2,1,0:T(8,128)S(1)} %get-tuple-element.54.inner_ref, f32[4,64,640]{2,1,0:T(8,128)S(1)} %get-tuple-element.55.refs_0_, ...), custom_call_target="tpu_custom_call" | custom-call | tf_op jit(solution)/shard_map/pallas_call | solution.py:307
Async XLA Ops:
  0.6 1.6 %copy-start.1 = (f32[26,4,8,640]{3,2,1,0:T(8,128)S(1)}, f32[26,4,8,640]{3,2,1,0:T(8,128)}, u32[]{:S(2)}) copy-start(f32[26,4,8,640]{3,2,1,0:T(8,128)} %param.6) | copy-start | bytes 6389764
  2.2 4.2 %copy-start = (f32[5,8,640]{2,1,0:T(8,128)S(1)}, f32[5,8,640]{2,1,0:T(8,128)}, u32[]{:S(2)}) copy-start(f32[5,8,640]{2,1,0:T(8,128)} %constant.2.clone.coef_ref) | copy-start | bytes 307204
  2.2 4.2 %copy-start.3 = (s32[8,640]{1,0:T(8,128)S(1)}, s32[8,640]{1,0:T(8,128)}, u32[]{:S(2)}) copy-start(s32[8,640]{1,0:T(8,128)} %mask_ref.1) | copy-start | bytes 61444
  2.2 4.2 %copy-start.4 = (s32[26]{0:T(128)S(1)}, s32[26]{0:T(128)}, u32[]{:S(2)}) copy-start(s32[26]{0:T(128)} %count_ref.1) | copy-start | bytes 316
  2.6 3.8 %collective-permute-start.1 = (f32[4,104,640]{2,1,0:T(8,128)S(1)}, f32[4,104,640]{2,1,0:T(8,128)S(1)}, u32[]{:S(2)}, u32[]{:S(2)}) collective-permute-start(f32[4,104,640]{2,1,0:T(8,128)S(1)} %get-tuple-element.33.inner_ref.scaled_ref), channel_id=1, source_target_pairs={{0,2},{2,0},{4,6},{6,4},{8,10},{10,8},{12,14},{14,12},{16,18},{18,... | collective-permute-start | bytes 3194888 | tf_op jit(solution)/shard_map/ppermute | solution.py:336
  4.1 32.1 %collective-permute-start.4 = (f32[4,64,640]{2,1,0:T(8,128)S(1)}, f32[4,64,640]{2,1,0:T(8,128)S(1)}, u32[]{:S(2)}, u32[]{:S(2)}) collective-permute-start(f32[4,64,640]{2,1,0:T(8,128)S(1)} %get-tuple-element.35.refs_0_.outer_ref.scaled_ref), channel_id=1, source_target_pairs={{0,126},{2,4},{4,2},{6,8},{8,6},{10,12},{12,10},{14,16},{16,14},{1... | collective-permute-start | bytes 1966088 | tf_op jit(solution)/shard_map/ppermute | solution.py:335
  6.4 1.6 %copy-start.2 = (f32[26,4,8,640]{3,2,1,0:T(8,128)S(1)}, f32[26,4,8,640]{3,2,1,0:T(8,128)}, u32[]{:S(2)}) copy-start(f32[26,4,8,640]{3,2,1,0:T(8,128)} %param.5) | copy-start | bytes 6389764
  13.3 31.3 %collective-permute-start.6 = (f32[4,104,640]{2,1,0:T(8,128)S(1)}, f32[4,104,640]{2,1,0:T(8,128)S(1)}, u32[]{:S(2)}, u32[]{:S(2)}) collective-permute-start(f32[4,104,640]{2,1,0:T(8,128)S(1)} %get-tuple-element.40.inner_ref), channel_id=1, source_target_pairs={{0,2},{2,0},{4,6},{6,4},{8,10},{10,8},{12,14},{14,12},{16,18},{18,... | collective-permute-start | bytes 3194888 | tf_op jit(solution)/shard_map/ppermute | solution.py:349
  17.8 22.7 %collective-permute-start = (f32[4,40,640]{2,1,0:T(8,128)S(1)}, f32[4,40,640]{2,1,0:T(8,128)S(1)}, u32[]{:S(2)}, u32[]{:S(2)}) collective-permute-start(f32[4,40,640]{2,1,0:T(8,128)S(1)} %get-tuple-element.31.refs_1_.outer_ref.scaled_ref), channel_id=1, source_target_pairs={{0,126},{2,4},{4,2},{6,8},{8,6},{10,12},{12,10},{14,16},{16,14},{1... | collective-permute-start | bytes 1228808 | tf_op jit(solution)/shard_map/ppermute | solution.py:335
  37.7 12.3 %collective-permute-start.5 = (f32[4,64,640]{2,1,0:T(8,128)S(1)}, f32[4,64,640]{2,1,0:T(8,128)S(1)}, u32[]{:S(2)}, u32[]{:S(2)}) collective-permute-start(f32[4,64,640]{2,1,0:T(8,128)S(1)} %shard_map.71.refs_0_.outer_ref), channel_id=1, source_target_pairs={{0,126},{2,4},{4,2},{6,8},{8,6},{10,12},{12,10},{14,16},{16,14},{1... | collective-permute-start | bytes 1966088 | tf_op jit(solution)/shard_map/ppermute | solution.py:355
  41.7 11.5 %collective-permute-start.3 = (f32[4,32,640]{2,1,0:T(8,128)S(1)}, f32[4,32,640]{2,1,0:T(8,128)S(1)}, u32[]{:S(2)}, u32[]{:S(2)}) collective-permute-start(f32[4,32,640]{2,1,0:T(8,128)S(1)} %get-tuple-element.39.refs_1_.outer_ref), channel_id=1, source_target_pairs={{0,126},{2,4},{4,2},{6,8},{8,6},{10,12},{12,10},{14,16},{16,14},{1... | collective-permute-start | bytes 983048 | tf_op jit(solution)/shard_map/ppermute | solution.py:355
  44.3 9.8 %collective-permute-start.2 = (f32[4,8,640]{2,1,0:T(8,128)S(1)}, f32[4,8,640]{2,1,0:T(8,128)S(1)}, u32[]{:S(2)}, u32[]{:S(2)}) collective-permute-start(f32[4,8,640]{2,1,0:T(8,128)S(1)} %get-tuple-element.38.refs_2_.outer_ref), channel_id=1, source_target_pairs={{0,126},{2,4},{4,2},{6,8},{8,6},{10,12},{12,10},{14,16},{16,14},{1... | collective-permute-start | bytes 245768 | tf_op jit(solution)/shard_map/ppermute | solution.py:355
  54.5 5.2 %collective-permute-start.7 = (f32[168,128]{1,0:T(8,128)S(1)}, f32[168,128]{1,0:T(8,128)S(1)}, u32[]{:S(2)}, u32[]{:S(2)}) collective-permute-start(f32[168,128]{1,0:T(8,128)S(1)} %get-tuple-element.50.own_ref), channel_id=1, source_target_pairs={{0,1},{1,0},{2,3},{3,2},{4,5},{5,4},{6,7},{7,6},{8,9},{9,8},{10,11... | collective-permute-start | bytes 258056 | tf_op jit(solution)/shard_map/ppermute | solution.py:379

commit v19 on v18

--- a/solution.py
+++ b/solution.py
@@ -243,13 +243,14 @@
         inner = inner + pltpu.roll(inner, SUB // 2, 0)
         both = jnp.where(low, outer, inner)
         for t in range(tiles):
-            logs_ref[rows_of(c * tiles + t), :] = both[:, t * 128 : (t + 1) * 128]
-    logs_ref[rows_of(REACH * tiles), :] = weight_ref[rows_of(weight_ref.shape[0] // SUB - 1), :]
-
-
-def merge_kernel(own_ref, other_ref, mass_ref, coef_ref, merged_ref, payload_ref):
+            logs_ref[:, rows_of(c * tiles + t), :] = jnp.stack([both[:, t * 128 : (t + 1) * 128]] * 2)
+    count = weight_ref[rows_of(weight_ref.shape[0] // SUB - 1), :]
+    logs_ref[:, rows_of(REACH * tiles), :] = jnp.stack([count] * 2)
+
+
+def merge_kernel(logs_ref, mass_ref, coef_ref, merged_ref, payload_ref):
     members, tiles = mass_ref.shape[0], merged_ref.shape[2] // 128
-    both = lambda n: own_ref[rows_of(n), :] + other_ref[rows_of(n), :]
+    both = lambda n: logs_ref[0, rows_of(n), :] + logs_ref[1, rows_of(n), :]
     scale = 1.0 / both(REACH * tiles)
     level = jnp.zeros((SUB, 128), jnp.float32)
     for c in range(REACH):
@@ -369,15 +370,15 @@
         else:
             inverse, logs = call(
                 partial(last_return_kernel, base, first),
-                (part, shape((REACH * lat // 128 + 1) * SUB, 128)),
+                (part, shape(2, (REACH * lat // 128 + 1) * SUB, 128)),
                 *operands,
                 inner_logs,
                 *earlier,
                 scratch=[pltpu.VMEM((REACH, SUB, lat), jnp.float32)],
             )
         inverses.append(inverse)
-    other = lax.ppermute(logs, "mem", [(0, 1), (1, 0)])
-    merged, payload = call(merge_kernel, (packed, shape(tiles, 1, 128)), logs, other, mass, coef)
+    logs = lax.all_to_all(logs, "mem", split_axis=0, concat_axis=0)
+    merged, payload = call(merge_kernel, (packed, shape(tiles, 1, 128)), logs, mass, coef)
     got = lax.all_to_all(payload, "tile", split_axis=0, concat_axis=0)
     barycenter, updated = call(
         partial(finish_kernel, float(cells)),

time: 78.9 us -> 83.1 us (1.053)
  blocking collectives: 17 us -> 26.1 us
  starting transfers between devices: 16.5 us -> 13.1 us
  waiting for transfers between devices: 24 us -> 22.5 us
    all_to_all x0 -> x1, blocking collectives: none -> 9.13 us  [body(): logs = lax.all_to_all(logs, 'mem', split_axis=0, concat_axis=0)]
    ppermute x1 -> x0, starting transfers between devices: 3.37 us -> none  [body(): other = lax.ppermute(logs, 'mem', [(0, 1), (1, 0)])]
    ppermute x1 -> x0, waiting for transfers between devices: 1.88 us -> none  [body(): other = lax.ppermute(logs, 'mem', [(0, 1), (1, 0)])]
  transfers between devices with their start and end apart: 8 -> 7, of which waited for: 7 -> 6; matrix products, arithmetic and copies ran while one was open for 0% -> 0% of each run, Pallas kernels for 18% -> 17%
where the time goes in v19:
time: 83.1 us; the launch traced here: 82.9 us
  blocking collectives  26.1 us (31%)
  waiting for transfers between devices  22.5 us (27%)
  Pallas kernels  17.1 us (21%)
  starting transfers between devices  13.1 us (16%)
  local copies, waits for them, and re-layouts  3.2 us (4%)
  between operations  0.88 us (1%)
    ppermute x2, waiting for transfers between devices, body(): outer_halo = [lax.ppermute(part, 'tile', with_neighbour) for part in outer]  18.7 us
    pallas_call x10, Pallas kernels, call(): pl.pallas_call(kernel, out_shape=outs, in_specs=[SMEM if arg.ndim == 1 el...  17.1 us
    all_to_all x1, blocking collectives, body(): got = lax.all_to_all(payload, 'tile', split_axis=0, concat_axis=0)  17 us
    all_to_all x1, blocking collectives, body(): logs = lax.all_to_all(logs, 'mem', split_axis=0, concat_axis=0)  9.13 us
    ppermute x3, starting transfers between devices, body(): lax.ppermute(value, 'tile', with_neighbour)  5.39 us
    ppermute x1, starting transfers between devices, body(): v_inner_halo = lax.ppermute(v_inner, 'tile', with_mate)  4.54 us
    unnamed x10, local copies, waits for them, and re-layouts  3.2 us
    ppermute x3, waiting for transfers between devices, body(): lax.ppermute(value, 'tile', with_neighbour)  3.18 us
  transfers between devices with their start and end apart: 7, of which 6 were waited for; matrix products, arithmetic and copies ran while one was open for 0% of the time, Pallas kernels for 17%

profile of v19, /device:TPU:1, one launch (start us, length us, event | category | flops | bytes accessed | tf_op | source)
XLA Modules:
  0.0 82.9 jit_solution(5090183132247347584)
XLA Ops:
  0.6 0.0 copy-start.1
  0.6 1.6 %copy-done.1 = f32[26,4,8,640]{3,2,1,0:T(8,128)S(1)} copy-done((f32[26,4,8,640]{3,2,1,0:T(8,128)S(1)}, f32[26,4,8,640]{3,2,1,0:T(8,128)}, u32[]{:S(2)}) %copy-start.1) | copy-done | bytes 2129944
  2.2 0.0 copy-start
  2.2 0.0 copy-start.3
  2.2 0.0 copy-start.4
  2.2 0.4 shard_map.68
  2.6 1.5 %collective-permute-start.1 = (f32[4,104,640]{2,1,0:T(8,128)S(1)}, f32[4,104,640]{2,1,0:T(8,128)S(1)}, u32[]{:S(2)}, u32[]{:S(2)}) collective-permute-start(f32[4,104,640]{2,1,0:T(8,128)S(1)} %get-tuple-element.33.inner_ref.scaled_ref), channel_id=1, source_target_pairs={{0,2},{2,0},{4,6},{6,4},{8,10},{10,8},{12,14},{14,12},{16,18},{18,... | collective-permute-start | bytes 3194888 | tf_op jit(solution)/shard_map/ppermute | solution.py:337
  4.1 1.7 %collective-permute-start.4 = (f32[4,64,640]{2,1,0:T(8,128)S(1)}, f32[4,64,640]{2,1,0:T(8,128)S(1)}, u32[]{:S(2)}, u32[]{:S(2)}) collective-permute-start(f32[4,64,640]{2,1,0:T(8,128)S(1)} %get-tuple-element.35.refs_0_.outer_ref.scaled_ref), channel_id=1, source_target_pairs={{0,126},{2,4},{4,2},{6,8},{8,6},{10,12},{12,10},{14,16},{16,14},{1... | collective-permute-start | bytes 1966088 | tf_op jit(solution)/shard_map/ppermute | solution.py:336
  5.8 0.6 collective-permute-done.1.halo_ref
  6.4 0.0 copy-done
  6.4 0.0 copy-done.3
  6.4 0.0 copy-done.4
  6.4 0.0 copy-start.2
  6.5 1.6 %copy-done.2 = f32[26,4,8,640]{3,2,1,0:T(8,128)S(1)} copy-done((f32[26,4,8,640]{3,2,1,0:T(8,128)S(1)}, f32[26,4,8,640]{3,2,1,0:T(8,128)}, u32[]{:S(2)}) %copy-start.2) | copy-done | bytes 2129944
  8.0 5.2 %shard_map.69 = (f32[4,104,640]{2,1,0:T(8,128)S(1)}, f32[6,104,640]{2,1,0:T(8,128)S(1)}, f32[4,104,640]{2,1,0:T(8,128)S(1)}, f32[104,128]{1,0:T(8,128)S(1)}, f32[112,128]{1,0:T(8,128)S(1)}) custom-call(f32[4,104,640]{2,1,0:T(8,128)S(1)} %collective-permute-done.1.halo_ref, f32[4,104,640]{2,1,0:T(8,128)S(1)} %get-tuple-element.33.inner_ref.scaled_ref, ...), custom_call_target="tpu_custom_call" | custom-call | tf_op jit(solution)/shard_map/pallas_call | solution.py:308
  13.3 4.5 %collective-permute-start.6 = (f32[4,104,640]{2,1,0:T(8,128)S(1)}, f32[4,104,640]{2,1,0:T(8,128)S(1)}, u32[]{:S(2)}, u32[]{:S(2)}) collective-permute-start(f32[4,104,640]{2,1,0:T(8,128)S(1)} %get-tuple-element.40.inner_ref), channel_id=1, source_target_pairs={{0,2},{2,0},{4,6},{6,4},{8,10},{10,8},{12,14},{14,12},{16,18},{18,... | collective-permute-start | bytes 3194888 | tf_op jit(solution)/shard_map/ppermute | solution.py:350
  17.8 0.0 collective-permute-start
  17.8 18.4 %collective-permute-done.4.halo_ref = f32[4,64,640]{2,1,0:T(8,128)S(1)} collective-permute-done((f32[4,64,640]{2,1,0:T(8,128)S(1)}, f32[4,64,640]{2,1,0:T(8,128)S(1)}, u32[]{:S(2)}, u32[]{:S(2)}) %collective-permute-start.4) | collective-permute-done | bytes 655392 | tf_op jit(solution)/shard_map/ppermute | solution.py:336
  36.2 1.5 %shard_map.71.refs_0_.outer_ref = f32[4,64,640]{2,1,0:T(8,128)S(1)} custom-call(f32[4,64,640]{2,1,0:T(8,128)S(1)} %collective-permute-done.4.halo_ref, f32[4,64,640]{2,1,0:T(8,128)S(1)} %get-tuple-element.35.refs_0_.outer_ref.scaled_ref, f32[6,104,640]{2,1,0:T(8,128)S(1)} %get-tuple-element.36.edge_ref, f32[4,104,640]{2,1,0:T(8,128)S(1)} %get-tuple-element.37.filled_ref, ...), custom_call_target="tpu_custom_call" | custom-call | tf_op jit(solution)/shard_map/pallas_call | solution.py:308
  37.7 2.6 %collective-permute-start.5 = (f32[4,64,640]{2,1,0:T(8,128)S(1)}, f32[4,64,640]{2,1,0:T(8,128)S(1)}, u32[]{:S(2)}, u32[]{:S(2)}) collective-permute-start(f32[4,64,640]{2,1,0:T(8,128)S(1)} %shard_map.71.refs_0_.outer_ref), channel_id=1, source_target_pairs={{0,126},{2,4},{4,2},{6,8},{8,6},{10,12},{12,10},{14,16},{16,14},{1... | collective-permute-start | bytes 1966088 | tf_op jit(solution)/shard_map/ppermute | solution.py:356
  40.3 0.3 collective-permute-done.halo_ref
  40.6 1.1 %shard_map.70 = (f32[4,32,640]{2,1,0:T(8,128)S(1)}, f32[4,8,640]{2,1,0:T(8,128)S(1)}) custom-call(f32[4,40,640]{2,1,0:T(8,128)S(1)} %collective-permute-done.halo_ref, f32[4,40,640]{2,1,0:T(8,128)S(1)} %get-tuple-element.31.refs_1_.outer_ref.scaled_ref, f32[6,104,640]{2,1,0:T(8,128)S(1)} %get-tuple-element.36.edge_ref, ...), custom_call_target="tpu_custom_call" | custom-call | tf_op jit(solution)/shard_map/pallas_call | solution.py:308
  41.7 2.6 %collective-permute-start.3 = (f32[4,32,640]{2,1,0:T(8,128)S(1)}, f32[4,32,640]{2,1,0:T(8,128)S(1)}, u32[]{:S(2)}, u32[]{:S(2)}) collective-permute-start(f32[4,32,640]{2,1,0:T(8,128)S(1)} %get-tuple-element.39.refs_1_.outer_ref), channel_id=1, source_target_pairs={{0,126},{2,4},{4,2},{6,8},{8,6},{10,12},{12,10},{14,16},{16,14},{1... | collective-permute-start | bytes 983048 | tf_op jit(solution)/shard_map/ppermute | solution.py:356
  44.3 0.3 collective-permute-start.2
  44.5 0.0 collective-permute-done.6.halo_ref
  44.6 4.3 %shard_map.72 = (f32[4,104,640]{2,1,0:T(8,128)S(1)}, f32[6,104,640]{2,1,0:T(8,128)S(1)}, f32[4,8,640]{2,1,0:T(8,128)S(1)}) custom-call(f32[4,104,640]{2,1,0:T(8,128)S(1)} %collective-permute-done.6.halo_ref, f32[4,104,640]{2,1,0:T(8,128)S(1)} %get-tuple-element.40.inner_ref, f32[4,104,640]{2,1,0:T(8,128)S(1)} %get-tuple-element.33.inner_ref.scaled_ref, ...), custom_call_target="tpu_custom_call" | custom-call | tf_op jit(solution)/shard_map/pallas_call | solution.py:308
  48.8 0.9 %collective-permute-done.5.halo_ref = f32[4,64,640]{2,1,0:T(8,128)S(1)} collective-permute-done((f32[4,64,640]{2,1,0:T(8,128)S(1)}, f32[4,64,640]{2,1,0:T(8,128)S(1)}, u32[]{:S(2)}, u32[]{:S(2)}) %collective-permute-start.5) | collective-permute-done | bytes 655392 | tf_op jit(solution)/shard_map/ppermute | solution.py:356
  49.7 1.5 %shard_map.73 = (f32[4,64,640]{2,1,0:T(8,128)S(1)}, f32[4,8,640]{2,1,0:T(8,128)S(1)}) custom-call(f32[4,64,640]{2,1,0:T(8,128)S(1)} %collective-permute-done.5.halo_ref, f32[4,64,640]{2,1,0:T(8,128)S(1)} %shard_map.71.refs_0_.outer_ref, f32[6,104,640]{2,1,0:T(8,128)S(1)} %get-tuple-element.42.edge_ref, ...), custom_call_target="tpu_custom_call" | custom-call | tf_op jit(solution)/shard_map/pallas_call | solution.py:308
  51.2 2.3 %collective-permute-done.3.halo_ref = f32[4,32,640]{2,1,0:T(8,128)S(1)} collective-permute-done((f32[4,32,640]{2,1,0:T(8,128)S(1)}, f32[4,32,640]{2,1,0:T(8,128)S(1)}, u32[]{:S(2)}, u32[]{:S(2)}) %collective-permute-start.3) | collective-permute-done | bytes 327712 | tf_op jit(solution)/shard_map/ppermute | solution.py:356
  53.5 0.8 shard_map.74
  54.3 0.1 collective-permute-done.2.halo_ref
  54.4 0.4 shard_map.75
  54.8 9.1 %all_to_all.10.logs_ref = f32[2,168,128]{2,1,0:T(8,128)S(1)} all-to-all(f32[2,168,128]{2,1,0:T(8,128)S(1)} %get-tuple-element.50), channel_id=1, replica_groups=mesh['tile'=64,'mem'=2] {'mem'}, dimensions={0} | all-to-all | bytes 344064 | tf_op jit(solution)/shard_map/all_to_all | solution.py:380
  63.9 0.1 shard_map.76
  64.0 17.0 %all_to_all.11.got_ref = f32[64,1,128]{2,1,0:T(1,128)S(1)} all-to-all(f32[64,1,128]{2,1,0:T(1,128)S(1)} %get-tuple-element.52), channel_id=1, replica_groups=mesh['tile'=64,'mem'=2] {'tile'}, dimensions={0} | all-to-all | bytes 65536 | tf_op jit(solution)/shard_map/all_to_all | solution.py:382
  81.0 1.7 %shard_map.77 = (f32[4,8,640]{2,1,0:T(8,128)}, f32[832,640]{1,0:T(8,128)}) custom-call(f32[64,1,128]{2,1,0:T(1,128)S(1)} %all_to_all.11.got_ref, f32[4,8,640]{2,1,0:T(8,128)S(1)} %get-tuple-element.53.merged_ref, f32[4,104,640]{2,1,0:T(8,128)S(1)} %get-tuple-element.54.inner_ref, f32[4,64,640]{2,1,0:T(8,128)S(1)} %get-tuple-element.55.refs_0_, ...), custom_call_target="tpu_custom_call" | custom-call | tf_op jit(solution)/shard_map/pallas_call | solution.py:308
Async XLA Ops:
  0.6 1.6 %copy-start.1 = (f32[26,4,8,640]{3,2,1,0:T(8,128)S(1)}, f32[26,4,8,640]{3,2,1,0:T(8,128)}, u32[]{:S(2)}) copy-start(f32[26,4,8,640]{3,2,1,0:T(8,128)} %param.6) | copy-start | bytes 6389764
  2.2 4.2 %copy-start = (f32[5,8,640]{2,1,0:T(8,128)S(1)}, f32[5,8,640]{2,1,0:T(8,128)}, u32[]{:S(2)}) copy-start(f32[5,8,640]{2,1,0:T(8,128)} %constant.2.clone.coef_ref) | copy-start | bytes 307204
  2.2 4.2 %copy-start.3 = (s32[8,640]{1,0:T(8,128)S(1)}, s32[8,640]{1,0:T(8,128)}, u32[]{:S(2)}) copy-start(s32[8,640]{1,0:T(8,128)} %mask_ref.1) | copy-start | bytes 61444
  2.2 4.2 %copy-start.4 = (s32[26]{0:T(128)S(1)}, s32[26]{0:T(128)}, u32[]{:S(2)}) copy-start(s32[26]{0:T(128)} %count_ref.1) | copy-start | bytes 316
  2.6 3.8 %collective-permute-start.1 = (f32[4,104,640]{2,1,0:T(8,128)S(1)}, f32[4,104,640]{2,1,0:T(8,128)S(1)}, u32[]{:S(2)}, u32[]{:S(2)}) collective-permute-start(f32[4,104,640]{2,1,0:T(8,128)S(1)} %get-tuple-element.33.inner_ref.scaled_ref), channel_id=1, source_target_pairs={{0,2},{2,0},{4,6},{6,4},{8,10},{10,8},{12,14},{14,12},{16,18},{18,... | collective-permute-start | bytes 3194888 | tf_op jit(solution)/shard_map/ppermute | solution.py:337
  4.1 32.1 %collective-permute-start.4 = (f32[4,64,640]{2,1,0:T(8,128)S(1)}, f32[4,64,640]{2,1,0:T(8,128)S(1)}, u32[]{:S(2)}, u32[]{:S(2)}) collective-permute-start(f32[4,64,640]{2,1,0:T(8,128)S(1)} %get-tuple-element.35.refs_0_.outer_ref.scaled_ref), channel_id=1, source_target_pairs={{0,126},{2,4},{4,2},{6,8},{8,6},{10,12},{12,10},{14,16},{16,14},{1... | collective-permute-start | bytes 1966088 | tf_op jit(solution)/shard_map/ppermute | solution.py:336
  6.4 1.6 %copy-start.2 = (f32[26,4,8,640]{3,2,1,0:T(8,128)S(1)}, f32[26,4,8,640]{3,2,1,0:T(8,128)}, u32[]{:S(2)}) copy-start(f32[26,4,8,640]{3,2,1,0:T(8,128)} %param.5) | copy-start | bytes 6389764
  13.3 31.3 %collective-permute-start.6 = (f32[4,104,640]{2,1,0:T(8,128)S(1)}, f32[4,104,640]{2,1,0:T(8,128)S(1)}, u32[]{:S(2)}, u32[]{:S(2)}) collective-permute-start(f32[4,104,640]{2,1,0:T(8,128)S(1)} %get-tuple-element.40.inner_ref), channel_id=1, source_target_pairs={{0,2},{2,0},{4,6},{6,4},{8,10},{10,8},{12,14},{14,12},{16,18},{18,... | collective-permute-start | bytes 3194888 | tf_op jit(solution)/shard_map/ppermute | solution.py:350
  17.8 22.7 %collective-permute-start = (f32[4,40,640]{2,1,0:T(8,128)S(1)}, f32[4,40,640]{2,1,0:T(8,128)S(1)}, u32[]{:S(2)}, u32[]{:S(2)}) collective-permute-start(f32[4,40,640]{2,1,0:T(8,128)S(1)} %get-tuple-element.31.refs_1_.outer_ref.scaled_ref), channel_id=1, source_target_pairs={{0,126},{2,4},{4,2},{6,8},{8,6},{10,12},{12,10},{14,16},{16,14},{1... | collective-permute-start | bytes 1228808 | tf_op jit(solution)/shard_map/ppermute | solution.py:336
  37.7 12.0 %collective-permute-start.5 = (f32[4,64,640]{2,1,0:T(8,128)S(1)}, f32[4,64,640]{2,1,0:T(8,128)S(1)}, u32[]{:S(2)}, u32[]{:S(2)}) collective-permute-start(f32[4,64,640]{2,1,0:T(8,128)S(1)} %shard_map.71.refs_0_.outer_ref), channel_id=1, source_target_pairs={{0,126},{2,4},{4,2},{6,8},{8,6},{10,12},{12,10},{14,16},{16,14},{1... | collective-permute-start | bytes 1966088 | tf_op jit(solution)/shard_map/ppermute | solution.py:356
  41.7 11.8 %collective-permute-start.3 = (f32[4,32,640]{2,1,0:T(8,128)S(1)}, f32[4,32,640]{2,1,0:T(8,128)S(1)}, u32[]{:S(2)}, u32[]{:S(2)}) collective-permute-start(f32[4,32,640]{2,1,0:T(8,128)S(1)} %get-tuple-element.39.refs_1_.outer_ref), channel_id=1, source_target_pairs={{0,126},{2,4},{4,2},{6,8},{8,6},{10,12},{12,10},{14,16},{16,14},{1... | collective-permute-start | bytes 983048 | tf_op jit(solution)/shard_map/ppermute | solution.py:356
  44.3 10.1 %collective-permute-start.2 = (f32[4,8,640]{2,1,0:T(8,128)S(1)}, f32[4,8,640]{2,1,0:T(8,128)S(1)}, u32[]{:S(2)}, u32[]{:S(2)}) collective-permute-start(f32[4,8,640]{2,1,0:T(8,128)S(1)} %get-tuple-element.38.refs_2_.outer_ref), channel_id=1, source_target_pairs={{0,126},{2,4},{4,2},{6,8},{8,6},{10,12},{12,10},{14,16},{16,14},{1... | collective-permute-start | bytes 245768 | tf_op jit(solution)/shard_map/ppermute | solution.py:356

commit v20 on v18

--- a/solution.py
+++ b/solution.py
@@ -48,7 +48,7 @@
 
 
 def chunk_groups(groups):
-    first = (groups * 3 + 2) // 5
+    first = (groups + 1) // 2
     return [[first], [groups - first - 1, 1]]
 
 

time: 78.9 us -> 79.2 us (level)
  waiting for transfers between devices: 24 us -> 26.1 us
  blocking collectives: 17 us -> 15.4 us
    ppermute x3, waiting for transfers between devices: 2.88 us -> 4.72 us  [body(): lax.ppermute(value, 'tile', with_neighbour)]
    all_to_all x1, blocking collectives: 17 us -> 15.4 us  [body(): got = lax.all_to_all(payload, 'tile', split_axis=0, concat_axis=0)]
  transfers between devices with their start and end apart: 8 -> 8, of which waited for: 7 -> 6; matrix products, arithmetic and copies ran while one was open for 0% -> 0% of each run, Pallas kernels for 18% -> 18%
where the time goes in v20:
time: 79.2 us; the launch traced here: 79 us
  waiting for transfers between devices  26.1 us (33%)
  Pallas kernels  17.1 us (22%)
  starting transfers between devices  16.4 us (21%)
  blocking collectives  15.4 us (19%)
  local copies, waits for them, and re-layouts  3.2 us (4%)
  between operations  0.89 us (1%)
    ppermute x2, waiting for transfers between devices, body(): outer_halo = [lax.ppermute(part, 'tile', with_neighbour) for part in outer]  18.9 us
    pallas_call x10, Pallas kernels, call(): pl.pallas_call(kernel, out_shape=outs, in_specs=[SMEM if arg.ndim == 1 el...  17.1 us
    all_to_all x1, blocking collectives, body(): got = lax.all_to_all(payload, 'tile', split_axis=0, concat_axis=0)  15.4 us
    ppermute x3, starting transfers between devices, body(): lax.ppermute(value, 'tile', with_neighbour)  5.39 us
    ppermute x3, waiting for transfers between devices, body(): lax.ppermute(value, 'tile', with_neighbour)  4.72 us
    ppermute x1, starting transfers between devices, body(): v_inner_halo = lax.ppermute(v_inner, 'tile', with_mate)  4.54 us
    ppermute x1, starting transfers between devices, body(): other = lax.ppermute(logs, 'mem', [(0, 1), (1, 0)])  3.22 us
    unnamed x10, local copies, waits for them, and re-layouts  3.2 us
  transfers between devices with their start and end apart: 8, of which 6 were waited for; matrix products, arithmetic and copies ran while one was open for 0% of the time, Pallas kernels for 18%

profile of v20, /device:TPU:1, one launch (start us, length us, event | category | flops | bytes accessed | tf_op | source)
XLA Modules:
  0.0 79.0 jit_solution(2975619098839402206)
XLA Ops:
  0.6 0.0 copy-start.1
  0.6 1.6 %copy-done.1 = f32[26,4,8,640]{3,2,1,0:T(8,128)S(1)} copy-done((f32[26,4,8,640]{3,2,1,0:T(8,128)S(1)}, f32[26,4,8,640]{3,2,1,0:T(8,128)}, u32[]{:S(2)}) %copy-start.1) | copy-done | bytes 2129944
  2.2 0.0 copy-start
  2.2 0.0 copy-start.3
  2.2 0.0 copy-start.4
  2.2 0.4 shard_map.68
  2.6 1.5 %collective-permute-start.1 = (f32[4,104,640]{2,1,0:T(8,128)S(1)}, f32[4,104,640]{2,1,0:T(8,128)S(1)}, u32[]{:S(2)}, u32[]{:S(2)}) collective-permute-start(f32[4,104,640]{2,1,0:T(8,128)S(1)} %get-tuple-element.33.inner_ref.scaled_ref), channel_id=1, source_target_pairs={{0,2},{2,0},{4,6},{6,4},{8,10},{10,8},{12,14},{14,12},{16,18},{18,... | collective-permute-start | bytes 3194888 | tf_op jit(solution)/shard_map/ppermute | solution.py:336
  4.1 1.7 %collective-permute-start.4 = (f32[4,56,640]{2,1,0:T(8,128)S(1)}, f32[4,56,640]{2,1,0:T(8,128)S(1)}, u32[]{:S(2)}, u32[]{:S(2)}) collective-permute-start(f32[4,56,640]{2,1,0:T(8,128)S(1)} %get-tuple-element.35.refs_0_.outer_ref.scaled_ref), channel_id=1, source_target_pairs={{0,126},{2,4},{4,2},{6,8},{8,6},{10,12},{12,10},{14,16},{16,14},{1... | collective-permute-start | bytes 1720328 | tf_op jit(solution)/shard_map/ppermute | solution.py:335
  5.8 0.6 collective-permute-done.1.halo_ref
  6.4 0.0 copy-done
  6.4 0.0 copy-done.3
  6.4 0.0 copy-done.4
  6.4 0.0 copy-start.2
  6.5 1.6 %copy-done.2 = f32[26,4,8,640]{3,2,1,0:T(8,128)S(1)} copy-done((f32[26,4,8,640]{3,2,1,0:T(8,128)S(1)}, f32[26,4,8,640]{3,2,1,0:T(8,128)}, u32[]{:S(2)}) %copy-start.2) | copy-done | bytes 2129944
  8.0 5.2 %shard_map.69 = (f32[4,104,640]{2,1,0:T(8,128)S(1)}, f32[6,104,640]{2,1,0:T(8,128)S(1)}, f32[4,104,640]{2,1,0:T(8,128)S(1)}, f32[104,128]{1,0:T(8,128)S(1)}, f32[112,128]{1,0:T(8,128)S(1)}) custom-call(f32[4,104,640]{2,1,0:T(8,128)S(1)} %collective-permute-done.1.halo_ref, f32[4,104,640]{2,1,0:T(8,128)S(1)} %get-tuple-element.33.inner_ref.scaled_ref, ...), custom_call_target="tpu_custom_call" | custom-call | tf_op jit(solution)/shard_map/pallas_call | solution.py:307
  13.3 4.5 %collective-permute-start.6 = (f32[4,104,640]{2,1,0:T(8,128)S(1)}, f32[4,104,640]{2,1,0:T(8,128)S(1)}, u32[]{:S(2)}, u32[]{:S(2)}) collective-permute-start(f32[4,104,640]{2,1,0:T(8,128)S(1)} %get-tuple-element.40.inner_ref), channel_id=1, source_target_pairs={{0,2},{2,0},{4,6},{6,4},{8,10},{10,8},{12,14},{14,12},{16,18},{18,... | collective-permute-start | bytes 3194888 | tf_op jit(solution)/shard_map/ppermute | solution.py:349
  17.8 0.0 collective-permute-start
  17.8 17.5 %collective-permute-done.4.halo_ref = f32[4,56,640]{2,1,0:T(8,128)S(1)} collective-permute-done((f32[4,56,640]{2,1,0:T(8,128)S(1)}, f32[4,56,640]{2,1,0:T(8,128)S(1)}, u32[]{:S(2)}, u32[]{:S(2)}) %collective-permute-start.4) | collective-permute-done | bytes 573472 | tf_op jit(solution)/shard_map/ppermute | solution.py:335
  35.3 1.3 %shard_map.71.refs_0_.outer_ref = f32[4,56,640]{2,1,0:T(8,128)S(1)} custom-call(f32[4,56,640]{2,1,0:T(8,128)S(1)} %collective-permute-done.4.halo_ref, f32[4,56,640]{2,1,0:T(8,128)S(1)} %get-tuple-element.35.refs_0_.outer_ref.scaled_ref, f32[6,104,640]{2,1,0:T(8,128)S(1)} %get-tuple-element.36.edge_ref, f32[4,104,640]{2,1,0:T(8,128)S(1)} %get-tuple-element.37.filled_ref, ...), custom_call_target="tpu_custom_call" | custom-call | tf_op jit(solution)/shard_map/pallas_call | solution.py:307
  36.6 2.6 %collective-permute-start.5 = (f32[4,56,640]{2,1,0:T(8,128)S(1)}, f32[4,56,640]{2,1,0:T(8,128)S(1)}, u32[]{:S(2)}, u32[]{:S(2)}) collective-permute-start(f32[4,56,640]{2,1,0:T(8,128)S(1)} %shard_map.71.refs_0_.outer_ref), channel_id=1, source_target_pairs={{0,126},{2,4},{4,2},{6,8},{8,6},{10,12},{12,10},{14,16},{16,14},{1... | collective-permute-start | bytes 1720328 | tf_op jit(solution)/shard_map/ppermute | solution.py:355
  39.2 1.4 %collective-permute-done.halo_ref = f32[4,48,640]{2,1,0:T(8,128)S(1)} collective-permute-done((f32[4,48,640]{2,1,0:T(8,128)S(1)}, f32[4,48,640]{2,1,0:T(8,128)S(1)}, u32[]{:S(2)}, u32[]{:S(2)}) %collective-permute-start) | collective-permute-done | bytes 491552 | tf_op jit(solution)/shard_map/ppermute | solution.py:335
  40.6 1.2 %shard_map.70 = (f32[4,40,640]{2,1,0:T(8,128)S(1)}, f32[4,8,640]{2,1,0:T(8,128)S(1)}) custom-call(f32[4,48,640]{2,1,0:T(8,128)S(1)} %collective-permute-done.halo_ref, f32[4,48,640]{2,1,0:T(8,128)S(1)} %get-tuple-element.31.refs_1_.outer_ref.scaled_ref, f32[6,104,640]{2,1,0:T(8,128)S(1)} %get-tuple-element.36.edge_ref, ...), custom_call_target="tpu_custom_call" | custom-call | tf_op jit(solution)/shard_map/pallas_call | solution.py:307
  41.7 2.6 %collective-permute-start.3 = (f32[4,40,640]{2,1,0:T(8,128)S(1)}, f32[4,40,640]{2,1,0:T(8,128)S(1)}, u32[]{:S(2)}, u32[]{:S(2)}) collective-permute-start(f32[4,40,640]{2,1,0:T(8,128)S(1)} %get-tuple-element.39.refs_1_.outer_ref), channel_id=1, source_target_pairs={{0,126},{2,4},{4,2},{6,8},{8,6},{10,12},{12,10},{14,16},{16,14},{1... | collective-permute-start | bytes 1228808 | tf_op jit(solution)/shard_map/ppermute | solution.py:355
  44.3 0.3 collective-permute-start.2
  44.6 0.0 collective-permute-done.6.halo_ref
  44.6 4.3 %shard_map.72 = (f32[4,104,640]{2,1,0:T(8,128)S(1)}, f32[6,104,640]{2,1,0:T(8,128)S(1)}, f32[4,8,640]{2,1,0:T(8,128)S(1)}) custom-call(f32[4,104,640]{2,1,0:T(8,128)S(1)} %collective-permute-done.6.halo_ref, f32[4,104,640]{2,1,0:T(8,128)S(1)} %get-tuple-element.40.inner_ref, f32[4,104,640]{2,1,0:T(8,128)S(1)} %get-tuple-element.33.inner_ref.scaled_ref, ...), custom_call_target="tpu_custom_call" | custom-call | tf_op jit(solution)/shard_map/pallas_call | solution.py:307
  48.9 2.0 %collective-permute-done.5.halo_ref = f32[4,56,640]{2,1,0:T(8,128)S(1)} collective-permute-done((f32[4,56,640]{2,1,0:T(8,128)S(1)}, f32[4,56,640]{2,1,0:T(8,128)S(1)}, u32[]{:S(2)}, u32[]{:S(2)}) %collective-permute-start.5) | collective-permute-done | bytes 573472 | tf_op jit(solution)/shard_map/ppermute | solution.py:355
  50.9 1.4 %shard_map.73 = (f32[4,56,640]{2,1,0:T(8,128)S(1)}, f32[4,8,640]{2,1,0:T(8,128)S(1)}) custom-call(f32[4,56,640]{2,1,0:T(8,128)S(1)} %collective-permute-done.5.halo_ref, f32[4,56,640]{2,1,0:T(8,128)S(1)} %shard_map.71.refs_0_.outer_ref, f32[6,104,640]{2,1,0:T(8,128)S(1)} %get-tuple-element.42.edge_ref, ...), custom_call_target="tpu_custom_call" | custom-call | tf_op jit(solution)/shard_map/pallas_call | solution.py:307
  52.3 2.7 %collective-permute-done.3.halo_ref = f32[4,40,640]{2,1,0:T(8,128)S(1)} collective-permute-done((f32[4,40,640]{2,1,0:T(8,128)S(1)}, f32[4,40,640]{2,1,0:T(8,128)S(1)}, u32[]{:S(2)}, u32[]{:S(2)}) %collective-permute-start.3) | collective-permute-done | bytes 409632 | tf_op jit(solution)/shard_map/ppermute | solution.py:355
  55.0 1.1 %shard_map.74 = (f32[4,40,640]{2,1,0:T(8,128)S(1)}, f32[4,8,640]{2,1,0:T(8,128)S(1)}) custom-call(f32[4,40,640]{2,1,0:T(8,128)S(1)} %collective-permute-done.3.halo_ref, f32[4,40,640]{2,1,0:T(8,128)S(1)} %get-tuple-element.39.refs_1_.outer_ref, f32[6,104,640]{2,1,0:T(8,128)S(1)} %get-tuple-element.42.edge_ref, ...), custom_call_target="tpu_custom_call" | custom-call | tf_op jit(solution)/shard_map/pallas_call | solution.py:307
  56.1 0.0 collective-permute-done.2.halo_ref
  56.1 0.4 shard_map.75
  56.5 3.2 %collective-permute-start.7 = (f32[168,128]{1,0:T(8,128)S(1)}, f32[168,128]{1,0:T(8,128)S(1)}, u32[]{:S(2)}, u32[]{:S(2)}) collective-permute-start(f32[168,128]{1,0:T(8,128)S(1)} %get-tuple-element.50.own_ref), channel_id=1, source_target_pairs={{0,1},{1,0},{2,3},{3,2},{4,5},{5,4},{6,7},{7,6},{8,9},{9,8},{10,11... | collective-permute-start | bytes 258056 | tf_op jit(solution)/shard_map/ppermute | solution.py:379
  59.8 1.9 %collective-permute-done.7.other_ref = f32[168,128]{1,0:T(8,128)S(1)} collective-permute-done((f32[168,128]{1,0:T(8,128)S(1)}, f32[168,128]{1,0:T(8,128)S(1)}, u32[]{:S(2)}, u32[]{:S(2)}) %collective-permute-start.7) | collective-permute-done | bytes 86048 | tf_op jit(solution)/shard_map/ppermute | solution.py:379
  61.6 0.1 shard_map.76
  61.8 15.4 %all_to_all.5.got_ref = f32[64,1,128]{2,1,0:T(1,128)S(1)} all-to-all(f32[64,1,128]{2,1,0:T(1,128)S(1)} %get-tuple-element.52), channel_id=1, replica_groups=mesh['tile'=64,'mem'=2] {'tile'}, dimensions={0} | all-to-all | bytes 65536 | tf_op jit(solution)/shard_map/all_to_all | solution.py:381
  77.1 1.7 %shard_map.77 = (f32[4,8,640]{2,1,0:T(8,128)}, f32[832,640]{1,0:T(8,128)}) custom-call(f32[64,1,128]{2,1,0:T(1,128)S(1)} %all_to_all.5.got_ref, f32[4,8,640]{2,1,0:T(8,128)S(1)} %get-tuple-element.53.merged_ref, f32[4,104,640]{2,1,0:T(8,128)S(1)} %get-tuple-element.54.inner_ref, f32[4,56,640]{2,1,0:T(8,128)S(1)} %get-tuple-element.55.refs_0_, ...), custom_call_target="tpu_custom_call" | custom-call | tf_op jit(solution)/shard_map/pallas_call | solution.py:307
Async XLA Ops:
  0.6 1.6 %copy-start.1 = (f32[26,4,8,640]{3,2,1,0:T(8,128)S(1)}, f32[26,4,8,640]{3,2,1,0:T(8,128)}, u32[]{:S(2)}) copy-start(f32[26,4,8,640]{3,2,1,0:T(8,128)} %param.6) | copy-start | bytes 6389764
  2.2 4.2 %copy-start = (f32[5,8,640]{2,1,0:T(8,128)S(1)}, f32[5,8,640]{2,1,0:T(8,128)}, u32[]{:S(2)}) copy-start(f32[5,8,640]{2,1,0:T(8,128)} %constant.2.clone.coef_ref) | copy-start | bytes 307204
  2.2 4.2 %copy-start.3 = (s32[8,640]{1,0:T(8,128)S(1)}, s32[8,640]{1,0:T(8,128)}, u32[]{:S(2)}) copy-start(s32[8,640]{1,0:T(8,128)} %mask_ref.1) | copy-start | bytes 61444
  2.2 4.2 %copy-start.4 = (s32[26]{0:T(128)S(1)}, s32[26]{0:T(128)}, u32[]{:S(2)}) copy-start(s32[26]{0:T(128)} %count_ref.1) | copy-start | bytes 316
  2.6 3.8 %collective-permute-start.1 = (f32[4,104,640]{2,1,0:T(8,128)S(1)}, f32[4,104,640]{2,1,0:T(8,128)S(1)}, u32[]{:S(2)}, u32[]{:S(2)}) collective-permute-start(f32[4,104,640]{2,1,0:T(8,128)S(1)} %get-tuple-element.33.inner_ref.scaled_ref), channel_id=1, source_target_pairs={{0,2},{2,0},{4,6},{6,4},{8,10},{10,8},{12,14},{14,12},{16,18},{18,... | collective-permute-start | bytes 3194888 | tf_op jit(solution)/shard_map/ppermute | solution.py:336
  4.1 31.2 %collective-permute-start.4 = (f32[4,56,640]{2,1,0:T(8,128)S(1)}, f32[4,56,640]{2,1,0:T(8,128)S(1)}, u32[]{:S(2)}, u32[]{:S(2)}) collective-permute-start(f32[4,56,640]{2,1,0:T(8,128)S(1)} %get-tuple-element.35.refs_0_.outer_ref.scaled_ref), channel_id=1, source_target_pairs={{0,126},{2,4},{4,2},{6,8},{8,6},{10,12},{12,10},{14,16},{16,14},{1... | collective-permute-start | bytes 1720328 | tf_op jit(solution)/shard_map/ppermute | solution.py:335
  6.4 1.6 %copy-start.2 = (f32[26,4,8,640]{3,2,1,0:T(8,128)S(1)}, f32[26,4,8,640]{3,2,1,0:T(8,128)}, u32[]{:S(2)}) copy-start(f32[26,4,8,640]{3,2,1,0:T(8,128)} %param.5) | copy-start | bytes 6389764
  13.3 31.3 %collective-permute-start.6 = (f32[4,104,640]{2,1,0:T(8,128)S(1)}, f32[4,104,640]{2,1,0:T(8,128)S(1)}, u32[]{:S(2)}, u32[]{:S(2)}) collective-permute-start(f32[4,104,640]{2,1,0:T(8,128)S(1)} %get-tuple-element.40.inner_ref), channel_id=1, source_target_pairs={{0,2},{2,0},{4,6},{6,4},{8,10},{10,8},{12,14},{14,12},{16,18},{18,... | collective-permute-start | bytes 3194888 | tf_op jit(solution)/shard_map/ppermute | solution.py:349
  17.8 22.7 %collective-permute-start = (f32[4,48,640]{2,1,0:T(8,128)S(1)}, f32[4,48,640]{2,1,0:T(8,128)S(1)}, u32[]{:S(2)}, u32[]{:S(2)}) collective-permute-start(f32[4,48,640]{2,1,0:T(8,128)S(1)} %get-tuple-element.31.refs_1_.outer_ref.scaled_ref), channel_id=1, source_target_pairs={{0,126},{2,4},{4,2},{6,8},{8,6},{10,12},{12,10},{14,16},{16,14},{1... | collective-permute-start | bytes 1474568 | tf_op jit(solution)/shard_map/ppermute | solution.py:335
  36.6 14.3 %collective-permute-start.5 = (f32[4,56,640]{2,1,0:T(8,128)S(1)}, f32[4,56,640]{2,1,0:T(8,128)S(1)}, u32[]{:S(2)}, u32[]{:S(2)}) collective-permute-start(f32[4,56,640]{2,1,0:T(8,128)S(1)} %shard_map.71.refs_0_.outer_ref), channel_id=1, source_target_pairs={{0,126},{2,4},{4,2},{6,8},{8,6},{10,12},{12,10},{14,16},{16,14},{1... | collective-permute-start | bytes 1720328 | tf_op jit(solution)/shard_map/ppermute | solution.py:355
  41.7 13.2 %collective-permute-start.3 = (f32[4,40,640]{2,1,0:T(8,128)S(1)}, f32[4,40,640]{2,1,0:T(8,128)S(1)}, u32[]{:S(2)}, u32[]{:S(2)}) collective-permute-start(f32[4,40,640]{2,1,0:T(8,128)S(1)} %get-tuple-element.39.refs_1_.outer_ref), channel_id=1, source_target_pairs={{0,126},{2,4},{4,2},{6,8},{8,6},{10,12},{12,10},{14,16},{16,14},{1... | collective-permute-start | bytes 1228808 | tf_op jit(solution)/shard_map/ppermute | solution.py:355
  44.3 11.8 %collective-permute-start.2 = (f32[4,8,640]{2,1,0:T(8,128)S(1)}, f32[4,8,640]{2,1,0:T(8,128)S(1)}, u32[]{:S(2)}, u32[]{:S(2)}) collective-permute-start(f32[4,8,640]{2,1,0:T(8,128)S(1)} %get-tuple-element.38.refs_2_.outer_ref), channel_id=1, source_target_pairs={{0,126},{2,4},{4,2},{6,8},{8,6},{10,12},{12,10},{14,16},{16,14},{1... | collective-permute-start | bytes 245768 | tf_op jit(solution)/shard_map/ppermute | solution.py:355
  56.5 5.1 %collective-permute-start.7 = (f32[168,128]{1,0:T(8,128)S(1)}, f32[168,128]{1,0:T(8,128)S(1)}, u32[]{:S(2)}, u32[]{:S(2)}) collective-permute-start(f32[168,128]{1,0:T(8,128)S(1)} %get-tuple-element.50.own_ref), channel_id=1, source_target_pairs={{0,1},{1,0},{2,3},{3,2},{4,5},{5,4},{6,7},{7,6},{8,9},{9,8},{10,11... | collective-permute-start | bytes 258056 | tf_op jit(solution)/shard_map/ppermute | solution.py:379
